TPU v7x, 32 devices: a whole 2x2x4 slice. The times are simulated.
32 devices in a mesh: seq: 16 (over z, y, x), fsdp: 2 (over core).
Axes of the slice: x: 2, y: 2, z: 4, core: 2. Of those that a mesh axis runs over, the one named last changes fastest.
Arguments:
- hidden_in: bfloat16 [2, 8192, 1536], P('fsdp', 'seq'), may hold values from -6 to 6
- norm_gain: float32 [1536], replicated, may hold values from 0.5 to 1.5
- in_weight: bfloat16 [1536, 6448], P('fsdp'), may hold values from -0.15625 to 0.15625
- conv_weight: float32 [4, 3328], replicated, may hold values from -3 to 3
- conv_bias: float32 [3328], replicated, may hold values from -3 to 3
- step_bias: float32 [48], replicated, may hold values from -2 to 0
- decay_log: float32 [48], replicated, as said below
- skip_gain: float32 [48], replicated, may hold values from 0.5 to 2
- gate_gain: float32 [3072], replicated, may hold values from 0.5 to 1.5
- out_weight: bfloat16 [3072, 1536], P('fsdp'), may hold values from -0.109375 to 0.109375
- cotangent: bfloat16 [2, 8192, 1536], P('fsdp', 'seq'), may hold values from -6 to 6
Outputs:
- block_out: bfloat16 [2, 8192, 1536], P('fsdp', 'seq')
- input_grad: bfloat16 [2, 8192, 1536], P('fsdp', 'seq')
- norm_gain_grad: float32 [1536], replicated
- in_weight_grad: float32 [1536, 6448], P('fsdp')
- conv_weight_grad: float32 [4, 3328], replicated
- conv_bias_grad: float32 [3328], replicated
- step_bias_grad: float32 [48], replicated
- decay_log_grad: float32 [48], replicated
- skip_gain_grad: float32 [48], replicated
- gate_gain_grad: float32 [3072], replicated
- out_weight_grad: float32 [3072, 1536], P('fsdp')
Inputs may be any that keep to these rules, and one draw needn't show every extreme that they name: `decay_log`: natural logarithm of each head's decay rate per unit of step size.
All inputs are finite; a program needn't handle non-finite values.
Results may differ from a plain program's by a relative error of at most 0.012.
The roundings to bfloat16 on the way count: a program that leaves them out, or rounds other values in their place, can miss the bound.
Values may be sent and summed in bfloat16 or wider, within the bound.
No kernel may reach another device: no remote copies, remote signals or barrier semaphores. Data moves between devices by JAX's collectives and lax.ppermute only.
A program may use at most 512 MiB of HBM per device.

v0:
```python
import jax
import jax.numpy as jnp
from jax import lax
from jax.sharding import PartitionSpec as P

HEADS = 48
HEAD_DIM = 64
STATE = 128
CONV = 4
SPAN = 256
INNER = 3072
CONV_CH = 3328


EPSILON = 1e-05
HIGHEST = lax.Precision.HIGHEST


def from_behind(value, axis, by):
    devices = lax.axis_size(axis)
    pairs = [(i, i + by) for i in range(devices) if 0 <= i + by < devices]
    return lax.ppermute(value, axis, pairs)


def carried_in(part, axis, combine, identity, reverse):
    count = lax.axis_size(axis)
    place = lax.axis_index(axis)
    ahead = count - 1 - place if reverse else place
    gathered = jax.tree.map(lambda a: lax.all_gather(a, axis), part)
    state = jax.tree.map(lambda a, e: jnp.zeros_like(a) + jnp.asarray(e, a.dtype), part, identity)

    def one(step, state):
        source = count - 1 - step if reverse else step
        return combine(
            state, jax.tree.map(lambda a: lax.dynamic_index_in_dim(a, source, 0, False), gathered)
        )

    return lax.fori_loop(0, ahead, one, state)


def norm_input(rows, gain):
    rescale = lax.rsqrt(jnp.mean(rows * rows, axis=-1, keepdims=True) + EPSILON)
    return rows * rescale * gain


def span_step(carry_state, pieces):
    values, writes, readout, log_decay, step_size = pieces
    extent = values.shape[0]
    running = jnp.cumsum(log_decay, axis=0)
    scaled = values * step_size[:, :, None]
    scores = jnp.dot(readout, writes.T, precision=HIGHEST)
    causal = (jnp.arange(extent)[:, None] >= jnp.arange(extent)[None, :])[:, :, None]
    spread = running[:, None, :] - running[None, :, :]
    weights = jnp.where(causal, jnp.exp(jnp.where(causal, spread, 0.0)), 0.0) * scores[:, :, None]
    inside = jnp.einsum("tsh,shp->thp", weights, scaled, precision=HIGHEST)
    carried = jnp.exp(running)[:, :, None] * jnp.einsum(
        "tn,hpn->thp", readout, carry_state, precision=HIGHEST
    )
    remain = jnp.exp(running[-1][None, :] - running)
    added_state = jnp.einsum("sh,shp,sn->hpn", remain, scaled, writes, precision=HIGHEST)
    return (jnp.exp(running[-1])[:, None, None] * carry_state + added_state, inside + carried)


def local_forward(projected, halo_rows, conv_weight, conv_bias, step_bias, decay_log, skip_gain):
    extent = projected.shape[0]
    padded = jnp.concatenate([halo_rows, projected[:, INNER : INNER + CONV_CH]], axis=0)
    mixture = conv_bias + conv_weight[0] * padded[0:extent]
    for offset in range(1, CONV):
        mixture = mixture + conv_weight[offset] * padded[offset : offset + extent]
    active = jax.nn.silu(mixture)
    values = active[:, :INNER].reshape(extent, HEADS, HEAD_DIM)
    writes = active[:, INNER : INNER + STATE]
    readout = active[:, INNER + STATE :]
    step_size = jax.nn.softplus(projected[:, INNER + CONV_CH :] + step_bias)
    log_decay = -jnp.exp(decay_log) * step_size
    blocks = extent // SPAN

    def block_view(array):
        return array.reshape((blocks, SPAN) + array.shape[1:])

    initial = jnp.zeros((HEADS, HEAD_DIM, STATE), jnp.float32)
    last_state, span_out = lax.scan(
        span_step,
        initial,
        (
            block_view(values),
            block_view(writes),
            block_view(readout),
            block_view(log_decay),
            block_view(step_size),
        ),
    )
    scanned_local = span_out.reshape(extent, HEADS, HEAD_DIM) + skip_gain[:, None] * values
    cumulative = jnp.cumsum(log_decay, axis=0)
    return (scanned_local, last_state, jnp.exp(cumulative[-1]), jnp.exp(cumulative), readout)


def local_output(projected, scanned_local, decay_start, readout, entering, gate_gain):
    extent = projected.shape[0]
    scanned = scanned_local + decay_start[:, :, None] * jnp.einsum(
        "tn,hpn->thp", readout, entering, precision=HIGHEST
    )
    gated_out = scanned.reshape(extent, INNER) * jax.nn.silu(projected[:, :INNER])
    return norm_input(gated_out, gate_gain)


def link_states(earlier, latter):
    return (earlier[0] * latter[1][..., None, None] + latter[0], earlier[1] * latter[1])


def link_back(earlier, latter):
    return (latter[0] + latter[1][..., None, None] * earlier[0], earlier[1] * latter[1])


def add_rows(left, shard_rows):
    return jnp.dot(left, shard_rows, preferred_element_type=jnp.float32)


def times_rows(left, shard_rows):
    return lax.dot_general(
        left, shard_rows, (((1,), (1,)), ((), ())), preferred_element_type=jnp.float32
    )


def weight_term(left, right):
    return lax.dot_general(
        left, right, (((0,), (0,)), ((), ())), preferred_element_type=jnp.float32
    )


def local(
    hidden_in,
    norm_gain,
    in_weight,
    conv_weight,
    conv_bias,
    step_bias,
    decay_log,
    skip_gain,
    gate_gain,
    out_weight,
    cotangent,
):
    rows_in = hidden_in[0].astype(jnp.float32)
    upstream = cotangent[0]
    tokens = rows_in.shape[0]
    half = tokens // 2
    forward_pair = jax.vmap(local_forward, in_axes=(0, 0, None, None, None, None, None))
    output_pair = jax.vmap(local_output, in_axes=(0, 0, 0, 0, 0, None))
    normed_f, norm_pull = jax.vjp(norm_input, rows_in, norm_gain)
    normed = normed_f.astype(jnp.bfloat16)
    projected = add_rows(normed, lax.all_gather(in_weight, "fsdp", axis=0, tiled=True))
    paired = projected.reshape(2, half, projected.shape[1])
    halo_rows = from_behind(paired[:, half - CONV + 1 :, INNER : INNER + CONV_CH], "seq", 1)
    (scanned_local, local_state, device_decay, decay_start, readout), local_pull = jax.vjp(
        forward_pair, paired, halo_rows, conv_weight, conv_bias, step_bias, decay_log, skip_gain
    )
    identity = (jnp.zeros_like(local_state), jnp.ones_like(device_decay))
    before = carried_in((local_state, device_decay), "seq", link_states, identity, False)
    entering = before[0]
    gated_norm, output_pull = jax.vjp(
        output_pair, paired, scanned_local, decay_start, readout, entering, gate_gain
    )
    normed_out = gated_norm.reshape(tokens, INNER).astype(jnp.bfloat16)
    branch_out = add_rows(normed_out, lax.all_gather(out_weight, "fsdp", axis=0, tiled=True))
    block_out = (rows_in + branch_out).astype(jnp.bfloat16)
    grad_normed_out = times_rows(upstream, lax.all_gather(out_weight, "fsdp", axis=0, tiled=True))
    out_grad_part = lax.psum_scatter(
        weight_term(normed_out, upstream).astype(jnp.bfloat16),
        "fsdp",
        scatter_dimension=0,
        tiled=True,
    ).astype(jnp.float32)
    (
        grad_proj_out,
        grad_scanned_local,
        grad_decay_start,
        grad_readout,
        grad_entering,
        gate_gain_grad,
    ) = output_pull(grad_normed_out.reshape(2, half, INNER))
    behind = carried_in((grad_entering, device_decay), "seq", link_back, identity, True)
    decay_grad = jnp.sum(entering * behind[0], axis=(2, 3))
    (
        grad_proj_local,
        grad_halo,
        conv_weight_grad,
        conv_bias_grad,
        step_bias_grad,
        decay_log_grad,
        skip_grad,
    ) = local_pull((grad_scanned_local, behind[0], decay_grad, grad_decay_start, grad_readout))
    returned = from_behind(grad_halo.astype(jnp.bfloat16), "seq", -1).astype(grad_halo.dtype)
    returned_full = jnp.pad(returned, ((0, 0), (half - CONV + 1, 0), (INNER, HEADS)))
    grad_projected = (
        (grad_proj_local + grad_proj_out + returned_full)
        .reshape(tokens, projected.shape[1])
        .astype(jnp.bfloat16)
    )
    in_grad_part = lax.psum_scatter(
        weight_term(normed, grad_projected).astype(jnp.bfloat16),
        "fsdp",
        scatter_dimension=0,
        tiled=True,
    ).astype(jnp.float32)
    grad_normed = times_rows(grad_projected, lax.all_gather(in_weight, "fsdp", axis=0, tiled=True))
    grad_rows, norm_gain_grad = norm_pull(grad_normed)
    input_grad = (upstream.astype(jnp.float32) + grad_rows).astype(jnp.bfloat16)
    summed = lax.psum(
        (
            in_grad_part,
            out_grad_part,
            norm_gain_grad,
            conv_weight_grad,
            conv_bias_grad,
            step_bias_grad,
            decay_log_grad,
            skip_grad,
            gate_gain_grad,
        ),
        "seq",
    )
    small_sums = (
        lax.psum(summed[2].astype(jnp.bfloat16), "fsdp").astype(jnp.float32),
        lax.psum(summed[3].astype(jnp.bfloat16), "fsdp").astype(jnp.float32),
        lax.psum(summed[4].astype(jnp.bfloat16), "fsdp").astype(jnp.float32),
        lax.psum(summed[5].astype(jnp.bfloat16), "fsdp").astype(jnp.float32),
        lax.psum(summed[6].astype(jnp.bfloat16), "fsdp").astype(jnp.float32),
        lax.psum(summed[7].astype(jnp.bfloat16), "fsdp").astype(jnp.float32),
        lax.psum(summed[8].astype(jnp.bfloat16), "fsdp").astype(jnp.float32),
    )
    return (
        block_out[None],
        input_grad[None],
        small_sums[0],
        summed[0],
        small_sums[1],
        small_sums[2],
        small_sums[3],
        small_sums[4],
        small_sums[5],
        small_sums[6],
        summed[1],
    )


def solution(mesh):
    return jax.shard_map(
        local,
        mesh=mesh,
        in_specs=(
            P("fsdp", "seq", None),
            P(),
            P("fsdp", None),
            P(),
            P(),
            P(),
            P(),
            P(),
            P(),
            P("fsdp", None),
            P("fsdp", "seq", None),
        ),
        out_specs=(
            P("fsdp", "seq", None),
            P("fsdp", "seq", None),
            P(),
            P("fsdp", None),
            P(),
            P(),
            P(),
            P(),
            P(),
            P(),
            P("fsdp", None),
        ),
        check_vma=False,
    )
```

profile of v0, /device:TPU:0, one launch (start us, length us, event | category | flops | bytes accessed | tf_op | source)
XLA Modules:
  0.0 2745.4 jit_solution(1721198932213076496)
XLA Ops:
  10.3 36.7 %all-gather.8.cloned.1.call-done = bf16[1536,6448]{0,1:T(8,128)(2,1)} async-done(((bf16[768,6448]{0,1:T(8,128)(2,1)}), bf16[1536,6448]{0,1:T(8,128)(2,1)}) %all-gather.8.cloned.1.call-update) | async-done | bytes 19808272 | tf_op jit(solution)/shard_map/all_gather | solution.py:152
  47.1 14.7 fusion.10
  61.8 3.1 slice.103
  64.9 2.9 copy-done.2
  71.2 2.6 copy.199
  73.8 4.4 collective-permute-start
  78.8 6.3 slice.104
  87.7 17.2 fusion.30
  105.3 2.4 copy-done.1
  109.8 7.4 fusion.77
  119.0 38.5 %all-gather = f32[32,1,48]{2,1,0:T(1,128)S(1)} all-gather(f32[2,1,48]{2,1,0:T(1,128)S(1)} %bitcast.230), channel_id=2, replica_groups=mesh['seq'=16,'fsdp'=2] {'seq'}, dimensions={0}, use_global_device_ids=true | all-gather | bytes 6528 | tf_op jit(solution)/shard_map/all_gather | solution.py:29
  157.5 2.5 fusion.113
  160.0 8.0 fusion.87
  167.9 458.3 %all-gather.12.cloned.1.call-done = f32[32,48,64,128]{3,2,1,0:T(8,128)} async-done(((f32[2,48,64,128]{3,2,1,0:T(8,128)}), f32[32,48,64,128]{3,2,1,0:T(8,128)}) %all-gather.12.cloned.1.call-update) | async-done | bytes 50331664 | tf_op jit(solution)/shard_map/all_gather | solution.py:29
  626.7 6.2 fusion.107
  632.9 33.2 %fusion.34 = f32[2,256,48,64]{1,3,2,0:T(8,128)S(1)} fusion(f32[2,256,48,64]{1,3,2,0:T(8,128)S(1)} %fusion.107, f32[2,256,48,64]{1,3,2,0:T(8,128)} %bitcast.209, f32[2,256,48,64]{1,3,2,0:T(8,128)S(1)} %copy-done.5, f32[2,256,256]{2,1,0:T(8,128)S(1)} %copy-done.32, f32[2,256,48]{1,2,0:T(8,128)S(1)} %copy.204, pred[256,256]{1,0:T(8,128)(4,1)S(1)} %copy-done.44, ...), kind=kOutput, calls=%fused_computation.62 | convolution fusion | flops 4868014080 | bytes 26050752 | tf_op jit(solution)/shard_map/jvp(vmap())/while/body/eval_jaxpr/tsh,shp->thp/dot_general | solution.py:55
  666.2 8.0 multiply_reduce_fusion.11
  674.3 13.0 multiply_reduce_fusion.5
  687.3 13.9 multiply_reduce_fusion.6
  701.1 2.6 copy-done
  703.8 8.2 fusion.44
  712.2 4.9 copy.214
  717.1 9.4 convolution_convert_fusion.1
  726.5 38.9 %fusion.13 = (f32[2,256,48]{1,2,0:T(8,128)}, f32[2,256,48]{1,2,0:T(8,128)}, f32[2,256,256]{2,1,0:T(8,128)}) fusion(f32[2,256,256]{2,1,0:T(8,128)} %fusion.113, f32[2,256,48]{1,2,0:T(8,128)S(1)} %copy.204, pred[256,256]{1,0:T(8,128)(4,1)} %iota_compare_fusion, f32[2,48,64,256]{3,2,1,0:T(8,128)} %bitcast.201, f32[2,256,48,64]{1,3,2,0:T(8,128)} %bitcast.210, ...), kind=kOutput, calls=%fused_computation.19 | convolution fusion | flops 4902436864 | bytes 14090240 | tf_op jit(solution)/shard_map/transpose(jvp(vmap()))/while/body/eval_jaxpr/tsh,shp->thp/dot_general | solution.py:55
  765.6 10.1 multiply_reduce_fusion.8
  781.8 5.6 fusion.95
  787.4 7.8 fusion.92
  795.2 2.4 fusion.91
  797.6 461.5 %all-gather.14.cloned.1.call-done = f32[32,48,64,128]{3,2,1,0:T(8,128)} async-done(((f32[2,48,64,128]{3,2,1,0:T(8,128)}), f32[32,48,64,128]{3,2,1,0:T(8,128)}) %all-gather.14.cloned.1.call-update) | async-done | bytes 50331664 | tf_op jit(solution)/shard_map/all_gather | solution.py:29
  1261.1 75.4 %while.21 = (s32[]{:T(128)}, f32[2,48,64,128]{3,2,1,0:T(8,128)}, s32[]{:T(128)}, f32[16,2,48,64,128]{4,3,2,1,0:T(8,128)}, f32[16,2,48]{2,1,0:T(2,128)S(1)}, /*index=5*/s32[]{:T(128)}, s32[]{:T(128)}, s32[]{:T(128)}, s32[]{:T(128)}) while((s32[]{:T(128)}, f32[2,48,64,128]{3,2,1,0:T(8,128)}, s32[]{:T(128)}, f32[16,2,48,64,128]{4,3,2,1,0:T(8,128)}, ...), condition=%wide.region_8.9_spmd, body=%wide.region_7.8_spmd.sunk | while | flops 1572870 | bytes 9438491 | solution.py:38
  1261.1 4.9 bitcast_add_fusion.8
  1266.0 5.7 bitcast_add_fusion.8
  1271.7 6.4 bitcast_add_fusion.8
  1278.2 4.9 bitcast_add_fusion.8
  1283.0 4.9 bitcast_add_fusion.8
  1287.9 4.9 bitcast_add_fusion.8
  1292.7 4.9 bitcast_add_fusion.8
  1297.6 4.9 bitcast_add_fusion.8
  1302.5 4.9 bitcast_add_fusion.8
  1307.4 4.9 bitcast_add_fusion.8
  1312.2 4.9 bitcast_add_fusion.8
  1317.1 4.9 bitcast_add_fusion.8
  1322.0 4.9 bitcast_add_fusion.8
  1326.8 4.9 bitcast_add_fusion.8
  1331.7 4.9 bitcast_add_fusion.8
  1336.6 7.1 fusion.103
  1343.7 26.3 multiply_reduce_fusion.4
  1373.3 2.6 multiply_reduce_fusion.13
  1377.4 5.0 reduce-window.46
  1382.6 5.9 reduce-window.44
  1389.6 9.8 fusion.100
  1400.9 5.5 bitcast_add_fusion.2
  1406.5 23.1 multiply_reduce_fusion.2
  1429.6 8.6 broadcast_multiply_fusion
  1438.2 10.9 pad_add_fusion
  1449.1 3.9 copy-done.6
  1456.6 8.6 split.9
  1466.1 9.2 add_convert_fusion
  1475.3 9.7 copy.235
  1485.0 16.8 convolution_convert_fusion
  1502.7 10.9 fusion.74
  1513.8 19.7 fusion.62
  1535.6 1195.2 %all-reduce.21 = (bf16[1536]{0:T(1024)(128)(2,1)S(1)}, f32[768,6448]{0,1:T(8,128)}, bf16[4,3328]{1,0:T(4,128)(2,1)S(1)}, bf16[3328]{0:T(1024)(128)(2,1)S(1)}, bf...) all-reduce(f32[1536]{0:T(1024)S(1)} %get-tuple-element.486, ...), channel_id=1, replica_groups=mesh['seq'=16,'fsdp'=2] {'seq'}, use_global_device_ids=true, to_apply=%region_24.25 | all-reduce | flops 7332752 | bytes 43996512 | tf_op jit(solution)/shard_map/psum | solution.py:209
  2730.8 3.5 all-reduce.19
  (233 shorter events, 41.9 us)
Async XLA Ops:
  7.2 39.9 %copy-start.56 = (f32[1536]{0:T(1024)S(1)}, f32[1536]{0:T(1024)}, u32[]{:S(2)}) copy-start(f32[1536]{0:T(1024)} %param.16) | copy-start | bytes 18436
  7.2 39.8 %all-gather.8.cloned.1.call-start = ((), (), s32[]{:S(2)}) async-start(), calls=%async_computation.2 | async-start | bytes 29712384 | tf_op jit(solution)/shard_map/all_gather | solution.py:152
  8.0 618.3 %all-gather.12.cloned.1.call-start = ((), (), s32[]{:S(2)}) async-start(), calls=%async_computation.6 | async-start | bytes 53477376 | tf_op jit(solution)/shard_map/all_gather | solution.py:29
  9.5 37.5 %copy-start.50 = (f32[512]{0:T(512)}, f32[512]{0:T(512)S(1)}, u32[]{:S(2)}) copy-start(f32[512]{0:T(512)S(1)} %fusion.127) | copy-start | bytes 6148
  10.3 77.4 %copy-start.34 = (f32[3328]{0:T(1024)}, f32[3328]{0:T(1024)S(1)}, u32[]{:S(2)}) copy-start(f32[3328]{0:T(1024)S(1)} %get-tuple-element.490) | copy-start | bytes 39940
  10.3 77.4 %copy-start.36 = (f32[3328]{0:T(1024)}, f32[3328]{0:T(1024)S(1)}, u32[]{:S(2)}) copy-start(f32[3328]{0:T(1024)S(1)} %get-tuple-element.491) | copy-start | bytes 39940
  10.3 77.4 %copy-start.38 = (f32[3328]{0:T(1024)}, f32[3328]{0:T(1024)S(1)}, u32[]{:S(2)}) copy-start(f32[3328]{0:T(1024)S(1)} %get-tuple-element.492) | copy-start | bytes 39940
  10.3 54.6 %copy-start.61 = (f32[48]{0:T(128)}, f32[48]{0:T(128)S(1)}, u32[]{:S(2)}) copy-start(f32[48]{0:T(128)S(1)} %exponential_negate_fusion) | copy-start | bytes 580
  61.7 6.0 copy-start.2
  61.7 6.0 copy-start.59
  69.6 15.4 copy-start.14
  71.2 13.8 copy-start.17
  73.8 12.0 collective-permute-start
  87.7 17.2 copy-start.7
  104.9 4.9 copy-start.29
  104.9 4.9 copy-start.54
  105.3 4.5 copy-start.3
  117.3 556.9 %all-gather.10.cloned.1.call-start = ((), (), s32[]{:S(2)}) async-start(), calls=%async_computation.3 | async-start | bytes 14155776 | tf_op jit(solution)/shard_map/all_gather | solution.py:165
  118.0 1141.1 %all-gather.14.cloned.1.call-start = ((), (), s32[]{:S(2)}) async-start(), calls=%async_computation.7 | async-start | bytes 53477376 | tf_op jit(solution)/shard_map/all_gather | solution.py:29
  118.8 607.6 %copy-start.41 = (f32[2,256,48]{1,2,0:T(8,128)}, f32[2,256,48]{1,2,0:T(8,128)S(1)}, u32[]{:S(2)}) copy-start(f32[2,256,48]{1,2,0:T(8,128)S(1)} %copy.204) | copy-start | bytes 294916
  626.7 6.2 copy-start.5
  626.7 6.2 copy-start.32
  626.7 6.2 copy-start.44
  626.7 6.2 copy-start.63
  632.9 33.2 %copy-start.4 = (f32[2,256,48,64]{1,3,2,0:T(8,128)}, f32[2,256,48,64]{1,3,2,0:T(8,128)S(1)}, u32[]{:S(2)}) copy-start(f32[2,256,48,64]{1,3,2,0:T(8,128)S(1)} %fusion.107) | copy-start | bytes 18874372
  666.2 8.0 copy-start.9
  666.2 8.0 copy-start.52
  674.2 13.0 copy-start.10
  674.2 13.0 copy-start.11
  712.0 801.6 %reduce-scatter.5.cloned.1.call-start = ((), (), s32[]{:S(2)}) async-start(), calls=%async_computation.5 | async-start | bytes 14155776 | tf_op jit(solution)/shard_map/reduce_scatter | solution.py:168
  765.4 770.2 %reduce-scatter.3.cloned.1.call-start = ((), (), s32[]{:S(2)}) async-start(), calls=%async_computation.4 | async-start | bytes 29712384 | tf_op jit(solution)/shard_map/reduce_scatter | solution.py:200
  787.4 7.8 copy-start.20
  1336.5 7.1 copy-start.30
  1336.5 7.1 copy-start.33
  1336.5 7.1 copy-start.42
  1336.5 7.2 copy-start.45
  1370.0 5.8 copy-start.16
  1371.8 4.1 copy-start.18
  1371.8 4.1 copy-start.19
  1371.8 4.1 copy-start.24
  1371.8 4.1 copy-start.25
  1371.8 4.1 copy-start.26
  1371.8 4.1 copy-start.27
  1375.9 23.5 copy-start.21
  1376.5 24.4 slice-start
  1389.6 11.3 slice-start.1
  1400.9 5.5 copy-start.8
  1400.9 5.5 copy-start.23
  1406.4 23.2 copy-start.35
  1406.4 23.2 copy-start.37
  1406.4 23.2 copy-start.39
  1406.4 23.1 copy-start.40
  1438.2 17.1 copy-start.55
  1438.2 17.1 copy-start.60
  1438.2 17.1 copy-start.62
  1449.1 3.9 copy-start.6
  1454.0 11.2 collective-permute-start.1
  1475.3 9.7 copy-start.13
  1475.3 9.7 copy-start.51
  1475.3 9.7 copy-start.57
  1502.7 10.9 copy-start.43
  1502.7 11.0 copy-start.65
  1513.7 19.7 copy-start.49
  1513.7 19.7 copy-start.22
  (12 other events, 21.3 us)
Sparse Core Ops, SparseCore 0:
  9.6 37.4 all-gather.7
  117.4 508.8 all-gather.11
  627.8 20.0 all-gather.9
  712.1 546.9 all-gather.13
  1261.8 15.9 reduce-scatter.4
  1502.0 29.0 reduce-scatter.2
where the time goes:
time: 2750 us
  blocking collectives  1240 us (45%)
  waiting for transfers between devices  958 us (35%)
  matrix products  249 us (9%)
  other arithmetic  209 us (8%)
  local copies, waits for them, and re-layouts  70.6 us (3%)
    psum x1, blocking collectives, local(): lax.psum((in_grad_part, out_grad_part, norm_gain_grad, conv_weight_grad,...  1200 us
    all_gather x2, waiting for transfers between devices, carried_in(): gathered = jax.tree.map(lambda a: lax.all_gather(a, axis), part)  920 us
    dot_general x3, matrix products, span_step(): inside = jnp.einsum('tsh,shp->thp', weights, scaled, precision=HIGHEST)  98.4 us
    add x15, other arithmetic, link_back(): latter[0] + latter[1][..., None, None] * earlier[0]  75.4 us
  transfers between devices with their start and end apart: 8, of which 3 were waited for; matrix products, arithmetic and copies ran while one was open for 15% of the time, Pallas kernels for 0%

commit v1 on v0

v1 whole, which is shorter than its diff:
```python
import functools

import jax
import jax.numpy as jnp
from jax import lax
from jax.experimental import pallas as pl
from jax.experimental.pallas import tpu as pltpu
from jax.sharding import PartitionSpec as P

HEADS = 48
HEAD_DIM = 64
STATE = 128
CONV = 4
INNER = 3072
CONV_CH = 3328
EPSILON = 1e-05

QUARTERS = 4
Q_HEADS = HEADS // QUARTERS
Q_LANES = INNER // QUARTERS
TILE = 128
Q_TILES = Q_LANES // TILE
EDGE = 16
PAYLOAD = STATE + EDGE
ROWS = 64
SUB = 128
FAR = -1e30
VMEM = 60 * 1024 * 1024
HIGHEST = lax.Precision.HIGHEST
F32 = jnp.float32
BF16 = jnp.bfloat16


def params():
    return pltpu.CompilerParams(vmem_limit_bytes=VMEM)


def low_lanes():
    return lax.broadcasted_iota(jnp.int32, (1, TILE), 1) < HEAD_DIM


def pick(per_head, tile):
    return jnp.where(
        low_lanes(),
        per_head[:, 2 * tile : 2 * tile + 1],
        per_head[:, 2 * tile + 1 : 2 * tile + 2],
    )


def head_columns(channels, columns, offset):
    row = lax.broadcasted_iota(jnp.int32, (channels, columns), 0)
    col = lax.broadcasted_iota(jnp.int32, (channels, columns), 1) - offset
    return ((row >= HEAD_DIM * col) & (row < HEAD_DIM * col + HEAD_DIM)).astype(BF16)


def head_sums(wide, selector):
    high = wide.astype(BF16)
    rest = (wide - high.astype(F32)).astype(BF16)
    return jnp.dot(high, selector, preferred_element_type=F32) + jnp.dot(
        rest, selector, preferred_element_type=F32
    )


def dot(left, right):
    return jnp.dot(left, right, preferred_element_type=F32)


def dot_last(left, right, precision=None):
    return lax.dot_general(
        left,
        right,
        (((1,), (1,)), ((), ())),
        preferred_element_type=F32,
        precision=precision,
    )


def dot_first(left, right, precision=None):
    return lax.dot_general(
        left,
        right,
        (((0,), (0,)), ((), ())),
        preferred_element_type=F32,
        precision=precision,
    )


def mixture_of(conv_input, seq, lanes, weight, bias):
    total = bias
    for tap in range(CONV):
        start = EDGE - CONV + 1 + tap
        total = total + weight[tap : tap + 1] * conv_input[seq, start : start + 256, lanes]
    return total


def silu_slope(value):
    gate = jax.nn.sigmoid(value)
    return gate * (1.0 + value * (1.0 - gate))


def step_kernel(
    conv_input,
    weight,
    bias,
    small,
    bc_ref,
    bt_ref,
    scores_ref,
    scores_t_ref,
    step_ref,
    sum_ref,
    step_q_ref,
    sum_q_ref,
    sum_t_ref,
):
    row = lax.broadcasted_iota(jnp.int32, (256, 256), 0)
    col = lax.broadcasted_iota(jnp.int32, (256, 256), 1)
    lower = (row >= col).astype(F32)
    head = lax.broadcasted_iota(jnp.int32, (1, TILE), 1) < HEADS
    for seq in range(2):
        mixture = mixture_of(conv_input, seq, slice(0, 256), weight[...], bias[...])
        active = mixture * jax.nn.sigmoid(mixture)
        bc_ref[seq] = active
        writes, readout = active[:, :STATE], active[:, STATE:]
        bt_ref[seq] = writes.T.astype(BF16)
        scores = dot_last(readout, writes, HIGHEST)
        scores_ref[seq] = scores
        scores_t_ref[seq] = scores.T
        raw = jnp.where(head, conv_input[seq, EDGE : EDGE + 256, 256:384] + small[0:1], 0.0)
        step = jnp.maximum(raw, 0.0) + jnp.log1p(jnp.exp(-jnp.abs(raw)))
        log_decay = -jnp.exp(small[1:2]) * step
        running = jnp.dot(lower, log_decay, preferred_element_type=F32, precision=HIGHEST)
        step_ref[seq] = step
        sum_ref[seq] = running
        for quarter in range(QUARTERS):
            shift = (TILE - Q_HEADS * quarter) % TILE
            step_q = pltpu.roll(step, shift, 1) if shift else step
            sum_q = pltpu.roll(running, shift, 1) if shift else running
            step_q_ref[quarter, seq] = step_q[:, :Q_HEADS]
            sum_q_ref[quarter, seq] = sum_q[:, :Q_HEADS]
            sum_t_ref[quarter, seq] = sum_q.T[:EDGE]


def state_kernel(conv_input, weight, bias, step_q, sum_q, bt_ref, x_ref, payload_ref):
    index = lax.broadcasted_iota(jnp.int32, (EDGE, TILE), 0)
    for seq in range(2):
        running = sum_q[0, seq]
        last = running[255:256]
        scale = step_q[0, seq] * jnp.exp(last - running)
        whole = jnp.exp(last)
        for tile in range(Q_TILES):
            lanes = slice(TILE * tile, TILE * tile + TILE)
            mixture = mixture_of(conv_input, seq, lanes, weight[:, lanes], bias[:, lanes])
            x = mixture * jax.nn.sigmoid(mixture)
            x_ref[seq, :, lanes] = x
            added = dot(bt_ref[seq], (x * pick(scale, tile)).astype(BF16))
            payload_ref[0, seq, :STATE, lanes] = added.astype(BF16)
            decay = pick(whole, tile)
            high = decay.astype(BF16).astype(F32)
            middle = (decay - high).astype(BF16).astype(F32)
            rest = decay - high - middle
            edge = jnp.where(
                index == 0, high, jnp.where(index == 1, middle, jnp.where(index == 2, rest, 0.0))
            )
            payload_ref[0, seq, STATE:, lanes] = edge.astype(BF16)


def intra_kernel(x_ref, step_q, sum_q, sum_t, scores, y_ref):
    row = lax.broadcasted_iota(jnp.int32, (SUB, SUB), 0)
    col = lax.broadcasted_iota(jnp.int32, (SUB, SUB), 1)
    causal = row >= col
    low = low_lanes()
    for seq in range(2):
        step, running = step_q[0, seq], sum_q[0, seq]
        middle = running[SUB - 1 : SUB]
        ahead = jnp.exp(middle - running[:SUB])
        after = jnp.exp(running[SUB:] - middle)
        across = scores[seq, SUB:, :SUB].astype(BF16)
        for tile in range(Q_TILES):
            lanes = slice(TILE * tile, TILE * tile + TILE)
            scaled = x_ref[seq, :, lanes] * pick(step, tile)
            low_part = jnp.where(low, scaled, 0.0).astype(BF16)
            high_part = jnp.where(low, 0.0, scaled).astype(BF16)
            for part in range(2):
                rows = slice(SUB * part, SUB * part + SUB)
                weights = []
                for h in (2 * tile, 2 * tile + 1):
                    spread = running[rows, h : h + 1] - sum_t[0, seq, h : h + 1, rows]
                    decayed = jnp.exp(jnp.where(causal, spread, FAR))
                    weights.append((decayed * scores[seq, rows, rows]).astype(BF16))
                inside = dot(
                    jnp.concatenate(weights, 1),
                    jnp.concatenate([low_part[rows], high_part[rows]], 0),
                )
                if part:
                    earlier = (scaled[:SUB] * pick(ahead, tile)).astype(BF16)
                    inside = inside + pick(after, tile) * dot(across, earlier)
                y_ref[seq, rows, lanes] = inside


def gate_kernel(
    y_ref,
    x_ref,
    z_ref,
    grad_ref,
    bc_ref,
    sum_ref,
    entering,
    skip,
    gain,
    out_ref,
    grad_z_ref,
    grad_scan_ref,
    grad_state_ref,
    grad_read_ref,
    products_ref,
    gain_grad_ref,
    whole_y,
    whole_gated,
    spread,
    product,
):
    step = pl.program_id(0)
    steps = pl.num_programs(0)
    start = jnp.exp(sum_ref[0])
    readout = bc_ref[0, :, STATE:].astype(BF16)
    squares = jnp.zeros((ROWS, TILE), F32)
    overlap = jnp.zeros((ROWS, TILE), F32)
    for tile in range(INNER // TILE):
        lanes = slice(TILE * tile, TILE * tile + TILE)
        carried = dot(readout, entering[0, :, lanes])
        y = y_ref[0, :, lanes] + pick(start, tile) * carried
        whole_y[:, lanes] = y
        z = z_ref[0, :, lanes]
        gated = (y + skip[:, lanes] * x_ref[0, :, lanes]) * (z * jax.nn.sigmoid(z))
        whole_gated[:, lanes] = gated
        squares = squares + gated * gated
        overlap = overlap + gated * (grad_ref[0, :, lanes] * gain[:, lanes])
    mean = jnp.sum(squares, axis=1, keepdims=True) / INNER
    inverse = lax.rsqrt(mean + EPSILON)
    back = jnp.sum(overlap, axis=1, keepdims=True) / INNER * inverse * inverse * inverse

    @pl.when(step == 0)
    def _():
        gain_grad_ref[...] = jnp.zeros_like(gain_grad_ref)

    for tile in range(INNER // TILE):
        lanes = slice(TILE * tile, TILE * tile + TILE)
        gated = whole_gated[:, lanes]
        grad = grad_ref[0, :, lanes]
        scaled = gated * inverse
        out_ref[0, :, lanes] = (scaled * gain[:, lanes]).astype(BF16)
        gain_grad_ref[:, lanes] += jnp.sum(grad * scaled, axis=0, keepdims=True)
        grad_gated = inverse * (grad * gain[:, lanes]) - gated * back
        z = z_ref[0, :, lanes]
        gate = jax.nn.sigmoid(z)
        y = whole_y[:, lanes]
        scanned = y + skip[:, lanes] * x_ref[0, :, lanes]
        grad_scan = grad_gated * (z * gate)
        grad_z_ref[0, :, lanes] = (
            grad_gated * scanned * (gate * (1.0 + z * (1.0 - gate)))
        ).astype(BF16)
        grad_scan_ref[0, :, lanes] = grad_scan
        rounded = grad_scan.astype(BF16).astype(F32)
        product[:, lanes] = rounded * y
        spread[:, lanes] = (rounded * pick(start, tile)).astype(BF16)
    products_ref[0] = head_sums(product[...], head_columns(INNER, TILE, 0))
    grad_read_ref[0] = dot_last(spread[...], entering[0])

    @pl.when(step % (steps // 2) == 0)
    def _():
        grad_state_ref[...] = jnp.zeros_like(grad_state_ref)

    grad_state_ref[0] += dot_first(readout, spread[...])


def intra_back_kernel(x_ref, grad_ref, step_q, sum_q, sum_t, scores_t, grad_x_ref, grad_scores_ref):
    row = lax.broadcasted_iota(jnp.int32, (SUB, SUB), 0)
    col = lax.broadcasted_iota(jnp.int32, (SUB, SUB), 1)
    causal = row <= col
    low = low_lanes()

    @pl.when(pl.program_id(0) == 0)
    def _():
        grad_scores_ref[...] = jnp.zeros_like(grad_scores_ref)

    for seq in range(2):
        step, running = step_q[0, seq], sum_q[0, seq]
        middle = running[SUB - 1 : SUB]
        ahead = jnp.exp(middle - running[:SUB])
        after = jnp.exp(running[SUB:] - middle)
        across = scores_t[seq, :SUB, SUB:].astype(BF16)
        inner = [jnp.zeros((SUB, SUB), F32) for _ in range(2)]
        outer = jnp.zeros((SUB, SUB), F32)
        for tile in range(Q_TILES):
            lanes = slice(TILE * tile, TILE * tile + TILE)
            scaled = x_ref[seq, :, lanes] * pick(step, tile)
            grad = grad_ref[seq, :, lanes]
            low_grad = jnp.where(low, grad, 0.0).astype(BF16)
            high_grad = jnp.where(low, 0.0, grad).astype(BF16)
            rounded = grad.astype(BF16)
            sides = (
                jnp.where(low, scaled, 0.0).astype(BF16),
                jnp.where(low, 0.0, scaled).astype(BF16),
            )
            for part in range(2):
                rows = slice(SUB * part, SUB * part + SUB)
                weights = []
                for side in range(2):
                    h = 2 * tile + side
                    spread = sum_t[0, seq, h : h + 1, rows] - running[rows, h : h + 1]
                    decayed = jnp.exp(jnp.where(causal, spread, FAR))
                    weights.append((decayed * scores_t[seq, rows, rows]).astype(BF16))
                    inner[part] = inner[part] + decayed * dot_last(
                        sides[side][rows], rounded[rows]
                    )
                inside = dot(
                    jnp.concatenate(weights, 1),
                    jnp.concatenate([low_grad[rows], high_grad[rows]], 0),
                )
                if not part:
                    later = (rounded[SUB:].astype(F32) * pick(after, tile)).astype(BF16)
                    factor = pick(ahead, tile)
                    inside = inside + factor * dot(across, later)
                    outer = outer + dot_last((scaled[:SUB] * factor).astype(BF16), later)
                grad_x_ref[seq, rows, lanes] = inside
        grad_scores_ref[seq, :SUB, :SUB] += inner[0]
        grad_scores_ref[seq, SUB:, SUB:] += inner[1]
        grad_scores_ref[seq, :SUB, SUB:] += outer


def channel_kernel(
    conv_input,
    weight,
    bias,
    x_ref,
    grad_ref,
    grad_x_ref,
    step_q,
    sum_q,
    bc_ref,
    leaving,
    entering,
    skip,
    grad_conv_ref,
    tail_ref,
    halo_ref,
    sums_ref,
    heads_ref,
    grad_writes_ref,
    padded,
    product,
    spread,
):
    quarter = pl.program_id(0)
    zeros = jnp.zeros((EDGE, TILE), F32)
    padded[:EDGE] = zeros
    padded[EDGE + 256 :] = zeros
    sums_ref[...] = jnp.zeros_like(sums_ref)

    @pl.when(quarter == 0)
    def _():
        grad_writes_ref[...] = jnp.zeros_like(grad_writes_ref)

    for seq in range(2):
        step, running = step_q[0, seq], sum_q[0, seq]
        remain = jnp.exp(running[255:256] - running)
        writes = bc_ref[seq, :, :STATE].astype(BF16)
        for tile in range(Q_TILES):
            lanes = slice(TILE * tile, TILE * tile + TILE)
            taps = weight[:, lanes]
            x = x_ref[seq, :, lanes]
            grad = grad_ref[seq, :, lanes]
            size = pick(step, tile)
            scaled = x * size
            left = pick(remain, tile)
            from_state = left * dot(writes, leaving[seq, :, lanes])
            inside = grad_x_ref[seq, :, lanes]
            whole = inside + from_state
            at_state = scaled * from_state
            product[0, :, lanes] = scaled.astype(BF16).astype(F32) * inside + at_state
            product[1, :, lanes] = x * whole
            product[2, :, lanes] = at_state
            spread[:, lanes] = (scaled * left).astype(BF16)
            mixture = mixture_of(conv_input, seq, lanes, taps, bias[:, lanes])
            grad_mix = (size * whole + skip[:, lanes] * grad) * silu_slope(mixture)
            padded[EDGE : EDGE + 256] = grad_mix
            grad_conv = taps[0:1] * padded[3 : 3 + EDGE + 256]
            for tap in range(1, CONV):
                grad_conv = (
                    grad_conv + taps[tap : tap + 1] * padded[3 - tap : 3 - tap + EDGE + 256]
                )
            halo_ref[seq, :, lanes] = grad_conv[:EDGE].astype(BF16)
            grad_conv_ref[seq, :, lanes] = grad_conv[EDGE:].astype(BF16)
            tail_ref[seq, :, lanes] = grad_conv[256:]
            for tap in range(CONV):
                begin = EDGE - CONV + 1 + tap
                sums_ref[tap : tap + 1, lanes] += jnp.sum(
                    grad_mix * conv_input[seq, begin : begin + 256, lanes], axis=0, keepdims=True
                )
            sums_ref[4:5, lanes] += jnp.sum(grad_mix, axis=0, keepdims=True)
            sums_ref[5:6, lanes] += jnp.sum(grad * x, axis=0, keepdims=True)
            meeting = entering[seq, :, lanes].astype(F32) * leaving[seq, :, lanes].astype(F32)
            sums_ref[6 + seq : 7 + seq, lanes] = jnp.sum(meeting, axis=0, keepdims=True)
        total = jnp.zeros((256, TILE), F32)
        for kind in range(3):
            total = total + head_sums(product[kind], head_columns(Q_LANES, TILE, Q_HEADS * kind))
        heads_ref[0, seq] = total
        grad_writes_ref[seq] += dot_last(spread[...], leaving[seq])


def last_kernel(
    conv_input,
    weight,
    bias,
    small,
    bc_ref,
    grad_scores,
    grad_writes,
    grad_read,
    products,
    heads,
    sums,
    step_ref,
    sum_ref,
    grad_conv_ref,
    tail_ref,
    halo_ref,
    sums_ref,
    small_ref,
    padded,
):
    row = lax.broadcasted_iota(jnp.int32, (256, 256), 0)
    col = lax.broadcasted_iota(jnp.int32, (256, 256), 1)
    upper = (row <= col).astype(F32)
    lane = lax.broadcasted_iota(jnp.int32, (1, TILE), 1)
    line = lax.broadcasted_iota(jnp.int32, (256, 1), 0)
    padded[:EDGE] = jnp.zeros((EDGE, 256), F32)
    padded[EDGE + 256 :] = jnp.zeros((EDGE, 256), F32)
    sums_ref[...] = jnp.zeros_like(sums_ref)
    small_ref[...] = jnp.zeros_like(small_ref)
    rate = jnp.exp(small[1:2])
    per_head = head_sums(sums[...], head_columns(INNER, TILE, 0))
    small_ref[2:3] = per_head[5:6]
    taps = weight[...]
    for seq in range(2):
        kinds = []
        for kind in range(3):
            total = jnp.zeros((256, TILE), F32)
            for quarter in range(QUARTERS):
                value = heads[quarter, seq]
                shift = (Q_HEADS * (quarter - kind)) % TILE
                if shift:
                    value = pltpu.roll(value, shift, 1)
                first = Q_HEADS * quarter
                total = total + jnp.where((lane >= first) & (lane < first + Q_HEADS), value, 0.0)
            kinds.append(total)
        met, by_value, at_state = kinds
        running = sum_ref[seq]
        end = jnp.exp(running[255:256]) * per_head[6 + seq : 7 + seq] + jnp.sum(
            at_state, axis=0, keepdims=True
        )
        grad_sum = products[seq] - met + jnp.where(line == 255, end, 0.0)
        grad_log = jnp.dot(upper, grad_sum, preferred_element_type=F32, precision=HIGHEST)
        step = step_ref[seq]
        small_ref[1:2] += jnp.sum(-rate * step * grad_log, axis=0, keepdims=True)
        raw = jnp.where(
            lane < HEADS, conv_input[seq, EDGE : EDGE + 256, 256:384] + small[0:1], 0.0
        )
        grad_raw = (by_value - rate * grad_log) * jax.nn.sigmoid(raw)
        small_ref[0:1] += jnp.sum(grad_raw, axis=0, keepdims=True)
        grad_conv_ref[seq, :, 256:] = grad_raw[:, :HEADS].astype(BF16)
        writes, readout = bc_ref[seq, :, :STATE], bc_ref[seq, :, STATE:]
        into_writes = dot(grad_scores[seq].astype(BF16), readout.astype(BF16)) + grad_writes[seq]
        into_read = dot_first(grad_scores[seq].astype(BF16), writes.astype(BF16)) + grad_read[seq]
        mixture = mixture_of(conv_input, seq, slice(0, 256), taps, bias[...])
        grad_mix = jnp.concatenate([into_writes, into_read], 1) * silu_slope(mixture)
        padded[EDGE : EDGE + 256] = grad_mix
        grad_conv = taps[0:1] * padded[3 : 3 + EDGE + 256]
        for tap in range(1, CONV):
            grad_conv = grad_conv + taps[tap : tap + 1] * padded[3 - tap : 3 - tap + EDGE + 256]
        halo_ref[seq] = grad_conv[:EDGE].astype(BF16)
        grad_conv_ref[seq, :, :256] = grad_conv[EDGE:].astype(BF16)
        tail_ref[seq] = grad_conv[256:]
        for tap in range(CONV):
            begin = EDGE - CONV + 1 + tap
            sums_ref[tap : tap + 1] += jnp.sum(
                grad_mix * conv_input[seq, begin : begin + 256, :256], axis=0, keepdims=True
            )
        sums_ref[4:5] += jnp.sum(grad_mix, axis=0, keepdims=True)


def shape(dims, dtype=F32):
    return jax.ShapeDtypeStruct(dims, dtype)


def whole_block(dims):
    return pl.BlockSpec(dims, lambda g: (0,) * len(dims))


def lane_block(dims, width=Q_LANES):
    return pl.BlockSpec(dims + (width,), lambda g: (0,) * len(dims) + (g,))


def quarter_block(dims):
    return pl.BlockSpec((1,) + dims, lambda g: (g,) + (0,) * len(dims))


def fixed_block(dims, index):
    return pl.BlockSpec(dims, lambda g: index)


def row_block(width, length=256):
    steps = length // ROWS
    return pl.BlockSpec((1, ROWS, width), lambda g: (g // steps, g % steps, 0))


def decay_row(edge):
    rows = edge.astype(F32)
    return (rows[..., 0:1, :] + rows[..., 1:2, :]) + rows[..., 2:3, :]


def join(state, decay):
    high = decay.astype(BF16).astype(F32)
    middle = (decay - high).astype(BF16).astype(F32)
    rest = decay - high - middle
    blank = jnp.zeros(decay.shape[:-2] + (EDGE - 3,) + decay.shape[-1:], BF16)
    parts = [state, high, middle, rest]
    return jnp.concatenate([p.astype(BF16) for p in parts] + [blank], axis=-2)


def split(payload):
    return payload[..., :STATE, :].astype(F32), decay_row(payload[..., STATE:, :])


def exchange(payload, axis, reverse):
    count = lax.axis_size(axis)
    place = lax.axis_index(axis)
    member = place % QUARTERS

    def swap(value, by):
        return lax.ppermute(value, axis, [(i, i ^ by) for i in range(count)])

    def quarter_of(array, by):
        return lax.dynamic_index_in_dim(array, member ^ by, 0, False)

    relative = [quarter_of(payload, 0)] + [
        swap(quarter_of(payload, by), by) for by in range(1, QUARTERS)
    ]

    def select(items, which):
        result = items[QUARTERS - 1]
        for by in range(QUARTERS - 1):
            result = jnp.where((member ^ by) == which, items[by], result)
        return result

    order = range(QUARTERS)[::-1] if reverse else range(QUARTERS)
    state = jnp.zeros((2, STATE, Q_LANES), F32)
    decay = jnp.ones((2, 1, Q_LANES), F32)
    before = {}
    for which in order:
        before[which] = (state, decay)
        here, factor = split(select(relative, which))
        state, decay = here + factor * state, factor * decay
    total = join(state, decay)
    span = 1
    inclusive = total
    entering = None
    while span < count // QUARTERS:
        shift = -QUARTERS * span if reverse else QUARTERS * span
        pairs = [(i, i + shift) for i in range(count) if 0 <= i + shift < count]
        received = lax.ppermute(inclusive, axis, pairs)
        got, factor = split(received)
        if entering is None:
            entering = (got, factor)
        else:
            entering = (entering[0] + entering[1] * got, entering[1] * factor)
        inclusive = join(state + decay * entering[0], decay * entering[1])
        span *= 2
    carried = entering[0]
    sends = [
        (before[which][0] + before[which][1] * carried).astype(BF16) for which in range(QUARTERS)
    ]

    def sent_to(by):
        result = sends[QUARTERS - 1]
        for which in range(QUARTERS - 1):
            result = jnp.where((member ^ by) == which, sends[which], result)
        return result

    back = [sent_to(0)] + [swap(sent_to(by), by) for by in range(1, QUARTERS)]
    return jnp.concatenate([select(back, which) for which in range(QUARTERS)], axis=-1)


def local(
    hidden_in,
    norm_gain,
    in_weight,
    conv_weight,
    conv_bias,
    step_bias,
    decay_log,
    skip_gain,
    gate_gain,
    out_weight,
    cotangent,
):
    hidden = hidden_in[0]
    upstream = cotangent[0]
    tokens, width = hidden.shape
    half = tokens // 2
    share = in_weight.shape[0]
    count = lax.axis_size("seq")
    core = lax.axis_index("fsdp")
    other = [(0, 1), (1, 0)]

    conv_rows = in_weight[:, INNER:]
    gate_rows = in_weight[:, :INNER]
    conv_rows_other = lax.ppermute(conv_rows, "fsdp", other)
    gate_rows_other = lax.ppermute(gate_rows, "fsdp", other)
    out_rows_other = lax.ppermute(out_weight, "fsdp", other)

    paired = hidden.reshape(2, half, width)
    halo = lax.ppermute(paired[:, half - EDGE :], "seq", [(i, i + 1) for i in range(count - 1)])
    extended = jnp.concatenate([halo, paired], axis=1).reshape(2 * (half + EDGE), width)
    rows = extended.astype(F32)
    rescale = lax.rsqrt(jnp.mean(rows * rows, axis=-1, keepdims=True) + EPSILON)
    normed_ext = (rows * rescale * norm_gain).astype(BF16)

    def mine(array, axis):
        first = lax.slice_in_dim(array, 0, share, axis=axis)
        second = lax.slice_in_dim(array, share, 2 * share, axis=axis)
        return (
            jnp.where(core == 0, first, second),
            jnp.where(core == 0, second, first),
        )

    def ordered(own, foreign, axis):
        return jnp.where(
            core == 0,
            jnp.concatenate([own, foreign], axis),
            jnp.concatenate([foreign, own], axis),
        )

    own_ext, other_ext = mine(normed_ext, 1)
    conv_input = (dot(own_ext, conv_rows) + dot(other_ext, conv_rows_other)).reshape(
        2, half + EDGE, CONV_CH + HEADS
    )
    normed = normed_ext.reshape(2, half + EDGE, width)[:, EDGE:].reshape(tokens, width)
    own_normed, other_normed = mine(normed, 1)

    small = jnp.pad(jnp.stack([step_bias, decay_log, skip_gain]), ((0, 5), (0, TILE - HEADS)))
    bias_row = conv_bias[None]
    gain_row = gate_gain[None]
    skip_row = jnp.repeat(skip_gain, HEAD_DIM)[None]

    last_columns = fixed_block((2, half + EDGE, 384), (0, 0, INNER // 384))
    last_taps = fixed_block((CONV, 256), (0, INNER // 256))
    last_bias = fixed_block((1, 256), (0, INNER // 256))
    per_quarter = (QUARTERS, 2, half, Q_HEADS)
    bc, bt, scores, scores_t, step, running, step_q, sum_q, sum_t = pl.pallas_call(
        step_kernel,
        grid=(1,),
        in_specs=[last_columns, last_taps, last_bias, whole_block((8, TILE))],
        out_specs=[
            whole_block((2, half, 256)),
            whole_block((2, STATE, half)),
            whole_block((2, half, half)),
            whole_block((2, half, half)),
            whole_block((2, half, TILE)),
            whole_block((2, half, TILE)),
            whole_block(per_quarter),
            whole_block(per_quarter),
            whole_block((QUARTERS, 2, EDGE, half)),
        ],
        out_shape=[
            shape((2, half, 256)),
            shape((2, STATE, half), BF16),
            shape((2, half, half)),
            shape((2, half, half)),
            shape((2, half, TILE)),
            shape((2, half, TILE)),
            shape(per_quarter),
            shape(per_quarter),
            shape((QUARTERS, 2, EDGE, half)),
        ],
        compiler_params=params(),
        name="steps",
    )(conv_input, conv_weight, bias_row, small)

    columns = lane_block((2, half + EDGE))
    taps_block = lane_block((CONV,))
    row_of = lane_block((1,))
    heads_block = quarter_block((2, half, Q_HEADS))
    line_block = quarter_block((2, EDGE, half))
    tokens_block = lane_block((2, half))
    x, payload = pl.pallas_call(
        state_kernel,
        grid=(QUARTERS,),
        in_specs=[
            columns,
            taps_block,
            row_of,
            heads_block,
            heads_block,
            whole_block((2, STATE, half)),
        ],
        out_specs=[tokens_block, quarter_block((2, PAYLOAD, Q_LANES))],
        out_shape=[shape((2, half, INNER)), shape((QUARTERS, 2, PAYLOAD, Q_LANES), BF16)],
        compiler_params=params(),
        name="states",
    )(conv_input, conv_weight, bias_row, step_q, sum_q, bt)

    entering = exchange(payload, "seq", False)

    y_inside = pl.pallas_call(
        intra_kernel,
        grid=(QUARTERS,),
        in_specs=[
            tokens_block,
            heads_block,
            heads_block,
            line_block,
            whole_block((2, half, half)),
        ],
        out_specs=tokens_block,
        out_shape=shape((2, half, INNER)),
        compiler_params=params(),
        name="inside",
    )(x, step_q, sum_q, sum_t, scores)
    z = (dot(own_normed, gate_rows) + dot(other_normed, gate_rows_other)).reshape(2, half, INNER)
    grad_normed_out = ordered(
        dot_last(upstream, out_weight), dot_last(upstream, out_rows_other), 1
    ).reshape(2, half, INNER)

    token_rows = row_block(INNER)
    steps = half // ROWS
    state_rows = pl.BlockSpec((1, STATE, INNER), lambda g: (g // steps, 0, 0))
    normed_out, grad_z, grad_scan, grad_state, grad_read, products, gate_gain_grad = pl.pallas_call(
        gate_kernel,
        grid=(2 * steps,),
        in_specs=[
            token_rows,
            token_rows,
            token_rows,
            token_rows,
            row_block(256),
            row_block(TILE),
            state_rows,
            whole_block((1, INNER)),
            whole_block((1, INNER)),
        ],
        out_specs=[
            token_rows,
            token_rows,
            token_rows,
            state_rows,
            row_block(STATE),
            row_block(TILE),
            whole_block((1, INNER)),
        ],
        out_shape=[
            shape((2, half, INNER), BF16),
            shape((2, half, INNER), BF16),
            shape((2, half, INNER)),
            shape((2, STATE, INNER)),
            shape((2, half, STATE)),
            shape((2, half, TILE)),
            shape((1, INNER)),
        ],
        scratch_shapes=[
            pltpu.VMEM((ROWS, INNER), F32),
            pltpu.VMEM((ROWS, INNER), F32),
            pltpu.VMEM((ROWS, INNER), BF16),
            pltpu.VMEM((ROWS, INNER), F32),
        ],
        compiler_params=params(),
        name="gates",
    )(y_inside, x, z, grad_normed_out, bc, running, entering, skip_row, gain_row)

    normed_out = normed_out.reshape(tokens, INNER)
    grad_z = grad_z.reshape(tokens, INNER)

    own_out, other_out = None, None
    first_out, second_out = normed_out[:, : INNER // 2], normed_out[:, INNER // 2 :]
    own_out = jnp.where(core == 0, first_out, second_out)
    other_out = jnp.where(core == 0, second_out, first_out)

    def weight_part(own, foreign, right):
        sent = lax.ppermute(dot_first(foreign, right).astype(BF16), "fsdp", other)
        return dot_first(own, right) + sent.astype(F32)

    out_grad = lax.psum(weight_part(own_out, other_out, upstream).astype(BF16), "seq")
    gate_grad = lax.psum(weight_part(own_normed, other_normed, grad_z).astype(BF16), "seq")

    edge = payload[:, :, STATE:].transpose(1, 2, 0, 3)
    back_payload = jnp.concatenate(
        [
            grad_state.astype(BF16).reshape(2, STATE, QUARTERS, Q_LANES),
            edge,
        ],
        axis=1,
    ).transpose(2, 0, 1, 3)
    leaving = exchange(back_payload, "seq", True)

    branch = dot(own_out, out_weight) + dot(other_out, out_rows_other)
    block_out = (hidden.astype(F32) + branch).astype(BF16)

    grad_x, grad_scores = pl.pallas_call(
        intra_back_kernel,
        grid=(QUARTERS,),
        in_specs=[
            tokens_block,
            tokens_block,
            heads_block,
            heads_block,
            line_block,
            whole_block((2, half, half)),
        ],
        out_specs=[tokens_block, whole_block((2, half, half))],
        out_shape=[shape((2, half, INNER)), shape((2, half, half))],
        compiler_params=params(),
        name="inside_back",
    )(x, grad_scan, step_q, sum_q, sum_t, scores_t)

    state_columns = lane_block((2, STATE))
    edge_columns = lane_block((2, EDGE))
    grad_conv, tail, halo_grad, sums, heads, grad_writes = pl.pallas_call(
        channel_kernel,
        grid=(QUARTERS,),
        in_specs=[
            columns,
            taps_block,
            row_of,
            tokens_block,
            tokens_block,
            tokens_block,
            heads_block,
            heads_block,
            whole_block((2, half, 256)),
            state_columns,
            state_columns,
            row_of,
        ],
        out_specs=[
            tokens_block,
            edge_columns,
            edge_columns,
            lane_block((8,)),
            quarter_block((2, half, TILE)),
            whole_block((2, half, STATE)),
        ],
        out_shape=[
            shape((2, half, INNER), BF16),
            shape((2, EDGE, INNER)),
            shape((2, EDGE, INNER), BF16),
            shape((8, INNER)),
            shape((QUARTERS, 2, half, TILE)),
            shape((2, half, STATE)),
        ],
        scratch_shapes=[
            pltpu.VMEM((half + 2 * EDGE, TILE), F32),
            pltpu.VMEM((3, half, Q_LANES), F32),
            pltpu.VMEM((half, Q_LANES), BF16),
        ],
        compiler_params=params(),
        name="channels",
    )(
        conv_input,
        conv_weight,
        bias_row,
        x,
        grad_scan,
        grad_x,
        step_q,
        sum_q,
        bc,
        leaving,
        entering,
        skip_row,
    )

    grad_conv_last, tail_last, halo_last, sums_last, small_grads = pl.pallas_call(
        last_kernel,
        grid=(1,),
        in_specs=[
            last_columns,
            last_taps,
            last_bias,
            whole_block((8, TILE)),
            whole_block((2, half, 256)),
            whole_block((2, half, half)),
            whole_block((2, half, STATE)),
            whole_block((2, half, STATE)),
            whole_block((2, half, TILE)),
            whole_block((QUARTERS, 2, half, TILE)),
            whole_block((8, INNER)),
            whole_block((2, half, TILE)),
            whole_block((2, half, TILE)),
        ],
        out_specs=[
            whole_block((2, half, 256 + HEADS)),
            whole_block((2, EDGE, 256)),
            whole_block((2, EDGE, 256)),
            whole_block((8, 256)),
            whole_block((8, TILE)),
        ],
        out_shape=[
            shape((2, half, 256 + HEADS), BF16),
            shape((2, EDGE, 256)),
            shape((2, EDGE, 256), BF16),
            shape((8, 256)),
            shape((8, TILE)),
        ],
        scratch_shapes=[pltpu.VMEM((half + 2 * EDGE, 256), F32)],
        compiler_params=params(),
        name="last",
    )(
        conv_input,
        conv_weight,
        bias_row,
        small,
        bc,
        grad_scores,
        grad_writes,
        grad_read,
        products,
        heads,
        sums,
        step,
        running,
    )

    returned = lax.ppermute(
        jnp.concatenate([halo_grad, halo_last], axis=-1),
        "seq",
        [(i, i - 1) for i in range(1, count)],
    )
    fixed_tail = jnp.concatenate([tail, tail_last], axis=-1) + returned.astype(F32)
    grad_proj = jnp.concatenate([grad_conv, grad_conv_last], axis=-1)
    fixed_tail = jnp.concatenate(
        [fixed_tail.astype(BF16), grad_conv_last[:, half - EDGE :, 256:]], axis=-1
    )
    grad_proj = jnp.concatenate([grad_proj[:, : half - EDGE], fixed_tail], axis=1).reshape(
        tokens, CONV_CH + HEADS
    )

    conv_grad = lax.psum(weight_part(own_normed, other_normed, grad_proj).astype(BF16), "seq")

    grad_normed = ordered(
        dot_last(grad_z, gate_rows) + dot_last(grad_proj, conv_rows),
        dot_last(grad_z, gate_rows_other) + dot_last(grad_proj, conv_rows_other),
        1,
    )
    u = hidden.astype(F32)
    r = lax.rsqrt(jnp.mean(u * u, axis=-1, keepdims=True) + EPSILON)
    norm_gain_grad = jnp.sum(grad_normed * u * r, axis=0)
    through = grad_normed * norm_gain
    input_grad = (
        upstream.astype(F32)
        + r * through
        - u * (r * r * r) * jnp.mean(through * u, axis=-1, keepdims=True)
    ).astype(BF16)

    vector = jnp.concatenate(
        [
            norm_gain_grad,
            sums[:5].reshape(-1),
            sums_last[:5].reshape(-1),
            small_grads[:3].reshape(-1),
            gate_gain_grad[0],
        ]
    )
    vector = lax.psum(vector, ("seq", "fsdp"))
    parts = []
    begin = 0
    for size in (width, 5 * INNER, 5 * 256, 3 * TILE, INNER):
        parts.append(vector[begin : begin + size])
        begin += size
    wide, narrow = parts[1].reshape(5, INNER), parts[2].reshape(5, 256)
    conv_sums = jnp.concatenate([wide, narrow], axis=1)
    smalls = parts[3].reshape(3, TILE)[:, :HEADS]
    in_weight_grad = jnp.concatenate([gate_grad, conv_grad], axis=1).astype(F32)
    return (
        block_out[None],
        input_grad[None],
        parts[0],
        in_weight_grad,
        conv_sums[:4],
        conv_sums[4],
        smalls[0],
        smalls[1],
        smalls[2],
        parts[4],
        out_grad.astype(F32),
    )


def solution(mesh):
    return jax.shard_map(
        local,
        mesh=mesh,
        in_specs=(
            P("fsdp", "seq", None),
            P(),
            P("fsdp", None),
            P(),
            P(),
            P(),
            P(),
            P(),
            P(),
            P("fsdp", None),
            P("fsdp", "seq", None),
        ),
        out_specs=(
            P("fsdp", "seq", None),
            P("fsdp", "seq", None),
            P(),
            P("fsdp", None),
            P(),
            P(),
            P(),
            P(),
            P(),
            P(),
            P("fsdp", None),
        ),
        check_vma=False,
    )
```

time: 2750 us -> 956 us (0.35)
  blocking collectives: 1240 us -> 0 us
  waiting for transfers between devices: 958 us -> 571 us
  other arithmetic: 209 us -> 59.6 us
  matrix products: 249 us -> 106 us
  Pallas kernels: 0 us -> 113 us
    psum x2 -> x0, blocking collectives: 1200 us -> none  [the longest x1 1200 us: local(): lax.psum((in_grad_part, out_grad_part, norm_gain_grad, conv_weight_grad,...]
    all_gather x4 -> x0, waiting for transfers between devices: 957 us -> none  [the longest x2 920 us: carried_in(): gathered = jax.tree.map(lambda a: lax.all_gather(a, axis), part)]
    psum x0 -> x2, waiting for transfers between devices: none -> 494 us  [the longest x1 412 us: local(): lax.psum(weight_part(own_normed, other_normed, grad_proj).astype(BF16), '...]
    dot_general x20 -> x18, matrix products: 249 us -> 106 us  [the longest x6 38.7 us: dot_first(): lax.dot_general(left, right, (((0,), (0,)), ((), ())), preferred_element_...]
    pallas_call x0 -> x7, Pallas kernels: none -> 113 us  [the longest x1 30.4 us: local(): pl.pallas_call(channel_kernel, grid=(QUARTERS,), in_specs=[columns, taps_...]
    ppermute x2 -> x24, waiting for transfers between devices: 0.01 us -> 76.8 us  [the longest x12 42.1 us: swap(): return lax.ppermute(value, axis, [(i, i ^ by) for i in range(count)])]
    add x15 -> x6, other arithmetic: 75.4 us -> 2.07 us  [the longest x1 1.22 us: exchange(): entering = (entering[0] + entering[1] * got, entering[1] * factor)]
    reduce_sum x9 -> x3, other arithmetic: 60.8 us -> 2 us  [the longest x1 1.21 us: local(): norm_gain_grad = jnp.sum(grad_normed * u * r, axis=0)]
  transfers between devices with their start and end apart: 8 -> 26, of which waited for: 3 -> 14; matrix products, arithmetic and copies ran while one was open for 15% -> 15% of each run, Pallas kernels for 0% -> 5%
where the time goes in v1:
time: 956 us; the launch traced here: 949 us
  waiting for transfers between devices  571 us (60%)
  Pallas kernels  113 us (12%)
  matrix products  106 us (11%)
  other arithmetic  59.6 us (6%)
  local copies, waits for them, and re-layouts  50.5 us (5%)
  starting transfers between devices  33.3 us (3%)
  between operations  15.5 us (2%)
    psum x1, waiting for transfers between devices, local(): lax.psum(weight_part(own_normed, other_normed, grad_proj).astype(BF16), '...  412 us
    psum x1, waiting for transfers between devices, local(): vector = lax.psum(vector, ('seq', 'fsdp'))  82 us
    ppermute x12, waiting for transfers between devices, swap(): return lax.ppermute(value, axis, [(i, i ^ by) for i in range(count)])  42.1 us
    dot_general x6, matrix products, dot_first(): lax.dot_general(left, right, (((0,), (0,)), ((), ())), preferred_element_...  38.7 us
    dot_general x6, matrix products, dot(): return jnp.dot(left, right, preferred_element_type=F32)  35.1 us
    ppermute x4, waiting for transfers between devices, exchange(): received = lax.ppermute(inclusive, axis, pairs)  34 us
    dot_general x6, matrix products, dot_last(): lax.dot_general(left, right, (((1,), (1,)), ((), ())), preferred_element_...  32.7 us
    pallas_call x1, Pallas kernels, local(): pl.pallas_call(channel_kernel, grid=(QUARTERS,), in_specs=[columns, taps_...  30.4 us
  transfers between devices with their start and end apart: 26, of which 14 were waited for; matrix products, arithmetic and copies ran while one was open for 15% of the time, Pallas kernels for 5%

profile of v1, /device:TPU:0, one launch (start us, length us, event | category | flops | bytes accessed | tf_op | source)
XLA Modules:
  0.0 949.3 jit_solution(11856268417207156094)
XLA Ops:
  7.2 5.3 slice.251
  13.0 4.5 collective-permute-start
  17.5 4.8 slice.255
  24.2 6.8 fusion.4
  36.4 3.2 fusion.34
  39.6 8.1 convolution_add_fusion
  47.7 4.7 steps.1
  52.4 10.7 %states.1 = (f32[2,256,3072]{2,1,0:T(8,128)}, bf16[4,2,144,768]{3,2,1,0:T(8,128)(2,1)}) custom-call(f32[2,272,3376]{2,1,0:T(8,128)} %bitcast.162, f32[4,3328]{1,0:T(4,128)} %weight.7, f32[1,3328]{1,0:T(1,128)} %broadcast_in_dim.8.bias, f32[4,2,256,12]{3,2,1,0:T(8,128)} %get-tuple-element.42.step_q, f32[4,2,256,12]{3,2,1,0:T(8,128)} %get-tuple-element.43.sum_q, ...), custom_call_target="tpu_custom_call" | custom-call | tf_op jit(solution)/shard_map/states/pallas_call | solution.py:697
  63.1 1.6 constant_dynamic-slice_fusion.2
  65.8 1.6 collective-permute-start.4
  67.4 1.5 collective-permute-start.5
  69.4 4.5 fusion.57
  73.9 4.3 collective-permute-done.4
  78.1 2.3 collective-permute-done.5
  80.4 8.4 collective-permute-done.6
  88.8 2.1 broadcast_select_fusion.13
  92.5 3.5 collective-permute-start.7
  96.0 7.1 convolution_add_fusion.1
  103.1 1.5 collective-permute-done.7
  105.2 5.4 collective-permute-start.8
  110.6 5.0 fusion.2
  115.6 2.8 collective-permute-done.8
  118.4 3.3 broadcast_select_fusion.33
  123.5 2.4 collective-permute-start.11
  127.0 3.0 maximum_select_fusion.grad_ref
  129.9 15.5 %inside.1.y_ref = f32[2,256,3072]{2,1,0:T(8,128)} custom-call(f32[2,256,3072]{2,1,0:T(8,128)} %get-tuple-element.45.x_ref, f32[4,2,256,12]{3,2,1,0:T(8,128)} %get-tuple-element.42.step_q, f32[4,2,256,12]{3,2,1,0:T(8,128)} %get-tuple-element.43.sum_q, f32[4,2,16,256]{3,2,1,0:T(8,128)} %get-tuple-element.46.sum_t, f32[2,256,256]{2,1,0:T(8,128)} %get-tuple-element.47.scores), custom_call_target="tpu_custom_call" | custom-call | tf_op jit(solution)/shard_map/inside/pallas_call | solution.py:716
  148.1 29.4 %gates.1 = (bf16[2,256,3072]{2,1,0:T(8,128)(2,1)}, bf16[2,256,3072]{2,1,0:T(8,128)(2,1)}, f32[2,256,3072]{2,1,0:T(8,128)}, f32[2,128,3072]{2,1,0:T(8,128)}, f32[...) custom-call(f32[2,256,3072]{2,1,0:T(8,128)} %inside.1.y_ref, ...), custom_call_target="tpu_custom_call" | custom-call | tf_op jit(solution)/shard_map/gates/pallas_call | solution.py:739
  177.5 3.2 convert_element_type.287
  180.8 3.5 reshape.254
  184.2 1.6 copy_dynamic-update-slice_fusion
  187.0 2.5 collective-permute-start.14
  190.5 10.5 %collective-permute-done.14 = bf16[2,144,768]{2,0,1:T(2,128)(2,1)S(1)} collective-permute-done((bf16[2,144,768]{2,0,1:T(2,128)(2,1)S(1)}, bf16[2,144,768]{2,0,1:T(2,128)(2,1)S(1)}, u32[]{:S(2)}, u32[]{:S(2)}) %collective-permute-start.14) | collective-permute-done | bytes 442400 | tf_op jit(solution)/shard_map/ppermute | solution.py:542
  201.0 5.0 collective-permute-done.13
  206.0 2.1 broadcast_select_fusion.12
  210.8 1.5 broadcast_multiply_fusion
  214.0 4.2 concatenate.91
  219.5 24.7 %collective-permute-done.15 = bf16[2,144,768]{2,1,0:T(8,128)(2,1)S(1)} collective-permute-done((bf16[2,144,768]{2,1,0:T(8,128)(2,1)}, bf16[2,144,768]{2,1,0:T(8,128)(2,1)S(1)}, u32[]{:S(2)}, u32[]{:S(2)}) %collective-permute-start.15) | collective-permute-done | bytes 442400 | tf_op jit(solution)/shard_map/ppermute | solution.py:572
  246.7 4.2 concatenate.92
  252.7 17.1 %inside_back.1 = (f32[2,256,3072]{2,1,0:T(8,128)}, f32[2,256,256]{2,1,0:T(8,128)}) custom-call(f32[2,256,3072]{2,1,0:T(8,128)} %get-tuple-element.45.x_ref, f32[2,256,3072]{2,1,0:T(8,128)} %get-tuple-element.53.grad_ref, f32[4,2,256,12]{3,2,1,0:T(8,128)} %get-tuple-element.42.step_q, f32[4,2,256,12]{3,2,1,0:T(8,128)} %get-tuple-element.43.sum_q, ...), custom_call_target="tpu_custom_call" | custom-call | tf_op jit(solution)/shard_map/inside_back/pallas_call | solution.py:809
  269.9 5.1 collective-permute-done.16
  277.5 1.7 collective-permute-start.19
  279.3 1.5 collective-permute-start.18
  281.2 4.3 convolution_convert_fusion.2
  285.5 5.0 collective-permute-done.19
  290.6 6.6 collective-permute-done.18
  298.8 30.4 %channels.1 = (bf16[2,256,3072]{2,1,0:T(8,128)(2,1)}, f32[2,16,3072]{2,1,0:T(8,128)}, bf16[2,16,3072]{2,1,0:T(8,128)(2,1)}, f32[8,3072]{1,0:T(8,128)}, f32[4,2,2...) custom-call(f32[2,272,3376]{2,1,0:T(8,128)} %bitcast.163, f32[4,3328]{1,0:T(4,128)} %weight.7, f32[1,3328]{1,0:T(1,128)} %broadcast_in_dim.8.bias, ...), custom_call_target="tpu_custom_call" | custom-call | tf_op jit(solution)/shard_map/channels/pallas_call | solution.py:828
  329.2 5.5 last.1
  336.8 6.3 convolution_convert_fusion
  345.6 5.3 convolution_convert_fusion.1
  350.9 6.1 fusion.55
  357.1 6.7 fusion.65
  363.8 5.1 convolution_add_fusion.3
  369.0 3.1 convolution_add_fusion.4
  375.5 8.8 add_convert_fusion.1
  384.3 6.1 add_convert_fusion.2
  390.4 7.8 add_convert_fusion
  398.3 5.7 fusion.50
  404.0 6.4 fusion.27
  410.4 2.3 fusion.21
  412.7 82.0 %all-reduce.5.cloned.1.call-done = f32[21632]{0:T(1024)} async-done(((f32[21632]{0:T(1024)}), f32[21632]{0:T(1024)}) %all-reduce.5.cloned.1.call-update) | async-done | bytes 86544 | tf_op jit(solution)/shard_map/psum | solution.py:974
  501.4 411.7 %all-reduce.7.cloned.1.call-done = (bf16[768,3376]{0,1:T(8,128)(2,1)}, bf16[768,3072]{1,0:T(8,128)(2,1)}, bf16[1536,1536]{1,0:T(8,128)(2,1)}) async-done(((bf16[768,3376]{0,1:T(8,128)(2,1)}, bf16[768,3072]{1,0:T(8,128)(2,1)}, bf16[1536,1536]{1,0:T(8,128)(2,1)}), (bf16[768,3376]{0,1:T(8,128)(2,1)}, bf16[768,3072]{1,0:T(8,128)(2,1)}, bf16[1536,1536]{1,0:T(8,128)(2,1)})) %all-reduce.7.cloned.1.call-update) | async-done | bytes 14622736 | tf_op jit(solution)/shard_map/psum | solution.py:948
  913.1 6.7 copy.127
  919.8 7.6 convert_element_type.329
  927.4 14.9 %maximum_convert_fusion = f32[768,6448]{0,1:T(8,128)} fusion(bf16[768,3376]{0,1:T(8,128)(2,1)S(1)} %bitcast.177, bf16[768,3072]{0,1:T(8,128)(2,1)S(1)} %copy-done.1), kind=kLoop, calls=%fused_computation.1 | loop fusion | flops 19808256 | bytes 29712384 | tf_op jit(solution)/shard_map/convert_element_type | solution.py:983
  (255 shorter events, 47.8 us)
Async XLA Ops:
  7.2 5.8 copy-start
  7.2 487.5 %all-reduce.5.cloned.1.call-start = ((), (), s32[]{:S(2)}) async-start(), calls=%async_computation | async-start | bytes 180224 | tf_op jit(solution)/shard_map/psum | solution.py:974
  12.5 27.1 %collective-permute-start.1 = (bf16[768,3376]{0,1:T(8,128)(2,1)}, bf16[768,3376]{0,1:T(8,128)(2,1)}, u32[]{:S(2)}, u32[]{:S(2)}) collective-permute-start(bf16[768,3376]{0,1:T(8,128)(2,1)} %slice.251), channel_id=1, source_target_pairs={{0,1},{1,0},{2,3},{3,2},{4,5},{5,4},{6,7},{7,6},{8,9},{9,8},{10,11... | collective-permute-start | bytes 15556616 | tf_op jit(solution)/shard_map/ppermute | solution.py:619
  13.0 9.9 %copy-start.37 = (f32[3328]{0:T(1024)S(1)}, f32[3328]{0:T(1024)}, u32[]{:S(2)}) copy-start(f32[3328]{0:T(1024)} %param.15) | copy-start | bytes 39940
  13.0 10.5 %copy-start.40 = (f32[48]{0:T(128)S(1)}, f32[48]{0:T(128)}, u32[]{:S(2)}) copy-start(f32[48]{0:T(128)} %param.18) | copy-start | bytes 580
  13.0 11.2 %copy-start.16 = (bf16[1,512,1536]{2,1,0:T(8,128)(2,1)S(1)}, bf16[1,512,1536]{2,1,0:T(8,128)(2,1)}, u32[]{:S(2)}) copy-start(bf16[1,512,1536]{2,1,0:T(8,128)(2,1)} %param.21) | copy-start | bytes 4718596
  13.0 18.6 %collective-permute-start = (bf16[2,16,1536]{2,1,0:T(8,128)(2,1)S(1)}, bf16[2,16,1536]{2,1,0:T(8,128)(2,1)S(1)}, u32[]{:S(2)}, u32[]{:S(2)}) collective-permute-start(bf16[2,16,1536]{2,1,0:T(8,128)(2,1)S(1)} %slice.327), channel_id=1, source_target_pairs={{0,2},{2,4},{4,6},{6,8},{8,10},{10,12},{12,14},{14,16},{16,18},{18... | collective-permute-start | bytes 294920 | tf_op jit(solution)/shard_map/ppermute | solution.py:624
  22.3 73.7 %collective-permute-start.2 = (bf16[768,3072]{0,1:T(8,128)(2,1)}, bf16[768,3072]{0,1:T(8,128)(2,1)}, u32[]{:S(2)}, u32[]{:S(2)}) collective-permute-start(bf16[768,3072]{0,1:T(8,128)(2,1)} %slice.255), channel_id=1, source_target_pairs={{0,1},{1,0},{2,3},{3,2},{4,5},{5,4},{6,7},{7,6},{8,9},{9,8},{10,11... | collective-permute-start | bytes 14155784 | tf_op jit(solution)/shard_map/ppermute | solution.py:620
  22.6 88.1 %collective-permute-start.3 = (bf16[1536,1536]{1,0:T(8,128)(2,1)}, bf16[1536,1536]{1,0:T(8,128)(2,1)}, u32[]{:S(2)}, u32[]{:S(2)}) collective-permute-start(bf16[1536,1536]{1,0:T(8,128)(2,1)} %param.20), channel_id=1, source_target_pairs={{0,1},{1,0},{2,3},{3,2},{4,5},{5,4},{6,7},{7,6},{8,9},{9,8},{10,11... | collective-permute-start | bytes 14155784 | tf_op jit(solution)/shard_map/ppermute | solution.py:621
  24.2 6.8 copy-start.42
  24.2 6.8 copy-start.43
  63.1 6.2 copy-start.20
  65.8 12.4 %collective-permute-start.4 = (bf16[2,144,768]{2,0,1:T(2,128)(2,1)S(1)}, bf16[2,144,768]{2,0,1:T(2,128)(2,1)S(1)}, u32[]{:S(2)}, u32[]{:S(2)}) collective-permute-start(bf16[2,144,768]{2,0,1:T(2,128)(2,1)S(1)} %bitcast.193), channel_id=1, source_target_pairs={{0,4},{2,6},{4,0},{6,2},{8,12},{10,14},{12,8},{14,10},{16,20},{18,... | collective-permute-start | bytes 1327112 | tf_op jit(solution)/shard_map/ppermute | solution.py:542
  67.4 13.0 %collective-permute-start.5 = (bf16[2,144,768]{2,0,1:T(2,128)(2,1)S(1)}, bf16[2,144,768]{2,0,1:T(2,128)(2,1)S(1)}, u32[]{:S(2)}, u32[]{:S(2)}) collective-permute-start(bf16[2,144,768]{2,0,1:T(2,128)(2,1)S(1)} %bitcast.192), channel_id=1, source_target_pairs={{0,2},{2,0},{4,6},{6,4},{8,10},{10,8},{12,14},{14,12},{16,18},{18,... | collective-permute-start | bytes 1327112 | tf_op jit(solution)/shard_map/ppermute | solution.py:542
  68.9 20.0 %collective-permute-start.6 = (bf16[2,144,768]{2,0,1:T(2,128)(2,1)S(1)}, bf16[2,144,768]{2,0,1:T(2,128)(2,1)S(1)}, u32[]{:S(2)}, u32[]{:S(2)}) collective-permute-start(bf16[2,144,768]{2,0,1:T(2,128)(2,1)S(1)} %bitcast.191), channel_id=1, source_target_pairs={{0,6},{2,4},{4,2},{6,0},{8,14},{10,12},{12,10},{14,8},{16,22},{18,... | collective-permute-start | bytes 1327112 | tf_op jit(solution)/shard_map/ppermute | solution.py:542
  88.8 7.2 copy-start.9
  92.5 12.2 %collective-permute-start.7 = (bf16[2,144,768]{2,0,1:T(2,128)(2,1)S(1)}, bf16[2,144,768]{2,0,1:T(2,128)(2,1)S(1)}, u32[]{:S(2)}, u32[]{:S(2)}) collective-permute-start(bf16[2,144,768]{2,0,1:T(2,128)(2,1)S(1)} %constant_dynamic-update-slice_fusion), channel_id=1, source_target_pairs={{0,8},{2,10},{4,12},{6,14},{8,16},{10,18},{12,20},{14,22},{16,24},... | collective-permute-start | bytes 1327112 | tf_op jit(solution)/shard_map/ppermute | solution.py:572
  96.0 14.6 %copy-start.17 = (bf16[1,512,1536]{2,1,0:T(8,128)(2,1)S(1)}, bf16[1,512,1536]{2,1,0:T(8,128)(2,1)}, u32[]{:S(2)}) copy-start(bf16[1,512,1536]{2,1,0:T(8,128)(2,1)} %param.21) | copy-start | bytes 4718596
  105.2 13.2 %collective-permute-start.8 = (bf16[2,144,768]{2,0,1:T(2,128)(2,1)S(1)}, bf16[2,144,768]{2,0,1:T(2,128)(2,1)S(1)}, u32[]{:S(2)}, u32[]{:S(2)}) collective-permute-start(bf16[2,144,768]{2,0,1:T(2,128)(2,1)S(1)} %constant_dynamic-update-slice_fusion.4), channel_id=1, source_target_pairs={{0,16},{2,18},{4,20},{6,22},{8,24},{10,26},{12,28},{14,30},{1,17},... | collective-permute-start | bytes 1327112 | tf_op jit(solution)/shard_map/ppermute | solution.py:572
  123.5 22.9 %collective-permute-start.11 = (bf16[2,128,768]{2,1,0:T(8,128)(2,1)}, bf16[2,128,768]{2,1,0:T(8,128)(2,1)S(1)}, u32[]{:S(2)}, u32[]{:S(2)}) collective-permute-start(bf16[2,128,768]{2,1,0:T(8,128)(2,1)} %copy.85), channel_id=1, source_target_pairs={{0,6},{2,4},{4,2},{6,0},{8,14},{10,12},{12,10},{14,8},{16,22},{18,... | collective-permute-start | bytes 1179656 | tf_op jit(solution)/shard_map/ppermute | solution.py:542
  125.9 20.5 %collective-permute-start.9 = (bf16[2,128,768]{2,1,0:T(8,128)(2,1)}, bf16[2,128,768]{2,1,0:T(8,128)(2,1)S(1)}, u32[]{:S(2)}, u32[]{:S(2)}) collective-permute-start(bf16[2,128,768]{2,1,0:T(8,128)(2,1)} %copy.82), channel_id=1, source_target_pairs={{0,4},{2,6},{4,0},{6,2},{8,12},{10,14},{12,8},{14,10},{16,20},{18,... | collective-permute-start | bytes 1179656 | tf_op jit(solution)/shard_map/ppermute | solution.py:542
  126.4 20.0 %collective-permute-start.10 = (bf16[2,128,768]{2,0,1:T(2,128)(2,1)}, bf16[2,128,768]{2,0,1:T(2,128)(2,1)S(1)}, u32[]{:S(2)}, u32[]{:S(2)}) collective-permute-start(bf16[2,128,768]{2,0,1:T(2,128)(2,1)} %get-tuple-element.98), channel_id=1, source_target_pairs={{0,2},{2,0},{4,6},{6,4},{8,10},{10,8},{12,14},{14,12},{16,18},{18,... | collective-permute-start | bytes 1179656 | tf_op jit(solution)/shard_map/ppermute | solution.py:542
  187.0 14.1 %collective-permute-start.14 = (bf16[2,144,768]{2,0,1:T(2,128)(2,1)S(1)}, bf16[2,144,768]{2,0,1:T(2,128)(2,1)S(1)}, u32[]{:S(2)}, u32[]{:S(2)}) collective-permute-start(bf16[2,144,768]{2,0,1:T(2,128)(2,1)S(1)} %get-tuple-element.117), channel_id=1, source_target_pairs={{0,6},{2,4},{4,2},{6,0},{8,14},{10,12},{12,10},{14,8},{16,22},{18,... | collective-permute-start | bytes 1327112 | tf_op jit(solution)/shard_map/ppermute | solution.py:542
  189.4 16.6 %collective-permute-start.13 = (bf16[2,144,768]{2,0,1:T(2,128)(2,1)S(1)}, bf16[2,144,768]{2,0,1:T(2,128)(2,1)S(1)}, u32[]{:S(2)}, u32[]{:S(2)}) collective-permute-start(bf16[2,144,768]{2,0,1:T(2,128)(2,1)S(1)} %get-tuple-element.118), channel_id=1, source_target_pairs={{0,2},{2,0},{4,6},{6,4},{8,10},{10,8},{12,14},{14,12},{16,18},{18,... | collective-permute-start | bytes 1327112 | tf_op jit(solution)/shard_map/ppermute | solution.py:542
  190.0 16.0 %collective-permute-start.12 = (bf16[2,144,768]{2,0,1:T(2,128)(2,1)S(1)}, bf16[2,144,768]{2,0,1:T(2,128)(2,1)S(1)}, u32[]{:S(2)}, u32[]{:S(2)}) collective-permute-start(bf16[2,144,768]{2,0,1:T(2,128)(2,1)S(1)} %get-tuple-element.119), channel_id=1, source_target_pairs={{0,4},{2,6},{4,0},{6,2},{8,12},{10,14},{12,8},{14,10},{16,20},{18,... | collective-permute-start | bytes 1327112 | tf_op jit(solution)/shard_map/ppermute | solution.py:542
  218.2 26.0 %collective-permute-start.15 = (bf16[2,144,768]{2,1,0:T(8,128)(2,1)}, bf16[2,144,768]{2,1,0:T(8,128)(2,1)S(1)}, u32[]{:S(2)}, u32[]{:S(2)}) collective-permute-start(bf16[2,144,768]{2,1,0:T(8,128)(2,1)} %concatenate.91), channel_id=1, source_target_pairs={{8,0},{10,2},{12,4},{14,6},{16,8},{18,10},{20,12},{22,14},{24,16},... | collective-permute-start | bytes 1327112 | tf_op jit(solution)/shard_map/ppermute | solution.py:572
  251.0 24.0 %collective-permute-start.16 = (bf16[2,144,768]{2,1,0:T(8,128)(2,1)}, bf16[2,144,768]{2,1,0:T(8,128)(2,1)}, u32[]{:S(2)}, u32[]{:S(2)}) collective-permute-start(bf16[2,144,768]{2,1,0:T(8,128)(2,1)} %concatenate.92), channel_id=1, source_target_pairs={{16,0},{18,2},{20,4},{22,6},{24,8},{26,10},{28,12},{30,14},{17,1},... | collective-permute-start | bytes 1327112 | tf_op jit(solution)/shard_map/ppermute | solution.py:572
  252.7 17.2 %copy-start.31 = (f32[2,1,768]{2,1,0:T(1,128)S(1)}, f32[2,1,768]{2,1,0:T(1,128)}, u32[]{:S(2)}) copy-start(f32[2,1,768]{2,1,0:T(1,128)} %copy-done.30) | copy-start | bytes 18436
  252.7 17.2 %copy-start.36 = (f32[2,1,768]{2,1,0:T(1,128)S(1)}, f32[2,1,768]{2,1,0:T(1,128)}, u32[]{:S(2)}) copy-start(f32[2,1,768]{2,1,0:T(1,128)} %get-tuple-element.89) | copy-start | bytes 18436
  252.7 17.2 %copy-start.35 = (f32[2,1,768]{2,1,0:T(1,128)S(1)}, f32[2,1,768]{2,1,0:T(1,128)}, u32[]{:S(2)}) copy-start(f32[2,1,768]{2,1,0:T(1,128)} %get-tuple-element.90) | copy-start | bytes 18436
  252.7 17.2 %copy-start.29 = (f32[2,1,768]{2,1,0:T(1,128)S(1)}, f32[2,1,768]{2,1,0:T(1,128)}, u32[]{:S(2)}) copy-start(f32[2,1,768]{2,1,0:T(1,128)} %copy-done.28) | copy-start | bytes 18436
  252.7 23.5 %copy-start.5 = (bf16[2,144,768]{2,0,1:T(2,128)(2,1)S(1)}, bf16[2,144,768]{2,0,1:T(2,128)(2,1)}, u32[]{:S(2)}) copy-start(bf16[2,144,768]{2,0,1:T(2,128)(2,1)} %copy-done.4) | copy-start | bytes 1327108
  252.7 23.5 %copy-start.33 = (f32[2,768]{1,0:T(2,128)S(1)}, f32[2,768]{1,0:T(2,128)}, u32[]{:S(2)}) copy-start(f32[2,768]{1,0:T(2,128)} %copy-done.32) | copy-start | bytes 18436
  269.8 7.3 copy-start.14
  277.5 13.1 %collective-permute-start.19 = (bf16[2,128,768]{2,1,0:T(8,128)(2,1)S(1)}, bf16[2,128,768]{2,1,0:T(8,128)(2,1)S(1)}, u32[]{:S(2)}, u32[]{:S(2)}) collective-permute-start(bf16[2,128,768]{2,1,0:T(8,128)(2,1)S(1)} %get-tuple-element.80), channel_id=1, source_target_pairs={{0,6},{2,4},{4,2},{6,0},{8,14},{10,12},{12,10},{14,8},{16,22},{18,... | collective-permute-start | bytes 1179656 | tf_op jit(solution)/shard_map/ppermute | solution.py:542
  279.3 17.9 %collective-permute-start.18 = (bf16[2,128,768]{2,1,0:T(8,128)(2,1)S(1)}, bf16[2,128,768]{2,1,0:T(8,128)(2,1)S(1)}, u32[]{:S(2)}, u32[]{:S(2)}) collective-permute-start(bf16[2,128,768]{2,1,0:T(8,128)(2,1)S(1)} %get-tuple-element.131), channel_id=1, source_target_pairs={{0,2},{2,0},{4,6},{6,4},{8,10},{10,8},{12,14},{14,12},{16,18},{18,... | collective-permute-start | bytes 1179656 | tf_op jit(solution)/shard_map/ppermute | solution.py:542
  280.8 16.4 %collective-permute-start.17 = (bf16[2,128,768]{2,1,0:T(8,128)(2,1)S(1)}, bf16[2,128,768]{2,1,0:T(8,128)(2,1)S(1)}, u32[]{:S(2)}, u32[]{:S(2)}) collective-permute-start(bf16[2,128,768]{2,1,0:T(8,128)(2,1)S(1)} %get-tuple-element.132), channel_id=1, source_target_pairs={{0,4},{2,6},{4,0},{6,2},{8,12},{10,14},{12,8},{14,10},{16,20},{18,... | collective-permute-start | bytes 1179656 | tf_op jit(solution)/shard_map/ppermute | solution.py:542
  329.2 5.5 copy-start.25
  329.2 7.6 copy-start.18
  335.5 8.9 collective-permute-start.20
  336.8 6.9 copy-start.22
  336.8 7.6 copy-start.24
  336.8 7.6 copy-start.34
  336.8 7.6 copy-start.12
  343.2 32.3 %collective-permute-start.23 = (bf16[1536,1536]{1,0:T(8,128)(2,1)}, bf16[1536,1536]{1,0:T(8,128)(2,1)}, u32[]{:S(2)}, u32[]{:S(2)}) collective-permute-start(bf16[1536,1536]{1,0:T(8,128)(2,1)} %convolution_convert_fusion), channel_id=1, source_target_pairs={{0,1},{1,0},{2,3},{3,2},{4,5},{5,4},{6,7},{7,6},{8,9},{9,8},{10,11... | collective-permute-start | bytes 14155784 | tf_op jit(solution)/shard_map/ppermute | solution.py:790
  343.2 41.1 %collective-permute-start.21 = (bf16[768,3072]{1,0:T(8,128)(2,1)}, bf16[768,3072]{1,0:T(8,128)(2,1)}, u32[]{:S(2)}, u32[]{:S(2)}) collective-permute-start(bf16[768,3072]{1,0:T(8,128)(2,1)} %convolution_convert_fusion.2), channel_id=1, source_target_pairs={{0,1},{1,0},{2,3},{3,2},{4,5},{5,4},{6,7},{7,6},{8,9},{9,8},{10,11... | collective-permute-start | bytes 14155784 | tf_op jit(solution)/shard_map/ppermute | solution.py:790
  344.9 6.0 copy-start.6
  345.6 5.3 copy-start.46
  350.9 6.2 copy-start.39
  350.9 6.2 copy-start.23
  350.9 39.5 %collective-permute-start.22 = (bf16[768,3376]{0,1:T(8,128)(2,1)}, bf16[768,3376]{0,1:T(8,128)(2,1)}, u32[]{:S(2)}, u32[]{:S(2)}) collective-permute-start(bf16[768,3376]{0,1:T(8,128)(2,1)} %convolution_convert_fusion.1), channel_id=1, source_target_pairs={{0,1},{1,0},{2,3},{3,2},{4,5},{5,4},{6,7},{7,6},{8,9},{9,8},{10,11... | collective-permute-start | bytes 15556616 | tf_op jit(solution)/shard_map/ppermute | solution.py:790
  357.1 6.7 copy-start.47
  357.1 11.9 %slice-start.3 = ((s8[9904128]{0:T(1024)(128)(4,1)}), s8[4194304]{0:T(1024)(128)(4,1)S(1)}, s32[]{:S(2)}) async-start(s8[9904128]{0:T(1024)(128)(4,1)} %bitcast.171), calls=%async_computation.5 | async-start | bytes 8388608
  357.1 11.9 %slice-start.4 = ((s8[9904128]{0:T(1024)(128)(4,1)}), s8[4194304]{0:T(1024)(128)(4,1)S(1)}, s32[]{:S(2)}) async-start(s8[9904128]{0:T(1024)(128)(4,1)} %bitcast.171), calls=%async_computation.6 | async-start | bytes 8388608
  375.2 537.9 %all-reduce.7.cloned.1.call-start = ((), (), s32[]{:S(2)}) async-start(), calls=%async_computation.1 | async-start | bytes 29245440 | tf_op jit(solution)/shard_map/psum | solution.py:948
  375.5 8.8 copy-start.21
  375.5 8.8 copy-start.48
  384.3 6.2 copy-start.8
  398.3 5.7 copy-start.44
  404.0 6.4 copy-start.3
  404.0 6.4 copy-start.19
  913.1 14.3 %slice-start.6 = ((s8[5185536]{0:T(1024)(128)(4,1)}), s8[991232]{0:T(1024)(128)(4,1)S(1)}, s32[]{:S(2)}) async-start(s8[5185536]{0:T(1024)(128)(4,1)} %bitcast.176), calls=%async_computation.8 | async-start | bytes 1982464
  919.8 7.6 copy-start.1
  919.8 7.6 slice-start.7
  (20 other events, 57.5 us)
Sparse Core Ops, SparseCore 0:
  375.3 119.3 all-reduce.4
  502.2 410.7 all-reduce.6

commit v2 on v1

v2 whole, which is shorter than its diff:
```python
import functools

import jax
import jax.numpy as jnp
from jax import lax
from jax.experimental import pallas as pl
from jax.experimental.pallas import tpu as pltpu
from jax.sharding import PartitionSpec as P

HEADS = 48
HEAD_DIM = 64
STATE = 128
CONV = 4
INNER = 3072
CONV_CH = 3328
EPSILON = 1e-05

QUARTERS = 4
Q_HEADS = HEADS // QUARTERS
Q_LANES = INNER // QUARTERS
TILE = 128
Q_TILES = Q_LANES // TILE
EDGE = 16
PAYLOAD = STATE + EDGE
ROWS = 128
SIDE = 16
SUB = 128
FAR = -1e30
VMEM = 60 * 1024 * 1024
HIGHEST = lax.Precision.HIGHEST
F32 = jnp.float32
BF16 = jnp.bfloat16


def params():
    return pltpu.CompilerParams(vmem_limit_bytes=VMEM)


def cost(microseconds):
    return pl.CostEstimate(
        flops=0, transcendentals=0, bytes_accessed=int(microseconds * 3_400_000)
    )


def low_lanes():
    return lax.broadcasted_iota(jnp.int32, (1, TILE), 1) < HEAD_DIM


def pick(per_head, tile):
    return jnp.where(
        low_lanes(),
        per_head[:, 2 * tile : 2 * tile + 1],
        per_head[:, 2 * tile + 1 : 2 * tile + 2],
    )


def head_columns(channels, columns, offset):
    row = lax.broadcasted_iota(jnp.int32, (channels, columns), 0)
    col = lax.broadcasted_iota(jnp.int32, (channels, columns), 1) - offset
    return ((row >= HEAD_DIM * col) & (row < HEAD_DIM * col + HEAD_DIM)).astype(BF16)


def head_sums(wide, selector):
    high = wide.astype(BF16)
    rest = (wide - high.astype(F32)).astype(BF16)
    return jnp.dot(high, selector, preferred_element_type=F32) + jnp.dot(
        rest, selector, preferred_element_type=F32
    )


def dot(left, right):
    return jnp.dot(left, right, preferred_element_type=F32)


def dot_last(left, right, precision=None):
    return lax.dot_general(
        left,
        right,
        (((1,), (1,)), ((), ())),
        preferred_element_type=F32,
        precision=precision,
    )


def dot_first(left, right, precision=None):
    return lax.dot_general(
        left,
        right,
        (((0,), (0,)), ((), ())),
        preferred_element_type=F32,
        precision=precision,
    )


def mixture_of(conv_input, seq, lanes, weight, bias):
    total = bias
    for tap in range(CONV):
        start = EDGE - CONV + 1 + tap
        total = total + weight[tap : tap + 1] * conv_input[seq, start : start + 256, lanes]
    return total


def silu_slope(value):
    gate = jax.nn.sigmoid(value)
    return gate * (1.0 + value * (1.0 - gate))


def three_parts(value):
    high = value.astype(BF16).astype(F32)
    middle = (value - high).astype(BF16).astype(F32)
    return high, middle, value - high - middle


def edge_rows(decay, along):
    index = lax.broadcasted_iota(jnp.int32, (EDGE, TILE), 0)
    rows = jnp.zeros((EDGE, TILE), F32)
    for row, part in enumerate(three_parts(decay) + three_parts(along)):
        rows = jnp.where(index == row, part, rows)
    return rows.astype(BF16)


def read_payload(ref, seq, lanes):
    state = ref[seq, :STATE, lanes].astype(F32)
    rows = ref[seq, STATE:, lanes].astype(F32)
    decay = rows[0:1] + rows[1:2] + rows[2:3]
    along = rows[3:4] + rows[4:5] + rows[5:6]
    return state, decay, along


def write_payload(ref, seq, lanes, state, decay, along):
    ref[seq, :STATE, lanes] = state.astype(BF16)
    ref[seq, STATE:, lanes] = edge_rows(decay, along)


def after(first, second):
    return (
        second[0] + second[1] * first[0],
        second[1] * first[1],
        second[2] + second[1] * first[2],
    )


def empty():
    return (
        jnp.zeros((STATE, TILE), F32),
        jnp.ones((1, TILE), F32),
        jnp.zeros((1, TILE), F32),
    )


def parts_of_quarter():
    for seq in range(2):
        for tile in range(Q_TILES):
            yield seq, slice(TILE * tile, TILE * tile + TILE)


def joined(refs, seq, lanes):
    result = read_payload(refs[0], seq, lanes)
    for ref in refs[1:]:
        result = after(read_payload(ref, seq, lanes), result)
    return result


def plane_kernel(reverse, member, *refs):
    members, total = refs[:QUARTERS], refs[QUARTERS]
    order = range(QUARTERS)[::-1] if reverse else range(QUARTERS)
    for place in range(QUARTERS):

        @pl.when(member[0] == place)
        def _(place=place):
            for seq, lanes in parts_of_quarter():
                whole = None
                for which in order:
                    here = read_payload(members[place ^ which], seq, lanes)
                    whole = here if whole is None else after(whole, here)
                write_payload(total, seq, lanes, *whole)


def link_kernel(*refs):
    total, received, result = refs[0], refs[1:-1], refs[-1]
    for seq, lanes in parts_of_quarter():
        whole = after(joined(received, seq, lanes), read_payload(total, seq, lanes))
        write_payload(result, seq, lanes, *whole)


def spread_kernel(reverse, member, *refs):
    members, received, results = refs[:QUARTERS], refs[QUARTERS:-QUARTERS], refs[-QUARTERS:]
    order = list(range(QUARTERS)[::-1] if reverse else range(QUARTERS))
    for place in range(QUARTERS):

        @pl.when(member[0] == place)
        def _(place=place):
            for seq, lanes in parts_of_quarter():
                whole = joined(received, seq, lanes)
                for which in order:
                    write_payload(results[place ^ which], seq, lanes, *whole)
                    if which != order[-1]:
                        whole = after(whole, read_payload(members[place ^ which], seq, lanes))


def arrange_kernel(member, *refs):
    pieces, state_ref, along_ref = refs[:QUARTERS], refs[QUARTERS], refs[QUARTERS + 1]
    for by in range(QUARTERS):

        @pl.when(pl.program_id(0) == by)
        def _(by=by):
            for seq, lanes in parts_of_quarter():
                state_ref[seq, :, lanes] = pieces[by][seq, :STATE, lanes]
                rows = pieces[by][seq, STATE:, lanes].astype(F32)
                along = rows[3:4] + rows[4:5] + rows[5:6]
                along_ref[seq, :, lanes] = jnp.broadcast_to(along, (8, TILE))


def step_kernel(
    conv_input,
    weight,
    bias,
    small,
    direction,
    bc_ref,
    bt_ref,
    scores_ref,
    scores_t_ref,
    step_ref,
    sum_ref,
    step_q_ref,
    sum_q_ref,
    sum_t_ref,
):
    row = lax.broadcasted_iota(jnp.int32, (256, 256), 0)
    col = lax.broadcasted_iota(jnp.int32, (256, 256), 1)
    lower = (row >= col).astype(F32)
    lane = lax.broadcasted_iota(jnp.int32, (1, TILE), 1)
    for seq in range(2):
        mixture = mixture_of(conv_input, seq, slice(0, 256), weight[...], bias[...])
        active = mixture * jax.nn.sigmoid(mixture)
        bc_ref[seq] = active
        writes, readout = active[:, :STATE], active[:, STATE:]
        bt_ref[seq] = writes.T.astype(BF16)
        scores = dot_last(readout, writes, HIGHEST)
        scores_ref[seq] = scores
        scores_t_ref[seq] = scores.T
        along = jnp.sum(readout * direction[...], axis=1, keepdims=True)
        raw = conv_input[seq, EDGE : EDGE + 256, 256:384] + small[0:1]
        raw = jnp.where(lane < HEADS, raw, 0.0)
        step = jnp.maximum(raw, 0.0) + jnp.log1p(jnp.exp(-jnp.abs(raw)))
        log_decay = -jnp.exp(small[1:2]) * step
        running = jnp.dot(lower, log_decay, preferred_element_type=F32, precision=HIGHEST)
        step_ref[seq] = step
        sum_ref[seq] = jnp.where(lane == HEADS, along, running)
        for quarter in range(QUARTERS):
            shift = (TILE - Q_HEADS * quarter) % TILE
            step_q = pltpu.roll(step, shift, 1) if shift else step
            sum_q = pltpu.roll(running, shift, 1) if shift else running
            step_q_ref[quarter, seq] = step_q[:, :SIDE]
            sum_q_ref[quarter, seq] = jnp.where(lane == Q_HEADS, along, sum_q)[:, :SIDE]
            sum_t_ref[quarter, seq] = sum_q.T[:EDGE]


def state_kernel(
    member, conv_input, weight, bias, step_q, sum_q, bt_ref, column, x_ref, payload_ref
):
    for seq in range(2):
        running = sum_q[0, seq]
        last = running[255:256]
        scale = step_q[0, seq] * jnp.exp(last - running)
        whole = jnp.exp(last)
        for tile in range(Q_TILES):
            lanes = slice(TILE * tile, TILE * tile + TILE)
            mixture = mixture_of(conv_input, seq, lanes, weight[:, lanes], bias[:, lanes])
            x = mixture * jax.nn.sigmoid(mixture)
            x_ref[seq, :, lanes] = x
            added = dot(bt_ref[seq], (x * pick(scale, tile)).astype(BF16))
            along = jnp.sum(added * column[...], axis=0, keepdims=True)
            payload_ref[0, seq, :STATE, lanes] = (added - column[...] * along).astype(BF16)
            payload_ref[0, seq, STATE:, lanes] = edge_rows(pick(whole, tile), along)


def intra_kernel(x_ref, step_q, sum_q, sum_t, scores, skip, *refs):
    y_ref = refs[-1]
    row = lax.broadcasted_iota(jnp.int32, (SUB, SUB), 0)
    col = lax.broadcasted_iota(jnp.int32, (SUB, SUB), 1)
    causal = row >= col
    low = low_lanes()
    for seq in range(2):
        step, running = step_q[0, seq], sum_q[0, seq]
        middle = running[SUB - 1 : SUB]
        ahead = jnp.exp(middle - running[:SUB])
        later = jnp.exp(running[SUB:] - middle)
        across = scores[seq, SUB:, :SUB].astype(BF16)
        for tile in range(Q_TILES):
            lanes = slice(TILE * tile, TILE * tile + TILE)
            x = x_ref[seq, :, lanes]
            scaled = x * pick(step, tile)
            low_part = jnp.where(low, scaled, 0.0).astype(BF16)
            high_part = jnp.where(low, 0.0, scaled).astype(BF16)
            for part in range(2):
                rows = slice(SUB * part, SUB * part + SUB)
                weights = []
                for h in (2 * tile, 2 * tile + 1):
                    spread = running[rows, h : h + 1] - sum_t[0, seq, h : h + 1, rows]
                    decayed = jnp.exp(jnp.where(causal, spread, FAR))
                    weights.append((decayed * scores[seq, rows, rows]).astype(BF16))
                inside = dot(
                    jnp.concatenate(weights, 1),
                    jnp.concatenate([low_part[rows], high_part[rows]], 0),
                )
                if part:
                    earlier = (scaled[:SUB] * pick(ahead, tile)).astype(BF16)
                    inside = inside + pick(later, tile) * dot(across, earlier)
                y_ref[seq, rows, lanes] = inside + skip[:, lanes] * x[rows]


def gate_kernel(
    member,
    y_ref,
    z_ref,
    grad_ref,
    bc_ref,
    sum_ref,
    entering,
    along,
    gain,
    out_ref,
    grad_z_ref,
    grad_scan_ref,
    payload_ref,
    gain_grad_ref,
    scanned_ref,
    gated_ref,
    gate_ref,
    spread,
    state_ref,
):
    step = pl.program_id(0)
    per_seq = pl.num_programs(0) // 2
    running = sum_ref[0]
    start = jnp.exp(running)
    read_along = running[:, HEADS : HEADS + 1]
    readout = bc_ref[0, :, STATE:].astype(BF16)
    scanned_ref[...] = dot(readout, entering[0])
    squares = jnp.zeros((ROWS, TILE), F32)
    overlap = jnp.zeros((ROWS, TILE), F32)
    for tile in range(INNER // TILE):
        lanes = slice(TILE * tile, TILE * tile + TILE)
        carried = scanned_ref[:, lanes] + read_along * along[0, 0:1, lanes]
        scanned = y_ref[0, :, lanes] + pick(start, tile) * carried
        scanned_ref[:, lanes] = scanned
        z = z_ref[0, :, lanes]
        gate = jax.nn.sigmoid(z)
        gate_ref[:, lanes] = gate
        gated = scanned * (z * gate)
        gated_ref[:, lanes] = gated
        squares = squares + gated * gated
        overlap = overlap + gated * (grad_ref[0, :, lanes] * gain[:, lanes])
    mean = jnp.sum(squares, axis=1, keepdims=True) / INNER
    inverse = lax.rsqrt(mean + EPSILON)
    back = jnp.sum(overlap, axis=1, keepdims=True) / INNER * inverse * inverse * inverse

    @pl.when(step == 0)
    def _():
        gain_grad_ref[...] = jnp.zeros_like(gain_grad_ref)

    for tile in range(INNER // TILE):
        lanes = slice(TILE * tile, TILE * tile + TILE)
        gated = gated_ref[:, lanes]
        grad = grad_ref[0, :, lanes]
        scaled = gated * inverse
        out_ref[0, :, lanes] = (scaled * gain[:, lanes]).astype(BF16)
        gain_grad_ref[:, lanes] += jnp.sum(grad * scaled, axis=0, keepdims=True)
        grad_gated = inverse * (grad * gain[:, lanes]) - gated * back
        z = z_ref[0, :, lanes]
        gate = gate_ref[:, lanes]
        grad_scan = grad_gated * (z * gate)
        grad_z_ref[0, :, lanes] = (
            grad_gated * scanned_ref[:, lanes] * (gate * (1.0 + z * (1.0 - gate)))
        ).astype(BF16)
        grad_scan_ref[0, :, lanes] = grad_scan
        rounded = grad_scan.astype(BF16).astype(F32)
        spread[:, lanes] = (rounded * pick(start, tile)).astype(BF16)
    added = dot_first(readout, spread[...])

    @pl.when(step % per_seq == 0)
    def _():
        state_ref[...] = added

    @pl.when(step % per_seq != 0)
    def _():
        state_ref[...] += added

    @pl.when(step % per_seq == per_seq - 1)
    def _():
        seq = step // per_seq
        whole = start[ROWS - 1 : ROWS]
        zero = jnp.zeros((1, TILE), F32)
        for tile in range(INNER // TILE):
            lanes = slice(TILE * tile, TILE * tile + TILE)
            place = slice(TILE * (tile % Q_TILES), TILE * (tile % Q_TILES) + TILE)
            slot = member[0] ^ (tile // Q_TILES)
            payload_ref[slot, seq, :STATE, place] = state_ref[:, lanes].astype(BF16)
            payload_ref[slot, seq, STATE:, place] = edge_rows(pick(whole, tile), zero)


def intra_back_kernel(
    x_ref,
    grad_ref,
    y_ref,
    conv_input,
    weight,
    bias,
    step_q,
    sum_q,
    sum_t,
    scores_t,
    bc_ref,
    entering,
    along,
    skip,
    direction,
    *refs,
):
    known_ref, slope_ref, grad_scores_ref, heads_ref, grad_read_ref, product, spread = refs[-7:]
    row = lax.broadcasted_iota(jnp.int32, (SUB, SUB), 0)
    col = lax.broadcasted_iota(jnp.int32, (SUB, SUB), 1)
    causal = row <= col
    low = low_lanes()

    @pl.when(pl.program_id(0) == 0)
    def _():
        grad_scores_ref[...] = jnp.zeros_like(grad_scores_ref)
        grad_read_ref[...] = jnp.zeros_like(grad_read_ref)

    for seq in range(2):
        step, running = step_q[0, seq], sum_q[0, seq]
        middle = running[SUB - 1 : SUB]
        start = jnp.exp(running)
        read_along = running[:, Q_HEADS : Q_HEADS + 1]
        ahead = jnp.exp(middle - running[:SUB])
        later = jnp.exp(running[SUB:] - middle)
        across = scores_t[seq, :SUB, SUB:].astype(BF16)
        readout = bc_ref[seq, :, STATE:].astype(BF16)
        inner = [jnp.zeros((SUB, SUB), F32) for _ in range(2)]
        outer = jnp.zeros((SUB, SUB), F32)
        meeting = jnp.zeros((256, TILE), F32)
        for tile in range(Q_TILES):
            lanes = slice(TILE * tile, TILE * tile + TILE)
            x = x_ref[seq, :, lanes]
            size = pick(step, tile)
            scaled = x * size
            grad = grad_ref[seq, :, lanes]
            begin = pick(start, tile)
            low_grad = jnp.where(low, grad, 0.0).astype(BF16)
            high_grad = jnp.where(low, 0.0, grad).astype(BF16)
            rounded = grad.astype(BF16)
            line = along[seq, 0:1, lanes]
            carried = dot(readout, entering[seq, :, lanes]) + read_along * line
            through = skip[:, lanes] * x
            product[2, :, lanes] = rounded.astype(F32) * (
                y_ref[seq, :, lanes] + begin * carried - through
            )
            widened = grad * begin
            meeting = meeting + widened * line
            spread[:, lanes] = widened.astype(BF16)
            mixture = mixture_of(conv_input, seq, lanes, weight[:, lanes], bias[:, lanes])
            slope = silu_slope(mixture)
            slope_ref[seq, :, lanes] = slope.astype(BF16)
            sides = (
                jnp.where(low, scaled, 0.0).astype(BF16),
                jnp.where(low, 0.0, scaled).astype(BF16),
            )
            for part in range(2):
                rows = slice(SUB * part, SUB * part + SUB)
                weights = []
                for side in range(2):
                    h = 2 * tile + side
                    apart = sum_t[0, seq, h : h + 1, rows] - running[rows, h : h + 1]
                    decayed = jnp.exp(jnp.where(causal, apart, FAR))
                    weights.append((decayed * scores_t[seq, rows, rows]).astype(BF16))
                    inner[part] = inner[part] + decayed * dot_last(
                        sides[side][rows], rounded[rows]
                    )
                inside = dot(
                    jnp.concatenate(weights, 1),
                    jnp.concatenate([low_grad[rows], high_grad[rows]], 0),
                )
                if not part:
                    beyond = (rounded[SUB:].astype(F32) * pick(later, tile)).astype(BF16)
                    factor = pick(ahead, tile)
                    inside = inside + factor * dot(across, beyond)
                    outer = outer + dot_last((scaled[:SUB] * factor).astype(BF16), beyond)
                product[0, rows, lanes] = scaled[rows].astype(BF16).astype(F32) * inside
                product[1, rows, lanes] = x[rows] * inside
                known_ref[seq, rows, lanes] = (
                    size[rows] * inside + skip[:, lanes] * grad[rows]
                ) * slope[rows]
        grad_scores_ref[seq, :SUB, :SUB] += inner[0]
        grad_scores_ref[seq, SUB:, SUB:] += inner[1]
        grad_scores_ref[seq, :SUB, SUB:] += outer
        total = jnp.zeros((256, TILE), F32)
        for kind in range(3):
            total = total + head_sums(product[kind], head_columns(Q_LANES, TILE, Q_HEADS * kind))
        heads_ref[0, seq] = total
        grad_read_ref[seq] += (
            dot_last(spread[...], entering[seq])
            + jnp.sum(meeting, axis=1, keepdims=True) * direction[...]
        )


def channel_kernel(
    known_ref,
    slope_ref,
    x_ref,
    weight,
    step_q,
    sum_q,
    bc_ref,
    leaving,
    entering,
    along,
    column,
    grad_conv_ref,
    tail_ref,
    halo_ref,
    grad_mix_ref,
    heads_ref,
    grad_writes_ref,
    meeting_ref,
    padded,
    product,
    spread,
):
    zeros = jnp.zeros((EDGE, TILE), F32)
    padded[:EDGE] = zeros
    padded[EDGE + 256 :] = zeros
    meeting_ref[...] = jnp.zeros_like(meeting_ref)

    @pl.when(pl.program_id(0) == 0)
    def _():
        grad_writes_ref[...] = jnp.zeros_like(grad_writes_ref)

    for seq in range(2):
        running = sum_q[0, seq]
        remain = jnp.exp(running[255:256] - running)
        scale = step_q[0, seq] * remain
        writes = bc_ref[seq, :, :STATE].astype(BF16)
        for tile in range(Q_TILES):
            lanes = slice(TILE * tile, TILE * tile + TILE)
            taps = weight[:, lanes]
            x = x_ref[seq, :, lanes]
            back = leaving[seq, :, lanes]
            shared = dot(writes, back)
            left = pick(remain, tile)
            product[:, lanes] = x * (left * shared)
            factor = pick(scale, tile)
            spread[:, lanes] = (x * factor).astype(BF16)
            slope = slope_ref[seq, :, lanes].astype(F32)
            grad_mix = known_ref[seq, :, lanes] + factor * slope * shared
            grad_mix_ref[seq, :, lanes] = grad_mix.astype(BF16)
            padded[EDGE : EDGE + 256] = grad_mix
            grad_conv = taps[0:1] * padded[3 : 3 + EDGE + 256]
            for tap in range(1, CONV):
                grad_conv = (
                    grad_conv + taps[tap : tap + 1] * padded[3 - tap : 3 - tap + EDGE + 256]
                )
            halo_ref[seq, :, lanes] = grad_conv[:EDGE].astype(BF16)
            grad_conv_ref[seq, :, lanes] = grad_conv[EDGE:].astype(BF16)
            tail_ref[seq, :, lanes] = grad_conv[256:]
            state = entering[seq, :, lanes].astype(F32) + column[...] * along[seq, 0:1, lanes]
            meeting_ref[seq : seq + 1, lanes] = jnp.sum(
                state * back.astype(F32), axis=0, keepdims=True
            )
        heads_ref[0, seq] = head_sums(product[...], head_columns(Q_LANES, TILE, 0))
        grad_writes_ref[seq] += dot_last(spread[...], leaving[seq])


def sums_kernel(conv_input, grad_mix_ref, grad_ref, x_ref, sums_ref):
    sums_ref[...] = jnp.zeros_like(sums_ref)
    for seq in range(2):
        for tile in range(Q_TILES):
            lanes = slice(TILE * tile, TILE * tile + TILE)
            grad_mix = grad_mix_ref[seq, :, lanes].astype(F32)
            for tap in range(CONV):
                begin = EDGE - CONV + 1 + tap
                sums_ref[tap : tap + 1, lanes] += jnp.sum(
                    grad_mix * conv_input[seq, begin : begin + 256, lanes], axis=0, keepdims=True
                )
            sums_ref[4:5, lanes] += jnp.sum(grad_mix, axis=0, keepdims=True)
            sums_ref[5:6, lanes] += jnp.sum(
                grad_ref[seq, :, lanes] * x_ref[seq, :, lanes], axis=0, keepdims=True
            )


def last_kernel(
    conv_input,
    weight,
    bias,
    small,
    bc_ref,
    grad_scores_0,
    grad_scores_1,
    grad_writes,
    grad_read_0,
    grad_read_1,
    known_heads,
    heads,
    meeting,
    step_ref,
    sum_ref,
    grad_conv_ref,
    tail_ref,
    halo_ref,
    sums_ref,
    small_ref,
    padded,
):
    row = lax.broadcasted_iota(jnp.int32, (256, 256), 0)
    col = lax.broadcasted_iota(jnp.int32, (256, 256), 1)
    upper = (row <= col).astype(F32)
    lane = lax.broadcasted_iota(jnp.int32, (1, TILE), 1)
    line = lax.broadcasted_iota(jnp.int32, (256, 1), 0)
    padded[:EDGE] = jnp.zeros((EDGE, 256), F32)
    padded[EDGE + 256 :] = jnp.zeros((EDGE, 256), F32)
    sums_ref[...] = jnp.zeros_like(sums_ref)
    small_ref[...] = jnp.zeros_like(small_ref)
    rate = jnp.exp(small[1:2])
    met_states = head_sums(meeting[...], head_columns(INNER, TILE, 0))
    taps = weight[...]

    def gather(source, seq, kind):
        total = jnp.zeros((256, TILE), F32)
        for quarter in range(QUARTERS):
            value = source[quarter, seq]
            shift = (Q_HEADS * (quarter - kind)) % TILE
            if shift:
                value = pltpu.roll(value, shift, 1)
            first = Q_HEADS * quarter
            total = total + jnp.where((lane >= first) & (lane < first + Q_HEADS), value, 0.0)
        return total

    for seq in range(2):
        step = step_ref[seq]
        by_state = gather(heads, seq, 0)
        at_state = step * by_state
        running = sum_ref[seq]
        last = jnp.where(lane < HEADS, running[255:256], 0.0)
        end = jnp.exp(last) * met_states[seq : seq + 1] + jnp.sum(
            at_state, axis=0, keepdims=True
        )
        grad_sum = (
            gather(known_heads, seq, 2)
            - gather(known_heads, seq, 0)
            - at_state
            + jnp.where(line == 255, end, 0.0)
        )
        grad_log = jnp.dot(upper, grad_sum, preferred_element_type=F32, precision=HIGHEST)
        small_ref[1:2] += jnp.sum(-rate * step * grad_log, axis=0, keepdims=True)
        raw = conv_input[seq, EDGE : EDGE + 256, 256:384] + small[0:1]
        raw = jnp.where(lane < HEADS, raw, 0.0)
        grad_step = gather(known_heads, seq, 1) + by_state - rate * grad_log
        grad_raw = grad_step * jax.nn.sigmoid(raw)
        small_ref[0:1] += jnp.sum(grad_raw, axis=0, keepdims=True)
        grad_conv_ref[seq, :, 256:] = grad_raw[:, :HEADS].astype(BF16)
        writes, readout = bc_ref[seq, :, :STATE], bc_ref[seq, :, STATE:]
        grad_scores = grad_scores_0[seq] + grad_scores_1[seq]
        into_writes = (
            jnp.dot(grad_scores, readout, preferred_element_type=F32, precision=HIGHEST)
            + grad_writes[seq]
        )
        into_read = dot_first(grad_scores, writes, HIGHEST) + grad_read_0[seq] + grad_read_1[seq]
        mixture = mixture_of(conv_input, seq, slice(0, 256), taps, bias[...])
        grad_mix = jnp.concatenate([into_writes, into_read], 1) * silu_slope(mixture)
        padded[EDGE : EDGE + 256] = grad_mix
        grad_conv = taps[0:1] * padded[3 : 3 + EDGE + 256]
        for tap in range(1, CONV):
            grad_conv = grad_conv + taps[tap : tap + 1] * padded[3 - tap : 3 - tap + EDGE + 256]
        halo_ref[seq] = grad_conv[:EDGE].astype(BF16)
        grad_conv_ref[seq, :, :256] = grad_conv[EDGE:].astype(BF16)
        tail_ref[seq] = grad_conv[256:]
        for tap in range(CONV):
            begin = EDGE - CONV + 1 + tap
            sums_ref[tap : tap + 1] += jnp.sum(
                grad_mix * conv_input[seq, begin : begin + 256, :256], axis=0, keepdims=True
            )
        sums_ref[4:5] += jnp.sum(grad_mix, axis=0, keepdims=True)


def shape(dims, dtype=F32):
    return jax.ShapeDtypeStruct(dims, dtype)


def whole_block(dims):
    return pl.BlockSpec(dims, lambda *g: (0,) * len(dims))


def lane_block(dims, width=Q_LANES):
    return pl.BlockSpec(dims + (width,), lambda g: (0,) * len(dims) + (g,))


def quarter_block(dims):
    return pl.BlockSpec((1,) + dims, lambda g, *_: (g,) + (0,) * len(dims))


def own_lanes(dims):
    return pl.BlockSpec(
        dims + (Q_LANES,), lambda g, member: (0,) * len(dims) + (g ^ member[0],)
    )


def own_quarter(dims):
    return pl.BlockSpec((1,) + dims, lambda g, member: (g ^ member[0],) + (0,) * len(dims))


def fixed_block(dims, index):
    return pl.BlockSpec(dims, lambda g: index)


def row_block(width, length=256):
    steps = length // ROWS
    return pl.BlockSpec((1, ROWS, width), lambda g: (g // steps, g % steps, 0))


SCALAR = pl.BlockSpec(memory_space=pltpu.SMEM)
MESSAGE = (2, PAYLOAD, Q_LANES)


def tie(value, *others):
    return lax.optimization_barrier((value,) + others)[0]


def exchange(payload, member, axis, reverse, stages):
    count = lax.axis_size(axis)
    stages = iter(stages)

    def swap(value, by):
        return lax.ppermute(value, axis, [(i, i ^ by) for i in range(count)])

    def meanwhile(sent, arrived):
        work = next(stages, None)
        return tie(arrived, *work(sent)) if work else arrived

    message = shape(MESSAGE, BF16)
    block = whole_block(MESSAGE)
    members = [payload[0]] + [swap(payload[by], by) for by in range(1, QUARTERS)]
    members[-1] = meanwhile(payload, members[-1])
    total = pl.pallas_call(
        functools.partial(plane_kernel, reverse),
        grid=(1,),
        in_specs=[SCALAR] + [block] * QUARTERS,
        out_specs=block,
        out_shape=message,
        compiler_params=params(),
        cost_estimate=cost(2),
        name="plane",
    )(member, *members)
    received = []
    inclusive = total
    span = 1
    while span < count // QUARTERS:
        shift = -QUARTERS * span if reverse else QUARTERS * span
        pairs = [(i, i + shift) for i in range(count) if 0 <= i + shift < count]
        arrived = lax.ppermute(inclusive, axis, pairs)
        received.append(meanwhile(inclusive, arrived) if span < 4 else arrived)
        span *= 2
        if span < count // QUARTERS:
            inclusive = pl.pallas_call(
                link_kernel,
                grid=(1,),
                in_specs=[block] * (1 + len(received)),
                out_specs=block,
                out_shape=message,
                compiler_params=params(),
                cost_estimate=cost(1.5),
                name="link",
            )(total, *received)
    results = pl.pallas_call(
        functools.partial(spread_kernel, reverse),
        grid=(1,),
        in_specs=[SCALAR] + [block] * (QUARTERS + len(received)),
        out_specs=[block] * QUARTERS,
        out_shape=[message] * QUARTERS,
        compiler_params=params(),
        cost_estimate=cost(3),
        name="spread",
    )(member, *members, *received)
    back = [results[0]] + [swap(results[by], by) for by in range(1, QUARTERS)]
    back[-1] = meanwhile(results[-1], back[-1])
    return pl.pallas_call(
        arrange_kernel,
        grid_spec=pltpu.PrefetchScalarGridSpec(
            num_scalar_prefetch=1,
            grid=(QUARTERS,),
            in_specs=[block] * QUARTERS,
            out_specs=[own_lanes((2, STATE)), own_lanes((2, 8))],
        ),
        out_shape=[shape((2, STATE, INNER), BF16), shape((2, 8, INNER))],
        compiler_params=params(),
        cost_estimate=cost(1.5),
        name="arrange",
    )(member, *back)


class Scatter:
    def __init__(self, arrays, axis):
        self.axis = axis
        self.count = lax.axis_size(axis)
        self.place = lax.axis_index(axis)
        self.bits = list(range(self.count.bit_length() - 1))[::-1]
        self.values = [
            a.reshape((2,) * len(self.bits) + (a.shape[0] // self.count, a.shape[1]))
            for a in arrays
        ]

    def wait_for(self, *others):
        self.values = list(lax.optimization_barrier(tuple(self.values) + others))[
            : len(self.values)
        ]

    def send(self, bit):
        position = self.bits.index(bit)
        mine = (self.place >> bit) & 1
        away = [lax.dynamic_index_in_dim(v, 1 - mine, position, False) for v in self.values]
        away = jnp.concatenate([v.astype(BF16) for v in away], axis=-2)
        self.values = [lax.dynamic_index_in_dim(v, mine, position, False) for v in self.values]
        self.bits.remove(bit)
        self.sent = lax.ppermute(
            away, self.axis, [(i, i ^ (1 << bit)) for i in range(self.count)]
        )

    def add(self):
        begin = 0
        for i, value in enumerate(self.values):
            end = begin + value.shape[-2]
            self.values[i] = value + self.sent[..., begin:end, :].astype(F32)
            begin = end


def add_up(value, axes):
    for axis in axes:
        count = lax.axis_size(axis)
        for bit in range(count.bit_length() - 1):
            value = value + lax.ppermute(value, axis, [(i, i ^ (1 << bit)) for i in range(count)])
    return value


def finish_kernel(gate_rows, last_rows, out_rows, in_grad, out_grad):
    step = pl.program_id(0)
    length, columns = gate_rows.shape[0] * gate_rows.shape[1], gate_rows.shape[2]

    @pl.when(step < 2 * INNER // length)
    def _():
        in_grad[...] = gate_rows[...].reshape(length, columns).astype(F32)

    @pl.when(step == 2 * INNER // length)
    def _():
        rows = last_rows.shape[0] * last_rows.shape[1]
        keep = min(rows, in_grad.shape[0])
        in_grad[:keep] = last_rows[...].reshape(rows, columns)[:keep].astype(F32)

    @pl.when(step < INNER // length)
    def _():
        group, per = out_rows.shape[0], out_rows.shape[1] // 2
        for side in range(2):
            out_grad[:, columns * side : columns * side + columns] = (
                out_rows[:, per * side : per * side + per].reshape(group * per, columns).astype(F32)
            )


def local(
    hidden_in,
    norm_gain,
    in_weight,
    conv_weight,
    conv_bias,
    step_bias,
    decay_log,
    skip_gain,
    gate_gain,
    out_weight,
    cotangent,
):
    hidden = hidden_in[0]
    upstream = cotangent[0]
    tokens, width = hidden.shape
    half = tokens // 2
    share = in_weight.shape[0]
    count = lax.axis_size("seq")
    core = lax.axis_index("fsdp")
    other = [(0, 1), (1, 0)]

    rows_of = in_weight.T
    conv_rows = rows_of[INNER:]
    conv_rows_other = lax.ppermute(conv_rows, "fsdp", other)

    paired = hidden.reshape(2, half, width)
    halo = lax.ppermute(paired[:, half - EDGE :], "seq", [(i, i + 1) for i in range(count - 1)])
    extended = jnp.concatenate([halo, paired], axis=1).reshape(2 * (half + EDGE), width)
    rows = extended.astype(F32)
    rescale = lax.rsqrt(jnp.mean(rows * rows, axis=-1, keepdims=True) + EPSILON)
    normed_ext = (rows * rescale * norm_gain).astype(BF16)

    rows_of_writes = rows_of[2 * INNER : 2 * INNER + STATE].astype(F32)
    power = 2.0 * jnp.sum(rows_of_writes * rows_of_writes, axis=1)
    deviation = jnp.sqrt(
        power * jnp.sum(jnp.square(conv_weight[:, INNER : INNER + STATE]), axis=0)
    )
    guess = jnp.zeros((STATE,), F32)
    for point, share_of in ((-1.7320508, 1 / 6), (0.0, 2 / 3), (1.7320508, 1 / 6)):
        guess = guess + share_of * jax.nn.silu(
            conv_bias[INNER : INNER + STATE] + point * deviation
        )
    direction = guess * lax.rsqrt(jnp.sum(guess * guess) + 1e-20)
    row_direction, column_direction = direction[None], direction[:, None]
    member = (lax.axis_index("seq") % QUARTERS).astype(jnp.int32).reshape(1)

    def mine(array, axis):
        first = lax.slice_in_dim(array, 0, share, axis=axis)
        second = lax.slice_in_dim(array, share, 2 * share, axis=axis)
        return (
            jnp.where(core == 0, first, second),
            jnp.where(core == 0, second, first),
        )

    def ordered(own, foreign, axis):
        return jnp.where(
            core == 0,
            jnp.concatenate([own, foreign], axis),
            jnp.concatenate([foreign, own], axis),
        )

    own_ext, other_ext = mine(normed_ext, 1)
    own_part = dot_last(own_ext, conv_rows)
    gate_rows = tie(rows_of[:INNER], own_part)
    gate_rows_other = lax.ppermute(gate_rows, "fsdp", other)
    conv_input = (own_part + dot_last(other_ext, conv_rows_other)).reshape(
        2, half + EDGE, CONV_CH + HEADS
    )
    out_rows = lax.all_gather(tie(out_weight, gate_rows_other), "fsdp", axis=0, tiled=True)
    normed = normed_ext.reshape(2, half + EDGE, width)[:, EDGE:].reshape(tokens, width)
    own_normed, other_normed = mine(normed, 1)

    small = jnp.pad(jnp.stack([step_bias, decay_log, skip_gain]), ((0, 5), (0, TILE - HEADS)))
    bias_row = conv_bias[None]
    gain_row = gate_gain[None]
    skip_row = jnp.repeat(skip_gain, HEAD_DIM)[None]

    last_columns = fixed_block((2, half + EDGE, 384), (0, 0, INNER // 384))
    last_taps = fixed_block((CONV, 256), (0, INNER // 256))
    last_bias = fixed_block((1, 256), (0, INNER // 256))
    per_quarter = (QUARTERS, 2, half, SIDE)
    bc, bt, scores, scores_t, step, running, step_q, sum_q, sum_t = pl.pallas_call(
        step_kernel,
        grid=(1,),
        in_specs=[
            last_columns,
            last_taps,
            last_bias,
            whole_block((8, TILE)),
            whole_block((1, STATE)),
        ],
        out_specs=[
            whole_block((2, half, 256)),
            whole_block((2, STATE, half)),
            whole_block((2, half, half)),
            whole_block((2, half, half)),
            whole_block((2, half, TILE)),
            whole_block((2, half, TILE)),
            whole_block(per_quarter),
            whole_block(per_quarter),
            whole_block((QUARTERS, 2, EDGE, half)),
        ],
        out_shape=[
            shape((2, half, 256)),
            shape((2, STATE, half), BF16),
            shape((2, half, half)),
            shape((2, half, half)),
            shape((2, half, TILE)),
            shape((2, half, TILE)),
            shape(per_quarter),
            shape(per_quarter),
            shape((QUARTERS, 2, EDGE, half)),
        ],
        compiler_params=params(),
        cost_estimate=cost(4),
        name="steps",
    )(conv_input, conv_weight, bias_row, small, row_direction)

    columns = lane_block((2, half + EDGE))
    taps_block = lane_block((CONV,))
    row_of = lane_block((1,))
    heads_block = quarter_block((2, half, SIDE))
    line_block = quarter_block((2, EDGE, half))
    tokens_block = lane_block((2, half))
    x, payload = pl.pallas_call(
        state_kernel,
        grid_spec=pltpu.PrefetchScalarGridSpec(
            num_scalar_prefetch=1,
            grid=(QUARTERS,),
            in_specs=[
                own_lanes((2, half + EDGE)),
                own_lanes((CONV,)),
                own_lanes((1,)),
                own_quarter((2, half, SIDE)),
                own_quarter((2, half, SIDE)),
                whole_block((2, STATE, half)),
                whole_block((STATE, 1)),
            ],
            out_specs=[own_lanes((2, half)), quarter_block(MESSAGE)],
        ),
        out_shape=[shape((2, half, INNER)), shape((QUARTERS,) + MESSAGE, BF16)],
        compiler_params=params(),
        cost_estimate=cost(8),
        name="states",
    )(member, conv_input, conv_weight, bias_row, step_q, sum_q, bt, column_direction)

    half_grid = QUARTERS // 2

    def later_half(spec, first):
        old = spec.index_map
        return pl.BlockSpec(spec.block_shape, lambda g: old(g + first))

    def shifted(specs, first):
        return [later_half(spec, first) for spec in specs]

    kept = {}

    def while_states_cross(sent):
        kept["grad"] = dot_last(tie(upstream, sent), out_rows).reshape(2, half, INNER)
        kept["gate"] = dot_last(tie(own_normed, sent), gate_rows)
        return kept["grad"], kept["gate"]

    def inside(first):
        def work(sent):
            specs = [
                tokens_block,
                heads_block,
                heads_block,
                line_block,
                whole_block((2, half, half)),
                row_of,
            ]
            inputs = [tie(x, sent), step_q, sum_q, sum_t, scores, skip_row]
            kept["inside"] = pl.pallas_call(
                intra_kernel,
                grid=(half_grid,),
                in_specs=shifted(specs, first)
                + [pl.BlockSpec(memory_space=pl.ANY)] * (first > 0),
                out_specs=later_half(tokens_block, first),
                out_shape=shape((2, half, INNER)),
                input_output_aliases={len(specs): 0} if first else {},
                compiler_params=params(),
                cost_estimate=cost(8),
                name="inside",
            )(*inputs, *([kept["inside"]] if first else []))
            return (kept["inside"],)

        return work

    def while_states_return(sent):
        kept["z"] = (
            kept["gate"] + dot_last(tie(other_normed, sent), gate_rows_other)
        ).reshape(2, half, INNER)
        return (kept["z"],)

    entering, along = exchange(
        payload,
        member,
        "seq",
        False,
        [while_states_cross, inside(0), inside(half_grid), while_states_return],
    )
    y_inside, z, grad_normed_out = kept["inside"], kept["z"], kept["grad"]

    token_rows = row_block(INNER)
    steps = half // ROWS
    normed_out, grad_z, grad_scan, back_payload, gate_gain_grad = pl.pallas_call(
        gate_kernel,
        grid=(2 * steps,),
        in_specs=[
            SCALAR,
            token_rows,
            token_rows,
            token_rows,
            row_block(256),
            row_block(TILE),
            pl.BlockSpec((1, STATE, INNER), lambda g: (g // steps, 0, 0)),
            pl.BlockSpec((1, 8, INNER), lambda g: (g // steps, 0, 0)),
            whole_block((1, INNER)),
        ],
        out_specs=[
            token_rows,
            token_rows,
            token_rows,
            whole_block((QUARTERS,) + MESSAGE),
            whole_block((1, INNER)),
        ],
        out_shape=[
            shape((2, half, INNER), BF16),
            shape((2, half, INNER), BF16),
            shape((2, half, INNER)),
            shape((QUARTERS,) + MESSAGE, BF16),
            shape((1, INNER)),
        ],
        scratch_shapes=[
            pltpu.VMEM((ROWS, INNER), F32),
            pltpu.VMEM((ROWS, INNER), F32),
            pltpu.VMEM((ROWS, INNER), F32),
            pltpu.VMEM((ROWS, INNER), BF16),
            pltpu.VMEM((STATE, INNER), F32),
        ],
        compiler_params=params(),
        cost_estimate=cost(14),
        name="gates",
    )(
        member,
        y_inside,
        z,
        grad_normed_out,
        bc,
        running,
        entering,
        along,
        gain_row,
    )

    normed_out = normed_out.reshape(tokens, INNER)
    grad_z = grad_z.reshape(tokens, INNER)
    first_out, second_out = normed_out[:, : INNER // 2], normed_out[:, INNER // 2 :]
    own_out = jnp.where(core == 0, first_out, second_out)
    other_out = jnp.where(core == 0, second_out, first_out)

    def weight_part(own, foreign):
        sent = lax.ppermute(dot_first(*foreign).astype(BF16), "fsdp", other)
        return dot_first(*own) + sent.astype(F32)

    def while_gradients_cross(sent):
        out_part = weight_part((own_out, upstream), (other_out, upstream))
        gate_part = weight_part((grad_z, own_normed), (grad_z, other_normed))
        kept["out"] = Scatter([out_part], "seq")
        kept["gates"] = Scatter([gate_part], "seq")
        return out_part, gate_part

    state_columns = lane_block((2, STATE))
    line_columns = lane_block((2, 8))
    edge_columns = lane_block((2, EDGE))
    back_parts = []

    def inside_back(first):
        def work(sent):
            if not first:
                for part, bit in ((kept["out"], 0), (kept["gates"], 1)):
                    part.wait_for(sent)
                    part.send(bit)
            specs = [
                tokens_block,
                tokens_block,
                tokens_block,
                columns,
                taps_block,
                row_of,
                heads_block,
                heads_block,
                line_block,
                whole_block((2, half, half)),
                whole_block((2, half, 256)),
                state_columns,
                line_columns,
                row_of,
                whole_block((1, STATE)),
            ]
            inputs = [
                x,
                tie(grad_scan, sent),
                y_inside,
                conv_input,
                conv_weight,
                bias_row,
                step_q,
                sum_q,
                sum_t,
                scores_t,
                bc,
                entering,
                along,
                skip_row,
                row_direction,
            ]
            earlier = [back_parts[0][i] for i in (0, 1, 3)] if first else []
            back_parts.append(
                pl.pallas_call(
                    intra_back_kernel,
                    grid=(half_grid,),
                    in_specs=shifted(specs, first)
                    + [pl.BlockSpec(memory_space=pl.ANY)] * len(earlier),
                    out_specs=shifted(
                        [
                            tokens_block,
                            tokens_block,
                            whole_block((2, half, half)),
                            quarter_block((2, half, TILE)),
                            whole_block((2, half, STATE)),
                        ],
                        first,
                    ),
                    out_shape=[
                        shape((2, half, INNER)),
                        shape((2, half, INNER), BF16),
                        shape((2, half, half)),
                        shape((QUARTERS, 2, half, TILE)),
                        shape((2, half, STATE)),
                    ],
                    scratch_shapes=[
                        pltpu.VMEM((3, half, Q_LANES), F32),
                        pltpu.VMEM((half, Q_LANES), BF16),
                    ],
                    input_output_aliases={
                        len(specs) + i: (0, 1, 3)[i] for i in range(len(earlier))
                    },
                    compiler_params=params(),
                    cost_estimate=cost(17),
                    name="inside_back",
                )(*inputs, *earlier)
            )
            return tuple(back_parts[-1])

        return work

    def while_gradients_return(sent):
        for part in (kept["out"], kept["gates"]):
            part.sent = tie(part.sent, sent)
            part.add()
        return kept["out"].values[0], kept["gates"].values[0]

    leaving, _ = exchange(
        back_payload,
        member,
        "seq",
        True,
        [while_gradients_cross, inside_back(0), inside_back(half_grid), while_gradients_return],
    )
    out_part, gate_part = kept["out"], kept["gates"]
    for part, bit in ((out_part, 1), (gate_part, 0)):
        part.wait_for(leaving)
        part.send(bit)
    known, slope, _, known_heads, _ = back_parts[1]
    grad_conv, tail, halo_grad, grad_mix, heads, grad_writes, meeting = pl.pallas_call(
        channel_kernel,
        grid=(QUARTERS,),
        in_specs=[
            tokens_block,
            tokens_block,
            tokens_block,
            taps_block,
            heads_block,
            heads_block,
            whole_block((2, half, 256)),
            state_columns,
            state_columns,
            line_columns,
            whole_block((STATE, 1)),
        ],
        out_specs=[
            tokens_block,
            edge_columns,
            edge_columns,
            tokens_block,
            quarter_block((2, half, TILE)),
            whole_block((2, half, STATE)),
            lane_block((8,)),
        ],
        out_shape=[
            shape((2, half, INNER), BF16),
            shape((2, EDGE, INNER)),
            shape((2, EDGE, INNER), BF16),
            shape((2, half, INNER), BF16),
            shape((QUARTERS, 2, half, TILE)),
            shape((2, half, STATE)),
            shape((8, INNER)),
        ],
        scratch_shapes=[
            pltpu.VMEM((half + 2 * EDGE, TILE), F32),
            pltpu.VMEM((half, Q_LANES), F32),
            pltpu.VMEM((half, Q_LANES), BF16),
        ],
        compiler_params=params(),
        cost_estimate=cost(12),
        name="channels",
    )(
        known,
        slope,
        x,
        conv_weight,
        step_q,
        sum_q,
        bc,
        leaving,
        entering,
        along,
        column_direction,
    )

    grad_conv_last, tail_last, halo_last, sums_last, small_grads = pl.pallas_call(
        last_kernel,
        grid=(1,),
        in_specs=[
            last_columns,
            last_taps,
            last_bias,
            whole_block((8, TILE)),
            whole_block((2, half, 256)),
            whole_block((2, half, half)),
            whole_block((2, half, half)),
            whole_block((2, half, STATE)),
            whole_block((2, half, STATE)),
            whole_block((2, half, STATE)),
            whole_block((QUARTERS, 2, half, TILE)),
            whole_block((QUARTERS, 2, half, TILE)),
            whole_block((8, INNER)),
            whole_block((2, half, TILE)),
            whole_block((2, half, TILE)),
        ],
        out_specs=[
            whole_block((2, half, 256 + HEADS)),
            whole_block((2, EDGE, 256)),
            whole_block((2, EDGE, 256)),
            whole_block((8, 256)),
            whole_block((8, TILE)),
        ],
        out_shape=[
            shape((2, half, 256 + HEADS), BF16),
            shape((2, EDGE, 256)),
            shape((2, EDGE, 256), BF16),
            shape((8, 256)),
            shape((8, TILE)),
        ],
        scratch_shapes=[pltpu.VMEM((half + 2 * EDGE, 256), F32)],
        compiler_params=params(),
        cost_estimate=cost(6),
        name="last",
    )(
        conv_input,
        conv_weight,
        bias_row,
        small,
        bc,
        back_parts[0][2],
        back_parts[1][2],
        grad_writes,
        back_parts[0][4],
        back_parts[1][4],
        known_heads,
        heads,
        meeting,
        step,
        running,
    )

    returned = lax.ppermute(
        jnp.concatenate([halo_grad, halo_last], axis=-1),
        "seq",
        [(i, i - 1) for i in range(1, count)],
    )
    fixed_tail = (jnp.concatenate([tail, tail_last], axis=-1) + returned.astype(F32)).astype(BF16)
    body = half - EDGE
    grad_wide = jnp.concatenate([grad_conv[:, :body], fixed_tail[:, :, :INNER]], axis=1)
    grad_wide = grad_wide.reshape(tokens, INNER)
    per = INNER // count
    per_last = -(-(CONV_CH + HEADS - INNER) // (16 * count)) * 16
    spare = per_last * count - (CONV_CH + HEADS - INNER)
    grad_narrow = jnp.concatenate(
        [
            grad_conv_last[:, :body],
            jnp.concatenate([fixed_tail[:, :, INNER:], grad_conv_last[:, body:, 256:]], axis=-1),
        ],
        axis=1,
    ).reshape(tokens, CONV_CH + HEADS - INNER)
    grad_padded = jnp.pad(grad_narrow, ((0, 0), (0, spare)))

    for part in (out_part, gate_part):
        part.sent = tie(part.sent, grad_wide)
        part.add()
    early = gate_part
    out_value = out_part.values[0]
    early.values.append(
        jnp.concatenate([out_value[..., :share], out_value[..., share:]], axis=-2)
    )
    bits = early.bits[::-1]
    early.send(bits[0])

    wide_part = weight_part((grad_wide, own_normed), (grad_wide, other_normed))
    last_part = weight_part((grad_padded, own_normed), (grad_padded, other_normed))
    cut = share // 2
    first_part = Scatter([wide_part[:, :cut], last_part[:, :cut]], "seq")
    second_part = Scatter([wide_part[:, cut:], last_part[:, cut:]], "seq")
    first_part.send(0)
    second_part.send(1)
    early.add()
    for bit in bits[1:]:
        early.send(bit)
        early.add()
    for part, bit in ((first_part, 1), (second_part, 0)):
        part.add()
        part.send(bit)
    for part in (first_part, second_part):
        part.add()
    late = second_part
    late.values = [
        jnp.concatenate(pair, axis=-1) for pair in zip(first_part.values, second_part.values)
    ]
    late.wait_for(*early.values)
    for bit in bits:
        late.send(bit)
        late.add()

    gate_value, out_value = early.values
    shard = jnp.concatenate([gate_value, out_value] + late.values, axis=-2).astype(BF16)
    gathered = lax.all_gather(shard, "seq", axis=0)

    grad_z, grad_wide, grad_narrow, normed_out, grad_mix = lax.optimization_barrier(
        (grad_z, grad_wide, grad_narrow, normed_out, grad_mix, shard)
    )[:5]

    def through_rows(first, second):
        return (
            dot(grad_z, first) + dot(grad_wide, second[:INNER]) + dot(grad_narrow, second[INNER:])
        )

    grad_normed = ordered(
        through_rows(gate_rows, conv_rows), through_rows(gate_rows_other, conv_rows_other), 1
    )
    u = hidden.astype(F32)
    r = lax.rsqrt(jnp.mean(u * u, axis=-1, keepdims=True) + EPSILON)
    norm_gain_grad = jnp.sum(grad_normed * u * r, axis=0)
    through = grad_normed * norm_gain
    input_grad = (
        upstream.astype(F32)
        + r * through
        - u * (r * r * r) * jnp.mean(through * u, axis=-1, keepdims=True)
    ).astype(BF16)
    block_out = (hidden.astype(F32) + dot(normed_out, out_rows)).astype(BF16)

    sums = pl.pallas_call(
        sums_kernel,
        grid=(QUARTERS,),
        in_specs=[columns, tokens_block, tokens_block, tokens_block],
        out_specs=lane_block((8,)),
        out_shape=shape((8, INNER)),
        compiler_params=params(),
        cost_estimate=cost(10),
        name="sums",
    )(conv_input, grad_mix, grad_scan, x)

    skip_grad = jnp.sum(sums[5].reshape(HEADS, HEAD_DIM), axis=1)
    vector = jnp.concatenate(
        [
            norm_gain_grad,
            sums[:5].reshape(-1),
            sums_last[:5].reshape(-1),
            small_grads[:2].reshape(-1),
            gate_gain_grad[0],
            jnp.pad(skip_grad, (0, TILE - HEADS)),
        ]
    )
    length = vector.shape[0]
    vector = add_up(vector.reshape(length // TILE, TILE), ("fsdp", "seq")).reshape(length)
    parts = []
    begin = 0
    for size in (width, 5 * INNER, 5 * 256, 2 * TILE, INNER, HEADS):
        parts.append(vector[begin : begin + size])
        begin += size
    conv_sums = jnp.concatenate(
        [parts[1].reshape(5, INNER), parts[2].reshape(5, 256)], axis=1
    )
    smalls = parts[3].reshape(2, TILE)[:, :HEADS]

    group = share // per
    parts_of = INNER // share
    gathered_block = (group, per, share)
    in_grad, out_grad = pl.pallas_call(
        finish_kernel,
        grid=(2 * parts_of + 1,),
        in_specs=[
            pl.BlockSpec(
                gathered_block,
                lambda g: (jnp.minimum(g, 2 * parts_of - 1) % parts_of, g // parts_of * 2 % 4, 0),
            ),
            pl.BlockSpec((count, per_last, share), lambda g: (0, 3 * per // per_last, 0)),
            pl.BlockSpec(gathered_block, lambda g: (jnp.minimum(g, parts_of - 1), 1, 0)),
        ],
        out_specs=[
            pl.BlockSpec((share, share), lambda g: (g, 0)),
            pl.BlockSpec((share // 2, width), lambda g: (jnp.minimum(g, parts_of - 1), 0)),
        ],
        out_shape=[shape((CONV_CH + HEADS + INNER, share)), shape((2 * share, width))],
        compiler_params=params(),
        cost_estimate=cost(14),
        name="finish",
    )(gathered, gathered, gathered)
    return (
        block_out[None],
        input_grad[None],
        parts[0],
        in_grad.T,
        conv_sums[:4],
        conv_sums[4],
        smalls[0],
        smalls[1],
        parts[5],
        parts[4],
        out_grad,
    )


def solution(mesh):
    return jax.shard_map(
        local,
        mesh=mesh,
        in_specs=(
            P("fsdp", "seq", None),
            P(),
            P("fsdp", None),
            P(),
            P(),
            P(),
            P(),
            P(),
            P(),
            P("fsdp", None),
            P("fsdp", "seq", None),
        ),
        out_specs=(
            P("fsdp", "seq", None),
            P("fsdp", "seq", None),
            P(),
            P("fsdp", None),
            P(),
            P(),
            P(),
            P(),
            P(),
            P(),
            P("fsdp", None),
        ),
        check_vma=False,
    )
```

time: 956 us -> 707 us (0.74)
  waiting for transfers between devices: 571 us -> 257 us
  Pallas kernels: 113 us -> 165 us
  starting transfers between devices: 33.3 us -> 50 us
  other arithmetic: 59.6 us -> 45 us
  local copies, waits for them, and re-layouts: 50.5 us -> 60.6 us
    psum x2 -> x0, waiting for transfers between devices: 494 us -> none  [the longest x1 412 us: local(): lax.psum(weight_part(own_normed, other_normed, grad_proj).astype(BF16), '...]
    all_gather x0 -> x2, waiting for transfers between devices: none -> 99.7 us  [the longest x1 99.7 us: local(): gathered = lax.all_gather(shard, 'seq', axis=0)]
    ppermute x8 -> x25, waiting for transfers between devices: 34 us -> 117 us  [the longest x12 84.7 us: send(): lax.ppermute(away, self.axis, [(i, i ^ 1 << bit) for i in range(self.coun...]
    pallas_call x5 -> x17, Pallas kernels: 103 us -> 154 us  [the longest x2 37.9 us: work(): pl.pallas_call(intra_back_kernel, grid=(half_grid,), in_specs=shifted(spe...]
    convert_element_type x20 -> x2, other arithmetic: 31.4 us -> 0.11 us  [the longest x1 0.07 us: send(): away = jnp.concatenate([v.astype(BF16) for v in away], axis=-2)]
    add x6 -> x21, other arithmetic: 2.07 us -> 27.6 us  [the longest x16 27.5 us: add(): self.values[i] = value + self.sent[..., begin:end, :].astype(F32)]
    ppermute x12, waiting for transfers between devices: 42.1 us -> 23 us  [swap(): return lax.ppermute(value, axis, [(i, i ^ by) for i in range(count)])]
    ppermute x8 -> x25, starting transfers between devices: 12.3 us -> 29.5 us  [the longest x12 13.2 us: send(): lax.ppermute(away, self.axis, [(i, i ^ 1 << bit) for i in range(self.coun...]
  transfers between devices with their start and end apart: 26 -> 43, of which waited for: 14 -> 27; matrix products, arithmetic and copies ran while one was open for 15% -> 24% of each run, Pallas kernels for 5% -> 13%
where the time goes in v2:
time: 707 us; the launch traced here: 703 us
  waiting for transfers between devices  257 us (36%)
  Pallas kernels  165 us (23%)
  matrix products  109 us (15%)
  local copies, waits for them, and re-layouts  60.6 us (9%)
  starting transfers between devices  50 us (7%)
  other arithmetic  45 us (6%)
  between operations  16.3 us (2%)
    all_gather x1, waiting for transfers between devices, local(): gathered = lax.all_gather(shard, 'seq', axis=0)  99.7 us
    ppermute x12, waiting for transfers between devices, send(): lax.ppermute(away, self.axis, [(i, i ^ 1 << bit) for i in range(self.coun...  84.7 us
    dot_general x5, matrix products, dot_last(): lax.dot_general(left, right, (((1,), (1,)), ((), ())), preferred_element_...  40.2 us
    pallas_call x2, Pallas kernels, work(): pl.pallas_call(intra_back_kernel, grid=(half_grid,), in_specs=shifted(spe...  37.9 us
    dot_general x8, matrix products, dot_first(): lax.dot_general(left, right, (((0,), (0,)), ((), ())), preferred_element_...  37.6 us
    dot_general x7, matrix products, dot(): return jnp.dot(left, right, preferred_element_type=F32)  30.8 us
    add x16, other arithmetic, add(): self.values[i] = value + self.sent[..., begin:end, :].astype(F32)  27.5 us
    ppermute x12, waiting for transfers between devices, swap(): return lax.ppermute(value, axis, [(i, i ^ by) for i in range(count)])  23 us
  transfers between devices with their start and end apart: 43, of which 27 were waited for; matrix products, arithmetic and copies ran while one was open for 24% of the time, Pallas kernels for 13%

profile of v2, /device:TPU:0, one launch (start us, length us, event | category | flops | bytes accessed | tf_op | source)
XLA Modules:
  0.0 702.6 jit_solution(2360904069350552907)
XLA Ops:
  8.1 4.8 collective-permute-start
  13.0 4.9 slice.286
  23.4 5.3 fusion.47
  28.8 8.0 %collective-permute-done.5 = bf16[3072,768]{1,0:T(8,128)(2,1)} collective-permute-done((bf16[3072,768]{1,0:T(8,128)(2,1)S(1)}, bf16[3072,768]{1,0:T(8,128)(2,1)}, u32[]{:S(2)}, u32[]{:S(2)}) %collective-permute-start.5) | collective-permute-done | bytes 4718624 | tf_op jit(solution)/shard_map/ppermute | solution.py:933
  37.2 5.3 slice.284
  51.4 10.5 %convolution_add_fusion = f32[544,3376]{1,0:T(8,128)} fusion(f32[544,3376]{1,0:T(8,128)} %fusion.47, bf16[3376,768]{1,0:T(8,128)(2,1)} %collective-permute-done.1, pred[]{:T(512)S(6)} %eq.4, bf16[544,1536]{1,0:T(8,128)(2,1)S(1)} %copy-done.39), kind=kOutput, calls=%fused_computation.4 | convolution fusion | flops 2823185920 | bytes 21549056 | tf_op jit(solution)/shard_map/dot_general | solution.py:76
  61.8 4.8 steps.1
  66.6 11.7 %states.1 = (f32[2,256,3072]{2,1,0:T(8,128)}, bf16[4,2,144,768]{3,2,1,0:T(8,128)(2,1)}) custom-call(s32[1]{0:T(128)} %bitcast.1.member, f32[2,272,3376]{2,1,0:T(8,128)} %bitcast.225, f32[4,3328]{1,0:T(4,128)} %weight.11, f32[1,3328]{1,0:T(1,128)} %broadcast_in_dim.24.bias, f32[4,2,256,16]{3,2,1,0:T(8,128)} %get-tuple-element.94.step_q, ...), custom_call_target="tpu_custom_call" | custom-call | bytes 27200000 | tf_op jit(solution)/shard_map/states/pallas_call | solution.py:993
  84.3 6.8 fusion.93
  91.2 9.8 %fusion.92 = f32[512,3072]{1,0:T(8,128)} fusion(bf16[512,1536]{1,0:T(8,128)(2,1)} %bitcast.274, bf16[3072,1536]{1,0:T(8,128)(2,1)} %all-gather.3.cloned.1.call-done), kind=kOutput, calls=%fused_computation.216 | convolution fusion | flops 4831838208 | bytes 17301504 | tf_op jit(solution)/shard_map/dot_general | solution.py:76
  100.9 2.8 collective-permute-done.4.refs_3_
  107.4 3.7 collective-permute-start.6
  111.9 9.1 %inside.2.refs_0_ = f32[2,256,3072]{2,1,0:T(8,128)} custom-call(f32[2,256,3072]{2,1,0:T(8,128)} %get-tuple-element.108.x_ref, f32[4,2,256,16]{3,2,1,0:T(8,128)} %get-tuple-element.94.step_q, f32[4,2,256,16]{3,2,1,0:T(8,128)} %get-tuple-element.95.sum_q, f32[4,2,16,256]{3,2,1,0:T(8,128)} %get-tuple-element.105.sum_t, ...), custom_call_target="tpu_custom_call" | custom-call | bytes 27200000 | tf_op jit(solution)/shard_map/inside/pallas_call | solution.py:1042
  123.9 4.5 collective-permute-start.7
  128.4 9.2 %inside.3.y_ref = f32[2,256,3072]{2,1,0:T(8,128)} custom-call(f32[2,256,3072]{2,1,0:T(8,128)} %get-tuple-element.108.x_ref, f32[4,2,256,16]{3,2,1,0:T(8,128)} %get-tuple-element.94.step_q, f32[4,2,256,16]{3,2,1,0:T(8,128)} %get-tuple-element.95.sum_q, f32[4,2,16,256]{3,2,1,0:T(8,128)} %get-tuple-element.105.sum_t, ...), custom_call_target="tpu_custom_call", output_to_operand_aliasing={{}: (6, {})} | custom-call | bytes 27200000 | tf_op jit(solution)/shard_map/inside/pallas_call | solution.py:1042
  138.4 4.0 spread.2
  145.9 7.8 %convolution_add_fusion.1 = f32[512,3072]{1,0:T(8,128)} fusion(f32[512,3072]{1,0:T(8,128)} %fusion.93, bf16[512,768]{1,0:T(8,128)(2,1)S(1)} %get-tuple-element.111, bf16[3072,768]{1,0:T(8,128)(2,1)} %collective-permute-done.5), kind=kOutput, calls=%fused_computation.15 | convolution fusion | flops 2417491968 | bytes 18087936 | tf_op jit(solution)/shard_map/dot_general | solution.py:76
  153.7 2.9 collective-permute-done.10.refs_3_
  156.6 6.2 collective-permute-done.8.refs_1_
  164.5 3.1 arrange.2
  167.7 18.9 %gates.1 = (bf16[2,256,3072]{2,1,0:T(8,128)(2,1)}, bf16[2,256,3072]{2,1,0:T(8,128)(2,1)}, f32[2,256,3072]{2,1,0:T(8,128)}, bf16[4,2,144,768]{3,2,1,0:T(8,128)(2,1)}, f32[1,3072]{1,0:T(1,128)}) custom-call(s32[1]{0:T(128)} %bitcast.1.member, f32[2,256,3072]{2,1,0:T(8,128)} %inside.3.y_ref, f32[2,256,3072]{2,1,0:T(8,128)} %bitcast.235, ...), custom_call_target="tpu_custom_call" | custom-call | bytes 47600000 | tf_op jit(solution)/shard_map/gates/pallas_call | solution.py:1075
  186.6 6.9 convolution_convert_fusion.2
  193.5 4.4 convolution_convert_fusion
  202.8 6.9 convert_add_fusion.1
  209.6 6.9 convert_add_fusion.2
  216.5 4.6 collective-permute-done.13.refs_3_
  228.9 4.1 fusion.25
  235.0 18.9 %inside_back.2 = (f32[2,256,3072]{2,1,0:T(8,128)}, bf16[2,256,3072]{2,1,0:T(8,128)(2,1)}, f32[2,256,256]{2,1,0:T(8,128)}, f32[4,2,256,128]{3,2,1,0:T(8,128)}, f32[2,256,128]{2,1,0:T(8,128)}) custom-call(f32[2,256,3072]{2,1,0:T(8,128)} %get-tuple-element.108.x_ref, f32[2,256,3072]{2,1,0:T(8,128)} %get-tuple-element.133.grad_ref, ...), custom_call_target="tpu_custom_call" | custom-call | bytes 57800000 | tf_op jit(solution)/shard_map/inside_back/pallas_call | solution.py:1189
  259.8 19.0 %inside_back.3 = (f32[2,256,3072]{2,1,0:T(8,128)}, bf16[2,256,3072]{2,1,0:T(8,128)(2,1)}, f32[2,256,256]{2,1,0:T(8,128)}, f32[4,2,256,128]{3,2,1,0:T(8,128)}, f32[2,256,128]{2,1,0:T(8,128)}) custom-call(f32[2,256,3072]{2,1,0:T(8,128)} %get-tuple-element.108.x_ref, ...), custom_call_target="tpu_custom_call", output_to_operand_aliasing={{0}: (15, {}), {1}: (16, {}), {3}: (17, {})} | custom-call | bytes 57800000 | tf_op jit(solution)/shard_map/inside_back/pallas_call | solution.py:1189
  278.8 10.5 %collective-permute-done.17.refs_5_ = bf16[2,144,768]{2,1,0:T(8,128)(2,1)S(1)} collective-permute-done((bf16[2,144,768]{2,1,0:T(8,128)(2,1)}, bf16[2,144,768]{2,1,0:T(8,128)(2,1)S(1)}, u32[]{:S(2)}, u32[]{:S(2)}) %collective-permute-start.17) | collective-permute-done | bytes 442400 | tf_op jit(solution)/shard_map/ppermute | solution.py:761
  290.1 4.0 spread.3
  297.6 6.1 bitcast_add_fusion.1
  303.6 5.8 bitcast_add_fusion
  309.4 5.2 collective-permute-done.20.refs_3_
  315.7 3.1 arrange.3
  318.8 16.4 %channels.1 = (bf16[2,256,3072]{2,1,0:T(8,128)(2,1)}, f32[2,16,3072]{2,1,0:T(8,128)}, bf16[2,16,3072]{2,1,0:T(8,128)(2,1)}, bf16[2,256,3072]{2,1,0:T(8,128)(2,1)...) custom-call(f32[2,256,3072]{2,1,0:T(8,128)} %get-tuple-element.134.known_ref, ...), custom_call_target="tpu_custom_call" | custom-call | bytes 40800000 | tf_op jit(solution)/shard_map/channels/pallas_call | solution.py:1245
  335.3 6.6 last.1
  344.1 6.2 collective-permute-done.23
  351.5 4.5 convolution_convert_fusion.1
  358.1 2.8 fusion.38
  362.0 2.8 fusion.37
  364.8 2.8 collective-permute-start.29
  370.7 18.5 %collective-permute-done.30 = bf16[2,2,96,1536]{3,2,1,0:T(8,128)(2,1)} collective-permute-done((bf16[2,2,96,1536]{3,2,1,0:T(8,128)(2,1)}, bf16[2,2,96,1536]{3,2,1,0:T(8,128)(2,1)}, u32[]{:S(2)}, u32[]{:S(2)}) %collective-permute-start.30) | collective-permute-done | bytes 1179680 | tf_op jit(solution)/shard_map/ppermute | solution.py:825
  389.1 4.7 collective-permute-done.29
  396.1 3.1 bitcast_add_fusion.4
  401.3 4.7 convert_add_fusion
  406.0 2.8 fusion.89
  416.6 11.5 %collective-permute-done.31 = bf16[2,384,768]{2,1,0:T(8,128)(2,1)} collective-permute-done((bf16[2,384,768]{2,1,0:T(8,128)(2,1)}, bf16[2,384,768]{2,1,0:T(8,128)(2,1)}, u32[]{:S(2)}, u32[]{:S(2)}) %collective-permute-start.31) | collective-permute-done | bytes 1179680 | tf_op jit(solution)/shard_map/ppermute | solution.py:825
  431.6 12.3 %collective-permute-done.37 = bf16[2,2,2,224,384]{4,3,0,1,2:T(8,128)(2,1)} collective-permute-done((bf16[2,2,2,224,384]{4,3,0,1,2:T(8,128)(2,1)}, bf16[2,2,2,224,384]{4,3,0,1,2:T(8,128)(2,1)}, u32[]{:S(2)}, u32[]{:S(2)}) %collective-permute-start.37) | collective-permute-done | bytes 1376288 | tf_op jit(solution)/shard_map/ppermute | solution.py:825
  453.0 5.1 collective-permute-done.32
  459.6 4.7 collective-permute-done.38
  473.0 13.4 %collective-permute-done.39 = bf16[2,224,768]{2,1,0:T(8,128)(2,1)S(1)} collective-permute-done((bf16[2,224,768]{2,1,0:T(8,128)(2,1)S(1)}, bf16[2,224,768]{2,1,0:T(8,128)(2,1)S(1)}, u32[]{:S(2)}, u32[]{:S(2)}) %collective-permute-start.39) | collective-permute-done | bytes 688160 | tf_op jit(solution)/shard_map/ppermute | solution.py:825
  488.1 12.3 %collective-permute-done.40 = bf16[224,768]{1,0:T(8,128)(2,1)S(1)} collective-permute-done((bf16[224,768]{1,0:T(8,128)(2,1)S(1)}, bf16[224,768]{1,0:T(8,128)(2,1)S(1)}, u32[]{:S(2)}, u32[]{:S(2)}) %collective-permute-start.40) | collective-permute-done | bytes 344096 | tf_op jit(solution)/shard_map/ppermute | solution.py:825
  501.9 10.6 %sums.1 = f32[8,3072]{1,0:T(8,128)} custom-call(f32[2,272,3376]{2,1,0:T(8,128)} %bitcast.229, bf16[2,256,3072]{2,1,0:T(8,128)(2,1)} %get-tuple-element.165.grad_mix_ref, f32[2,256,3072]{2,1,0:T(8,128)} %get-tuple-element.133.grad_ref, f32[2,256,3072]{2,1,0:T(8,128)} %get-tuple-element.108.x_ref), custom_call_target="tpu_custom_call" | custom-call | bytes 34000000 | tf_op jit(solution)/shard_map/sums/pallas_call | solution.py:1441
  515.7 6.1 fusion.94
  521.8 5.0 fusion.2
  528.8 5.0 fusion.95
  533.8 5.1 fusion
  545.7 5.6 collective-permute-done.25
  552.6 6.2 fusion.23
  558.9 7.2 %collective-permute-done.27 = f32[169,128]{1,0:T(8,128)S(1)} collective-permute-done((f32[169,128]{1,0:T(8,128)S(1)}, f32[169,128]{1,0:T(8,128)S(1)}, u32[]{:S(2)}, u32[]{:S(2)}) %collective-permute-start.27) | collective-permute-done | bytes 86560 | tf_op jit(solution)/shard_map/ppermute | solution.py:841
  569.5 6.3 collective-permute-done.28
  579.4 99.7 %all-gather.5.cloned.1.call-done.gate_rows.last_rows.out_rows = bf16[16,608,768]{2,1,0:T(8,128)(2,1)} async-done(((bf16[1,608,768]{2,1,0:T(8,128)(2,1)}), bf16[16,608,768]{2,1,0:T(8,128)(2,1)}) %all-gather.5.cloned.1.call-update) | async-done | bytes 14942224 | tf_op jit(solution)/shard_map/all_gather | solution.py:1416
  679.2 16.4 %finish.1 = (f32[6448,768]{1,0:T(8,128)}, f32[1536,1536]{1,0:T(8,128)}) custom-call(bf16[16,608,768]{2,1,0:T(8,128)(2,1)} %all-gather.5.cloned.1.call-done.gate_rows.last_rows.out_rows, bf16[16,608,768]{2,1,0:T(8,128)(2,1)} %all-gather.5.cloned.1.call-done.gate_rows.last_rows.out_rows, ...), custom_call_target="tpu_custom_call" | custom-call | bytes 47600000 | tf_op jit(solution)/shard_map/finish/pallas_call | solution.py:1478
  (347 shorter events, 127.8 us)
Async XLA Ops:
  7.2 84.0 %all-gather.3.cloned.1.call-start = ((), (), s32[]{:S(2)}) async-start(), calls=%async_computation | async-start | bytes 14155776 | tf_op jit(solution)/shard_map/all_gather | solution.py:937
  8.1 9.7 %collective-permute-start = (bf16[2,16,1536]{2,1,0:T(8,128)(2,1)S(1)}, bf16[2,16,1536]{2,1,0:T(8,128)(2,1)S(1)}, u32[]{:S(2)}, u32[]{:S(2)}) collective-permute-start(bf16[2,16,1536]{2,1,0:T(8,128)(2,1)S(1)} %slice.281), channel_id=1, source_target_pairs={{0,2},{2,4},{4,6},{6,8},{8,10},{10,12},{12,14},{14,16},{16,18},{18... | collective-permute-start | bytes 294920 | tf_op jit(solution)/shard_map/ppermute | solution.py:895
  28.8 8.1 %collective-permute-start.5 = (bf16[3072,768]{1,0:T(8,128)(2,1)S(1)}, bf16[3072,768]{1,0:T(8,128)(2,1)}, u32[]{:S(2)}, u32[]{:S(2)}) collective-permute-start(bf16[3072,768]{1,0:T(8,128)(2,1)S(1)} %bitcast.269), channel_id=1, source_target_pairs={{0,1},{1,0},{2,3},{3,2},{4,5},{5,4},{6,7},{7,6},{8,9},{9,8},{10,11... | collective-permute-start | bytes 14155784 | tf_op jit(solution)/shard_map/ppermute | solution.py:933
  36.9 11.4 %copy-start.3 = (f32[2,272,1536]{2,1,0:T(8,128)S(1)}, f32[2,272,1536]{2,1,0:T(8,128)}, u32[]{:S(2)}) copy-start(f32[2,272,1536]{2,1,0:T(8,128)} %copy-done.2) | copy-start | bytes 10027012
  36.9 642.2 %all-gather.5.cloned.1.call-start = ((), (), s32[]{:S(2)}) async-start(), calls=%async_computation.1 | async-start | bytes 15876096 | tf_op jit(solution)/shard_map/all_gather | solution.py:1416
  42.5 8.9 %collective-permute-start.1 = (bf16[3376,768]{1,0:T(8,128)(2,1)}, bf16[3376,768]{1,0:T(8,128)(2,1)}, u32[]{:S(2)}, u32[]{:S(2)}) collective-permute-start(bf16[3376,768]{1,0:T(8,128)(2,1)} %slice.284), channel_id=1, source_target_pairs={{0,1},{1,0},{2,3},{3,2},{4,5},{5,4},{6,7},{7,6},{8,9},{9,8},{10,11... | collective-permute-start | bytes 15556616 | tf_op jit(solution)/shard_map/ppermute | solution.py:892
  48.7 137.8 %copy-start.22 = (bf16[512,768]{1,0:T(8,128)(2,1)}, bf16[512,768]{1,0:T(8,128)(2,1)S(1)}, u32[]{:S(2)}) copy-start(bf16[512,768]{1,0:T(8,128)(2,1)S(1)} %get-tuple-element.111) | copy-start | bytes 2359300
  48.7 154.0 %copy-start.7 = (bf16[512,768]{1,0:T(8,128)(2,1)}, bf16[512,768]{1,0:T(8,128)(2,1)S(1)}, u32[]{:S(2)}) copy-start(bf16[512,768]{1,0:T(8,128)(2,1)S(1)} %get-tuple-element.102) | copy-start | bytes 2359300
  80.8 22.9 %collective-permute-start.2 = (bf16[2,144,768]{2,1,0:T(8,128)(2,1)}, bf16[2,144,768]{2,1,0:T(8,128)(2,1)S(1)}, u32[]{:S(2)}, u32[]{:S(2)}) collective-permute-start(bf16[2,144,768]{2,1,0:T(8,128)(2,1)} %get-tuple-element.191), channel_id=1, source_target_pairs={{0,2},{2,0},{4,6},{6,4},{8,10},{10,8},{12,14},{14,12},{16,18},{18,... | collective-permute-start | bytes 1327112 | tf_op jit(solution)/shard_map/ppermute | solution.py:735
  82.3 21.4 %collective-permute-start.3 = (bf16[2,144,768]{2,1,0:T(8,128)(2,1)S(1)}, bf16[2,144,768]{2,1,0:T(8,128)(2,1)S(1)}, u32[]{:S(2)}, u32[]{:S(2)}) collective-permute-start(bf16[2,144,768]{2,1,0:T(8,128)(2,1)S(1)} %get-tuple-element.190), channel_id=1, source_target_pairs={{0,4},{2,6},{4,0},{6,2},{8,12},{10,14},{12,8},{14,10},{16,20},{18,... | collective-permute-start | bytes 1327112 | tf_op jit(solution)/shard_map/ppermute | solution.py:735
  83.8 19.9 %collective-permute-start.4 = (bf16[2,144,768]{2,1,0:T(8,128)(2,1)}, bf16[2,144,768]{2,1,0:T(8,128)(2,1)S(1)}, u32[]{:S(2)}, u32[]{:S(2)}) collective-permute-start(bf16[2,144,768]{2,1,0:T(8,128)(2,1)} %get-tuple-element.189), channel_id=1, source_target_pairs={{0,6},{2,4},{4,2},{6,0},{8,14},{10,12},{12,10},{14,8},{16,22},{18,... | collective-permute-start | bytes 1327112 | tf_op jit(solution)/shard_map/ppermute | solution.py:735
  107.4 13.6 %collective-permute-start.6 = (bf16[2,144,768]{2,1,0:T(8,128)(2,1)}, bf16[2,144,768]{2,1,0:T(8,128)(2,1)S(1)}, u32[]{:S(2)}, u32[]{:S(2)}) collective-permute-start(bf16[2,144,768]{2,1,0:T(8,128)(2,1)} %plane.2.refs_0_), channel_id=1, source_target_pairs={{0,8},{2,10},{4,12},{6,14},{8,16},{10,18},{12,20},{14,22},{16,24},... | collective-permute-start | bytes 1327112 | tf_op jit(solution)/shard_map/ppermute | solution.py:761
  123.9 13.7 %collective-permute-start.7 = (bf16[2,144,768]{2,1,0:T(8,128)(2,1)}, bf16[2,144,768]{2,1,0:T(8,128)(2,1)S(1)}, u32[]{:S(2)}, u32[]{:S(2)}) collective-permute-start(bf16[2,144,768]{2,1,0:T(8,128)(2,1)} %link.2), channel_id=1, source_target_pairs={{0,16},{2,18},{4,20},{6,22},{8,24},{10,26},{12,28},{14,30},{1,17},... | collective-permute-start | bytes 1327112 | tf_op jit(solution)/shard_map/ppermute | solution.py:761
  142.4 14.2 %collective-permute-start.10 = (bf16[2,144,768]{2,1,0:T(8,128)(2,1)}, bf16[2,144,768]{2,1,0:T(8,128)(2,1)S(1)}, u32[]{:S(2)}, u32[]{:S(2)}) collective-permute-start(bf16[2,144,768]{2,1,0:T(8,128)(2,1)} %get-tuple-element.110), channel_id=1, source_target_pairs={{0,6},{2,4},{4,2},{6,0},{8,14},{10,12},{12,10},{14,8},{16,22},{18,... | collective-permute-start | bytes 1327112 | tf_op jit(solution)/shard_map/ppermute | solution.py:735
  143.8 19.0 %collective-permute-start.8 = (bf16[2,144,768]{2,1,0:T(8,128)(2,1)}, bf16[2,144,768]{2,1,0:T(8,128)(2,1)S(1)}, u32[]{:S(2)}, u32[]{:S(2)}) collective-permute-start(bf16[2,144,768]{2,1,0:T(8,128)(2,1)} %get-tuple-element.115), channel_id=1, source_target_pairs={{0,2},{2,0},{4,6},{6,4},{8,10},{10,8},{12,14},{14,12},{16,18},{18,... | collective-permute-start | bytes 1327112 | tf_op jit(solution)/shard_map/ppermute | solution.py:735
  144.3 19.5 %collective-permute-start.9 = (bf16[2,144,768]{2,1,0:T(8,128)(2,1)}, bf16[2,144,768]{2,1,0:T(8,128)(2,1)S(1)}, u32[]{:S(2)}, u32[]{:S(2)}) collective-permute-start(bf16[2,144,768]{2,1,0:T(8,128)(2,1)} %get-tuple-element.116), channel_id=1, source_target_pairs={{0,4},{2,6},{4,0},{6,2},{8,12},{10,14},{12,8},{14,10},{16,20},{18,... | collective-permute-start | bytes 1327112 | tf_op jit(solution)/shard_map/ppermute | solution.py:735
  193.5 9.3 %collective-permute-start.15 = (bf16[3072,768]{1,0:T(8,128)(2,1)}, bf16[3072,768]{1,0:T(8,128)(2,1)}, u32[]{:S(2)}, u32[]{:S(2)}) collective-permute-start(bf16[3072,768]{1,0:T(8,128)(2,1)} %convolution_convert_fusion.2), channel_id=1, source_target_pairs={{0,1},{1,0},{2,3},{3,2},{4,5},{5,4},{6,7},{7,6},{8,9},{9,8},{10,11... | collective-permute-start | bytes 14155784 | tf_op jit(solution)/shard_map/ppermute | solution.py:1132
  197.9 11.8 %collective-permute-start.14 = (bf16[1536,1536]{1,0:T(8,128)(2,1)}, bf16[1536,1536]{1,0:T(8,128)(2,1)}, u32[]{:S(2)}, u32[]{:S(2)}) collective-permute-start(bf16[1536,1536]{1,0:T(8,128)(2,1)} %convolution_convert_fusion), channel_id=1, source_target_pairs={{0,1},{1,0},{2,3},{3,2},{4,5},{5,4},{6,7},{7,6},{8,9},{9,8},{10,11... | collective-permute-start | bytes 14155784 | tf_op jit(solution)/shard_map/ppermute | solution.py:1132
  199.3 21.9 %collective-permute-start.11 = (bf16[2,144,768]{2,1,0:T(8,128)(2,1)S(1)}, bf16[2,144,768]{2,1,0:T(8,128)(2,1)S(1)}, u32[]{:S(2)}, u32[]{:S(2)}) collective-permute-start(bf16[2,144,768]{2,1,0:T(8,128)(2,1)S(1)} %get-tuple-element.187), channel_id=1, source_target_pairs={{0,2},{2,0},{4,6},{6,4},{8,10},{10,8},{12,14},{14,12},{16,18},{18,... | collective-permute-start | bytes 1327112 | tf_op jit(solution)/shard_map/ppermute | solution.py:735
  200.0 21.3 %collective-permute-start.12 = (bf16[2,144,768]{2,1,0:T(8,128)(2,1)S(1)}, bf16[2,144,768]{2,1,0:T(8,128)(2,1)S(1)}, u32[]{:S(2)}, u32[]{:S(2)}) collective-permute-start(bf16[2,144,768]{2,1,0:T(8,128)(2,1)S(1)} %get-tuple-element.186), channel_id=1, source_target_pairs={{0,4},{2,6},{4,0},{6,2},{8,12},{10,14},{12,8},{14,10},{16,20},{18,... | collective-permute-start | bytes 1327112 | tf_op jit(solution)/shard_map/ppermute | solution.py:735
  201.3 19.9 %collective-permute-start.13 = (bf16[2,144,768]{2,1,0:T(8,128)(2,1)S(1)}, bf16[2,144,768]{2,1,0:T(8,128)(2,1)S(1)}, u32[]{:S(2)}, u32[]{:S(2)}) collective-permute-start(bf16[2,144,768]{2,1,0:T(8,128)(2,1)S(1)} %get-tuple-element.185), channel_id=1, source_target_pairs={{0,6},{2,4},{4,2},{6,0},{8,14},{10,12},{12,10},{14,8},{16,22},{18,... | collective-permute-start | bytes 1327112 | tf_op jit(solution)/shard_map/ppermute | solution.py:735
  227.6 69.9 %collective-permute-start.21 = (bf16[2,2,2,96,1536]{4,3,2,1,0:T(8,128)(2,1)S(1)}, bf16[2,2,2,96,1536]{4,3,2,1,0:T(8,128)(2,1)}, u32[]{:S(2)}, u32[]{:S(2)}) collective-permute-start(bf16[2,2,2,96,1536]{4,3,2,1,0:T(8,128)(2,1)S(1)} %fusion.24), channel_id=1, source_target_pairs={{0,2},{2,0},{4,6},{6,4},{8,10},{10,8},{12,14},{14,12},{16,18},{18,... | collective-permute-start | bytes 7077896 | tf_op jit(solution)/shard_map/ppermute | solution.py:825
  233.0 70.7 %collective-permute-start.22 = (bf16[2,2,2,192,768]{4,3,0,1,2:T(8,128)(2,1)}, bf16[2,2,2,192,768]{4,3,0,1,2:T(8,128)(2,1)}, u32[]{:S(2)}, u32[]{:S(2)}) collective-permute-start(bf16[2,2,2,192,768]{4,3,0,1,2:T(8,128)(2,1)} %fusion.25), channel_id=1, source_target_pairs={{0,4},{2,6},{4,0},{6,2},{8,12},{10,14},{12,8},{14,10},{16,20},{18,... | collective-permute-start | bytes 7077896 | tf_op jit(solution)/shard_map/ppermute | solution.py:825
  233.7 21.6 %collective-permute-start.16 = (bf16[2,144,768]{2,1,0:T(8,128)(2,1)S(1)}, bf16[2,144,768]{2,1,0:T(8,128)(2,1)S(1)}, u32[]{:S(2)}, u32[]{:S(2)}) collective-permute-start(bf16[2,144,768]{2,1,0:T(8,128)(2,1)S(1)} %copy-done.29), channel_id=1, source_target_pairs={{8,0},{10,2},{12,4},{14,6},{16,8},{18,10},{20,12},{22,14},{24,16},... | collective-permute-start | bytes 1327112 | tf_op jit(solution)/shard_map/ppermute | solution.py:761
  258.3 31.0 %collective-permute-start.17 = (bf16[2,144,768]{2,1,0:T(8,128)(2,1)}, bf16[2,144,768]{2,1,0:T(8,128)(2,1)S(1)}, u32[]{:S(2)}, u32[]{:S(2)}) collective-permute-start(bf16[2,144,768]{2,1,0:T(8,128)(2,1)} %link.3), channel_id=1, source_target_pairs={{16,0},{18,2},{20,4},{22,6},{24,8},{26,10},{28,12},{30,14},{17,1},... | collective-permute-start | bytes 1327112 | tf_op jit(solution)/shard_map/ppermute | solution.py:761
  294.1 20.6 %collective-permute-start.18 = (bf16[2,144,768]{2,1,0:T(8,128)(2,1)}, bf16[2,144,768]{2,1,0:T(8,128)(2,1)S(1)}, u32[]{:S(2)}, u32[]{:S(2)}) collective-permute-start(bf16[2,144,768]{2,1,0:T(8,128)(2,1)} %get-tuple-element.141), channel_id=1, source_target_pairs={{0,2},{2,0},{4,6},{6,4},{8,10},{10,8},{12,14},{14,12},{16,18},{18,... | collective-permute-start | bytes 1327112 | tf_op jit(solution)/shard_map/ppermute | solution.py:735
  295.0 19.9 %collective-permute-start.19 = (bf16[2,144,768]{2,1,0:T(8,128)(2,1)}, bf16[2,144,768]{2,1,0:T(8,128)(2,1)S(1)}, u32[]{:S(2)}, u32[]{:S(2)}) collective-permute-start(bf16[2,144,768]{2,1,0:T(8,128)(2,1)} %get-tuple-element.142), channel_id=1, source_target_pairs={{0,4},{2,6},{4,0},{6,2},{8,12},{10,14},{12,8},{14,10},{16,20},{18,... | collective-permute-start | bytes 1327112 | tf_op jit(solution)/shard_map/ppermute | solution.py:735
  295.7 18.9 %collective-permute-start.20 = (bf16[2,144,768]{2,1,0:T(8,128)(2,1)}, bf16[2,144,768]{2,1,0:T(8,128)(2,1)S(1)}, u32[]{:S(2)}, u32[]{:S(2)}) collective-permute-start(bf16[2,144,768]{2,1,0:T(8,128)(2,1)} %get-tuple-element.143), channel_id=1, source_target_pairs={{0,6},{2,4},{4,2},{6,0},{8,14},{10,12},{12,10},{14,8},{16,22},{18,... | collective-permute-start | bytes 1327112 | tf_op jit(solution)/shard_map/ppermute | solution.py:735
  342.6 7.7 %collective-permute-start.23 = (bf16[2,16,3328]{2,1,0:T(8,128)(2,1)S(1)}, bf16[2,16,3328]{2,1,0:T(8,128)(2,1)S(1)}, u32[]{:S(2)}, u32[]{:S(2)}) collective-permute-start(bf16[2,16,3328]{2,1,0:T(8,128)(2,1)S(1)} %pad_maximum_fusion.12), channel_id=1, source_target_pairs={{2,0},{4,2},{6,4},{8,6},{10,8},{12,10},{14,12},{16,14},{18,16},{20... | collective-permute-start | bytes 638984 | tf_op jit(solution)/shard_map/ppermute | solution.py:1357
  350.6 50.1 %copy-start.4 = (bf16[2,256,3072]{2,1,0:T(8,128)(2,1)}, bf16[2,256,3072]{2,1,0:T(8,128)(2,1)S(1)}, u32[]{:S(2)}) copy-start(bf16[2,256,3072]{2,1,0:T(8,128)(2,1)S(1)} %pad_maximum_fusion) | copy-start | bytes 9437188
  356.0 44.8 %collective-permute-start.33 = (bf16[3072,768]{1,0:T(8,128)(2,1)}, bf16[3072,768]{1,0:T(8,128)(2,1)}, u32[]{:S(2)}, u32[]{:S(2)}) collective-permute-start(bf16[3072,768]{1,0:T(8,128)(2,1)} %convolution_convert_fusion.1), channel_id=1, source_target_pairs={{0,1},{1,0},{2,3},{3,2},{4,5},{5,4},{6,7},{7,6},{8,9},{9,8},{10,11... | collective-permute-start | bytes 14155784 | tf_op jit(solution)/shard_map/ppermute | solution.py:1132
  357.6 10.0 %collective-permute-start.34 = (bf16[512,768]{1,0:T(8,128)(2,1)}, bf16[512,768]{1,0:T(8,128)(2,1)}, u32[]{:S(2)}, u32[]{:S(2)}) collective-permute-start(bf16[512,768]{1,0:T(8,128)(2,1)} %convolution_convert_fusion.3), channel_id=1, source_target_pairs={{0,1},{1,0},{2,3},{3,2},{4,5},{5,4},{6,7},{7,6},{8,9},{9,8},{10,11... | collective-permute-start | bytes 2359304 | tf_op jit(solution)/shard_map/ppermute | solution.py:1132
  360.9 28.2 %collective-permute-start.30 = (bf16[2,2,96,1536]{3,2,1,0:T(8,128)(2,1)}, bf16[2,2,96,1536]{3,2,1,0:T(8,128)(2,1)}, u32[]{:S(2)}, u32[]{:S(2)}) collective-permute-start(bf16[2,2,96,1536]{3,2,1,0:T(8,128)(2,1)} %fusion.38), channel_id=1, source_target_pairs={{0,4},{2,6},{4,0},{6,2},{8,12},{10,14},{12,8},{14,10},{16,20},{18,... | collective-permute-start | bytes 3538952 | tf_op jit(solution)/shard_map/ppermute | solution.py:825
  364.8 29.0 %collective-permute-start.29 = (bf16[2,2,192,768]{3,2,0,1:T(8,128)(2,1)}, bf16[2,2,192,768]{3,2,0,1:T(8,128)(2,1)}, u32[]{:S(2)}, u32[]{:S(2)}) collective-permute-start(bf16[2,2,192,768]{3,2,0,1:T(8,128)(2,1)} %fusion.37), channel_id=1, source_target_pairs={{0,2},{2,0},{4,6},{6,4},{8,10},{10,8},{12,14},{14,12},{16,18},{18,... | collective-permute-start | bytes 3538952 | tf_op jit(solution)/shard_map/ppermute | solution.py:825
  370.6 18.5 %copy-start.26 = (f32[512,384]{1,0:T(8,128)}, f32[512,384]{1,0:T(8,128)S(1)}, u32[]{:S(2)}) copy-start(f32[512,384]{1,0:T(8,128)S(1)} %get-tuple-element.194) | copy-start | bytes 2359300
  400.7 27.3 %collective-permute-start.31 = (bf16[2,384,768]{2,1,0:T(8,128)(2,1)}, bf16[2,384,768]{2,1,0:T(8,128)(2,1)}, u32[]{:S(2)}, u32[]{:S(2)}) collective-permute-start(bf16[2,384,768]{2,1,0:T(8,128)(2,1)} %pad_maximum_fusion.4), channel_id=1, source_target_pairs={{0,8},{2,10},{4,12},{6,14},{8,0},{10,2},{12,4},{14,6},{16,24},{18,... | collective-permute-start | bytes 3538952 | tf_op jit(solution)/shard_map/ppermute | solution.py:825
  412.3 15.8 %copy-start.11 = (f32[2,2,96,768]{3,2,1,0:T(8,128)S(1)}, f32[2,2,96,768]{3,2,1,0:T(8,128)}, u32[]{:S(2)}) copy-start(f32[2,2,96,768]{3,2,1,0:T(8,128)} %copy-done.10) | copy-start | bytes 3538948
  412.3 15.8 %copy-start.13 = (f32[2,2,96,768]{3,2,1,0:T(8,128)S(1)}, f32[2,2,96,768]{3,2,1,0:T(8,128)}, u32[]{:S(2)}) copy-start(f32[2,2,96,768]{3,2,1,0:T(8,128)} %copy-done.12) | copy-start | bytes 3538948
  412.3 31.6 %collective-permute-start.37 = (bf16[2,2,2,224,384]{4,3,0,1,2:T(8,128)(2,1)}, bf16[2,2,2,224,384]{4,3,0,1,2:T(8,128)(2,1)}, u32[]{:S(2)}, u32[]{:S(2)}) collective-permute-start(bf16[2,2,2,224,384]{4,3,0,1,2:T(8,128)(2,1)} %pad_maximum_fusion.3), channel_id=1, source_target_pairs={{0,4},{2,6},{4,0},{6,2},{8,12},{10,14},{12,8},{14,10},{16,20},{18,... | collective-permute-start | bytes 4128776 | tf_op jit(solution)/shard_map/ppermute | solution.py:825
  412.6 15.5 %copy-start.15 = (f32[2,2,192,768]{3,2,0,1:T(8,128)S(1)}, f32[2,2,192,768]{3,2,0,1:T(8,128)}, u32[]{:S(2)}) copy-start(f32[2,2,192,768]{3,2,0,1:T(8,128)} %copy-done.14) | copy-start | bytes 7077892
  414.6 31.0 %slice-start.2 = ((s8[4718592]{0:T(1024)(128)(4,1)}), s8[4194304]{0:T(1024)(128)(4,1)S(1)}, s32[]{:S(2)}) async-start(s8[4718592]{0:T(1024)(128)(4,1)} %bitcast.245), calls=%async_computation.4 | async-start | bytes 8388608
  414.8 29.1 %copy-start.27 = (f32[512,384]{1,0:T(8,128)S(1)}, f32[512,384]{1,0:T(8,128)}, u32[]{:S(2)}) copy-start(f32[512,384]{1,0:T(8,128)} %copy-done.26) | copy-start | bytes 2359300
  414.8 30.9 %slice-start.3 = ((s8[4718592]{0:T(1024)(128)(4,1)}), s8[524288]{0:T(1024)(128)(4,1)S(1)}, s32[]{:S(2)}) async-start(s8[4718592]{0:T(1024)(128)(4,1)} %bitcast.245), calls=%async_computation.5 | async-start | bytes 1048576
  414.8 35.0 %collective-permute-start.35 = (bf16[2,2,2,224,384]{4,3,0,1,2:T(8,128)(2,1)S(1)}, bf16[2,2,2,224,384]{4,3,0,1,2:T(8,128)(2,1)S(1)}, u32[]{:S(2)}, u32[]{:S(2)}) collective-permute-start(bf16[2,2,2,224,384]{4,3,0,1,2:T(8,128)(2,1)S(1)} %pad_maximum_fusion.2), channel_id=1, source_target_pairs={{0,2},{2,0},{4,6},{6,4},{8,10},{10,8},{12,14},{14,12},{16,18},{18,... | collective-permute-start | bytes 4128776 | tf_op jit(solution)/shard_map/ppermute | solution.py:825
  429.6 17.8 %copy-start.20 = (f32[2,192,768]{2,1,0:T(8,128)}, f32[2,192,768]{2,1,0:T(8,128)S(1)}, u32[]{:S(2)}) copy-start(f32[2,192,768]{2,1,0:T(8,128)S(1)} %get-tuple-element.197) | copy-start | bytes 3538948
  429.6 17.8 %copy-start.21 = (f32[2,192,768]{2,1,0:T(8,128)}, f32[2,192,768]{2,1,0:T(8,128)S(1)}, u32[]{:S(2)}) copy-start(f32[2,192,768]{2,1,0:T(8,128)S(1)} %get-tuple-element.198) | copy-start | bytes 3538948
  430.7 27.3 %collective-permute-start.32 = (bf16[384,768]{1,0:T(8,128)(2,1)}, bf16[384,768]{1,0:T(8,128)(2,1)}, u32[]{:S(2)}, u32[]{:S(2)}) collective-permute-start(bf16[384,768]{1,0:T(8,128)(2,1)} %pad_maximum_fusion.9), channel_id=1, source_target_pairs={{0,16},{2,18},{4,20},{6,22},{8,24},{10,26},{12,28},{14,30},{16,0},... | collective-permute-start | bytes 1769480 | tf_op jit(solution)/shard_map/ppermute | solution.py:825
  448.4 15.9 %collective-permute-start.38 = (bf16[2,2,224,384]{3,2,0,1:T(8,128)(2,1)}, bf16[2,2,224,384]{3,2,0,1:T(8,128)(2,1)}, u32[]{:S(2)}, u32[]{:S(2)}) collective-permute-start(bf16[2,2,224,384]{3,2,0,1:T(8,128)(2,1)} %pad_maximum_fusion.7), channel_id=1, source_target_pairs={{0,2},{2,0},{4,6},{6,4},{8,10},{10,8},{12,14},{14,12},{16,18},{18,... | collective-permute-start | bytes 2064392 | tf_op jit(solution)/shard_map/ppermute | solution.py:825
  452.4 15.3 %collective-permute-start.36 = (bf16[2,2,224,384]{3,2,0,1:T(8,128)(2,1)}, bf16[2,2,224,384]{3,2,0,1:T(8,128)(2,1)}, u32[]{:S(2)}, u32[]{:S(2)}) collective-permute-start(bf16[2,2,224,384]{3,2,0,1:T(8,128)(2,1)} %pad_maximum_fusion.6), channel_id=1, source_target_pairs={{0,4},{2,6},{4,0},{6,2},{8,12},{10,14},{12,8},{14,10},{16,20},{18,... | collective-permute-start | bytes 2064392 | tf_op jit(solution)/shard_map/ppermute | solution.py:825
  453.0 14.8 %copy-start.17 = (f32[2,2,2,192,384]{4,3,0,1,2:T(8,128)S(1)}, f32[2,2,2,192,384]{4,3,0,1,2:T(8,128)}, u32[]{:S(2)}) copy-start(f32[2,2,2,192,384]{4,3,0,1,2:T(8,128)} %copy-done.16) | copy-start | bytes 7077892
  471.9 14.5 %collective-permute-start.39 = (bf16[2,224,768]{2,1,0:T(8,128)(2,1)S(1)}, bf16[2,224,768]{2,1,0:T(8,128)(2,1)S(1)}, u32[]{:S(2)}, u32[]{:S(2)}) collective-permute-start(bf16[2,224,768]{2,1,0:T(8,128)(2,1)S(1)} %pad_maximum_fusion.8), channel_id=1, source_target_pairs={{0,8},{2,10},{4,12},{6,14},{8,0},{10,2},{12,4},{14,6},{16,24},{18,... | collective-permute-start | bytes 2064392 | tf_op jit(solution)/shard_map/ppermute | solution.py:825
  486.6 14.9 %copy-start.1 = (bf16[1,512,1536]{2,1,0:T(8,128)(2,1)S(1)}, bf16[1,512,1536]{2,1,0:T(8,128)(2,1)}, u32[]{:S(2)}) copy-start(bf16[1,512,1536]{2,1,0:T(8,128)(2,1)} %param.11) | copy-start | bytes 4718596
  486.7 15.2 %copy-start.65 = (f32[8,256]{1,0:T(8,128)S(1)}, f32[8,256]{1,0:T(8,128)}, u32[]{:S(2)}) copy-start(f32[8,256]{1,0:T(8,128)} %get-tuple-element.166) | copy-start | bytes 24580
  486.7 13.7 %collective-permute-start.40 = (bf16[224,768]{1,0:T(8,128)(2,1)S(1)}, bf16[224,768]{1,0:T(8,128)(2,1)S(1)}, u32[]{:S(2)}, u32[]{:S(2)}) collective-permute-start(bf16[224,768]{1,0:T(8,128)(2,1)S(1)} %pad_maximum_fusion.11), channel_id=1, source_target_pairs={{0,16},{2,18},{4,20},{6,22},{8,24},{10,26},{12,28},{14,30},{16,0},... | collective-permute-start | bytes 1032200 | tf_op jit(solution)/shard_map/ppermute | solution.py:825
  533.8 18.8 %slice-start.6 = ((s8[9437184]{0:T(1024)(128)(4,1)}), s8[4194304]{0:T(1024)(128)(4,1)S(1)}, s32[]{:S(2)}) async-start(s8[9437184]{0:T(1024)(128)(4,1)} %bitcast.287), calls=%async_computation.8 | async-start | bytes 8388608
  533.8 18.8 %slice-start.7 = ((s8[9437184]{0:T(1024)(128)(4,1)}), s8[4194304]{0:T(1024)(128)(4,1)S(1)}, s32[]{:S(2)}) async-start(s8[9437184]{0:T(1024)(128)(4,1)} %bitcast.287), calls=%async_computation.9 | async-start | bytes 8388608
  538.9 13.7 %slice-start.8 = ((s8[9437184]{0:T(1024)(128)(4,1)}), s8[1048576]{0:T(1024)(128)(4,1)S(1)}, s32[]{:S(2)}) async-start(s8[9437184]{0:T(1024)(128)(4,1)} %bitcast.287), calls=%async_computation.10 | async-start | bytes 2097152
  540.7 11.9 %copy-start.72 = (bf16[2,256,3072]{2,1,0:T(8,128)(2,1)S(1)}, bf16[2,256,3072]{2,1,0:T(8,128)(2,1)}, u32[]{:S(2)}) copy-start(bf16[2,256,3072]{2,1,0:T(8,128)(2,1)} %get-tuple-element.123) | copy-start | bytes 9437188
  542.8 1.4 collective-permute-start.24
  544.2 7.2 %collective-permute-start.25 = (f32[169,128]{1,0:T(8,128)S(1)}, f32[169,128]{1,0:T(8,128)S(1)}, u32[]{:S(2)}, u32[]{:S(2)}) collective-permute-start(f32[169,128]{1,0:T(8,128)S(1)} %bitcast_add_fusion.19), channel_id=1, source_target_pairs={{0,2},{2,0},{4,6},{6,4},{8,10},{10,8},{12,14},{14,12},{16,18},{18,... | collective-permute-start | bytes 259592 | tf_op jit(solution)/shard_map/ppermute | solution.py:841
  551.4 16.0 %copy-start.42 = (bf16[1,512,1536]{2,1,0:T(8,128)(2,1)S(1)}, bf16[1,512,1536]{2,1,0:T(8,128)(2,1)}, u32[]{:S(2)}) copy-start(bf16[1,512,1536]{2,1,0:T(8,128)(2,1)} %param.21) | copy-start | bytes 4718596
  551.4 7.4 %collective-permute-start.26 = (f32[169,128]{1,0:T(8,128)S(1)}, f32[169,128]{1,0:T(8,128)S(1)}, u32[]{:S(2)}, u32[]{:S(2)}) collective-permute-start(f32[169,128]{1,0:T(8,128)S(1)} %fusion.123), channel_id=1, source_target_pairs={{0,4},{2,6},{4,0},{6,2},{8,12},{10,14},{12,8},{14,10},{16,20},{18,... | collective-permute-start | bytes 259592 | tf_op jit(solution)/shard_map/ppermute | solution.py:841
  558.8 7.3 %collective-permute-start.27 = (f32[169,128]{1,0:T(8,128)S(1)}, f32[169,128]{1,0:T(8,128)S(1)}, u32[]{:S(2)}, u32[]{:S(2)}) collective-permute-start(f32[169,128]{1,0:T(8,128)S(1)} %add.287), channel_id=1, source_target_pairs={{0,8},{2,10},{4,12},{6,14},{8,0},{10,2},{12,4},{14,6},{16,24},{18,... | collective-permute-start | bytes 259592 | tf_op jit(solution)/shard_map/ppermute | solution.py:841
  566.1 9.8 %collective-permute-start.28 = (f32[169,128]{1,0:T(8,128)S(1)}, f32[169,128]{1,0:T(8,128)S(1)}, u32[]{:S(2)}, u32[]{:S(2)}) collective-permute-start(f32[169,128]{1,0:T(8,128)S(1)} %add.288), channel_id=1, source_target_pairs={{0,16},{2,18},{4,20},{6,22},{8,24},{10,26},{12,28},{14,30},{16,0},... | collective-permute-start | bytes 259592 | tf_op jit(solution)/shard_map/ppermute | solution.py:841
  (61 other events, 220.5 us)
Sparse Core Ops, SparseCore 0:
  37.0 22.1 all-gather.2
  501.6 177.5 all-gather.4

commit v3 on v2

--- a/solution.py
+++ b/solution.py
@@ -822,6 +822,7 @@
         away = jnp.concatenate([v.astype(BF16) for v in away], axis=-2)
         self.values = [lax.dynamic_index_in_dim(v, mine, position, False) for v in self.values]
         self.bits.remove(bit)
+        self.away = away
         self.sent = lax.ppermute(
             away, self.axis, [(i, i ^ (1 << bit)) for i in range(self.count)]
         )
@@ -888,11 +889,13 @@
     other = [(0, 1), (1, 0)]
 
     rows_of = in_weight.T
-    conv_rows = rows_of[INNER:]
+    conv_rows = lax.optimization_barrier(rows_of[INNER:])
     conv_rows_other = lax.ppermute(conv_rows, "fsdp", other)
 
     paired = hidden.reshape(2, half, width)
-    halo = lax.ppermute(paired[:, half - EDGE :], "seq", [(i, i + 1) for i in range(count - 1)])
+    halo = lax.ppermute(
+        tie(paired[:, half - EDGE :], conv_rows), "seq", [(i, i + 1) for i in range(count - 1)]
+    )
     extended = jnp.concatenate([halo, paired], axis=1).reshape(2 * (half + EDGE), width)
     rows = extended.astype(F32)
     rescale = lax.rsqrt(jnp.mean(rows * rows, axis=-1, keepdims=True) + EPSILON)
@@ -928,13 +931,6 @@
         )
 
     own_ext, other_ext = mine(normed_ext, 1)
-    own_part = dot_last(own_ext, conv_rows)
-    gate_rows = tie(rows_of[:INNER], own_part)
-    gate_rows_other = lax.ppermute(gate_rows, "fsdp", other)
-    conv_input = (own_part + dot_last(other_ext, conv_rows_other)).reshape(
-        2, half + EDGE, CONV_CH + HEADS
-    )
-    out_rows = lax.all_gather(tie(out_weight, gate_rows_other), "fsdp", axis=0, tiled=True)
     normed = normed_ext.reshape(2, half + EDGE, width)[:, EDGE:].reshape(tokens, width)
     own_normed, other_normed = mine(normed, 1)
 
@@ -942,6 +938,11 @@
     bias_row = conv_bias[None]
     gain_row = gate_gain[None]
     skip_row = jnp.repeat(skip_gain, HEAD_DIM)[None]
+
+    own_ext = tie(own_ext, conv_rows_other, row_direction, column_direction, small, bias_row)
+    conv_input = (dot_last(own_ext, conv_rows) + dot_last(other_ext, conv_rows_other)).reshape(
+        2, half + EDGE, CONV_CH + HEADS
+    )
 
     last_columns = fixed_block((2, half + EDGE, 384), (0, 0, INNER // 384))
     last_taps = fixed_block((CONV, 256), (0, INNER // 256))
@@ -1012,6 +1013,8 @@
         name="states",
     )(member, conv_input, conv_weight, bias_row, step_q, sum_q, bt, column_direction)
 
+    gate_rows = rows_of[:INNER]
+    out_rows = lax.all_gather(tie(out_weight, payload), "fsdp", axis=0, tiled=True)
     half_grid = QUARTERS // 2
 
     def later_half(spec, first):
@@ -1024,9 +1027,13 @@
     kept = {}
 
     def while_states_cross(sent):
+        kept["gate"] = dot_last(tie(own_normed, sent), gate_rows)
+        return inside(0)(sent) + (kept["gate"],)
+
+    def while_first_states(sent):
+        kept["rows"] = lax.ppermute(tie(rows_of, sent)[:INNER], "fsdp", other)
         kept["grad"] = dot_last(tie(upstream, sent), out_rows).reshape(2, half, INNER)
-        kept["gate"] = dot_last(tie(own_normed, sent), gate_rows)
-        return kept["grad"], kept["gate"]
+        return (kept["grad"],)
 
     def inside(first):
         def work(sent):
@@ -1057,7 +1064,7 @@
 
     def while_states_return(sent):
         kept["z"] = (
-            kept["gate"] + dot_last(tie(other_normed, sent), gate_rows_other)
+            kept["gate"] + dot_last(tie(other_normed, sent), kept["rows"])
         ).reshape(2, half, INNER)
         return (kept["z"],)
 
@@ -1066,8 +1073,9 @@
         member,
         "seq",
         False,
-        [while_states_cross, inside(0), inside(half_grid), while_states_return],
-    )
+        [while_states_cross, while_first_states, inside(half_grid), while_states_return],
+    )
+    gate_rows_other = kept["rows"]
     y_inside, z, grad_normed_out = kept["inside"], kept["z"], kept["grad"]
 
     token_rows = row_block(INNER)
@@ -1241,6 +1249,7 @@
     for part, bit in ((out_part, 1), (gate_part, 0)):
         part.wait_for(leaving)
         part.send(bit)
+    leaving = tie(leaving, out_part.away, gate_part.away)
     known, slope, _, known_heads, _ = back_parts[1]
     grad_conv, tail, halo_grad, grad_mix, heads, grad_writes, meeting = pl.pallas_call(
         channel_kernel,
@@ -1355,7 +1364,7 @@
     )
 
     returned = lax.ppermute(
-        jnp.concatenate([halo_grad, halo_last], axis=-1),
+        tie(jnp.concatenate([halo_grad, halo_last], axis=-1), out_part.sent, gate_part.sent),
         "seq",
         [(i, i - 1) for i in range(1, count)],
     )
@@ -1376,7 +1385,6 @@
     grad_padded = jnp.pad(grad_narrow, ((0, 0), (0, spare)))
 
     for part in (out_part, gate_part):
-        part.sent = tie(part.sent, grad_wide)
         part.add()
     early = gate_part
     out_value = out_part.values[0]
@@ -1386,6 +1394,7 @@
     bits = early.bits[::-1]
     early.send(bits[0])
 
+    grad_wide, grad_padded = lax.optimization_barrier((grad_wide, grad_padded, early.away))[:2]
     wide_part = weight_part((grad_wide, own_normed), (grad_wide, other_normed))
     last_part = weight_part((grad_padded, own_normed), (grad_padded, other_normed))
     cut = share // 2

time: 707 us -> 676 us (0.956)
  waiting for transfers between devices: 257 us -> 229 us
  matrix products: 109 us -> 100 us
    ppermute x12, waiting for transfers between devices: 84.7 us -> 62.5 us  [send(): lax.ppermute(away, self.axis, [(i, i ^ 1 << bit) for i in range(self.coun...]
    ppermute x3, waiting for transfers between devices: 14.2 us -> 0.53 us  [the longest x1 0.52 us: local(): lax.ppermute(tie(jnp.concatenate([halo_grad, halo_last], axis=-1), out_pa...]
    unnamed x170 -> x148, local copies, waits for them, and re-layouts: 18.6 us -> 16.5 us
  transfers between devices with their start and end apart: 43 -> 43, of which waited for: 27 -> 25; matrix products, arithmetic and copies ran while one was open for 24% -> 22% of each run, Pallas kernels for 13% -> 16%
where the time goes in v3:
time: 676 us; the launch traced here: 668 us
  waiting for transfers between devices  229 us (34%)
  Pallas kernels  166 us (25%)
  matrix products  100 us (15%)
  local copies, waits for them, and re-layouts  58.7 us (9%)
  starting transfers between devices  54.3 us (8%)
  other arithmetic  42.9 us (6%)
  between operations  16.3 us (2%)
    all_gather x1, waiting for transfers between devices, local(): gathered = lax.all_gather(shard, 'seq', axis=0)  97.1 us
    ppermute x12, waiting for transfers between devices, send(): lax.ppermute(away, self.axis, [(i, i ^ 1 << bit) for i in range(self.coun...  62.5 us
    pallas_call x2, Pallas kernels, work(): pl.pallas_call(intra_back_kernel, grid=(half_grid,), in_specs=shifted(spe...  37.9 us
    dot_general x5, matrix products, dot_last(): lax.dot_general(left, right, (((1,), (1,)), ((), ())), preferred_element_...  37.6 us
    dot_general x8, matrix products, dot_first(): lax.dot_general(left, right, (((0,), (0,)), ((), ())), preferred_element_...  32.1 us
    dot_general x7, matrix products, dot(): return jnp.dot(left, right, preferred_element_type=F32)  30.8 us
    ppermute x5, waiting for transfers between devices, add_up(): lax.ppermute(value, axis, [(i, i ^ 1 << bit) for i in range(count)])  27.1 us
    add x16, other arithmetic, add(): self.values[i] = value + self.sent[..., begin:end, :].astype(F32)  26.1 us
  transfers between devices with their start and end apart: 43, of which 25 were waited for; matrix products, arithmetic and copies ran while one was open for 22% of the time, Pallas kernels for 16%

profile of v3, /device:TPU:0, one launch (start us, length us, event | category | flops | bytes accessed | tf_op | source)
XLA Modules:
  0.0 668.2 jit_solution(2282334373882004760)
XLA Ops:
  7.3 5.2 slice.284
  12.9 4.4 collective-permute-start
  25.6 5.3 fusion.50
  30.9 7.8 %convolution_add_fusion = f32[544,3376]{1,0:T(8,128)} fusion(f32[544,3376]{1,0:T(8,128)S(1)} %fusion.50, bf16[544,768]{1,0:T(8,128)(2,1)S(1)} %broadcast_select_fusion, bf16[3376,768]{1,0:T(8,128)(2,1)} %slice.284), kind=kOutput, calls=%fused_computation.4 | convolution fusion | flops 2822768128 | bytes 20713472 | tf_op jit(solution)/shard_map/dot_general | solution.py:76
  38.7 4.8 steps.1
  43.6 11.7 %states.1 = (f32[2,256,3072]{2,1,0:T(8,128)}, bf16[4,2,144,768]{3,2,1,0:T(8,128)(2,1)}) custom-call(s32[1]{0:T(128)} %bitcast.1.member, f32[2,272,3376]{2,1,0:T(8,128)} %bitcast.227, f32[4,3328]{1,0:T(4,128)} %weight.11, f32[1,3328]{1,0:T(1,128)} %broadcast_in_dim.26.bias, f32[4,2,256,16]{3,2,1,0:T(8,128)} %get-tuple-element.100.step_q, ...), custom_call_target="tpu_custom_call" | custom-call | bytes 27200000 | tf_op jit(solution)/shard_map/states/pallas_call | solution.py:994
  63.3 9.8 %inside.2.refs_0_ = f32[2,256,3072]{2,1,0:T(8,128)} custom-call(f32[2,256,3072]{2,1,0:T(8,128)} %get-tuple-element.112.x_ref, f32[4,2,256,16]{3,2,1,0:T(8,128)} %get-tuple-element.100.step_q, f32[4,2,256,16]{3,2,1,0:T(8,128)} %get-tuple-element.101.sum_q, f32[4,2,16,256]{3,2,1,0:T(8,128)} %get-tuple-element.105.sum_t, ...), custom_call_target="tpu_custom_call" | custom-call | bytes 27200000 | tf_op jit(solution)/shard_map/inside/pallas_call | solution.py:1049
  73.1 6.8 %fusion.6 = f32[512,3072]{1,0:T(8,128)} fusion(bf16[512,768]{1,0:T(8,128)(2,1)S(1)} %get-tuple-element.107, bf16[6448,768]{1,0:T(8,128)(2,1)} %bitcast.256), kind=kOutput, calls=%fused_computation.18 | convolution fusion | flops 2415919104 | bytes 11796480 | tf_op jit(solution)/shard_map/dot_general | solution.py:76
  79.9 2.7 collective-permute-done.4.refs_3_
  83.7 2.6 plane.2.refs_0_
  86.3 4.9 slice.230
  91.2 3.5 collective-permute-start.5
  94.7 9.8 %fusion.84 = f32[512,3072]{1,0:T(8,128)} fusion(bf16[512,1536]{1,0:T(8,128)(2,1)} %bitcast.274, bf16[3072,1536]{1,0:T(8,128)(2,1)} %all-gather.3.cloned.1.call-done), kind=kOutput, calls=%fused_computation.211 | convolution fusion | flops 4831838208 | bytes 17301504 | tf_op jit(solution)/shard_map/dot_general | solution.py:76
  107.6 5.4 collective-permute-start.6
  113.1 9.2 %inside.3.y_ref = f32[2,256,3072]{2,1,0:T(8,128)} custom-call(f32[2,256,3072]{2,1,0:T(8,128)} %get-tuple-element.112.x_ref, f32[4,2,256,16]{3,2,1,0:T(8,128)} %get-tuple-element.100.step_q, f32[4,2,256,16]{3,2,1,0:T(8,128)} %get-tuple-element.101.sum_q, f32[4,2,16,256]{3,2,1,0:T(8,128)} %get-tuple-element.105.sum_t, ...), custom_call_target="tpu_custom_call", output_to_operand_aliasing={{}: (6, {})} | custom-call | bytes 27200000 | tf_op jit(solution)/shard_map/inside/pallas_call | solution.py:1049
  123.5 4.0 spread.2
  130.9 7.8 %convolution_add_fusion.1 = f32[512,3072]{1,0:T(8,128)} fusion(f32[512,3072]{1,0:T(8,128)} %fusion.6, bf16[512,768]{1,0:T(8,128)(2,1)S(1)} %get-tuple-element.115, bf16[3072,768]{1,0:T(8,128)(2,1)} %collective-permute-done.7), kind=kOutput, calls=%fused_computation.15 | convolution fusion | flops 2417491968 | bytes 18087936 | tf_op jit(solution)/shard_map/dot_general | solution.py:76
  138.8 2.9 collective-permute-done.10.refs_3_
  141.7 7.3 %collective-permute-done.8.refs_1_ = bf16[2,144,768]{2,1,0:T(8,128)(2,1)S(1)} collective-permute-done((bf16[2,144,768]{2,1,0:T(8,128)(2,1)}, bf16[2,144,768]{2,1,0:T(8,128)(2,1)S(1)}, u32[]{:S(2)}, u32[]{:S(2)}) %collective-permute-start.8) | collective-permute-done | bytes 442400 | tf_op jit(solution)/shard_map/ppermute | solution.py:735
  149.9 3.1 arrange.2
  153.1 19.0 %gates.1 = (bf16[2,256,3072]{2,1,0:T(8,128)(2,1)}, bf16[2,256,3072]{2,1,0:T(8,128)(2,1)}, f32[2,256,3072]{2,1,0:T(8,128)}, bf16[4,2,144,768]{3,2,1,0:T(8,128)(2,1)}, f32[1,3072]{1,0:T(1,128)}) custom-call(s32[1]{0:T(128)} %bitcast.1.member, f32[2,256,3072]{2,1,0:T(8,128)} %inside.3.y_ref, f32[2,256,3072]{2,1,0:T(8,128)} %bitcast.237, ...), custom_call_target="tpu_custom_call" | custom-call | bytes 47600000 | tf_op jit(solution)/shard_map/gates/pallas_call | solution.py:1083
  172.2 6.9 %convolution_convert_fusion.2 = bf16[3072,768]{1,0:T(8,128)(2,1)} fusion(bf16[512,3072]{1,0:T(8,128)(2,1)} %bitcast.266, bf16[512,768]{1,0:T(8,128)(2,1)S(1)} %get-tuple-element.115), kind=kOutput, calls=%fused_computation.6 | convolution fusion | flops 2418278400 | bytes 8650752 | tf_op jit(solution)/shard_map/dot_general | solution.py:86
  179.1 4.4 convolution_convert_fusion
  188.3 6.9 %convert_add_fusion.1 = f32[3072,768]{1,0:T(8,128)} fusion(bf16[3072,768]{1,0:T(8,128)(2,1)} %collective-permute-done.15, bf16[512,3072]{1,0:T(8,128)(2,1)S(1)} %bitcast.268, bf16[512,768]{1,0:T(8,128)(2,1)S(1)} %get-tuple-element.107), kind=kOutput, calls=%fused_computation.1 | convolution fusion | flops 2420637696 | bytes 18087936 | tf_op jit(solution)/shard_map/dot_general | solution.py:86
  195.2 6.9 %convert_add_fusion.2 = f32[1536,1536]{1,0:T(8,128)} fusion(bf16[1536,1536]{1,0:T(8,128)(2,1)} %collective-permute-done.14, pred[]{:T(512)S(6)} %eq.4, bf16[512,3072]{1,0:T(8,128)(2,1)S(1)} %bitcast.290, bf16[1,512,1536]{2,1,0:T(8,128)(2,1)S(1)} %copy-done.32), kind=kOutput, calls=%fused_computation.2 | convolution fusion | flops 2421424128 | bytes 18874368 | tf_op jit(solution)/shard_map/dot_general | solution.py:86
  202.1 5.1 collective-permute-done.13.refs_3_
  208.3 2.8 plane.3.refs_0_
  211.1 2.6 fusion.28
  214.5 4.1 fusion.29
  221.2 18.9 %inside_back.2 = (f32[2,256,3072]{2,1,0:T(8,128)}, bf16[2,256,3072]{2,1,0:T(8,128)(2,1)}, f32[2,256,256]{2,1,0:T(8,128)}, f32[4,2,256,128]{3,2,1,0:T(8,128)}, f32[2,256,128]{2,1,0:T(8,128)}) custom-call(f32[2,256,3072]{2,1,0:T(8,128)} %get-tuple-element.112.x_ref, f32[2,256,3072]{2,1,0:T(8,128)} %get-tuple-element.138.grad_ref, ...), custom_call_target="tpu_custom_call" | custom-call | bytes 57800000 | tf_op jit(solution)/shard_map/inside_back/pallas_call | solution.py:1197
  245.7 19.0 %inside_back.3 = (f32[2,256,3072]{2,1,0:T(8,128)}, bf16[2,256,3072]{2,1,0:T(8,128)(2,1)}, f32[2,256,256]{2,1,0:T(8,128)}, f32[4,2,256,128]{3,2,1,0:T(8,128)}, f32[2,256,128]{2,1,0:T(8,128)}) custom-call(f32[2,256,3072]{2,1,0:T(8,128)} %get-tuple-element.112.x_ref, ...), custom_call_target="tpu_custom_call", output_to_operand_aliasing={{0}: (15, {}), {1}: (16, {}), {3}: (17, {})} | custom-call | bytes 57800000 | tf_op jit(solution)/shard_map/inside_back/pallas_call | solution.py:1197
  264.6 10.6 %collective-permute-done.17.refs_5_ = bf16[2,144,768]{2,1,0:T(8,128)(2,1)} collective-permute-done((bf16[2,144,768]{2,1,0:T(8,128)(2,1)}, bf16[2,144,768]{2,1,0:T(8,128)(2,1)}, u32[]{:S(2)}, u32[]{:S(2)}) %collective-permute-start.17) | collective-permute-done | bytes 442400 | tf_op jit(solution)/shard_map/ppermute | solution.py:761
  275.2 4.0 spread.3
  282.7 6.1 bitcast_add_fusion.1
  288.8 5.8 bitcast_add_fusion
  294.6 5.6 collective-permute-done.20.refs_3_
  301.7 3.1 arrange.3
  310.5 16.5 %channels.1 = (bf16[2,256,3072]{2,1,0:T(8,128)(2,1)}, f32[2,16,3072]{2,1,0:T(8,128)}, bf16[2,16,3072]{2,1,0:T(8,128)(2,1)}, bf16[2,256,3072]{2,1,0:T(8,128)(2,1)...) custom-call(f32[2,256,3072]{2,1,0:T(8,128)} %get-tuple-element.139.known_ref, ...), custom_call_target="tpu_custom_call" | custom-call | bytes 40800000 | tf_op jit(solution)/shard_map/channels/pallas_call | solution.py:1254
  327.0 6.4 last.1
  339.0 2.4 bitcast_add_fusion.4
  346.6 3.1 convolution_convert_fusion.1
  350.9 3.0 collective-permute-start.31
  353.9 4.8 collective-permute-done.34
  361.3 2.8 convert_add_fusion
  364.1 2.8 fusion.81
  370.5 2.3 collective-permute-start.37
  377.5 3.0 collective-permute-done.31
  384.7 18.9 %collective-permute-done.37 = bf16[2,2,2,224,384]{4,3,0,1,2:T(8,128)(2,1)} collective-permute-done((bf16[2,2,2,224,384]{4,3,0,1,2:T(8,128)(2,1)}, bf16[2,2,2,224,384]{4,3,0,1,2:T(8,128)(2,1)}, u32[]{:S(2)}, u32[]{:S(2)}) %collective-permute-start.37) | collective-permute-done | bytes 1376288 | tf_op jit(solution)/shard_map/ppermute | solution.py:826
  415.7 9.7 %collective-permute-done.38 = bf16[2,2,224,384]{3,2,0,1:T(8,128)(2,1)} collective-permute-done((bf16[2,2,224,384]{3,2,0,1:T(8,128)(2,1)}, bf16[2,2,224,384]{3,2,0,1:T(8,128)(2,1)}, u32[]{:S(2)}, u32[]{:S(2)}) %collective-permute-start.38) | collective-permute-done | bytes 688160 | tf_op jit(solution)/shard_map/ppermute | solution.py:826
  426.5 2.4 collective-permute-done.36
  434.5 14.0 %collective-permute-done.39 = bf16[2,224,768]{2,1,0:T(8,128)(2,1)S(1)} collective-permute-done((bf16[2,224,768]{2,1,0:T(8,128)(2,1)S(1)}, bf16[2,224,768]{2,1,0:T(8,128)(2,1)S(1)}, u32[]{:S(2)}, u32[]{:S(2)}) %collective-permute-start.39) | collective-permute-done | bytes 688160 | tf_op jit(solution)/shard_map/ppermute | solution.py:826
  450.4 14.5 %collective-permute-done.40 = bf16[224,768]{1,0:T(8,128)(2,1)S(1)} collective-permute-done((bf16[224,768]{1,0:T(8,128)(2,1)S(1)}, bf16[224,768]{1,0:T(8,128)(2,1)S(1)}, u32[]{:S(2)}, u32[]{:S(2)}) %collective-permute-start.40) | collective-permute-done | bytes 344096 | tf_op jit(solution)/shard_map/ppermute | solution.py:826
  466.4 10.6 %sums.1 = f32[8,3072]{1,0:T(8,128)} custom-call(f32[2,272,3376]{2,1,0:T(8,128)} %bitcast.231, bf16[2,256,3072]{2,1,0:T(8,128)(2,1)} %get-tuple-element.175.grad_mix_ref, f32[2,256,3072]{2,1,0:T(8,128)} %get-tuple-element.138.grad_ref, f32[2,256,3072]{2,1,0:T(8,128)} %get-tuple-element.112.x_ref), custom_call_target="tpu_custom_call" | custom-call | bytes 34000000 | tf_op jit(solution)/shard_map/sums/pallas_call | solution.py:1450
  480.1 6.1 fusion.4
  486.2 5.0 fusion.2
  493.2 5.0 fusion.85
  498.2 5.1 fusion
  508.7 7.0 %collective-permute-done.27 = f32[169,128]{1,0:T(8,128)S(1)} collective-permute-done((f32[169,128]{1,0:T(8,128)S(1)}, f32[169,128]{1,0:T(8,128)S(1)}, u32[]{:S(2)}, u32[]{:S(2)}) %collective-permute-start.27) | collective-permute-done | bytes 86560 | tf_op jit(solution)/shard_map/ppermute | solution.py:842
  515.9 6.2 fusion.27
  523.0 9.8 %collective-permute-done.29 = f32[169,128]{1,0:T(8,128)S(1)} collective-permute-done((f32[169,128]{1,0:T(8,128)S(1)}, f32[169,128]{1,0:T(8,128)S(1)}, u32[]{:S(2)}, u32[]{:S(2)}) %collective-permute-start.29) | collective-permute-done | bytes 86560 | tf_op jit(solution)/shard_map/ppermute | solution.py:842
  532.8 2.2 fusion.20
  535.0 9.1 %collective-permute-done.30 = f32[169,128]{1,0:T(8,128)S(1)} collective-permute-done((f32[169,128]{1,0:T(8,128)S(1)}, f32[169,128]{1,0:T(8,128)S(1)}, u32[]{:S(2)}, u32[]{:S(2)}) %collective-permute-start.30) | collective-permute-done | bytes 86560 | tf_op jit(solution)/shard_map/ppermute | solution.py:842
  547.7 97.1 %all-gather.5.cloned.1.call-done.gate_rows.last_rows.out_rows = bf16[16,608,768]{2,1,0:T(8,128)(2,1)} async-done(((bf16[1,608,768]{2,1,0:T(8,128)(2,1)}), bf16[16,608,768]{2,1,0:T(8,128)(2,1)}) %all-gather.5.cloned.1.call-update) | async-done | bytes 14942224 | tf_op jit(solution)/shard_map/all_gather | solution.py:1425
  644.8 16.4 %finish.1 = (f32[6448,768]{1,0:T(8,128)}, f32[1536,1536]{1,0:T(8,128)}) custom-call(bf16[16,608,768]{2,1,0:T(8,128)(2,1)} %all-gather.5.cloned.1.call-done.gate_rows.last_rows.out_rows, bf16[16,608,768]{2,1,0:T(8,128)(2,1)} %all-gather.5.cloned.1.call-done.gate_rows.last_rows.out_rows, ...), custom_call_target="tpu_custom_call" | custom-call | bytes 47600000 | tf_op jit(solution)/shard_map/finish/pallas_call | solution.py:1487
  (327 shorter events, 115.2 us)
Async XLA Ops:
  7.2 87.5 %all-gather.3.cloned.1.call-start = ((), (), s32[]{:S(2)}) async-start(), calls=%async_computation | async-start | bytes 14155776 | tf_op jit(solution)/shard_map/all_gather | solution.py:1017
  7.2 10.1 %copy-start.51 = (f32[3328]{0:T(1024)S(1)}, f32[3328]{0:T(1024)}, u32[]{:S(2)}) copy-start(f32[3328]{0:T(1024)} %param.15) | copy-start | bytes 39940
  7.2 15.0 %copy-start.55 = (f32[48]{0:T(128)S(1)}, f32[48]{0:T(128)}, u32[]{:S(2)}) copy-start(f32[48]{0:T(128)} %param.18) | copy-start | bytes 580
  7.3 15.0 %copy-start.57 = (f32[48]{0:T(128)S(1)}, f32[48]{0:T(128)}, u32[]{:S(2)}) copy-start(f32[48]{0:T(128)} %param.17) | copy-start | bytes 580
  7.3 15.0 %copy-start.58 = (f32[48]{0:T(128)S(1)}, f32[48]{0:T(128)}, u32[]{:S(2)}) copy-start(f32[48]{0:T(128)} %param.16) | copy-start | bytes 580
  12.5 13.1 %collective-permute-start.1 = (bf16[3376,768]{1,0:T(8,128)(2,1)}, bf16[3376,768]{1,0:T(8,128)(2,1)}, u32[]{:S(2)}, u32[]{:S(2)}) collective-permute-start(bf16[3376,768]{1,0:T(8,128)(2,1)} %slice.284), channel_id=1, source_target_pairs={{0,1},{1,0},{2,3},{3,2},{4,5},{5,4},{6,7},{7,6},{8,9},{9,8},{10,11... | collective-permute-start | bytes 15556616 | tf_op jit(solution)/shard_map/ppermute | solution.py:893
  12.9 10.0 %collective-permute-start = (bf16[2,16,1536]{2,1,0:T(8,128)(2,1)S(1)}, bf16[2,16,1536]{2,1,0:T(8,128)(2,1)S(1)}, u32[]{:S(2)}, u32[]{:S(2)}) collective-permute-start(bf16[2,16,1536]{2,1,0:T(8,128)(2,1)S(1)} %slice.283), channel_id=1, source_target_pairs={{0,2},{2,4},{4,6},{6,8},{8,10},{10,12},{12,14},{14,16},{16,18},{18... | collective-permute-start | bytes 294920 | tf_op jit(solution)/shard_map/ppermute | solution.py:896
  55.3 589.5 %all-gather.5.cloned.1.call-start = ((), (), s32[]{:S(2)}) async-start(), calls=%async_computation.1 | async-start | bytes 15876096 | tf_op jit(solution)/shard_map/all_gather | solution.py:1425
  58.7 113.5 %copy-start.15 = (bf16[512,768]{1,0:T(8,128)(2,1)}, bf16[512,768]{1,0:T(8,128)(2,1)S(1)}, u32[]{:S(2)}) copy-start(bf16[512,768]{1,0:T(8,128)(2,1)S(1)} %get-tuple-element.115) | copy-start | bytes 2359300
  59.8 22.9 %collective-permute-start.2 = (bf16[2,144,768]{2,1,0:T(8,128)(2,1)S(1)}, bf16[2,144,768]{2,1,0:T(8,128)(2,1)S(1)}, u32[]{:S(2)}, u32[]{:S(2)}) collective-permute-start(bf16[2,144,768]{2,1,0:T(8,128)(2,1)S(1)} %get-tuple-element.198), channel_id=1, source_target_pairs={{0,2},{2,0},{4,6},{6,4},{8,10},{10,8},{12,14},{14,12},{16,18},{18,... | collective-permute-start | bytes 1327112 | tf_op jit(solution)/shard_map/ppermute | solution.py:735
  61.3 21.5 %collective-permute-start.3 = (bf16[2,144,768]{2,1,0:T(8,128)(2,1)S(1)}, bf16[2,144,768]{2,1,0:T(8,128)(2,1)S(1)}, u32[]{:S(2)}, u32[]{:S(2)}) collective-permute-start(bf16[2,144,768]{2,1,0:T(8,128)(2,1)S(1)} %get-tuple-element.197), channel_id=1, source_target_pairs={{0,4},{2,6},{4,0},{6,2},{8,12},{10,14},{12,8},{14,10},{16,20},{18,... | collective-permute-start | bytes 1327112 | tf_op jit(solution)/shard_map/ppermute | solution.py:735
  62.8 19.8 %collective-permute-start.4 = (bf16[2,144,768]{2,1,0:T(8,128)(2,1)}, bf16[2,144,768]{2,1,0:T(8,128)(2,1)S(1)}, u32[]{:S(2)}, u32[]{:S(2)}) collective-permute-start(bf16[2,144,768]{2,1,0:T(8,128)(2,1)} %get-tuple-element.196), channel_id=1, source_target_pairs={{0,6},{2,4},{4,2},{6,0},{8,14},{10,12},{12,10},{14,8},{16,22},{18,... | collective-permute-start | bytes 1327112 | tf_op jit(solution)/shard_map/ppermute | solution.py:735
  91.2 39.8 %collective-permute-start.7 = (bf16[3072,768]{1,0:T(8,128)(2,1)}, bf16[3072,768]{1,0:T(8,128)(2,1)}, u32[]{:S(2)}, u32[]{:S(2)}) collective-permute-start(bf16[3072,768]{1,0:T(8,128)(2,1)} %slice.230), channel_id=1, source_target_pairs={{0,1},{1,0},{2,3},{3,2},{4,5},{5,4},{6,7},{7,6},{8,9},{9,8},{10,11... | collective-permute-start | bytes 14155784 | tf_op jit(solution)/shard_map/ppermute | solution.py:1034
  91.2 13.6 %collective-permute-start.5 = (bf16[2,144,768]{2,1,0:T(8,128)(2,1)S(1)}, bf16[2,144,768]{2,1,0:T(8,128)(2,1)S(1)}, u32[]{:S(2)}, u32[]{:S(2)}) collective-permute-start(bf16[2,144,768]{2,1,0:T(8,128)(2,1)S(1)} %copy-done.23), channel_id=1, source_target_pairs={{0,8},{2,10},{4,12},{6,14},{8,16},{10,18},{12,20},{14,22},{16,24},... | collective-permute-start | bytes 1327112 | tf_op jit(solution)/shard_map/ppermute | solution.py:761
  107.6 15.1 %collective-permute-start.6 = (bf16[2,144,768]{2,1,0:T(8,128)(2,1)}, bf16[2,144,768]{2,1,0:T(8,128)(2,1)S(1)}, u32[]{:S(2)}, u32[]{:S(2)}) collective-permute-start(bf16[2,144,768]{2,1,0:T(8,128)(2,1)} %link.2), channel_id=1, source_target_pairs={{0,16},{2,18},{4,20},{6,22},{8,24},{10,26},{12,28},{14,30},{1,17},... | collective-permute-start | bytes 1327112 | tf_op jit(solution)/shard_map/ppermute | solution.py:761
  127.4 14.3 %collective-permute-start.10 = (bf16[2,144,768]{2,1,0:T(8,128)(2,1)}, bf16[2,144,768]{2,1,0:T(8,128)(2,1)S(1)}, u32[]{:S(2)}, u32[]{:S(2)}) collective-permute-start(bf16[2,144,768]{2,1,0:T(8,128)(2,1)} %get-tuple-element.114), channel_id=1, source_target_pairs={{0,6},{2,4},{4,2},{6,0},{8,14},{10,12},{12,10},{14,8},{16,22},{18,... | collective-permute-start | bytes 1327112 | tf_op jit(solution)/shard_map/ppermute | solution.py:735
  128.8 20.2 %collective-permute-start.8 = (bf16[2,144,768]{2,1,0:T(8,128)(2,1)}, bf16[2,144,768]{2,1,0:T(8,128)(2,1)S(1)}, u32[]{:S(2)}, u32[]{:S(2)}) collective-permute-start(bf16[2,144,768]{2,1,0:T(8,128)(2,1)} %get-tuple-element.120), channel_id=1, source_target_pairs={{0,2},{2,0},{4,6},{6,4},{8,10},{10,8},{12,14},{14,12},{16,18},{18,... | collective-permute-start | bytes 1327112 | tf_op jit(solution)/shard_map/ppermute | solution.py:735
  130.3 18.8 %collective-permute-start.9 = (bf16[2,144,768]{2,1,0:T(8,128)(2,1)}, bf16[2,144,768]{2,1,0:T(8,128)(2,1)S(1)}, u32[]{:S(2)}, u32[]{:S(2)}) collective-permute-start(bf16[2,144,768]{2,1,0:T(8,128)(2,1)} %get-tuple-element.121), channel_id=1, source_target_pairs={{0,4},{2,6},{4,0},{6,2},{8,12},{10,14},{12,8},{14,10},{16,20},{18,... | collective-permute-start | bytes 1327112 | tf_op jit(solution)/shard_map/ppermute | solution.py:735
  179.1 9.3 %collective-permute-start.15 = (bf16[3072,768]{1,0:T(8,128)(2,1)}, bf16[3072,768]{1,0:T(8,128)(2,1)}, u32[]{:S(2)}, u32[]{:S(2)}) collective-permute-start(bf16[3072,768]{1,0:T(8,128)(2,1)} %convolution_convert_fusion.2), channel_id=1, source_target_pairs={{0,1},{1,0},{2,3},{3,2},{4,5},{5,4},{6,7},{7,6},{8,9},{9,8},{10,11... | collective-permute-start | bytes 14155784 | tf_op jit(solution)/shard_map/ppermute | solution.py:1140
  183.4 11.7 %collective-permute-start.14 = (bf16[1536,1536]{1,0:T(8,128)(2,1)}, bf16[1536,1536]{1,0:T(8,128)(2,1)}, u32[]{:S(2)}, u32[]{:S(2)}) collective-permute-start(bf16[1536,1536]{1,0:T(8,128)(2,1)} %convolution_convert_fusion), channel_id=1, source_target_pairs={{0,1},{1,0},{2,3},{3,2},{4,5},{5,4},{6,7},{7,6},{8,9},{9,8},{10,11... | collective-permute-start | bytes 14155784 | tf_op jit(solution)/shard_map/ppermute | solution.py:1140
  184.8 22.4 %collective-permute-start.11 = (bf16[2,144,768]{2,1,0:T(8,128)(2,1)S(1)}, bf16[2,144,768]{2,1,0:T(8,128)(2,1)S(1)}, u32[]{:S(2)}, u32[]{:S(2)}) collective-permute-start(bf16[2,144,768]{2,1,0:T(8,128)(2,1)S(1)} %get-tuple-element.194), channel_id=1, source_target_pairs={{0,2},{2,0},{4,6},{6,4},{8,10},{10,8},{12,14},{14,12},{16,18},{18,... | collective-permute-start | bytes 1327112 | tf_op jit(solution)/shard_map/ppermute | solution.py:735
  186.1 21.3 %collective-permute-start.12 = (bf16[2,144,768]{2,1,0:T(8,128)(2,1)S(1)}, bf16[2,144,768]{2,1,0:T(8,128)(2,1)S(1)}, u32[]{:S(2)}, u32[]{:S(2)}) collective-permute-start(bf16[2,144,768]{2,1,0:T(8,128)(2,1)S(1)} %get-tuple-element.193), channel_id=1, source_target_pairs={{0,4},{2,6},{4,0},{6,2},{8,12},{10,14},{12,8},{14,10},{16,20},{18,... | collective-permute-start | bytes 1327112 | tf_op jit(solution)/shard_map/ppermute | solution.py:735
  186.9 8.3 %copy-start.32 = (bf16[1,512,1536]{2,1,0:T(8,128)(2,1)S(1)}, bf16[1,512,1536]{2,1,0:T(8,128)(2,1)}, u32[]{:S(2)}) copy-start(bf16[1,512,1536]{2,1,0:T(8,128)(2,1)} %param.21) | copy-start | bytes 4718596
  186.9 8.3 %copy-start.60 = (bf16[2,256,3072]{2,1,0:T(8,128)(2,1)S(1)}, bf16[2,256,3072]{2,1,0:T(8,128)(2,1)}, u32[]{:S(2)}) copy-start(bf16[2,256,3072]{2,1,0:T(8,128)(2,1)} %get-tuple-element.128) | copy-start | bytes 9437188
  186.9 20.3 %collective-permute-start.13 = (bf16[2,144,768]{2,1,0:T(8,128)(2,1)S(1)}, bf16[2,144,768]{2,1,0:T(8,128)(2,1)S(1)}, u32[]{:S(2)}, u32[]{:S(2)}) collective-permute-start(bf16[2,144,768]{2,1,0:T(8,128)(2,1)S(1)} %get-tuple-element.192), channel_id=1, source_target_pairs={{0,6},{2,4},{4,2},{6,0},{8,14},{10,12},{12,10},{14,8},{16,22},{18,... | collective-permute-start | bytes 1327112 | tf_op jit(solution)/shard_map/ppermute | solution.py:735
  213.7 69.1 %collective-permute-start.21 = (bf16[2,2,2,96,1536]{4,3,2,1,0:T(8,128)(2,1)S(1)}, bf16[2,2,2,96,1536]{4,3,2,1,0:T(8,128)(2,1)}, u32[]{:S(2)}, u32[]{:S(2)}) collective-permute-start(bf16[2,2,2,96,1536]{4,3,2,1,0:T(8,128)(2,1)S(1)} %fusion.28), channel_id=1, source_target_pairs={{0,2},{2,0},{4,6},{6,4},{8,10},{10,8},{12,14},{14,12},{16,18},{18,... | collective-permute-start | bytes 7077896 | tf_op jit(solution)/shard_map/ppermute | solution.py:826
  218.6 70.1 %collective-permute-start.22 = (bf16[2,2,2,192,768]{4,3,0,1,2:T(8,128)(2,1)}, bf16[2,2,2,192,768]{4,3,0,1,2:T(8,128)(2,1)}, u32[]{:S(2)}, u32[]{:S(2)}) collective-permute-start(bf16[2,2,2,192,768]{4,3,0,1,2:T(8,128)(2,1)} %fusion.29), channel_id=1, source_target_pairs={{0,4},{2,6},{4,0},{6,2},{8,12},{10,14},{12,8},{14,10},{16,20},{18,... | collective-permute-start | bytes 7077896 | tf_op jit(solution)/shard_map/ppermute | solution.py:826
  219.9 22.1 %collective-permute-start.16 = (bf16[2,144,768]{2,1,0:T(8,128)(2,1)S(1)}, bf16[2,144,768]{2,1,0:T(8,128)(2,1)}, u32[]{:S(2)}, u32[]{:S(2)}) collective-permute-start(bf16[2,144,768]{2,1,0:T(8,128)(2,1)S(1)} %copy-done.22), channel_id=1, source_target_pairs={{8,0},{10,2},{12,4},{14,6},{16,8},{18,10},{20,12},{22,14},{24,16},... | collective-permute-start | bytes 1327112 | tf_op jit(solution)/shard_map/ppermute | solution.py:761
  244.2 31.1 %collective-permute-start.17 = (bf16[2,144,768]{2,1,0:T(8,128)(2,1)}, bf16[2,144,768]{2,1,0:T(8,128)(2,1)}, u32[]{:S(2)}, u32[]{:S(2)}) collective-permute-start(bf16[2,144,768]{2,1,0:T(8,128)(2,1)} %link.3), channel_id=1, source_target_pairs={{16,0},{18,2},{20,4},{22,6},{24,8},{26,10},{28,12},{30,14},{17,1},... | collective-permute-start | bytes 1327112 | tf_op jit(solution)/shard_map/ppermute | solution.py:761
  279.2 20.9 %collective-permute-start.18 = (bf16[2,144,768]{2,1,0:T(8,128)(2,1)}, bf16[2,144,768]{2,1,0:T(8,128)(2,1)S(1)}, u32[]{:S(2)}, u32[]{:S(2)}) collective-permute-start(bf16[2,144,768]{2,1,0:T(8,128)(2,1)} %get-tuple-element.146), channel_id=1, source_target_pairs={{0,2},{2,0},{4,6},{6,4},{8,10},{10,8},{12,14},{14,12},{16,18},{18,... | collective-permute-start | bytes 1327112 | tf_op jit(solution)/shard_map/ppermute | solution.py:735
  280.6 20.3 %collective-permute-start.19 = (bf16[2,144,768]{2,1,0:T(8,128)(2,1)}, bf16[2,144,768]{2,1,0:T(8,128)(2,1)}, u32[]{:S(2)}, u32[]{:S(2)}) collective-permute-start(bf16[2,144,768]{2,1,0:T(8,128)(2,1)} %get-tuple-element.147), channel_id=1, source_target_pairs={{0,4},{2,6},{4,0},{6,2},{8,12},{10,14},{12,8},{14,10},{16,20},{18,... | collective-permute-start | bytes 1327112 | tf_op jit(solution)/shard_map/ppermute | solution.py:735
  281.3 18.8 %collective-permute-start.20 = (bf16[2,144,768]{2,1,0:T(8,128)(2,1)}, bf16[2,144,768]{2,1,0:T(8,128)(2,1)S(1)}, u32[]{:S(2)}, u32[]{:S(2)}) collective-permute-start(bf16[2,144,768]{2,1,0:T(8,128)(2,1)} %get-tuple-element.148), channel_id=1, source_target_pairs={{0,6},{2,4},{4,2},{6,0},{8,14},{10,12},{12,10},{14,8},{16,22},{18,... | collective-permute-start | bytes 1327112 | tf_op jit(solution)/shard_map/ppermute | solution.py:735
  308.4 29.0 %collective-permute-start.23 = (bf16[2,2,96,1536]{3,2,1,0:T(8,128)(2,1)S(1)}, bf16[2,2,96,1536]{3,2,1,0:T(8,128)(2,1)}, u32[]{:S(2)}, u32[]{:S(2)}) collective-permute-start(bf16[2,2,96,1536]{3,2,1,0:T(8,128)(2,1)S(1)} %fusion.41), channel_id=1, source_target_pairs={{0,4},{2,6},{4,0},{6,2},{8,12},{10,14},{12,8},{14,10},{16,20},{18,... | collective-permute-start | bytes 3538952 | tf_op jit(solution)/shard_map/ppermute | solution.py:826
  309.2 28.2 %collective-permute-start.24 = (bf16[2,2,192,768]{3,2,0,1:T(8,128)(2,1)S(1)}, bf16[2,2,192,768]{3,2,0,1:T(8,128)(2,1)}, u32[]{:S(2)}, u32[]{:S(2)}) collective-permute-start(bf16[2,2,192,768]{3,2,0,1:T(8,128)(2,1)S(1)} %fusion.42), channel_id=1, source_target_pairs={{0,2},{2,0},{4,6},{6,4},{8,10},{10,8},{12,14},{14,12},{16,18},{18,... | collective-permute-start | bytes 3538952 | tf_op jit(solution)/shard_map/ppermute | solution.py:826
  337.4 8.0 %collective-permute-start.25 = (bf16[2,16,3328]{2,1,0:T(8,128)(2,1)S(1)}, bf16[2,16,3328]{2,1,0:T(8,128)(2,1)S(1)}, u32[]{:S(2)}, u32[]{:S(2)}) collective-permute-start(bf16[2,16,3328]{2,1,0:T(8,128)(2,1)S(1)} %pad_maximum_fusion.12), channel_id=1, source_target_pairs={{2,0},{4,2},{6,4},{8,6},{10,8},{12,10},{14,12},{16,14},{18,16},{20... | collective-permute-start | bytes 638984 | tf_op jit(solution)/shard_map/ppermute | solution.py:1366
  345.7 15.6 %copy-start.4 = (bf16[2,256,3072]{2,1,0:T(8,128)(2,1)}, bf16[2,256,3072]{2,1,0:T(8,128)(2,1)S(1)}, u32[]{:S(2)}) copy-start(bf16[2,256,3072]{2,1,0:T(8,128)(2,1)S(1)} %pad_maximum_fusion) | copy-start | bytes 9437188
  349.7 11.6 %collective-permute-start.33 = (bf16[3072,768]{1,0:T(8,128)(2,1)S(1)}, bf16[3072,768]{1,0:T(8,128)(2,1)S(1)}, u32[]{:S(2)}, u32[]{:S(2)}) collective-permute-start(bf16[3072,768]{1,0:T(8,128)(2,1)S(1)} %convolution_convert_fusion.1), channel_id=1, source_target_pairs={{0,1},{1,0},{2,3},{3,2},{4,5},{5,4},{6,7},{7,6},{8,9},{9,8},{10,11... | collective-permute-start | bytes 14155784 | tf_op jit(solution)/shard_map/ppermute | solution.py:1140
  350.4 8.4 %collective-permute-start.34 = (bf16[512,768]{1,0:T(8,128)(2,1)S(1)}, bf16[512,768]{1,0:T(8,128)(2,1)S(1)}, u32[]{:S(2)}, u32[]{:S(2)}) collective-permute-start(bf16[512,768]{1,0:T(8,128)(2,1)S(1)} %convolution_convert_fusion.3), channel_id=1, source_target_pairs={{0,1},{1,0},{2,3},{3,2},{4,5},{5,4},{6,7},{7,6},{8,9},{9,8},{10,11... | collective-permute-start | bytes 2359304 | tf_op jit(solution)/shard_map/ppermute | solution.py:1140
  350.9 29.5 %collective-permute-start.31 = (bf16[2,384,768]{2,1,0:T(8,128)(2,1)}, bf16[2,384,768]{2,1,0:T(8,128)(2,1)}, u32[]{:S(2)}, u32[]{:S(2)}) collective-permute-start(bf16[2,384,768]{2,1,0:T(8,128)(2,1)} %pad_maximum_fusion.4), channel_id=1, source_target_pairs={{0,8},{2,10},{4,12},{6,14},{8,0},{10,2},{12,4},{14,6},{16,24},{18,... | collective-permute-start | bytes 3538952 | tf_op jit(solution)/shard_map/ppermute | solution.py:826
  370.5 33.1 %collective-permute-start.37 = (bf16[2,2,2,224,384]{4,3,0,1,2:T(8,128)(2,1)}, bf16[2,2,2,224,384]{4,3,0,1,2:T(8,128)(2,1)}, u32[]{:S(2)}, u32[]{:S(2)}) collective-permute-start(bf16[2,2,2,224,384]{4,3,0,1,2:T(8,128)(2,1)} %pad_maximum_fusion.3), channel_id=1, source_target_pairs={{0,4},{2,6},{4,0},{6,2},{8,12},{10,14},{12,8},{14,10},{16,20},{18,... | collective-permute-start | bytes 4128776 | tf_op jit(solution)/shard_map/ppermute | solution.py:826
  375.8 29.6 %slice-start.4 = ((s8[4718592]{0:T(1024)(128)(4,1)}), s8[4194304]{0:T(1024)(128)(4,1)S(1)}, s32[]{:S(2)}) async-start(s8[4718592]{0:T(1024)(128)(4,1)} %bitcast.249), calls=%async_computation.6 | async-start | bytes 8388608
  375.9 27.6 %copy-start.19 = (f32[512,384]{1,0:T(8,128)S(1)}, f32[512,384]{1,0:T(8,128)}, u32[]{:S(2)}) copy-start(f32[512,384]{1,0:T(8,128)} %copy-done.18) | copy-start | bytes 2359300
  375.9 29.4 %slice-start.5 = ((s8[4718592]{0:T(1024)(128)(4,1)}), s8[524288]{0:T(1024)(128)(4,1)S(1)}, s32[]{:S(2)}) async-start(s8[4718592]{0:T(1024)(128)(4,1)} %bitcast.249), calls=%async_computation.7 | async-start | bytes 1048576
  375.9 33.7 %collective-permute-start.35 = (bf16[2,2,2,224,384]{4,3,0,1,2:T(8,128)(2,1)S(1)}, bf16[2,2,2,224,384]{4,3,0,1,2:T(8,128)(2,1)S(1)}, u32[]{:S(2)}, u32[]{:S(2)}) collective-permute-start(bf16[2,2,2,224,384]{4,3,0,1,2:T(8,128)(2,1)S(1)} %pad_maximum_fusion.2), channel_id=1, source_target_pairs={{0,2},{2,0},{4,6},{6,4},{8,10},{10,8},{12,14},{14,12},{16,18},{18,... | collective-permute-start | bytes 4128776 | tf_op jit(solution)/shard_map/ppermute | solution.py:826
  382.0 25.1 %copy-start.13 = (f32[2,192,768]{2,1,0:T(8,128)}, f32[2,192,768]{2,1,0:T(8,128)S(1)}, u32[]{:S(2)}) copy-start(f32[2,192,768]{2,1,0:T(8,128)S(1)} %get-tuple-element.204) | copy-start | bytes 3538948
  382.0 25.1 %copy-start.14 = (f32[2,192,768]{2,1,0:T(8,128)}, f32[2,192,768]{2,1,0:T(8,128)S(1)}, u32[]{:S(2)}) copy-start(f32[2,192,768]{2,1,0:T(8,128)S(1)} %get-tuple-element.205) | copy-start | bytes 3538948
  383.1 30.9 %collective-permute-start.32 = (bf16[384,768]{1,0:T(8,128)(2,1)}, bf16[384,768]{1,0:T(8,128)(2,1)}, u32[]{:S(2)}, u32[]{:S(2)}) collective-permute-start(bf16[384,768]{1,0:T(8,128)(2,1)} %pad_maximum_fusion.9), channel_id=1, source_target_pairs={{0,16},{2,18},{4,20},{6,22},{8,24},{10,26},{12,28},{14,30},{16,0},... | collective-permute-start | bytes 1769480 | tf_op jit(solution)/shard_map/ppermute | solution.py:826
  408.1 17.3 %collective-permute-start.38 = (bf16[2,2,224,384]{3,2,0,1:T(8,128)(2,1)}, bf16[2,2,224,384]{3,2,0,1:T(8,128)(2,1)}, u32[]{:S(2)}, u32[]{:S(2)}) collective-permute-start(bf16[2,2,224,384]{3,2,0,1:T(8,128)(2,1)} %pad_maximum_fusion.7), channel_id=1, source_target_pairs={{0,2},{2,0},{4,6},{6,4},{8,10},{10,8},{12,14},{14,12},{16,18},{18,... | collective-permute-start | bytes 2064392 | tf_op jit(solution)/shard_map/ppermute | solution.py:826
  412.3 16.7 %collective-permute-start.36 = (bf16[2,2,224,384]{3,2,0,1:T(8,128)(2,1)}, bf16[2,2,224,384]{3,2,0,1:T(8,128)(2,1)}, u32[]{:S(2)}, u32[]{:S(2)}) collective-permute-start(bf16[2,2,224,384]{3,2,0,1:T(8,128)(2,1)} %pad_maximum_fusion.6), channel_id=1, source_target_pairs={{0,4},{2,6},{4,0},{6,2},{8,12},{10,14},{12,8},{14,10},{16,20},{18,... | collective-permute-start | bytes 2064392 | tf_op jit(solution)/shard_map/ppermute | solution.py:826
  414.0 15.0 %copy-start.10 = (f32[2,2,2,192,384]{4,3,0,1,2:T(8,128)S(1)}, f32[2,2,2,192,384]{4,3,0,1,2:T(8,128)}, u32[]{:S(2)}) copy-start(f32[2,2,2,192,384]{4,3,0,1,2:T(8,128)} %copy-done.9) | copy-start | bytes 7077892
  432.4 16.1 %collective-permute-start.39 = (bf16[2,224,768]{2,1,0:T(8,128)(2,1)S(1)}, bf16[2,224,768]{2,1,0:T(8,128)(2,1)S(1)}, u32[]{:S(2)}, u32[]{:S(2)}) collective-permute-start(bf16[2,224,768]{2,1,0:T(8,128)(2,1)S(1)} %pad_maximum_fusion.8), channel_id=1, source_target_pairs={{0,8},{2,10},{4,12},{6,14},{8,0},{10,2},{12,4},{14,6},{16,24},{18,... | collective-permute-start | bytes 2064392 | tf_op jit(solution)/shard_map/ppermute | solution.py:826
  448.7 17.3 %copy-start.1 = (bf16[1,512,1536]{2,1,0:T(8,128)(2,1)S(1)}, bf16[1,512,1536]{2,1,0:T(8,128)(2,1)}, u32[]{:S(2)}) copy-start(bf16[1,512,1536]{2,1,0:T(8,128)(2,1)} %param.11) | copy-start | bytes 4718596
  448.7 17.6 %copy-start.54 = (f32[8,256]{1,0:T(8,128)S(1)}, f32[8,256]{1,0:T(8,128)}, u32[]{:S(2)}) copy-start(f32[8,256]{1,0:T(8,128)} %get-tuple-element.176) | copy-start | bytes 24580
  448.8 16.0 %collective-permute-start.40 = (bf16[224,768]{1,0:T(8,128)(2,1)S(1)}, bf16[224,768]{1,0:T(8,128)(2,1)S(1)}, u32[]{:S(2)}, u32[]{:S(2)}) collective-permute-start(bf16[224,768]{1,0:T(8,128)(2,1)S(1)} %pad_maximum_fusion.11), channel_id=1, source_target_pairs={{0,16},{2,18},{4,20},{6,22},{8,24},{10,26},{12,28},{14,30},{16,0},... | collective-permute-start | bytes 1032200 | tf_op jit(solution)/shard_map/ppermute | solution.py:826
  498.2 17.7 %slice-start.6 = ((s8[9437184]{0:T(1024)(128)(4,1)}), s8[4194304]{0:T(1024)(128)(4,1)S(1)}, s32[]{:S(2)}) async-start(s8[9437184]{0:T(1024)(128)(4,1)} %bitcast.287), calls=%async_computation.8 | async-start | bytes 8388608
  498.2 17.7 %slice-start.7 = ((s8[9437184]{0:T(1024)(128)(4,1)}), s8[4194304]{0:T(1024)(128)(4,1)S(1)}, s32[]{:S(2)}) async-start(s8[9437184]{0:T(1024)(128)(4,1)} %bitcast.287), calls=%async_computation.9 | async-start | bytes 8388608
  503.3 12.6 %slice-start.8 = ((s8[9437184]{0:T(1024)(128)(4,1)}), s8[1048576]{0:T(1024)(128)(4,1)S(1)}, s32[]{:S(2)}) async-start(s8[9437184]{0:T(1024)(128)(4,1)} %bitcast.287), calls=%async_computation.10 | async-start | bytes 2097152
  505.1 10.8 %copy-start.61 = (bf16[2,256,3072]{2,1,0:T(8,128)(2,1)S(1)}, bf16[2,256,3072]{2,1,0:T(8,128)(2,1)}, u32[]{:S(2)}) copy-start(bf16[2,256,3072]{2,1,0:T(8,128)(2,1)} %get-tuple-element.128) | copy-start | bytes 9437188
  507.2 1.4 collective-permute-start.26
  508.6 7.2 %collective-permute-start.27 = (f32[169,128]{1,0:T(8,128)S(1)}, f32[169,128]{1,0:T(8,128)S(1)}, u32[]{:S(2)}, u32[]{:S(2)}) collective-permute-start(f32[169,128]{1,0:T(8,128)S(1)} %bitcast_add_fusion.19), channel_id=1, source_target_pairs={{0,2},{2,0},{4,6},{6,4},{8,10},{10,8},{12,14},{14,12},{16,18},{18,... | collective-permute-start | bytes 259592 | tf_op jit(solution)/shard_map/ppermute | solution.py:842
  515.8 17.0 %copy-start.33 = (bf16[1,512,1536]{2,1,0:T(8,128)(2,1)S(1)}, bf16[1,512,1536]{2,1,0:T(8,128)(2,1)}, u32[]{:S(2)}) copy-start(bf16[1,512,1536]{2,1,0:T(8,128)(2,1)} %param.21) | copy-start | bytes 4718596
  515.8 6.3 collective-permute-start.28
  522.1 10.6 %collective-permute-start.29 = (f32[169,128]{1,0:T(8,128)S(1)}, f32[169,128]{1,0:T(8,128)S(1)}, u32[]{:S(2)}, u32[]{:S(2)}) collective-permute-start(f32[169,128]{1,0:T(8,128)S(1)} %add.290), channel_id=1, source_target_pairs={{0,8},{2,10},{4,12},{6,14},{8,0},{10,2},{12,4},{14,6},{16,24},{18,... | collective-permute-start | bytes 259592 | tf_op jit(solution)/shard_map/ppermute | solution.py:842
  532.7 11.3 %collective-permute-start.30 = (f32[169,128]{1,0:T(8,128)S(1)}, f32[169,128]{1,0:T(8,128)S(1)}, u32[]{:S(2)}, u32[]{:S(2)}) collective-permute-start(f32[169,128]{1,0:T(8,128)S(1)} %add.291), channel_id=1, source_target_pairs={{0,16},{2,18},{4,20},{6,22},{8,24},{10,26},{12,28},{14,30},{16,0},... | collective-permute-start | bytes 259592 | tf_op jit(solution)/shard_map/ppermute | solution.py:842
  (50 other events, 134.4 us)
Sparse Core Ops, SparseCore 0:
  55.4 22.1 all-gather.2
  466.1 178.6 all-gather.4

commit v4 on v3

--- a/solution.py
+++ b/solution.py
@@ -26,14 +26,14 @@
 SIDE = 16
 SUB = 128
 FAR = -1e30
-VMEM = 60 * 1024 * 1024
+MIB = 1024 * 1024
 HIGHEST = lax.Precision.HIGHEST
 F32 = jnp.float32
 BF16 = jnp.bfloat16
 
 
-def params():
-    return pltpu.CompilerParams(vmem_limit_bytes=VMEM)
+def params(mebibytes):
+    return pltpu.CompilerParams(vmem_limit_bytes=mebibytes * MIB)
 
 
 def cost(microseconds):
@@ -329,6 +329,7 @@
     scanned_ref,
     gated_ref,
     gate_ref,
+    start_ref,
     spread,
     state_ref,
 ):
@@ -338,13 +339,18 @@
     start = jnp.exp(running)
     read_along = running[:, HEADS : HEADS + 1]
     readout = bc_ref[0, :, STATE:].astype(BF16)
-    scanned_ref[...] = dot(readout, entering[0])
+    readout_t = bc_ref[0, :, STATE:].T.astype(BF16)
     squares = jnp.zeros((ROWS, TILE), F32)
     overlap = jnp.zeros((ROWS, TILE), F32)
     for tile in range(INNER // TILE):
         lanes = slice(TILE * tile, TILE * tile + TILE)
-        carried = scanned_ref[:, lanes] + read_along * along[0, 0:1, lanes]
-        scanned = y_ref[0, :, lanes] + pick(start, tile) * carried
+        if tile % 2 == 0:
+            wide = dot(readout, entering[0, :, TILE * tile : TILE * tile + 2 * TILE])
+        carried = wide[:, TILE * (tile % 2) : TILE * (tile % 2) + TILE]
+        carried = carried + read_along * along[0, 0:1, lanes]
+        begin = pick(start, tile)
+        start_ref[:, lanes] = begin
+        scanned = y_ref[0, :, lanes] + begin * carried
         scanned_ref[:, lanes] = scanned
         z = z_ref[0, :, lanes]
         gate = jax.nn.sigmoid(z)
@@ -360,6 +366,10 @@
     @pl.when(step == 0)
     def _():
         gain_grad_ref[...] = jnp.zeros_like(gain_grad_ref)
+
+    @pl.when(step % per_seq == 0)
+    def _():
+        state_ref[...] = jnp.zeros_like(state_ref)
 
     for tile in range(INNER // TILE):
         lanes = slice(TILE * tile, TILE * tile + TILE)
@@ -376,17 +386,10 @@
             grad_gated * scanned_ref[:, lanes] * (gate * (1.0 + z * (1.0 - gate)))
         ).astype(BF16)
         grad_scan_ref[0, :, lanes] = grad_scan
-        rounded = grad_scan.astype(BF16).astype(F32)
-        spread[:, lanes] = (rounded * pick(start, tile)).astype(BF16)
-    added = dot_first(readout, spread[...])
-
-    @pl.when(step % per_seq == 0)
-    def _():
-        state_ref[...] = added
-
-    @pl.when(step % per_seq != 0)
-    def _():
-        state_ref[...] += added
+        spread[:, lanes] = (grad_scan * start_ref[:, lanes]).astype(BF16)
+        if tile % 2:
+            both = slice(TILE * tile - TILE, TILE * tile + TILE)
+            state_ref[:, both] += dot(readout_t, spread[:, both])
 
     @pl.when(step % per_seq == per_seq - 1)
     def _():
@@ -442,6 +445,7 @@
         inner = [jnp.zeros((SUB, SUB), F32) for _ in range(2)]
         outer = jnp.zeros((SUB, SUB), F32)
         meeting = jnp.zeros((256, TILE), F32)
+        product[2] = dot(readout, entering[seq])
         for tile in range(Q_TILES):
             lanes = slice(TILE * tile, TILE * tile + TILE)
             x = x_ref[seq, :, lanes]
@@ -453,7 +457,7 @@
             high_grad = jnp.where(low, 0.0, grad).astype(BF16)
             rounded = grad.astype(BF16)
             line = along[seq, 0:1, lanes]
-            carried = dot(readout, entering[seq, :, lanes]) + read_along * line
+            carried = product[2, :, lanes] + read_along * line
             through = skip[:, lanes] * x
             product[2, :, lanes] = rounded.astype(F32) * (
                 y_ref[seq, :, lanes] + begin * carried - through
@@ -471,14 +475,15 @@
             for part in range(2):
                 rows = slice(SUB * part, SUB * part + SUB)
                 weights = []
+                pairs = dot_last(
+                    jnp.concatenate([sides[0][rows], sides[1][rows]], 0), rounded[rows]
+                )
                 for side in range(2):
                     h = 2 * tile + side
                     apart = sum_t[0, seq, h : h + 1, rows] - running[rows, h : h + 1]
                     decayed = jnp.exp(jnp.where(causal, apart, FAR))
                     weights.append((decayed * scores_t[seq, rows, rows]).astype(BF16))
-                    inner[part] = inner[part] + decayed * dot_last(
-                        sides[side][rows], rounded[rows]
-                    )
+                    inner[part] = inner[part] + decayed * pairs[SUB * side : SUB * side + SUB]
                 inside = dot(
                     jnp.concatenate(weights, 1),
                     jnp.concatenate([low_grad[rows], high_grad[rows]], 0),
@@ -543,14 +548,14 @@
         remain = jnp.exp(running[255:256] - running)
         scale = step_q[0, seq] * remain
         writes = bc_ref[seq, :, :STATE].astype(BF16)
+        product[...] = dot(writes, leaving[seq])
         for tile in range(Q_TILES):
             lanes = slice(TILE * tile, TILE * tile + TILE)
             taps = weight[:, lanes]
             x = x_ref[seq, :, lanes]
             back = leaving[seq, :, lanes]
-            shared = dot(writes, back)
-            left = pick(remain, tile)
-            product[:, lanes] = x * (left * shared)
+            shared = product[:, lanes]
+            product[:, lanes] = x * shared
             factor = pick(scale, tile)
             spread[:, lanes] = (x * factor).astype(BF16)
             slope = slope_ref[seq, :, lanes].astype(F32)
@@ -569,7 +574,9 @@
             meeting_ref[seq : seq + 1, lanes] = jnp.sum(
                 state * back.astype(F32), axis=0, keepdims=True
             )
-        heads_ref[0, seq] = head_sums(product[...], head_columns(Q_LANES, TILE, 0))
+        total = dot(product[...].astype(BF16), head_columns(Q_LANES, TILE, 0))
+        heads_ref[0, seq] = jnp.zeros((256, TILE), F32)
+        heads_ref[0, seq, :, :SIDE] = total[:, :SIDE] * remain
         grad_writes_ref[seq] += dot_last(spread[...], leaving[seq])
 
 
@@ -748,7 +755,7 @@
         in_specs=[SCALAR] + [block] * QUARTERS,
         out_specs=block,
         out_shape=message,
-        compiler_params=params(),
+        compiler_params=params(14),
         cost_estimate=cost(2),
         name="plane",
     )(member, *members)
@@ -768,7 +775,7 @@
                 in_specs=[block] * (1 + len(received)),
                 out_specs=block,
                 out_shape=message,
-                compiler_params=params(),
+                compiler_params=params(14),
                 cost_estimate=cost(1.5),
                 name="link",
             )(total, *received)
@@ -778,7 +785,7 @@
         in_specs=[SCALAR] + [block] * (QUARTERS + len(received)),
         out_specs=[block] * QUARTERS,
         out_shape=[message] * QUARTERS,
-        compiler_params=params(),
+        compiler_params=params(16),
         cost_estimate=cost(3),
         name="spread",
     )(member, *members, *received)
@@ -793,7 +800,7 @@
             out_specs=[own_lanes((2, STATE)), own_lanes((2, 8))],
         ),
         out_shape=[shape((2, STATE, INNER), BF16), shape((2, 8, INNER))],
-        compiler_params=params(),
+        compiler_params=params(14),
         cost_estimate=cost(1.5),
         name="arrange",
     )(member, *back)
@@ -815,7 +822,7 @@
             : len(self.values)
         ]
 
-    def send(self, bit):
+    def send(self, bit, *others):
         position = self.bits.index(bit)
         mine = (self.place >> bit) & 1
         away = [lax.dynamic_index_in_dim(v, 1 - mine, position, False) for v in self.values]
@@ -823,6 +830,8 @@
         self.values = [lax.dynamic_index_in_dim(v, mine, position, False) for v in self.values]
         self.bits.remove(bit)
         self.away = away
+        if others:
+            away = tie(away, *others)
         self.sent = lax.ppermute(
             away, self.axis, [(i, i ^ (1 << bit)) for i in range(self.count)]
         )
@@ -939,7 +948,7 @@
     gain_row = gate_gain[None]
     skip_row = jnp.repeat(skip_gain, HEAD_DIM)[None]
 
-    own_ext = tie(own_ext, conv_rows_other, row_direction, column_direction, small, bias_row)
+    own_ext = tie(own_ext, row_direction, column_direction, small, bias_row, skip_row)
     conv_input = (dot_last(own_ext, conv_rows) + dot_last(other_ext, conv_rows_other)).reshape(
         2, half + EDGE, CONV_CH + HEADS
     )
@@ -980,7 +989,7 @@
             shape(per_quarter),
             shape((QUARTERS, 2, EDGE, half)),
         ],
-        compiler_params=params(),
+        compiler_params=params(20),
         cost_estimate=cost(4),
         name="steps",
     )(conv_input, conv_weight, bias_row, small, row_direction)
@@ -1008,7 +1017,7 @@
             out_specs=[own_lanes((2, half)), quarter_block(MESSAGE)],
         ),
         out_shape=[shape((2, half, INNER)), shape((QUARTERS,) + MESSAGE, BF16)],
-        compiler_params=params(),
+        compiler_params=params(16),
         cost_estimate=cost(8),
         name="states",
     )(member, conv_input, conv_weight, bias_row, step_q, sum_q, bt, column_direction)
@@ -1027,11 +1036,11 @@
     kept = {}
 
     def while_states_cross(sent):
+        kept["rows"] = lax.ppermute(tie(rows_of, sent), "fsdp", other)[:INNER]
         kept["gate"] = dot_last(tie(own_normed, sent), gate_rows)
         return inside(0)(sent) + (kept["gate"],)
 
     def while_first_states(sent):
-        kept["rows"] = lax.ppermute(tie(rows_of, sent)[:INNER], "fsdp", other)
         kept["grad"] = dot_last(tie(upstream, sent), out_rows).reshape(2, half, INNER)
         return (kept["grad"],)
 
@@ -1054,7 +1063,7 @@
                 out_specs=later_half(tokens_block, first),
                 out_shape=shape((2, half, INNER)),
                 input_output_aliases={len(specs): 0} if first else {},
-                compiler_params=params(),
+                compiler_params=params(60),
                 cost_estimate=cost(8),
                 name="inside",
             )(*inputs, *([kept["inside"]] if first else []))
@@ -1112,10 +1121,11 @@
             pltpu.VMEM((ROWS, INNER), F32),
             pltpu.VMEM((ROWS, INNER), F32),
             pltpu.VMEM((ROWS, INNER), F32),
+            pltpu.VMEM((ROWS, INNER), F32),
             pltpu.VMEM((ROWS, INNER), BF16),
             pltpu.VMEM((STATE, INNER), F32),
         ],
-        compiler_params=params(),
+        compiler_params=params(38),
         cost_estimate=cost(14),
         name="gates",
     )(
@@ -1156,8 +1166,7 @@
         def work(sent):
             if not first:
                 for part, bit in ((kept["out"], 0), (kept["gates"], 1)):
-                    part.wait_for(sent)
-                    part.send(bit)
+                    part.send(bit, sent)
             specs = [
                 tokens_block,
                 tokens_block,
@@ -1223,7 +1232,7 @@
                     input_output_aliases={
                         len(specs) + i: (0, 1, 3)[i] for i in range(len(earlier))
                     },
-                    compiler_params=params(),
+                    compiler_params=params(60),
                     cost_estimate=cost(17),
                     name="inside_back",
                 )(*inputs, *earlier)
@@ -1290,7 +1299,7 @@
             pltpu.VMEM((half, Q_LANES), F32),
             pltpu.VMEM((half, Q_LANES), BF16),
         ],
-        compiler_params=params(),
+        compiler_params=params(60),
         cost_estimate=cost(12),
         name="channels",
     )(
@@ -1342,7 +1351,7 @@
             shape((8, TILE)),
         ],
         scratch_shapes=[pltpu.VMEM((half + 2 * EDGE, 256), F32)],
-        compiler_params=params(),
+        compiler_params=params(60),
         cost_estimate=cost(6),
         name="last",
     )(
@@ -1453,7 +1462,7 @@
         in_specs=[columns, tokens_block, tokens_block, tokens_block],
         out_specs=lane_block((8,)),
         out_shape=shape((8, INNER)),
-        compiler_params=params(),
+        compiler_params=params(60),
         cost_estimate=cost(10),
         name="sums",
     )(conv_input, grad_mix, grad_scan, x)
@@ -1500,7 +1509,7 @@
             pl.BlockSpec((share // 2, width), lambda g: (jnp.minimum(g, parts_of - 1), 0)),
         ],
         out_shape=[shape((CONV_CH + HEADS + INNER, share)), shape((2 * share, width))],
-        compiler_params=params(),
+        compiler_params=params(60),
         cost_estimate=cost(14),
         name="finish",
     )(gathered, gathered, gathered)

time: 676 us -> 655 us (0.969)
  Pallas kernels: 166 us -> 140 us
  starting transfers between devices: 54.3 us -> 70.5 us
    all_gather x1, starting transfers between devices: 0.22 us -> 10.3 us  [local(): gathered = lax.all_gather(shard, 'seq', axis=0)]
    unnamed x148 -> x218, local copies, waits for them, and re-layouts: 16.5 us -> 23.8 us
  transfers between devices with their start and end apart: 43 -> 43, of which waited for: 25 -> 22; matrix products, arithmetic and copies ran while one was open for 22% -> 23% of each run, Pallas kernels for 16% -> 14%
where the time goes in v4:
time: 655 us; the launch traced here: 652 us
  waiting for transfers between devices  228 us (35%)
  Pallas kernels  140 us (21%)
  matrix products  95 us (15%)
  starting transfers between devices  70.5 us (11%)
  local copies, waits for them, and re-layouts  58.4 us (9%)
  other arithmetic  43.4 us (7%)
  between operations  16.7 us (3%)
    all_gather x1, waiting for transfers between devices, local(): gathered = lax.all_gather(shard, 'seq', axis=0)  99.9 us
    ppermute x12, waiting for transfers between devices, send(): lax.ppermute(away, self.axis, [(i, i ^ 1 << bit) for i in range(self.coun...  60.6 us
    pallas_call x2, Pallas kernels, work(): pl.pallas_call(intra_back_kernel, grid=(half_grid,), in_specs=shifted(spe...  37.6 us
    dot_general x5, matrix products, dot_last(): lax.dot_general(left, right, (((1,), (1,)), ((), ())), preferred_element_...  37.2 us
    dot_general x7, matrix products, dot(): return jnp.dot(left, right, preferred_element_type=F32)  29.8 us
    dot_general x8, matrix products, dot_first(): lax.dot_general(left, right, (((0,), (0,)), ((), ())), preferred_element_...  28 us
    ppermute x12, waiting for transfers between devices, swap(): return lax.ppermute(value, axis, [(i, i ^ by) for i in range(count)])  27.8 us
    unnamed x218, local copies, waits for them, and re-layouts  23.8 us
  transfers between devices with their start and end apart: 43, of which 22 were waited for; matrix products, arithmetic and copies ran while one was open for 23% of the time, Pallas kernels for 14%

profile of v4, /device:TPU:0, one launch (start us, length us, event | category | flops | bytes accessed | tf_op | source)
XLA Modules:
  0.0 651.9 jit_solution(1455007736712976074)
XLA Ops:
  7.3 5.2 slice.284
  12.9 4.4 collective-permute-start
  23.9 5.4 fusion.86
  29.3 5.4 convolution_add_fusion
  34.7 2.0 steps.1
  40.2 9.8 %states.1 = (f32[2,256,3072]{2,1,0:T(8,128)S(1)}, bf16[4,2,144,768]{3,2,1,0:T(8,128)(2,1)S(1)}) custom-call(s32[1]{0:T(128)} %bitcast.1.member, f32[2,272,3376]{2,1,0:T(8,128)S(1)} %bitcast.225, f32[4,3328]{1,0:T(4,128)S(1)} %copy-done.14, f32[1,3328]{1,0:T(1,128)S(1)} %broadcast_in_dim.26.bias, f32[4,2,256,16]{3,2,1,0:T(8,128)S(1)} %get-tuple-element.100.step_q, ...), custom_call_target="tpu_custom_call" | custom-call | bytes 27200000 | tf_op jit(solution)/shard_map/states/pallas_call | solution.py:1003
  50.0 2.6 copy-done.1
  53.8 10.3 %all-gather.5.cloned.1.call-start = ((), (), s32[]{:S(2)}) async-start(), calls=%async_computation.1 | async-start | bytes 15876096 | tf_op jit(solution)/shard_map/all_gather | solution.py:1434
  64.5 3.1 fusion.25
  73.8 9.2 %inside.2.refs_0_ = f32[2,256,3072]{2,1,0:T(8,128)} custom-call(f32[2,256,3072]{2,1,0:T(8,128)} %copy-done.1, f32[4,2,256,16]{3,2,1,0:T(8,128)} %copy-done.2, f32[4,2,256,16]{3,2,1,0:T(8,128)} %copy-done.3, f32[4,2,16,256]{3,2,1,0:T(8,128)} %copy-done.12, f32[2,256,256]{2,1,0:T(8,128)} %copy-done.13, f32[1,3072]{1,0:T(1,128)} %broadcast_in_dim_reshape.3.skip), custom_call_target="tpu_custom_call" | custom-call | bytes 27200000 | tf_op jit(solution)/shard_map/inside/pallas_call | solution.py:1058
  83.0 6.9 %fusion.9 = f32[512,3072]{1,0:T(8,128)} fusion(bf16[512,768]{1,0:T(8,128)(2,1)S(1)} %copy-done.57, bf16[6448,768]{1,0:T(8,128)(2,1)} %bitcast.271), kind=kOutput, calls=%fused_computation.21 | convolution fusion | flops 2415919104 | bytes 11796480 | tf_op jit(solution)/shard_map/dot_general | solution.py:76
  89.9 4.1 collective-permute-done.4.refs_3_
  95.2 3.5 collective-permute-start.5
  98.7 9.8 %fusion.87 = f32[512,3072]{1,0:T(8,128)} fusion(bf16[512,1536]{1,0:T(8,128)(2,1)} %bitcast.277, bf16[3072,1536]{1,0:T(8,128)(2,1)} %all-gather.3.cloned.1.call-done), kind=kOutput, calls=%fused_computation.215 | convolution fusion | flops 4831838208 | bytes 17301504 | tf_op jit(solution)/shard_map/dot_general | solution.py:76
  110.6 5.7 collective-permute-start.6
  116.2 9.2 %inside.3.y_ref = f32[2,256,3072]{2,1,0:T(8,128)} custom-call(f32[2,256,3072]{2,1,0:T(8,128)} %copy-done.1, f32[4,2,256,16]{3,2,1,0:T(8,128)} %copy-done.2, f32[4,2,256,16]{3,2,1,0:T(8,128)} %copy-done.3, f32[4,2,16,256]{3,2,1,0:T(8,128)} %copy-done.12, f32[2,256,256]{2,1,0:T(8,128)} %copy-done.13, ...), custom_call_target="tpu_custom_call", output_to_operand_aliasing={{}: (6, {})} | custom-call | bytes 27200000 | tf_op jit(solution)/shard_map/inside/pallas_call | solution.py:1058
  125.4 1.9 spread.2
  130.9 9.8 %convolution_add_fusion.1 = f32[512,3072]{1,0:T(8,128)} fusion(f32[512,3072]{1,0:T(8,128)} %fusion.9, bf16[512,768]{1,0:T(8,128)(2,1)} %get-tuple-element.115, bf16[6448,768]{1,0:T(8,128)(2,1)} %collective-permute-done.7), kind=kOutput, calls=%fused_computation.15 | convolution fusion | flops 2417491968 | bytes 18087936 | tf_op jit(solution)/shard_map/dot_general | solution.py:76
  141.5 7.1 %collective-permute-done.8.refs_1_ = bf16[2,144,768]{2,1,0:T(8,128)(2,1)S(1)} collective-permute-done((bf16[2,144,768]{2,1,0:T(8,128)(2,1)S(1)}, bf16[2,144,768]{2,1,0:T(8,128)(2,1)S(1)}, u32[]{:S(2)}, u32[]{:S(2)}) %collective-permute-start.8) | collective-permute-done | bytes 442400 | tf_op jit(solution)/shard_map/ppermute | solution.py:742
  149.2 16.7 %gates.1 = (bf16[2,256,3072]{2,1,0:T(8,128)(2,1)S(1)}, bf16[2,256,3072]{2,1,0:T(8,128)(2,1)S(1)}, f32[2,256,3072]{2,1,0:T(8,128)}, bf16[4,2,144,768]{3,2,1,0:T(8,128)(2,1)S(1)}, f32[1,3072]{1,0:T(1,128)S(1)}) custom-call(s32[1]{0:T(128)} %bitcast.1.member, f32[2,256,3072]{2,1,0:T(8,128)} %inside.3.y_ref, f32[2,256,3072]{2,1,0:T(8,128)} %bitcast.244, ...), custom_call_target="tpu_custom_call" | custom-call | bytes 47600000 | tf_op jit(solution)/shard_map/gates/pallas_call | solution.py:1092
  166.0 4.6 convolution_convert_fusion.2
  170.6 4.4 convolution_convert_fusion
  180.8 7.0 %convert_add_fusion.1 = f32[3072,768]{1,0:T(8,128)} fusion(bf16[3072,768]{1,0:T(8,128)(2,1)} %collective-permute-done.15, bf16[512,3072]{1,0:T(8,128)(2,1)S(1)} %bitcast.231, bf16[512,768]{1,0:T(8,128)(2,1)} %get-tuple-element.107), kind=kOutput, calls=%fused_computation.1 | convolution fusion | flops 2420637696 | bytes 18087936 | tf_op jit(solution)/shard_map/dot_general | solution.py:86
  187.9 4.7 convert_add_fusion.2
  192.5 7.1 %collective-permute-done.13.refs_3_ = bf16[2,144,768]{2,1,0:T(8,128)(2,1)S(1)} collective-permute-done((bf16[2,144,768]{2,1,0:T(8,128)(2,1)S(1)}, bf16[2,144,768]{2,1,0:T(8,128)(2,1)S(1)}, u32[]{:S(2)}, u32[]{:S(2)}) %collective-permute-start.13) | collective-permute-done | bytes 442400 | tf_op jit(solution)/shard_map/ppermute | solution.py:742
  203.6 4.1 fusion.32
  210.4 18.7 %inside_back.2 = (f32[2,256,3072]{2,1,0:T(8,128)}, bf16[2,256,3072]{2,1,0:T(8,128)(2,1)}, f32[2,256,256]{2,1,0:T(8,128)}, f32[4,2,256,128]{3,2,1,0:T(8,128)}, f32[2,256,128]{2,1,0:T(8,128)}) custom-call(f32[2,256,3072]{2,1,0:T(8,128)} %copy-done.1, f32[2,256,3072]{2,1,0:T(8,128)} %get-tuple-element.138.grad_ref, f32[2,256,3072]{2,1,0:T(8,128)} %inside.3.y_ref, ...), custom_call_target="tpu_custom_call" | custom-call | bytes 57800000 | tf_op jit(solution)/shard_map/inside_back/pallas_call | solution.py:1206
  232.0 18.9 %inside_back.3 = (f32[2,256,3072]{2,1,0:T(8,128)}, bf16[2,256,3072]{2,1,0:T(8,128)(2,1)}, f32[2,256,256]{2,1,0:T(8,128)}, f32[4,2,256,128]{3,2,1,0:T(8,128)}, f32[2,256,128]{2,1,0:T(8,128)}) custom-call(f32[2,256,3072]{2,1,0:T(8,128)} %copy-done.1, ...), custom_call_target="tpu_custom_call", output_to_operand_aliasing={{0}: (15, {}), {1}: (16, {}), {3}: (17, {})} | custom-call | bytes 57800000 | tf_op jit(solution)/shard_map/inside_back/pallas_call | solution.py:1206
  250.9 10.6 %collective-permute-done.17.refs_5_ = bf16[2,144,768]{2,1,0:T(8,128)(2,1)} collective-permute-done((bf16[2,144,768]{2,1,0:T(8,128)(2,1)}, bf16[2,144,768]{2,1,0:T(8,128)(2,1)}, u32[]{:S(2)}, u32[]{:S(2)}) %collective-permute-start.17) | collective-permute-done | bytes 442400 | tf_op jit(solution)/shard_map/ppermute | solution.py:768
  270.1 3.7 bitcast_add_fusion.1
  273.9 5.3 bitcast_add_fusion
  279.2 8.4 %collective-permute-done.20.refs_3_ = bf16[2,144,768]{2,1,0:T(8,128)(2,1)S(1)} collective-permute-done((bf16[2,144,768]{2,1,0:T(8,128)(2,1)S(1)}, bf16[2,144,768]{2,1,0:T(8,128)(2,1)S(1)}, u32[]{:S(2)}, u32[]{:S(2)}) %collective-permute-start.20) | collective-permute-done | bytes 442400 | tf_op jit(solution)/shard_map/ppermute | solution.py:742
  294.7 13.9 %channels.1 = (bf16[2,256,3072]{2,1,0:T(8,128)(2,1)}, f32[2,16,3072]{2,1,0:T(8,128)}, bf16[2,16,3072]{2,1,0:T(8,128)(2,1)}, bf16[2,256,3072]{2,1,0:T(8,128)(2,1)...) custom-call(f32[2,256,3072]{2,1,0:T(8,128)} %get-tuple-element.139.known_ref, ...), custom_call_target="tpu_custom_call" | custom-call | bytes 40800000 | tf_op jit(solution)/shard_map/channels/pallas_call | solution.py:1263
  308.6 6.4 last.1
  316.8 2.2 slice.237
  322.5 2.4 bitcast_add_fusion.5
  328.3 3.3 convolution_convert_fusion.1
  332.8 3.3 collective-permute-start.31
  336.1 4.5 collective-permute-done.34
  342.4 2.8 convert_add_fusion
  345.2 2.8 fusion.83
  348.0 2.2 copy-done.56
  351.6 3.1 collective-permute-start.37
  355.8 2.2 fusion.46
  359.2 3.5 collective-permute-done.31
  365.4 3.3 collective-permute-start.32
  368.7 16.7 %collective-permute-done.37 = bf16[2,2,2,224,384]{4,3,0,1,2:T(8,128)(2,1)} collective-permute-done((bf16[2,2,2,224,384]{4,3,0,1,2:T(8,128)(2,1)}, bf16[2,2,2,224,384]{4,3,0,1,2:T(8,128)(2,1)}, u32[]{:S(2)}, u32[]{:S(2)}) %collective-permute-start.37) | collective-permute-done | bytes 1376288 | tf_op jit(solution)/shard_map/ppermute | solution.py:835
  397.1 10.2 %collective-permute-done.38 = bf16[2,2,224,384]{3,2,0,1:T(8,128)(2,1)} collective-permute-done((bf16[2,2,224,384]{3,2,0,1:T(8,128)(2,1)}, bf16[2,2,224,384]{3,2,0,1:T(8,128)(2,1)}, u32[]{:S(2)}, u32[]{:S(2)}) %collective-permute-start.38) | collective-permute-done | bytes 688160 | tf_op jit(solution)/shard_map/ppermute | solution.py:835
  408.5 2.4 collective-permute-done.36
  417.0 14.2 %collective-permute-done.39 = bf16[2,224,768]{2,1,0:T(8,128)(2,1)S(1)} collective-permute-done((bf16[2,224,768]{2,1,0:T(8,128)(2,1)S(1)}, bf16[2,224,768]{2,1,0:T(8,128)(2,1)S(1)}, u32[]{:S(2)}, u32[]{:S(2)}) %collective-permute-start.39) | collective-permute-done | bytes 688160 | tf_op jit(solution)/shard_map/ppermute | solution.py:835
  431.4 3.9 collective-permute-start.40
  435.3 13.6 %collective-permute-done.40 = bf16[224,768]{1,0:T(8,128)(2,1)S(1)} collective-permute-done((bf16[224,768]{1,0:T(8,128)(2,1)S(1)}, bf16[224,768]{1,0:T(8,128)(2,1)S(1)}, u32[]{:S(2)}, u32[]{:S(2)}) %collective-permute-start.40) | collective-permute-done | bytes 344096 | tf_op jit(solution)/shard_map/ppermute | solution.py:835
  451.8 10.6 %sums.1 = f32[8,3072]{1,0:T(8,128)} custom-call(f32[2,272,3376]{2,1,0:T(8,128)} %bitcast.229, bf16[2,256,3072]{2,1,0:T(8,128)(2,1)} %get-tuple-element.175.grad_mix_ref, f32[2,256,3072]{2,1,0:T(8,128)} %get-tuple-element.138.grad_ref, f32[2,256,3072]{2,1,0:T(8,128)} %copy-done.1), custom_call_target="tpu_custom_call" | custom-call | bytes 34000000 | tf_op jit(solution)/shard_map/sums/pallas_call | solution.py:1459
  464.4 5.1 fusion.7
  469.6 5.0 fusion.2
  476.3 5.1 fusion.4
  481.4 5.0 fusion
  491.9 6.9 %collective-permute-done.27 = f32[169,128]{1,0:T(8,128)S(1)} collective-permute-done((f32[169,128]{1,0:T(8,128)S(1)}, f32[169,128]{1,0:T(8,128)S(1)}, u32[]{:S(2)}, u32[]{:S(2)}) %collective-permute-start.27) | collective-permute-done | bytes 86560 | tf_op jit(solution)/shard_map/ppermute | solution.py:851
  500.1 6.2 fusion.30
  506.6 9.1 %collective-permute-done.29 = f32[169,128]{1,0:T(8,128)S(1)} collective-permute-done((f32[169,128]{1,0:T(8,128)S(1)}, f32[169,128]{1,0:T(8,128)S(1)}, u32[]{:S(2)}, u32[]{:S(2)}) %collective-permute-start.29) | collective-permute-done | bytes 86560 | tf_op jit(solution)/shard_map/ppermute | solution.py:851
  516.6 2.1 fusion.23
  518.8 6.3 collective-permute-done.30
  528.6 99.9 %all-gather.5.cloned.1.call-done.gate_rows.last_rows.out_rows = bf16[16,608,768]{2,1,0:T(8,128)(2,1)} async-done(((bf16[1,608,768]{2,1,0:T(8,128)(2,1)}), bf16[16,608,768]{2,1,0:T(8,128)(2,1)}) %all-gather.5.cloned.1.call-update) | async-done | bytes 14942224 | tf_op jit(solution)/shard_map/all_gather | solution.py:1434
  628.5 16.4 %finish.1 = (f32[6448,768]{1,0:T(8,128)}, f32[1536,1536]{1,0:T(8,128)}) custom-call(bf16[16,608,768]{2,1,0:T(8,128)(2,1)} %all-gather.5.cloned.1.call-done.gate_rows.last_rows.out_rows, bf16[16,608,768]{2,1,0:T(8,128)(2,1)} %all-gather.5.cloned.1.call-done.gate_rows.last_rows.out_rows, ...), custom_call_target="tpu_custom_call" | custom-call | bytes 47600000 | tf_op jit(solution)/shard_map/finish/pallas_call | solution.py:1496
  (396 shorter events, 111.3 us)
Async XLA Ops:
  7.2 91.5 %all-gather.3.cloned.1.call-start = ((), (), s32[]{:S(2)}) async-start(), calls=%async_computation | async-start | bytes 14155776 | tf_op jit(solution)/shard_map/all_gather | solution.py:1026
  12.5 16.8 %collective-permute-start.1 = (bf16[3376,768]{1,0:T(8,128)(2,1)}, bf16[3376,768]{1,0:T(8,128)(2,1)}, u32[]{:S(2)}, u32[]{:S(2)}) collective-permute-start(bf16[3376,768]{1,0:T(8,128)(2,1)} %slice.284), channel_id=1, source_target_pairs={{0,1},{1,0},{2,3},{3,2},{4,5},{5,4},{6,7},{7,6},{8,9},{9,8},{10,11... | collective-permute-start | bytes 15556616 | tf_op jit(solution)/shard_map/ppermute | solution.py:902
  12.9 7.8 %collective-permute-start = (bf16[2,16,1536]{2,1,0:T(8,128)(2,1)S(1)}, bf16[2,16,1536]{2,1,0:T(8,128)(2,1)S(1)}, u32[]{:S(2)}, u32[]{:S(2)}) collective-permute-start(bf16[2,16,1536]{2,1,0:T(8,128)(2,1)S(1)} %slice.283), channel_id=1, source_target_pairs={{0,2},{2,4},{4,6},{6,8},{8,10},{10,12},{12,14},{14,16},{16,18},{18... | collective-permute-start | bytes 294920 | tf_op jit(solution)/shard_map/ppermute | solution.py:905
  17.4 22.7 %copy-start.40 = (f32[1,3328]{1,0:T(1,128)}, f32[1,3328]{1,0:T(1,128)S(1)}, u32[]{:S(2)}) copy-start(f32[1,3328]{1,0:T(1,128)S(1)} %broadcast_in_dim.26.bias) | copy-start | bytes 39940
  20.7 19.5 %copy-start.39 = (f32[128,1]{1,0:T(8,128)}, f32[128,1]{1,0:T(8,128)S(1)}, u32[]{:S(2)}) copy-start(f32[128,1]{1,0:T(8,128)S(1)} %copy.42.column) | copy-start | bytes 1540
  40.1 109.0 %copy-start.5 = (f32[2,256,256]{2,1,0:T(8,128)}, f32[2,256,256]{2,1,0:T(8,128)S(1)}, u32[]{:S(2)}) copy-start(f32[2,256,256]{2,1,0:T(8,128)S(1)} %get-tuple-element.117.bc_ref) | copy-start | bytes 1572868
  40.1 109.0 %copy-start.38 = (f32[2,256,128]{2,1,0:T(8,128)}, f32[2,256,128]{2,1,0:T(8,128)S(1)}, u32[]{:S(2)}) copy-start(f32[2,256,128]{2,1,0:T(8,128)S(1)} %get-tuple-element.118.sum_ref) | copy-start | bytes 786436
  53.8 574.7 %all-gather.5.cloned.1.call-start = ((), (), s32[]{:S(2)}) async-start(), calls=%async_computation.1 | async-start | bytes 15876096 | tf_op jit(solution)/shard_map/all_gather | solution.py:1434
  64.1 66.8 %collective-permute-start.7 = (bf16[6448,768]{1,0:T(8,128)(2,1)}, bf16[6448,768]{1,0:T(8,128)(2,1)}, u32[]{:S(2)}, u32[]{:S(2)}) collective-permute-start(bf16[6448,768]{1,0:T(8,128)(2,1)} %bitcast.270), channel_id=1, source_target_pairs={{0,1},{1,0},{2,3},{3,2},{4,5},{5,4},{6,7},{7,6},{8,9},{9,8},{10,11... | collective-permute-start | bytes 29712392 | tf_op jit(solution)/shard_map/ppermute | solution.py:1039
  70.0 24.0 %collective-permute-start.2 = (bf16[2,144,768]{2,1,0:T(8,128)(2,1)}, bf16[2,144,768]{2,1,0:T(8,128)(2,1)S(1)}, u32[]{:S(2)}, u32[]{:S(2)}) collective-permute-start(bf16[2,144,768]{2,1,0:T(8,128)(2,1)} %get-tuple-element.198), channel_id=1, source_target_pairs={{0,2},{2,0},{4,6},{6,4},{8,10},{10,8},{12,14},{14,12},{16,18},{18,... | collective-permute-start | bytes 1327112 | tf_op jit(solution)/shard_map/ppermute | solution.py:742
  71.5 22.5 %collective-permute-start.3 = (bf16[2,144,768]{2,1,0:T(8,128)(2,1)}, bf16[2,144,768]{2,1,0:T(8,128)(2,1)S(1)}, u32[]{:S(2)}, u32[]{:S(2)}) collective-permute-start(bf16[2,144,768]{2,1,0:T(8,128)(2,1)} %get-tuple-element.197), channel_id=1, source_target_pairs={{0,4},{2,6},{4,0},{6,2},{8,12},{10,14},{12,8},{14,10},{16,20},{18,... | collective-permute-start | bytes 1327112 | tf_op jit(solution)/shard_map/ppermute | solution.py:742
  73.0 21.0 %collective-permute-start.4 = (bf16[2,144,768]{2,1,0:T(8,128)(2,1)}, bf16[2,144,768]{2,1,0:T(8,128)(2,1)S(1)}, u32[]{:S(2)}, u32[]{:S(2)}) collective-permute-start(bf16[2,144,768]{2,1,0:T(8,128)(2,1)} %get-tuple-element.196), channel_id=1, source_target_pairs={{0,6},{2,4},{4,2},{6,0},{8,14},{10,12},{12,10},{14,8},{16,22},{18,... | collective-permute-start | bytes 1327112 | tf_op jit(solution)/shard_map/ppermute | solution.py:742
  95.2 13.3 %collective-permute-start.5 = (bf16[2,144,768]{2,1,0:T(8,128)(2,1)S(1)}, bf16[2,144,768]{2,1,0:T(8,128)(2,1)S(1)}, u32[]{:S(2)}, u32[]{:S(2)}) collective-permute-start(bf16[2,144,768]{2,1,0:T(8,128)(2,1)S(1)} %plane.2.refs_0_), channel_id=1, source_target_pairs={{0,8},{2,10},{4,12},{6,14},{8,16},{10,18},{12,20},{14,22},{16,24},... | collective-permute-start | bytes 1327112 | tf_op jit(solution)/shard_map/ppermute | solution.py:768
  110.6 14.8 %collective-permute-start.6 = (bf16[2,144,768]{2,1,0:T(8,128)(2,1)S(1)}, bf16[2,144,768]{2,1,0:T(8,128)(2,1)}, u32[]{:S(2)}, u32[]{:S(2)}) collective-permute-start(bf16[2,144,768]{2,1,0:T(8,128)(2,1)S(1)} %link.2), channel_id=1, source_target_pairs={{0,16},{2,18},{4,20},{6,22},{8,24},{10,26},{12,28},{14,30},{1,17},... | collective-permute-start | bytes 1327112 | tf_op jit(solution)/shard_map/ppermute | solution.py:768
  127.4 14.1 %collective-permute-start.10 = (bf16[2,144,768]{2,1,0:T(8,128)(2,1)S(1)}, bf16[2,144,768]{2,1,0:T(8,128)(2,1)S(1)}, u32[]{:S(2)}, u32[]{:S(2)}) collective-permute-start(bf16[2,144,768]{2,1,0:T(8,128)(2,1)S(1)} %get-tuple-element.114), channel_id=1, source_target_pairs={{0,6},{2,4},{4,2},{6,0},{8,14},{10,12},{12,10},{14,8},{16,22},{18,... | collective-permute-start | bytes 1327112 | tf_op jit(solution)/shard_map/ppermute | solution.py:742
  128.8 19.8 %collective-permute-start.8 = (bf16[2,144,768]{2,1,0:T(8,128)(2,1)S(1)}, bf16[2,144,768]{2,1,0:T(8,128)(2,1)S(1)}, u32[]{:S(2)}, u32[]{:S(2)}) collective-permute-start(bf16[2,144,768]{2,1,0:T(8,128)(2,1)S(1)} %get-tuple-element.120), channel_id=1, source_target_pairs={{0,2},{2,0},{4,6},{6,4},{8,10},{10,8},{12,14},{14,12},{16,18},{18,... | collective-permute-start | bytes 1327112 | tf_op jit(solution)/shard_map/ppermute | solution.py:742
  130.2 18.9 %copy-start.43 = (f32[3072]{0:T(1024)S(1)}, f32[3072]{0:T(1024)}, u32[]{:S(2)}) copy-start(f32[3072]{0:T(1024)} %param.19) | copy-start | bytes 36868
  130.3 18.4 %collective-permute-start.9 = (bf16[2,144,768]{2,1,0:T(8,128)(2,1)S(1)}, bf16[2,144,768]{2,1,0:T(8,128)(2,1)S(1)}, u32[]{:S(2)}, u32[]{:S(2)}) collective-permute-start(bf16[2,144,768]{2,1,0:T(8,128)(2,1)S(1)} %get-tuple-element.121), channel_id=1, source_target_pairs={{0,4},{2,6},{4,0},{6,2},{8,12},{10,14},{12,8},{14,10},{16,20},{18,... | collective-permute-start | bytes 1327112 | tf_op jit(solution)/shard_map/ppermute | solution.py:742
  149.1 16.8 %copy-start.4 = (bf16[2,128,3072]{2,1,0:T(8,128)(2,1)}, bf16[2,128,3072]{2,1,0:T(8,128)(2,1)S(1)}, u32[]{:S(2)}) copy-start(bf16[2,128,3072]{2,1,0:T(8,128)(2,1)S(1)} %get-tuple-element.123.entering) | copy-start | bytes 4718596
  149.1 16.8 %copy-start.10 = (f32[2,8,3072]{2,1,0:T(8,128)}, f32[2,8,3072]{2,1,0:T(8,128)S(1)}, u32[]{:S(2)}) copy-start(f32[2,8,3072]{2,1,0:T(8,128)S(1)} %get-tuple-element.124.along) | copy-start | bytes 589828
  149.2 16.8 %copy-start.74 = (bf16[512,768]{1,0:T(8,128)(2,1)S(1)}, bf16[512,768]{1,0:T(8,128)(2,1)}, u32[]{:S(2)}) copy-start(bf16[512,768]{1,0:T(8,128)(2,1)} %get-tuple-element.115) | copy-start | bytes 2359300
  170.6 10.2 %collective-permute-start.15 = (bf16[3072,768]{1,0:T(8,128)(2,1)}, bf16[3072,768]{1,0:T(8,128)(2,1)}, u32[]{:S(2)}, u32[]{:S(2)}) collective-permute-start(bf16[3072,768]{1,0:T(8,128)(2,1)} %convolution_convert_fusion.2), channel_id=1, source_target_pairs={{0,1},{1,0},{2,3},{3,2},{4,5},{5,4},{6,7},{7,6},{8,9},{9,8},{10,11... | collective-permute-start | bytes 14155784 | tf_op jit(solution)/shard_map/ppermute | solution.py:1150
  175.0 12.9 %collective-permute-start.14 = (bf16[1536,1536]{1,0:T(8,128)(2,1)}, bf16[1536,1536]{1,0:T(8,128)(2,1)}, u32[]{:S(2)}, u32[]{:S(2)}) collective-permute-start(bf16[1536,1536]{1,0:T(8,128)(2,1)} %convolution_convert_fusion), channel_id=1, source_target_pairs={{0,1},{1,0},{2,3},{3,2},{4,5},{5,4},{6,7},{7,6},{8,9},{9,8},{10,11... | collective-permute-start | bytes 14155784 | tf_op jit(solution)/shard_map/ppermute | solution.py:1150
  177.2 24.1 %copy-start.8 = (bf16[2,144,768]{2,1,0:T(8,128)(2,1)}, bf16[2,144,768]{2,1,0:T(8,128)(2,1)S(1)}, u32[]{:S(2)}) copy-start(bf16[2,144,768]{2,1,0:T(8,128)(2,1)S(1)} %get-tuple-element.195.refs_0_) | copy-start | bytes 1327108
  177.3 24.1 %collective-permute-start.11 = (bf16[2,144,768]{2,1,0:T(8,128)(2,1)S(1)}, bf16[2,144,768]{2,1,0:T(8,128)(2,1)S(1)}, u32[]{:S(2)}, u32[]{:S(2)}) collective-permute-start(bf16[2,144,768]{2,1,0:T(8,128)(2,1)S(1)} %get-tuple-element.194), channel_id=1, source_target_pairs={{0,2},{2,0},{4,6},{6,4},{8,10},{10,8},{12,14},{14,12},{16,18},{18,... | collective-permute-start | bytes 1327112 | tf_op jit(solution)/shard_map/ppermute | solution.py:742
  178.6 22.8 %collective-permute-start.12 = (bf16[2,144,768]{2,1,0:T(8,128)(2,1)S(1)}, bf16[2,144,768]{2,1,0:T(8,128)(2,1)S(1)}, u32[]{:S(2)}, u32[]{:S(2)}) collective-permute-start(bf16[2,144,768]{2,1,0:T(8,128)(2,1)S(1)} %get-tuple-element.193), channel_id=1, source_target_pairs={{0,4},{2,6},{4,0},{6,2},{8,12},{10,14},{12,8},{14,10},{16,20},{18,... | collective-permute-start | bytes 1327112 | tf_op jit(solution)/shard_map/ppermute | solution.py:742
  179.2 20.5 %collective-permute-start.13 = (bf16[2,144,768]{2,1,0:T(8,128)(2,1)S(1)}, bf16[2,144,768]{2,1,0:T(8,128)(2,1)S(1)}, u32[]{:S(2)}, u32[]{:S(2)}) collective-permute-start(bf16[2,144,768]{2,1,0:T(8,128)(2,1)S(1)} %get-tuple-element.192), channel_id=1, source_target_pairs={{0,6},{2,4},{4,2},{6,0},{8,14},{10,12},{12,10},{14,8},{16,22},{18,... | collective-permute-start | bytes 1327112 | tf_op jit(solution)/shard_map/ppermute | solution.py:742
  203.1 67.0 %collective-permute-start.21 = (bf16[2,2,2,96,1536]{4,3,2,1,0:T(8,128)(2,1)}, bf16[2,2,2,96,1536]{4,3,2,1,0:T(8,128)(2,1)}, u32[]{:S(2)}, u32[]{:S(2)}) collective-permute-start(bf16[2,2,2,96,1536]{4,3,2,1,0:T(8,128)(2,1)} %fusion.31), channel_id=1, source_target_pairs={{0,2},{2,0},{4,6},{6,4},{8,10},{10,8},{12,14},{14,12},{16,18},{18,... | collective-permute-start | bytes 7077896 | tf_op jit(solution)/shard_map/ppermute | solution.py:835
  207.7 66.2 %collective-permute-start.22 = (bf16[2,2,2,192,768]{4,3,0,1,2:T(8,128)(2,1)}, bf16[2,2,2,192,768]{4,3,0,1,2:T(8,128)(2,1)}, u32[]{:S(2)}, u32[]{:S(2)}) collective-permute-start(bf16[2,2,2,192,768]{4,3,0,1,2:T(8,128)(2,1)} %fusion.32), channel_id=1, source_target_pairs={{0,4},{2,6},{4,0},{6,2},{8,12},{10,14},{12,8},{14,10},{16,20},{18,... | collective-permute-start | bytes 7077896 | tf_op jit(solution)/shard_map/ppermute | solution.py:835
  209.1 20.5 %collective-permute-start.16 = (bf16[2,144,768]{2,1,0:T(8,128)(2,1)S(1)}, bf16[2,144,768]{2,1,0:T(8,128)(2,1)S(1)}, u32[]{:S(2)}, u32[]{:S(2)}) collective-permute-start(bf16[2,144,768]{2,1,0:T(8,128)(2,1)S(1)} %copy-done.19), channel_id=1, source_target_pairs={{8,0},{10,2},{12,4},{14,6},{16,8},{18,10},{20,12},{22,14},{24,16},... | collective-permute-start | bytes 1327112 | tf_op jit(solution)/shard_map/ppermute | solution.py:768
  230.6 31.0 %collective-permute-start.17 = (bf16[2,144,768]{2,1,0:T(8,128)(2,1)}, bf16[2,144,768]{2,1,0:T(8,128)(2,1)}, u32[]{:S(2)}, u32[]{:S(2)}) collective-permute-start(bf16[2,144,768]{2,1,0:T(8,128)(2,1)} %link.3), channel_id=1, source_target_pairs={{16,0},{18,2},{20,4},{22,6},{24,8},{26,10},{28,12},{30,14},{17,1},... | collective-permute-start | bytes 1327112 | tf_op jit(solution)/shard_map/ppermute | solution.py:768
  232.0 29.5 %copy-start.9 = (bf16[2,144,768]{2,1,0:T(8,128)(2,1)S(1)}, bf16[2,144,768]{2,1,0:T(8,128)(2,1)}, u32[]{:S(2)}) copy-start(bf16[2,144,768]{2,1,0:T(8,128)(2,1)} %copy-done.8) | copy-start | bytes 1327108
  232.0 29.5 %copy-start.21 = (bf16[2,144,768]{2,1,0:T(8,128)(2,1)S(1)}, bf16[2,144,768]{2,1,0:T(8,128)(2,1)}, u32[]{:S(2)}) copy-start(bf16[2,144,768]{2,1,0:T(8,128)(2,1)} %copy-done.20) | copy-start | bytes 1327108
  266.5 21.0 %collective-permute-start.18 = (bf16[2,144,768]{2,1,0:T(8,128)(2,1)S(1)}, bf16[2,144,768]{2,1,0:T(8,128)(2,1)S(1)}, u32[]{:S(2)}, u32[]{:S(2)}) collective-permute-start(bf16[2,144,768]{2,1,0:T(8,128)(2,1)S(1)} %get-tuple-element.146), channel_id=1, source_target_pairs={{0,2},{2,0},{4,6},{6,4},{8,10},{10,8},{12,14},{14,12},{16,18},{18,... | collective-permute-start | bytes 1327112 | tf_op jit(solution)/shard_map/ppermute | solution.py:742
  268.0 19.7 %collective-permute-start.19 = (bf16[2,144,768]{2,1,0:T(8,128)(2,1)S(1)}, bf16[2,144,768]{2,1,0:T(8,128)(2,1)S(1)}, u32[]{:S(2)}, u32[]{:S(2)}) collective-permute-start(bf16[2,144,768]{2,1,0:T(8,128)(2,1)S(1)} %get-tuple-element.147), channel_id=1, source_target_pairs={{0,4},{2,6},{4,0},{6,2},{8,12},{10,14},{12,8},{14,10},{16,20},{18,... | collective-permute-start | bytes 1327112 | tf_op jit(solution)/shard_map/ppermute | solution.py:742
  269.4 18.1 %collective-permute-start.20 = (bf16[2,144,768]{2,1,0:T(8,128)(2,1)S(1)}, bf16[2,144,768]{2,1,0:T(8,128)(2,1)S(1)}, u32[]{:S(2)}, u32[]{:S(2)}) collective-permute-start(bf16[2,144,768]{2,1,0:T(8,128)(2,1)S(1)} %get-tuple-element.148), channel_id=1, source_target_pairs={{0,6},{2,4},{4,2},{6,0},{8,14},{10,12},{12,10},{14,8},{16,22},{18,... | collective-permute-start | bytes 1327112 | tf_op jit(solution)/shard_map/ppermute | solution.py:742
  292.7 26.4 %collective-permute-start.23 = (bf16[2,2,96,1536]{3,2,1,0:T(8,128)(2,1)}, bf16[2,2,96,1536]{3,2,1,0:T(8,128)(2,1)}, u32[]{:S(2)}, u32[]{:S(2)}) collective-permute-start(bf16[2,2,96,1536]{3,2,1,0:T(8,128)(2,1)} %fusion.44), channel_id=1, source_target_pairs={{0,4},{2,6},{4,0},{6,2},{8,12},{10,14},{12,8},{14,10},{16,20},{18,... | collective-permute-start | bytes 3538952 | tf_op jit(solution)/shard_map/ppermute | solution.py:835
  294.1 25.0 %collective-permute-start.24 = (bf16[2,2,192,768]{3,2,0,1:T(8,128)(2,1)}, bf16[2,2,192,768]{3,2,0,1:T(8,128)(2,1)}, u32[]{:S(2)}, u32[]{:S(2)}) collective-permute-start(bf16[2,2,192,768]{3,2,0,1:T(8,128)(2,1)} %fusion.45), channel_id=1, source_target_pairs={{0,2},{2,0},{4,6},{6,4},{8,10},{10,8},{12,14},{14,12},{16,18},{18,... | collective-permute-start | bytes 3538952 | tf_op jit(solution)/shard_map/ppermute | solution.py:835
  319.0 8.0 %collective-permute-start.25 = (bf16[2,16,3328]{2,1,0:T(8,128)(2,1)S(1)}, bf16[2,16,3328]{2,1,0:T(8,128)(2,1)S(1)}, u32[]{:S(2)}, u32[]{:S(2)}) collective-permute-start(bf16[2,16,3328]{2,1,0:T(8,128)(2,1)S(1)} %pad_maximum_fusion.12), channel_id=1, source_target_pairs={{2,0},{4,2},{6,4},{8,6},{10,8},{12,10},{14,12},{16,14},{18,16},{20... | collective-permute-start | bytes 638984 | tf_op jit(solution)/shard_map/ppermute | solution.py:1375
  331.6 10.8 %collective-permute-start.33 = (bf16[3072,768]{1,0:T(8,128)(2,1)S(1)}, bf16[3072,768]{1,0:T(8,128)(2,1)S(1)}, u32[]{:S(2)}, u32[]{:S(2)}) collective-permute-start(bf16[3072,768]{1,0:T(8,128)(2,1)S(1)} %convolution_convert_fusion.1), channel_id=1, source_target_pairs={{0,1},{1,0},{2,3},{3,2},{4,5},{5,4},{6,7},{7,6},{8,9},{9,8},{10,11... | collective-permute-start | bytes 14155784 | tf_op jit(solution)/shard_map/ppermute | solution.py:1150
  332.3 8.4 %collective-permute-start.34 = (bf16[512,768]{1,0:T(8,128)(2,1)S(1)}, bf16[512,768]{1,0:T(8,128)(2,1)S(1)}, u32[]{:S(2)}, u32[]{:S(2)}) collective-permute-start(bf16[512,768]{1,0:T(8,128)(2,1)S(1)} %convolution_convert_fusion.3), channel_id=1, source_target_pairs={{0,1},{1,0},{2,3},{3,2},{4,5},{5,4},{6,7},{7,6},{8,9},{9,8},{10,11... | collective-permute-start | bytes 2359304 | tf_op jit(solution)/shard_map/ppermute | solution.py:1150
  332.8 29.9 %collective-permute-start.31 = (bf16[2,384,768]{2,1,0:T(8,128)(2,1)}, bf16[2,384,768]{2,1,0:T(8,128)(2,1)}, u32[]{:S(2)}, u32[]{:S(2)}) collective-permute-start(bf16[2,384,768]{2,1,0:T(8,128)(2,1)} %pad_maximum_fusion.4), channel_id=1, source_target_pairs={{0,8},{2,10},{4,12},{6,14},{8,0},{10,2},{12,4},{14,6},{16,24},{18,... | collective-permute-start | bytes 3538952 | tf_op jit(solution)/shard_map/ppermute | solution.py:835
  351.6 33.9 %collective-permute-start.37 = (bf16[2,2,2,224,384]{4,3,0,1,2:T(8,128)(2,1)}, bf16[2,2,2,224,384]{4,3,0,1,2:T(8,128)(2,1)}, u32[]{:S(2)}, u32[]{:S(2)}) collective-permute-start(bf16[2,2,2,224,384]{4,3,0,1,2:T(8,128)(2,1)} %pad_maximum_fusion.3), channel_id=1, source_target_pairs={{0,4},{2,6},{4,0},{6,2},{8,12},{10,14},{12,8},{14,10},{16,20},{18,... | collective-permute-start | bytes 4128776 | tf_op jit(solution)/shard_map/ppermute | solution.py:835
  358.0 29.2 %slice-start.4 = ((s8[4718592]{0:T(1024)(128)(4,1)}), s8[4194304]{0:T(1024)(128)(4,1)S(1)}, s32[]{:S(2)}) async-start(s8[4718592]{0:T(1024)(128)(4,1)} %bitcast.256), calls=%async_computation.6 | async-start | bytes 8388608
  358.1 27.3 %copy-start.78 = (f32[512,384]{1,0:T(8,128)S(1)}, f32[512,384]{1,0:T(8,128)}, u32[]{:S(2)}) copy-start(f32[512,384]{1,0:T(8,128)} %copy-done.77) | copy-start | bytes 2359300
  358.2 29.0 %slice-start.5 = ((s8[4718592]{0:T(1024)(128)(4,1)}), s8[524288]{0:T(1024)(128)(4,1)S(1)}, s32[]{:S(2)}) async-start(s8[4718592]{0:T(1024)(128)(4,1)} %bitcast.256), calls=%async_computation.7 | async-start | bytes 1048576
  358.2 32.9 %collective-permute-start.35 = (bf16[2,2,2,224,384]{4,3,0,1,2:T(8,128)(2,1)S(1)}, bf16[2,2,2,224,384]{4,3,0,1,2:T(8,128)(2,1)S(1)}, u32[]{:S(2)}, u32[]{:S(2)}) collective-permute-start(bf16[2,2,2,224,384]{4,3,0,1,2:T(8,128)(2,1)S(1)} %pad_maximum_fusion.2), channel_id=1, source_target_pairs={{0,2},{2,0},{4,6},{6,4},{8,10},{10,8},{12,14},{14,12},{16,18},{18,... | collective-permute-start | bytes 4128776 | tf_op jit(solution)/shard_map/ppermute | solution.py:835
  364.3 24.7 %copy-start.72 = (f32[2,192,768]{2,1,0:T(8,128)}, f32[2,192,768]{2,1,0:T(8,128)S(1)}, u32[]{:S(2)}) copy-start(f32[2,192,768]{2,1,0:T(8,128)S(1)} %get-tuple-element.204) | copy-start | bytes 3538948
  364.3 24.7 %copy-start.73 = (f32[2,192,768]{2,1,0:T(8,128)}, f32[2,192,768]{2,1,0:T(8,128)S(1)}, u32[]{:S(2)}) copy-start(f32[2,192,768]{2,1,0:T(8,128)S(1)} %get-tuple-element.205) | copy-start | bytes 3538948
  365.4 30.1 %collective-permute-start.32 = (bf16[384,768]{1,0:T(8,128)(2,1)}, bf16[384,768]{1,0:T(8,128)(2,1)}, u32[]{:S(2)}, u32[]{:S(2)}) collective-permute-start(bf16[384,768]{1,0:T(8,128)(2,1)} %pad_maximum_fusion.9), channel_id=1, source_target_pairs={{0,16},{2,18},{4,20},{6,22},{8,24},{10,26},{12,28},{14,30},{16,0},... | collective-permute-start | bytes 1769480 | tf_op jit(solution)/shard_map/ppermute | solution.py:835
  390.1 17.3 %collective-permute-start.38 = (bf16[2,2,224,384]{3,2,0,1:T(8,128)(2,1)}, bf16[2,2,224,384]{3,2,0,1:T(8,128)(2,1)}, u32[]{:S(2)}, u32[]{:S(2)}) collective-permute-start(bf16[2,2,224,384]{3,2,0,1:T(8,128)(2,1)} %pad_maximum_fusion.7), channel_id=1, source_target_pairs={{0,2},{2,0},{4,6},{6,4},{8,10},{10,8},{12,14},{14,12},{16,18},{18,... | collective-permute-start | bytes 2064392 | tf_op jit(solution)/shard_map/ppermute | solution.py:835
  393.7 17.2 %collective-permute-start.36 = (bf16[2,2,224,384]{3,2,0,1:T(8,128)(2,1)}, bf16[2,2,224,384]{3,2,0,1:T(8,128)(2,1)}, u32[]{:S(2)}, u32[]{:S(2)}) collective-permute-start(bf16[2,2,224,384]{3,2,0,1:T(8,128)(2,1)} %pad_maximum_fusion.6), channel_id=1, source_target_pairs={{0,4},{2,6},{4,0},{6,2},{8,12},{10,14},{12,8},{14,10},{16,20},{18,... | collective-permute-start | bytes 2064392 | tf_op jit(solution)/shard_map/ppermute | solution.py:835
  415.1 16.0 %collective-permute-start.39 = (bf16[2,224,768]{2,1,0:T(8,128)(2,1)S(1)}, bf16[2,224,768]{2,1,0:T(8,128)(2,1)S(1)}, u32[]{:S(2)}, u32[]{:S(2)}) collective-permute-start(bf16[2,224,768]{2,1,0:T(8,128)(2,1)S(1)} %pad_maximum_fusion.8), channel_id=1, source_target_pairs={{0,8},{2,10},{4,12},{6,14},{8,0},{10,2},{12,4},{14,6},{16,24},{18,... | collective-permute-start | bytes 2064392 | tf_op jit(solution)/shard_map/ppermute | solution.py:835
  431.4 20.4 %copy-start.93 = (f32[8,256]{1,0:T(8,128)S(1)}, f32[8,256]{1,0:T(8,128)}, u32[]{:S(2)}) copy-start(f32[8,256]{1,0:T(8,128)} %get-tuple-element.176) | copy-start | bytes 24580
  431.4 17.4 %collective-permute-start.40 = (bf16[224,768]{1,0:T(8,128)(2,1)S(1)}, bf16[224,768]{1,0:T(8,128)(2,1)S(1)}, u32[]{:S(2)}, u32[]{:S(2)}) collective-permute-start(bf16[224,768]{1,0:T(8,128)(2,1)S(1)} %pad_maximum_fusion.11), channel_id=1, source_target_pairs={{0,16},{2,18},{4,20},{6,22},{8,24},{10,26},{12,28},{14,30},{16,0},... | collective-permute-start | bytes 1032200 | tf_op jit(solution)/shard_map/ppermute | solution.py:835
  476.2 23.8 %slice-start.6 = ((s8[9437184]{0:T(1024)(128)(4,1)}), s8[4194304]{0:T(1024)(128)(4,1)S(1)}, s32[]{:S(2)}) async-start(s8[9437184]{0:T(1024)(128)(4,1)} %bitcast.288), calls=%async_computation.8 | async-start | bytes 8388608
  476.3 23.8 %slice-start.7 = ((s8[9437184]{0:T(1024)(128)(4,1)}), s8[4194304]{0:T(1024)(128)(4,1)S(1)}, s32[]{:S(2)}) async-start(s8[9437184]{0:T(1024)(128)(4,1)} %bitcast.288), calls=%async_computation.9 | async-start | bytes 8388608
  481.4 18.7 %slice-start.8 = ((s8[9437184]{0:T(1024)(128)(4,1)}), s8[1048576]{0:T(1024)(128)(4,1)S(1)}, s32[]{:S(2)}) async-start(s8[9437184]{0:T(1024)(128)(4,1)} %bitcast.288), calls=%async_computation.10 | async-start | bytes 2097152
  490.2 1.4 collective-permute-start.26
  491.6 7.2 %collective-permute-start.27 = (f32[169,128]{1,0:T(8,128)S(1)}, f32[169,128]{1,0:T(8,128)S(1)}, u32[]{:S(2)}, u32[]{:S(2)}) collective-permute-start(f32[169,128]{1,0:T(8,128)S(1)} %bitcast_add_fusion.19), channel_id=1, source_target_pairs={{0,2},{2,0},{4,6},{6,4},{8,10},{10,8},{12,14},{14,12},{16,18},{18,... | collective-permute-start | bytes 259592 | tf_op jit(solution)/shard_map/ppermute | solution.py:851
  498.8 17.8 %copy-start.81 = (bf16[1,512,1536]{2,1,0:T(8,128)(2,1)S(1)}, bf16[1,512,1536]{2,1,0:T(8,128)(2,1)}, u32[]{:S(2)}) copy-start(bf16[1,512,1536]{2,1,0:T(8,128)(2,1)} %param.21) | copy-start | bytes 4718596
  498.8 7.4 %collective-permute-start.28 = (f32[169,128]{1,0:T(8,128)S(1)}, f32[169,128]{1,0:T(8,128)S(1)}, u32[]{:S(2)}, u32[]{:S(2)}) collective-permute-start(f32[169,128]{1,0:T(8,128)S(1)} %fusion.115), channel_id=1, source_target_pairs={{0,4},{2,6},{4,0},{6,2},{8,12},{10,14},{12,8},{14,10},{16,20},{18,... | collective-permute-start | bytes 259592 | tf_op jit(solution)/shard_map/ppermute | solution.py:851
  506.2 9.5 %collective-permute-start.29 = (f32[169,128]{1,0:T(8,128)S(1)}, f32[169,128]{1,0:T(8,128)S(1)}, u32[]{:S(2)}, u32[]{:S(2)}) collective-permute-start(f32[169,128]{1,0:T(8,128)S(1)} %add.290), channel_id=1, source_target_pairs={{0,8},{2,10},{4,12},{6,14},{8,0},{10,2},{12,4},{14,6},{16,24},{18,... | collective-permute-start | bytes 259592 | tf_op jit(solution)/shard_map/ppermute | solution.py:851
  515.7 9.3 %collective-permute-start.30 = (f32[169,128]{1,0:T(8,128)S(1)}, f32[169,128]{1,0:T(8,128)S(1)}, u32[]{:S(2)}, u32[]{:S(2)}) collective-permute-start(f32[169,128]{1,0:T(8,128)S(1)} %add.291), channel_id=1, source_target_pairs={{0,16},{2,18},{4,20},{6,22},{8,24},{10,26},{12,28},{14,30},{16,0},... | collective-permute-start | bytes 259592 | tf_op jit(solution)/shard_map/ppermute | solution.py:851
  (85 other events, 491.9 us)
Sparse Core Ops, SparseCore 0:
  54.0 32.4 all-gather.2
  450.1 178.3 all-gather.4

commit v5 on v4

--- a/solution.py
+++ b/solution.py
@@ -216,7 +216,7 @@
     weight,
     bias,
     small,
-    direction,
+    in_rows,
     bc_ref,
     bt_ref,
     scores_ref,
@@ -226,7 +226,21 @@
     step_q_ref,
     sum_q_ref,
     sum_t_ref,
+    direction,
+    column,
 ):
+    values = in_rows[...].astype(F32)
+    power = 2.0 * jnp.sum(values * values, axis=1, keepdims=True)
+    power = jnp.broadcast_to(power, (STATE, STATE)).T[0:1]
+    taps = weight[:, :STATE]
+    deviation = jnp.sqrt(power * jnp.sum(taps * taps, axis=0, keepdims=True))
+    guess = jnp.zeros((1, STATE), F32)
+    for point, share in ((-1.7320508, 1 / 6), (0.0, 2 / 3), (1.7320508, 1 / 6)):
+        level = bias[:, :STATE] + point * deviation
+        guess = guess + share * (level * jax.nn.sigmoid(level))
+    guess = guess * lax.rsqrt(jnp.sum(guess * guess, axis=1, keepdims=True) + 1e-20)
+    direction[...] = guess
+    column[...] = jnp.broadcast_to(guess, (STATE, STATE)).T[:, 0:1]
     row = lax.broadcasted_iota(jnp.int32, (256, 256), 0)
     col = lax.broadcasted_iota(jnp.int32, (256, 256), 1)
     lower = (row >= col).astype(F32)
@@ -258,7 +272,19 @@
 
 
 def state_kernel(
-    member, conv_input, weight, bias, step_q, sum_q, bt_ref, column, x_ref, payload_ref
+    member, conv_input, weight, bias, step_q, sum_q, bt_ref, column, x_ref, *payloads
+):
+    for by, payload_ref in enumerate(payloads[:QUARTERS]):
+
+        @pl.when(pl.program_id(0) == by)
+        def _(payload_ref=payload_ref):
+            state_of_quarter(
+                conv_input, weight, bias, step_q, sum_q, bt_ref, column, x_ref, payload_ref
+            )
+
+
+def state_of_quarter(
+    conv_input, weight, bias, step_q, sum_q, bt_ref, column, x_ref, payload_ref
 ):
     for seq in range(2):
         running = sum_q[0, seq]
@@ -272,8 +298,8 @@
             x_ref[seq, :, lanes] = x
             added = dot(bt_ref[seq], (x * pick(scale, tile)).astype(BF16))
             along = jnp.sum(added * column[...], axis=0, keepdims=True)
-            payload_ref[0, seq, :STATE, lanes] = (added - column[...] * along).astype(BF16)
-            payload_ref[0, seq, STATE:, lanes] = edge_rows(pick(whole, tile), along)
+            payload_ref[seq, :STATE, lanes] = (added - column[...] * along).astype(BF16)
+            payload_ref[seq, STATE:, lanes] = edge_rows(pick(whole, tile), along)
 
 
 def intra_kernel(x_ref, step_q, sum_q, sum_t, scores, skip, *refs):
@@ -324,7 +350,10 @@
     out_ref,
     grad_z_ref,
     grad_scan_ref,
-    payload_ref,
+    payload_0,
+    payload_1,
+    payload_2,
+    payload_3,
     gain_grad_ref,
     scanned_ref,
     gated_ref,
@@ -400,8 +429,14 @@
             lanes = slice(TILE * tile, TILE * tile + TILE)
             place = slice(TILE * (tile % Q_TILES), TILE * (tile % Q_TILES) + TILE)
             slot = member[0] ^ (tile // Q_TILES)
-            payload_ref[slot, seq, :STATE, place] = state_ref[:, lanes].astype(BF16)
-            payload_ref[slot, seq, STATE:, place] = edge_rows(pick(whole, tile), zero)
+            state = state_ref[:, lanes].astype(BF16)
+            edge = edge_rows(pick(whole, tile), zero)
+            for by, payload_ref in enumerate((payload_0, payload_1, payload_2, payload_3)):
+
+                @pl.when(slot == by)
+                def _(payload_ref=payload_ref, state=state, edge=edge, place=place):
+                    payload_ref[seq, :STATE, place] = state
+                    payload_ref[seq, STATE:, place] = edge
 
 
 def intra_back_kernel(
@@ -748,7 +783,7 @@
     message = shape(MESSAGE, BF16)
     block = whole_block(MESSAGE)
     members = [payload[0]] + [swap(payload[by], by) for by in range(1, QUARTERS)]
-    members[-1] = meanwhile(payload, members[-1])
+    members[-1] = meanwhile(payload[-1], members[-1])
     total = pl.pallas_call(
         functools.partial(plane_kernel, reverse),
         grid=(1,),
@@ -910,18 +945,6 @@
     rescale = lax.rsqrt(jnp.mean(rows * rows, axis=-1, keepdims=True) + EPSILON)
     normed_ext = (rows * rescale * norm_gain).astype(BF16)
 
-    rows_of_writes = rows_of[2 * INNER : 2 * INNER + STATE].astype(F32)
-    power = 2.0 * jnp.sum(rows_of_writes * rows_of_writes, axis=1)
-    deviation = jnp.sqrt(
-        power * jnp.sum(jnp.square(conv_weight[:, INNER : INNER + STATE]), axis=0)
-    )
-    guess = jnp.zeros((STATE,), F32)
-    for point, share_of in ((-1.7320508, 1 / 6), (0.0, 2 / 3), (1.7320508, 1 / 6)):
-        guess = guess + share_of * jax.nn.silu(
-            conv_bias[INNER : INNER + STATE] + point * deviation
-        )
-    direction = guess * lax.rsqrt(jnp.sum(guess * guess) + 1e-20)
-    row_direction, column_direction = direction[None], direction[:, None]
     member = (lax.axis_index("seq") % QUARTERS).astype(jnp.int32).reshape(1)
 
     def mine(array, axis):
@@ -948,7 +971,7 @@
     gain_row = gate_gain[None]
     skip_row = jnp.repeat(skip_gain, HEAD_DIM)[None]
 
-    own_ext = tie(own_ext, row_direction, column_direction, small, bias_row, skip_row)
+    own_ext = tie(own_ext, small, bias_row, skip_row)
     conv_input = (dot_last(own_ext, conv_rows) + dot_last(other_ext, conv_rows_other)).reshape(
         2, half + EDGE, CONV_CH + HEADS
     )
@@ -957,7 +980,19 @@
     last_taps = fixed_block((CONV, 256), (0, INNER // 256))
     last_bias = fixed_block((1, 256), (0, INNER // 256))
     per_quarter = (QUARTERS, 2, half, SIDE)
-    bc, bt, scores, scores_t, step, running, step_q, sum_q, sum_t = pl.pallas_call(
+    (
+        bc,
+        bt,
+        scores,
+        scores_t,
+        step,
+        running,
+        step_q,
+        sum_q,
+        sum_t,
+        row_direction,
+        column_direction,
+    ) = pl.pallas_call(
         step_kernel,
         grid=(1,),
         in_specs=[
@@ -965,7 +1000,7 @@
             last_taps,
             last_bias,
             whole_block((8, TILE)),
-            whole_block((1, STATE)),
+            fixed_block((STATE, share), (2 * INNER // STATE, 0)),
         ],
         out_specs=[
             whole_block((2, half, 256)),
@@ -977,6 +1012,8 @@
             whole_block(per_quarter),
             whole_block(per_quarter),
             whole_block((QUARTERS, 2, EDGE, half)),
+            whole_block((1, STATE)),
+            whole_block((STATE, 1)),
         ],
         out_shape=[
             shape((2, half, 256)),
@@ -988,11 +1025,13 @@
             shape(per_quarter),
             shape(per_quarter),
             shape((QUARTERS, 2, EDGE, half)),
+            shape((1, STATE)),
+            shape((STATE, 1)),
         ],
         compiler_params=params(20),
         cost_estimate=cost(4),
         name="steps",
-    )(conv_input, conv_weight, bias_row, small, row_direction)
+    )(conv_input, conv_weight, bias_row, small, rows_of)
 
     columns = lane_block((2, half + EDGE))
     taps_block = lane_block((CONV,))
@@ -1000,7 +1039,7 @@
     heads_block = quarter_block((2, half, SIDE))
     line_block = quarter_block((2, EDGE, half))
     tokens_block = lane_block((2, half))
-    x, payload = pl.pallas_call(
+    x, *payload = pl.pallas_call(
         state_kernel,
         grid_spec=pltpu.PrefetchScalarGridSpec(
             num_scalar_prefetch=1,
@@ -1014,16 +1053,16 @@
                 whole_block((2, STATE, half)),
                 whole_block((STATE, 1)),
             ],
-            out_specs=[own_lanes((2, half)), quarter_block(MESSAGE)],
+            out_specs=[own_lanes((2, half))] + [whole_block(MESSAGE)] * QUARTERS,
         ),
-        out_shape=[shape((2, half, INNER)), shape((QUARTERS,) + MESSAGE, BF16)],
+        out_shape=[shape((2, half, INNER))] + [shape(MESSAGE, BF16)] * QUARTERS,
         compiler_params=params(16),
         cost_estimate=cost(8),
         name="states",
     )(member, conv_input, conv_weight, bias_row, step_q, sum_q, bt, column_direction)
 
     gate_rows = rows_of[:INNER]
-    out_rows = lax.all_gather(tie(out_weight, payload), "fsdp", axis=0, tiled=True)
+    out_rows = lax.all_gather(tie(out_weight, *payload), "fsdp", axis=0, tiled=True)
     half_grid = QUARTERS // 2
 
     def later_half(spec, first):
@@ -1089,7 +1128,7 @@
 
     token_rows = row_block(INNER)
     steps = half // ROWS
-    normed_out, grad_z, grad_scan, back_payload, gate_gain_grad = pl.pallas_call(
+    normed_out, grad_z, grad_scan, *back_payload, gate_gain_grad = pl.pallas_call(
         gate_kernel,
         grid=(2 * steps,),
         in_specs=[
@@ -1107,14 +1146,14 @@
             token_rows,
             token_rows,
             token_rows,
-            whole_block((QUARTERS,) + MESSAGE),
+            *[whole_block(MESSAGE)] * QUARTERS,
             whole_block((1, INNER)),
         ],
         out_shape=[
             shape((2, half, INNER), BF16),
             shape((2, half, INNER), BF16),
             shape((2, half, INNER)),
-            shape((QUARTERS,) + MESSAGE, BF16),
+            *[shape(MESSAGE, BF16)] * QUARTERS,
             shape((1, INNER)),
         ],
         scratch_shapes=[

time: 655 us -> 643 us (0.982)
  starting transfers between devices: 70.5 us -> 56.5 us
  local copies, waits for them, and re-layouts: 58.4 us -> 50.2 us
    all_gather x1, starting transfers between devices: 10.3 us -> 0.04 us  [local(): gathered = lax.all_gather(shard, 'seq', axis=0)]
    unnamed x218 -> x212, local copies, waits for them, and re-layouts: 23.8 us -> 18.6 us
  transfers between devices with their start and end apart: 43 -> 43, of which waited for: 22 -> 22; matrix products, arithmetic and copies ran while one was open for 23% -> 23% of each run, Pallas kernels for 14% -> 15%
where the time goes in v5:
time: 643 us; the launch traced here: 636 us
  waiting for transfers between devices  230 us (36%)
  Pallas kernels  142 us (22%)
  matrix products  100 us (16%)
  starting transfers between devices  56.5 us (9%)
  local copies, waits for them, and re-layouts  50.2 us (8%)
  other arithmetic  40.7 us (6%)
  between operations  16.3 us (3%)
    all_gather x1, waiting for transfers between devices, local(): gathered = lax.all_gather(shard, 'seq', axis=0)  98.9 us
    ppermute x12, waiting for transfers between devices, send(): lax.ppermute(away, self.axis, [(i, i ^ 1 << bit) for i in range(self.coun...  62.2 us
    dot_general x5, matrix products, dot_last(): lax.dot_general(left, right, (((1,), (1,)), ((), ())), preferred_element_...  42.7 us
    pallas_call x2, Pallas kernels, work(): pl.pallas_call(intra_back_kernel, grid=(half_grid,), in_specs=shifted(spe...  37.4 us
    dot_general x7, matrix products, dot(): return jnp.dot(left, right, preferred_element_type=F32)  29.8 us
    dot_general x8, matrix products, dot_first(): lax.dot_general(left, right, (((0,), (0,)), ((), ())), preferred_element_...  27.8 us
    ppermute x12, waiting for transfers between devices, swap(): return lax.ppermute(value, axis, [(i, i ^ by) for i in range(count)])  25.7 us
    ppermute x5, waiting for transfers between devices, add_up(): lax.ppermute(value, axis, [(i, i ^ 1 << bit) for i in range(count)])  24.1 us
  transfers between devices with their start and end apart: 43, of which 22 were waited for; matrix products, arithmetic and copies ran while one was open for 23% of the time, Pallas kernels for 15%

profile of v5, /device:TPU:0, one launch (start us, length us, event | category | flops | bytes accessed | tf_op | source)
XLA Modules:
  0.0 636.2 jit_solution(10785471197529476143)
XLA Ops:
  7.3 5.2 slice.238
  12.9 4.4 collective-permute-start
  22.8 8.0 %fusion.86 = f32[544,3376]{1,0:T(8,128)} fusion(bf16[544,768]{1,0:T(8,128)(2,1)S(1)} %broadcast_select_fusion, bf16[3376,768]{1,0:T(8,128)(2,1)} %slice.238), kind=kOutput, calls=%fused_computation.197 | convolution fusion | flops 2820931584 | bytes 13367296 | tf_op jit(solution)/shard_map/dot_general | solution.py:76
  30.8 7.2 %convolution_add_fusion = f32[544,3376]{1,0:T(8,128)S(1)} fusion(f32[544,3376]{1,0:T(8,128)} %fusion.86, bf16[3376,768]{1,0:T(8,128)(2,1)} %collective-permute-done.1, pred[]{:T(512)S(6)} %eq.4, bf16[544,1536]{1,0:T(8,128)(2,1)S(1)} %fusion.16), kind=kOutput, calls=%fused_computation.4 | convolution fusion | flops 2823185920 | bytes 21549056 | tf_op jit(solution)/shard_map/dot_general | solution.py:76
  38.1 2.0 steps.1
  41.0 10.1 %states.1 = (f32[2,256,3072]{2,1,0:T(8,128)S(1)}, bf16[2,144,768]{2,1,0:T(8,128)(2,1)S(1)}, bf16[2,144,768]{2,1,0:T(8,128)(2,1)S(1)}, bf16[2,144,768]{2,1,0:T(8,128)(2,1)S(1)}, bf16[2,144,768]{2,1,0:T(8,128)(2,1)S(1)}) custom-call(s32[1]{0:T(128)} %bitcast.1.member, f32[2,272,3376]{2,1,0:T(8,128)S(1)} %bitcast.205, f32[4,3328]{1,0:T(4,128)S(1)} %copy-done.12, ...), custom_call_target="tpu_custom_call" | custom-call | bytes 27200000 | tf_op jit(solution)/shard_map/states/pallas_call | solution.py:1042
  51.3 2.6 copy-done.1
  54.1 2.2 fusion.25
  57.6 2.5 collective-permute-start.2
  62.5 10.1 %inside.2.refs_0_ = f32[2,256,3072]{2,1,0:T(8,128)} custom-call(f32[2,256,3072]{2,1,0:T(8,128)} %copy-done.1, f32[4,2,256,16]{3,2,1,0:T(8,128)} %copy-done.2, f32[4,2,256,16]{3,2,1,0:T(8,128)} %copy-done.3, f32[4,2,16,256]{3,2,1,0:T(8,128)} %copy-done.10, f32[2,256,256]{2,1,0:T(8,128)} %copy-done.11, f32[1,3072]{1,0:T(1,128)} %broadcast_in_dim_reshape.3.skip), custom_call_target="tpu_custom_call" | custom-call | bytes 27200000 | tf_op jit(solution)/shard_map/inside/pallas_call | solution.py:1097
  72.6 7.9 %fusion.9 = f32[512,3072]{1,0:T(8,128)} fusion(bf16[512,768]{1,0:T(8,128)(2,1)} %get-tuple-element.120, bf16[6448,768]{1,0:T(8,128)(2,1)} %bitcast.212), kind=kOutput, calls=%fused_computation.21 | convolution fusion | flops 2415919104 | bytes 11796480 | tf_op jit(solution)/shard_map/dot_general | solution.py:76
  82.9 3.5 collective-permute-start.5
  86.4 9.8 %fusion.87 = f32[512,3072]{1,0:T(8,128)} fusion(bf16[512,1536]{1,0:T(8,128)(2,1)} %bitcast.259, bf16[3072,1536]{1,0:T(8,128)(2,1)} %all-gather.3.cloned.1.call-done), kind=kOutput, calls=%fused_computation.198 | convolution fusion | flops 4831838208 | bytes 17301504 | tf_op jit(solution)/shard_map/dot_general | solution.py:76
  96.4 4.9 collective-permute-start.6
  101.3 9.2 %inside.3.y_ref = f32[2,256,3072]{2,1,0:T(8,128)} custom-call(f32[2,256,3072]{2,1,0:T(8,128)} %copy-done.1, f32[4,2,256,16]{3,2,1,0:T(8,128)} %copy-done.2, f32[4,2,256,16]{3,2,1,0:T(8,128)} %copy-done.3, f32[4,2,16,256]{3,2,1,0:T(8,128)} %copy-done.10, f32[2,256,256]{2,1,0:T(8,128)} %copy-done.11, ...), custom_call_target="tpu_custom_call", output_to_operand_aliasing={{}: (6, {})} | custom-call | bytes 27200000 | tf_op jit(solution)/shard_map/inside/pallas_call | solution.py:1097
  116.5 9.8 %convolution_add_fusion.1 = f32[512,3072]{1,0:T(8,128)} fusion(f32[512,3072]{1,0:T(8,128)} %fusion.9, bf16[512,768]{1,0:T(8,128)(2,1)} %get-tuple-element.128, bf16[6448,768]{1,0:T(8,128)(2,1)} %collective-permute-done.7), kind=kOutput, calls=%fused_computation.15 | convolution fusion | flops 2417491968 | bytes 18087936 | tf_op jit(solution)/shard_map/dot_general | solution.py:76
  127.1 7.2 %collective-permute-done.8.refs_1_ = bf16[2,144,768]{2,1,0:T(8,128)(2,1)S(1)} collective-permute-done((bf16[2,144,768]{2,1,0:T(8,128)(2,1)S(1)}, bf16[2,144,768]{2,1,0:T(8,128)(2,1)S(1)}, u32[]{:S(2)}, u32[]{:S(2)}) %collective-permute-start.8) | collective-permute-done | bytes 442400 | tf_op jit(solution)/shard_map/ppermute | solution.py:777
  134.9 17.8 %gates.1 = (bf16[2,256,3072]{2,1,0:T(8,128)(2,1)S(1)}, bf16[2,256,3072]{2,1,0:T(8,128)(2,1)S(1)}, f32[2,256,3072]{2,1,0:T(8,128)}, bf16[2,144,768]{2,1,0:T(8,128...) custom-call(s32[1]{0:T(128)} %bitcast.1.member, ...), custom_call_target="tpu_custom_call" | custom-call | bytes 47600000 | tf_op jit(solution)/shard_map/gates/pallas_call | solution.py:1131
  152.8 4.7 convolution_convert_fusion.2
  157.5 4.4 convolution_convert_fusion
  165.9 7.0 %convert_add_fusion.1 = f32[3072,768]{1,0:T(8,128)} fusion(bf16[3072,768]{1,0:T(8,128)(2,1)} %collective-permute-done.15, bf16[512,3072]{1,0:T(8,128)(2,1)S(1)} %bitcast.218, bf16[512,768]{1,0:T(8,128)(2,1)} %get-tuple-element.120), kind=kOutput, calls=%fused_computation.1 | convolution fusion | flops 2420637696 | bytes 18087936 | tf_op jit(solution)/shard_map/dot_general | solution.py:86
  173.0 4.7 convert_add_fusion.2
  177.7 7.5 %collective-permute-done.13.refs_3_ = bf16[2,144,768]{2,1,0:T(8,128)(2,1)S(1)} collective-permute-done((bf16[2,144,768]{2,1,0:T(8,128)(2,1)}, bf16[2,144,768]{2,1,0:T(8,128)(2,1)S(1)}, u32[]{:S(2)}, u32[]{:S(2)}) %collective-permute-start.13) | collective-permute-done | bytes 442400 | tf_op jit(solution)/shard_map/ppermute | solution.py:777
  189.1 4.1 fusion.32
  195.9 18.6 %inside_back.2 = (f32[2,256,3072]{2,1,0:T(8,128)}, bf16[2,256,3072]{2,1,0:T(8,128)(2,1)}, f32[2,256,256]{2,1,0:T(8,128)}, f32[4,2,256,128]{3,2,1,0:T(8,128)}, f32[2,256,128]{2,1,0:T(8,128)}) custom-call(f32[2,256,3072]{2,1,0:T(8,128)} %copy-done.1, f32[2,256,3072]{2,1,0:T(8,128)} %get-tuple-element.155.grad_ref, f32[2,256,3072]{2,1,0:T(8,128)} %inside.3.y_ref, ...), custom_call_target="tpu_custom_call" | custom-call | bytes 57800000 | tf_op jit(solution)/shard_map/inside_back/pallas_call | solution.py:1245
  216.2 2.0 link.3
  219.8 18.7 %inside_back.3 = (f32[2,256,3072]{2,1,0:T(8,128)}, bf16[2,256,3072]{2,1,0:T(8,128)(2,1)}, f32[2,256,256]{2,1,0:T(8,128)}, f32[4,2,256,128]{3,2,1,0:T(8,128)}, f32[2,256,128]{2,1,0:T(8,128)}) custom-call(f32[2,256,3072]{2,1,0:T(8,128)} %copy-done.1, ...), custom_call_target="tpu_custom_call", output_to_operand_aliasing={{0}: (15, {}), {1}: (16, {}), {3}: (17, {})} | custom-call | bytes 57800000 | tf_op jit(solution)/shard_map/inside_back/pallas_call | solution.py:1245
  238.6 10.4 %collective-permute-done.17.refs_5_ = bf16[2,144,768]{2,1,0:T(8,128)(2,1)} collective-permute-done((bf16[2,144,768]{2,1,0:T(8,128)(2,1)}, bf16[2,144,768]{2,1,0:T(8,128)(2,1)}, u32[]{:S(2)}, u32[]{:S(2)}) %collective-permute-start.17) | collective-permute-done | bytes 442400 | tf_op jit(solution)/shard_map/ppermute | solution.py:803
  252.0 2.0 spread.3
  257.6 3.7 bitcast_add_fusion.1
  261.4 5.3 bitcast_add_fusion
  266.6 8.1 %collective-permute-done.20.refs_3_ = bf16[2,144,768]{2,1,0:T(8,128)(2,1)S(1)} collective-permute-done((bf16[2,144,768]{2,1,0:T(8,128)(2,1)S(1)}, bf16[2,144,768]{2,1,0:T(8,128)(2,1)S(1)}, u32[]{:S(2)}, u32[]{:S(2)}) %collective-permute-start.20) | collective-permute-done | bytes 442400 | tf_op jit(solution)/shard_map/ppermute | solution.py:777
  281.9 14.0 %channels.1 = (bf16[2,256,3072]{2,1,0:T(8,128)(2,1)}, f32[2,16,3072]{2,1,0:T(8,128)}, bf16[2,16,3072]{2,1,0:T(8,128)(2,1)}, bf16[2,256,3072]{2,1,0:T(8,128)(2,1)...) custom-call(f32[2,256,3072]{2,1,0:T(8,128)} %get-tuple-element.156.known_ref, ...), custom_call_target="tpu_custom_call" | custom-call | bytes 40800000 | tf_op jit(solution)/shard_map/channels/pallas_call | solution.py:1302
  295.9 6.4 %last.1 = (bf16[2,256,304]{2,1,0:T(8,128)(2,1)}, f32[2,16,256]{2,1,0:T(8,128)}, bf16[2,16,256]{2,1,0:T(8,128)(2,1)}, f32[8,256]{1,0:T(8,128)}, f32[8,128]{1,0:T(8,128)}) custom-call(f32[2,272,3376]{2,1,0:T(8,128)} %bitcast.208, f32[4,3328]{1,0:T(4,128)} %weight.11, f32[1,3328]{1,0:T(1,128)} %copy-done.27, f32[8,128]{1,0:T(8,128)} %copy-done.32, ...), custom_call_target="tpu_custom_call" | custom-call | bytes 20400000 | tf_op jit(solution)/shard_map/last/pallas_call | solution.py:1358
  304.1 2.2 slice.191
  309.8 2.4 bitcast_add_fusion.5
  315.6 3.1 convolution_convert_fusion.1
  319.9 3.2 collective-permute-start.31
  323.1 4.7 collective-permute-done.34
  329.5 2.8 convert_add_fusion
  332.4 2.8 fusion.83
  335.2 2.2 copy-done.51
  338.7 3.1 collective-permute-start.37
  343.0 2.2 fusion.46
  346.1 3.5 collective-permute-done.31
  352.3 2.5 collective-permute-start.32
  354.9 17.7 %collective-permute-done.37 = bf16[2,2,2,224,384]{4,3,0,1,2:T(8,128)(2,1)} collective-permute-done((bf16[2,2,2,224,384]{4,3,0,1,2:T(8,128)(2,1)}, bf16[2,2,2,224,384]{4,3,0,1,2:T(8,128)(2,1)}, u32[]{:S(2)}, u32[]{:S(2)}) %collective-permute-start.37) | collective-permute-done | bytes 1376288 | tf_op jit(solution)/shard_map/ppermute | solution.py:870
  384.2 10.3 %collective-permute-done.38 = bf16[2,2,224,384]{3,2,0,1:T(8,128)(2,1)} collective-permute-done((bf16[2,2,224,384]{3,2,0,1:T(8,128)(2,1)}, bf16[2,2,224,384]{3,2,0,1:T(8,128)(2,1)}, u32[]{:S(2)}, u32[]{:S(2)}) %collective-permute-start.38) | collective-permute-done | bytes 688160 | tf_op jit(solution)/shard_map/ppermute | solution.py:870
  395.7 2.3 collective-permute-done.36
  403.1 14.5 %collective-permute-done.39 = bf16[2,224,768]{2,1,0:T(8,128)(2,1)S(1)} collective-permute-done((bf16[2,224,768]{2,1,0:T(8,128)(2,1)S(1)}, bf16[2,224,768]{2,1,0:T(8,128)(2,1)S(1)}, u32[]{:S(2)}, u32[]{:S(2)}) %collective-permute-start.39) | collective-permute-done | bytes 688160 | tf_op jit(solution)/shard_map/ppermute | solution.py:870
  417.8 2.1 collective-permute-start.40
  419.9 13.9 %collective-permute-done.40 = bf16[224,768]{1,0:T(8,128)(2,1)S(1)} collective-permute-done((bf16[224,768]{1,0:T(8,128)(2,1)S(1)}, bf16[224,768]{1,0:T(8,128)(2,1)S(1)}, u32[]{:S(2)}, u32[]{:S(2)}) %collective-permute-start.40) | collective-permute-done | bytes 344096 | tf_op jit(solution)/shard_map/ppermute | solution.py:870
  436.7 10.8 %sums.1 = f32[8,3072]{1,0:T(8,128)} custom-call(f32[2,272,3376]{2,1,0:T(8,128)} %bitcast.209, bf16[2,256,3072]{2,1,0:T(8,128)(2,1)} %get-tuple-element.192.grad_mix_ref, f32[2,256,3072]{2,1,0:T(8,128)} %get-tuple-element.155.grad_ref, f32[2,256,3072]{2,1,0:T(8,128)} %copy-done.1), custom_call_target="tpu_custom_call" | custom-call | bytes 34000000 | tf_op jit(solution)/shard_map/sums/pallas_call | solution.py:1498
  449.6 5.1 fusion.7
  454.7 5.0 fusion.2
  461.4 5.1 fusion.4
  466.5 5.0 fusion
  477.1 6.9 %collective-permute-done.27 = f32[169,128]{1,0:T(8,128)S(1)} collective-permute-done((f32[169,128]{1,0:T(8,128)S(1)}, f32[169,128]{1,0:T(8,128)S(1)}, u32[]{:S(2)}, u32[]{:S(2)}) %collective-permute-start.27) | collective-permute-done | bytes 86560 | tf_op jit(solution)/shard_map/ppermute | solution.py:886
  484.8 6.2 fusion.30
  491.1 9.4 %collective-permute-done.29 = f32[169,128]{1,0:T(8,128)S(1)} collective-permute-done((f32[169,128]{1,0:T(8,128)S(1)}, f32[169,128]{1,0:T(8,128)S(1)}, u32[]{:S(2)}, u32[]{:S(2)}) %collective-permute-start.29) | collective-permute-done | bytes 86560 | tf_op jit(solution)/shard_map/ppermute | solution.py:886
  501.3 2.1 fusion.23
  503.5 6.5 %collective-permute-done.30 = f32[169,128]{1,0:T(8,128)S(1)} collective-permute-done((f32[169,128]{1,0:T(8,128)S(1)}, f32[169,128]{1,0:T(8,128)S(1)}, u32[]{:S(2)}, u32[]{:S(2)}) %collective-permute-start.30) | collective-permute-done | bytes 86560 | tf_op jit(solution)/shard_map/ppermute | solution.py:886
  513.6 98.9 %all-gather.5.cloned.1.call-done.gate_rows.last_rows.out_rows = bf16[16,608,768]{2,1,0:T(8,128)(2,1)} async-done(((bf16[1,608,768]{2,1,0:T(8,128)(2,1)}), bf16[16,608,768]{2,1,0:T(8,128)(2,1)}) %all-gather.5.cloned.1.call-update) | async-done | bytes 14942224 | tf_op jit(solution)/shard_map/all_gather | solution.py:1473
  612.5 16.4 %finish.1 = (f32[6448,768]{1,0:T(8,128)}, f32[1536,1536]{1,0:T(8,128)}) custom-call(bf16[16,608,768]{2,1,0:T(8,128)(2,1)} %all-gather.5.cloned.1.call-done.gate_rows.last_rows.out_rows, bf16[16,608,768]{2,1,0:T(8,128)(2,1)} %all-gather.5.cloned.1.call-done.gate_rows.last_rows.out_rows, ...), custom_call_target="tpu_custom_call" | custom-call | bytes 47600000 | tf_op jit(solution)/shard_map/finish/pallas_call | solution.py:1535
  (384 shorter events, 101.1 us)
Async XLA Ops:
  7.2 79.3 %all-gather.3.cloned.1.call-start = ((), (), s32[]{:S(2)}) async-start(), calls=%async_computation | async-start | bytes 14155776 | tf_op jit(solution)/shard_map/all_gather | solution.py:1065
  12.5 18.3 %collective-permute-start.1 = (bf16[3376,768]{1,0:T(8,128)(2,1)}, bf16[3376,768]{1,0:T(8,128)(2,1)}, u32[]{:S(2)}, u32[]{:S(2)}) collective-permute-start(bf16[3376,768]{1,0:T(8,128)(2,1)} %slice.238), channel_id=1, source_target_pairs={{0,1},{1,0},{2,3},{3,2},{4,5},{5,4},{6,7},{7,6},{8,9},{9,8},{10,11... | collective-permute-start | bytes 15556616 | tf_op jit(solution)/shard_map/ppermute | solution.py:937
  12.9 7.1 %collective-permute-start = (bf16[2,16,1536]{2,1,0:T(8,128)(2,1)S(1)}, bf16[2,16,1536]{2,1,0:T(8,128)(2,1)S(1)}, u32[]{:S(2)}, u32[]{:S(2)}) collective-permute-start(bf16[2,16,1536]{2,1,0:T(8,128)(2,1)S(1)} %slice.237), channel_id=1, source_target_pairs={{0,2},{2,4},{4,6},{6,8},{8,10},{10,12},{12,14},{14,16},{16,18},{18... | collective-permute-start | bytes 294920 | tf_op jit(solution)/shard_map/ppermute | solution.py:940
  17.4 22.8 %copy-start.27 = (f32[1,3328]{1,0:T(1,128)}, f32[1,3328]{1,0:T(1,128)S(1)}, u32[]{:S(2)}) copy-start(f32[1,3328]{1,0:T(1,128)S(1)} %broadcast_in_dim.8.bias) | copy-start | bytes 39940
  18.2 19.8 %copy-start.32 = (f32[8,128]{1,0:T(8,128)}, f32[8,128]{1,0:T(8,128)S(1)}, u32[]{:S(2)}) copy-start(f32[8,128]{1,0:T(8,128)S(1)} %select_maximum_fusion.small) | copy-start | bytes 12292
  40.2 94.7 %copy-start.5 = (f32[2,256,256]{2,1,0:T(8,128)}, f32[2,256,256]{2,1,0:T(8,128)S(1)}, u32[]{:S(2)}) copy-start(f32[2,256,256]{2,1,0:T(8,128)S(1)} %get-tuple-element.130.bc_ref) | copy-start | bytes 1572868
  53.9 558.7 %all-gather.5.cloned.1.call-start = ((), (), s32[]{:S(2)}) async-start(), calls=%async_computation.1 | async-start | bytes 15876096 | tf_op jit(solution)/shard_map/all_gather | solution.py:1473
  53.9 62.6 %collective-permute-start.7 = (bf16[6448,768]{1,0:T(8,128)(2,1)}, bf16[6448,768]{1,0:T(8,128)(2,1)}, u32[]{:S(2)}, u32[]{:S(2)}) collective-permute-start(bf16[6448,768]{1,0:T(8,128)(2,1)} %bitcast.211), channel_id=1, source_target_pairs={{0,1},{1,0},{2,3},{3,2},{4,5},{5,4},{6,7},{7,6},{8,9},{9,8},{10,11... | collective-permute-start | bytes 29712392 | tf_op jit(solution)/shard_map/ppermute | solution.py:1078
  57.6 24.9 %collective-permute-start.2 = (bf16[2,144,768]{2,1,0:T(8,128)(2,1)S(1)}, bf16[2,144,768]{2,1,0:T(8,128)(2,1)S(1)}, u32[]{:S(2)}, u32[]{:S(2)}) collective-permute-start(bf16[2,144,768]{2,1,0:T(8,128)(2,1)S(1)} %get-tuple-element.114), channel_id=1, source_target_pairs={{0,2},{2,0},{4,6},{6,4},{8,10},{10,8},{12,14},{14,12},{16,18},{18,... | collective-permute-start | bytes 1327112 | tf_op jit(solution)/shard_map/ppermute | solution.py:777
  60.1 22.4 %collective-permute-start.3 = (bf16[2,144,768]{2,1,0:T(8,128)(2,1)S(1)}, bf16[2,144,768]{2,1,0:T(8,128)(2,1)S(1)}, u32[]{:S(2)}, u32[]{:S(2)}) collective-permute-start(bf16[2,144,768]{2,1,0:T(8,128)(2,1)S(1)} %get-tuple-element.115), channel_id=1, source_target_pairs={{0,4},{2,6},{4,0},{6,2},{8,12},{10,14},{12,8},{14,10},{16,20},{18,... | collective-permute-start | bytes 1327112 | tf_op jit(solution)/shard_map/ppermute | solution.py:777
  61.6 20.9 %collective-permute-start.4 = (bf16[2,144,768]{2,1,0:T(8,128)(2,1)S(1)}, bf16[2,144,768]{2,1,0:T(8,128)(2,1)S(1)}, u32[]{:S(2)}, u32[]{:S(2)}) collective-permute-start(bf16[2,144,768]{2,1,0:T(8,128)(2,1)S(1)} %copy-done.42), channel_id=1, source_target_pairs={{0,6},{2,4},{4,2},{6,0},{8,14},{10,12},{12,10},{14,8},{16,22},{18,... | collective-permute-start | bytes 1327112 | tf_op jit(solution)/shard_map/ppermute | solution.py:777
  82.9 13.3 %collective-permute-start.5 = (bf16[2,144,768]{2,1,0:T(8,128)(2,1)S(1)}, bf16[2,144,768]{2,1,0:T(8,128)(2,1)S(1)}, u32[]{:S(2)}, u32[]{:S(2)}) collective-permute-start(bf16[2,144,768]{2,1,0:T(8,128)(2,1)S(1)} %plane.2.refs_0_), channel_id=1, source_target_pairs={{0,8},{2,10},{4,12},{6,14},{8,16},{10,18},{12,20},{14,22},{16,24},... | collective-permute-start | bytes 1327112 | tf_op jit(solution)/shard_map/ppermute | solution.py:803
  96.4 14.0 %collective-permute-start.6 = (bf16[2,144,768]{2,1,0:T(8,128)(2,1)S(1)}, bf16[2,144,768]{2,1,0:T(8,128)(2,1)S(1)}, u32[]{:S(2)}, u32[]{:S(2)}) collective-permute-start(bf16[2,144,768]{2,1,0:T(8,128)(2,1)S(1)} %link.2), channel_id=1, source_target_pairs={{0,16},{2,18},{4,20},{6,22},{8,24},{10,26},{12,28},{14,30},{1,17},... | collective-permute-start | bytes 1327112 | tf_op jit(solution)/shard_map/ppermute | solution.py:803
  113.0 14.1 %collective-permute-start.10 = (bf16[2,144,768]{2,1,0:T(8,128)(2,1)S(1)}, bf16[2,144,768]{2,1,0:T(8,128)(2,1)S(1)}, u32[]{:S(2)}, u32[]{:S(2)}) collective-permute-start(bf16[2,144,768]{2,1,0:T(8,128)(2,1)S(1)} %get-tuple-element.127), channel_id=1, source_target_pairs={{0,6},{2,4},{4,2},{6,0},{8,14},{10,12},{12,10},{14,8},{16,22},{18,... | collective-permute-start | bytes 1327112 | tf_op jit(solution)/shard_map/ppermute | solution.py:777
  114.4 19.9 %collective-permute-start.8 = (bf16[2,144,768]{2,1,0:T(8,128)(2,1)S(1)}, bf16[2,144,768]{2,1,0:T(8,128)(2,1)S(1)}, u32[]{:S(2)}, u32[]{:S(2)}) collective-permute-start(bf16[2,144,768]{2,1,0:T(8,128)(2,1)S(1)} %get-tuple-element.133), channel_id=1, source_target_pairs={{0,2},{2,0},{4,6},{6,4},{8,10},{10,8},{12,14},{14,12},{16,18},{18,... | collective-permute-start | bytes 1327112 | tf_op jit(solution)/shard_map/ppermute | solution.py:777
  115.9 19.0 %copy-start.26 = (f32[2,256,128]{2,1,0:T(8,128)S(1)}, f32[2,256,128]{2,1,0:T(8,128)}, u32[]{:S(2)}) copy-start(f32[2,256,128]{2,1,0:T(8,128)} %copy-done.25) | copy-start | bytes 786436
  115.9 19.0 %copy-start.33 = (f32[3072]{0:T(1024)S(1)}, f32[3072]{0:T(1024)}, u32[]{:S(2)}) copy-start(f32[3072]{0:T(1024)} %param.19) | copy-start | bytes 36868
  115.9 18.4 %collective-permute-start.9 = (bf16[2,144,768]{2,1,0:T(8,128)(2,1)S(1)}, bf16[2,144,768]{2,1,0:T(8,128)(2,1)S(1)}, u32[]{:S(2)}, u32[]{:S(2)}) collective-permute-start(bf16[2,144,768]{2,1,0:T(8,128)(2,1)S(1)} %get-tuple-element.134), channel_id=1, source_target_pairs={{0,4},{2,6},{4,0},{6,2},{8,12},{10,14},{12,8},{14,10},{16,20},{18,... | collective-permute-start | bytes 1327112 | tf_op jit(solution)/shard_map/ppermute | solution.py:777
  134.9 17.9 %copy-start.4 = (bf16[2,128,3072]{2,1,0:T(8,128)(2,1)}, bf16[2,128,3072]{2,1,0:T(8,128)(2,1)S(1)}, u32[]{:S(2)}) copy-start(bf16[2,128,3072]{2,1,0:T(8,128)(2,1)S(1)} %get-tuple-element.136.entering) | copy-start | bytes 4718596
  134.9 17.9 %copy-start.8 = (f32[2,8,3072]{2,1,0:T(8,128)}, f32[2,8,3072]{2,1,0:T(8,128)S(1)}, u32[]{:S(2)}) copy-start(f32[2,8,3072]{2,1,0:T(8,128)S(1)} %get-tuple-element.137.along) | copy-start | bytes 589828
  134.9 17.9 %copy-start.68 = (bf16[512,768]{1,0:T(8,128)(2,1)S(1)}, bf16[512,768]{1,0:T(8,128)(2,1)}, u32[]{:S(2)}) copy-start(bf16[512,768]{1,0:T(8,128)(2,1)} %get-tuple-element.128) | copy-start | bytes 2359300
  157.5 8.5 %collective-permute-start.15 = (bf16[3072,768]{1,0:T(8,128)(2,1)}, bf16[3072,768]{1,0:T(8,128)(2,1)}, u32[]{:S(2)}, u32[]{:S(2)}) collective-permute-start(bf16[3072,768]{1,0:T(8,128)(2,1)} %convolution_convert_fusion.2), channel_id=1, source_target_pairs={{0,1},{1,0},{2,3},{3,2},{4,5},{5,4},{6,7},{7,6},{8,9},{9,8},{10,11... | collective-permute-start | bytes 14155784 | tf_op jit(solution)/shard_map/ppermute | solution.py:1189
  161.9 11.1 %collective-permute-start.14 = (bf16[1536,1536]{1,0:T(8,128)(2,1)}, bf16[1536,1536]{1,0:T(8,128)(2,1)}, u32[]{:S(2)}, u32[]{:S(2)}) collective-permute-start(bf16[1536,1536]{1,0:T(8,128)(2,1)} %convolution_convert_fusion), channel_id=1, source_target_pairs={{0,1},{1,0},{2,3},{3,2},{4,5},{5,4},{6,7},{7,6},{8,9},{9,8},{10,11... | collective-permute-start | bytes 14155784 | tf_op jit(solution)/shard_map/ppermute | solution.py:1189
  162.4 24.4 %collective-permute-start.11 = (bf16[2,144,768]{2,1,0:T(8,128)(2,1)}, bf16[2,144,768]{2,1,0:T(8,128)(2,1)S(1)}, u32[]{:S(2)}, u32[]{:S(2)}) collective-permute-start(bf16[2,144,768]{2,1,0:T(8,128)(2,1)} %copy-done.39), channel_id=1, source_target_pairs={{0,2},{2,0},{4,6},{6,4},{8,10},{10,8},{12,14},{14,12},{16,18},{18,... | collective-permute-start | bytes 1327112 | tf_op jit(solution)/shard_map/ppermute | solution.py:777
  163.8 23.1 %collective-permute-start.12 = (bf16[2,144,768]{2,1,0:T(8,128)(2,1)}, bf16[2,144,768]{2,1,0:T(8,128)(2,1)S(1)}, u32[]{:S(2)}, u32[]{:S(2)}) collective-permute-start(bf16[2,144,768]{2,1,0:T(8,128)(2,1)} %copy-done.38), channel_id=1, source_target_pairs={{0,4},{2,6},{4,0},{6,2},{8,12},{10,14},{12,8},{14,10},{16,20},{18,... | collective-permute-start | bytes 1327112 | tf_op jit(solution)/shard_map/ppermute | solution.py:777
  164.4 20.8 %collective-permute-start.13 = (bf16[2,144,768]{2,1,0:T(8,128)(2,1)}, bf16[2,144,768]{2,1,0:T(8,128)(2,1)S(1)}, u32[]{:S(2)}, u32[]{:S(2)}) collective-permute-start(bf16[2,144,768]{2,1,0:T(8,128)(2,1)} %copy-done.40), channel_id=1, source_target_pairs={{0,6},{2,4},{4,2},{6,0},{8,14},{10,12},{12,10},{14,8},{16,22},{18,... | collective-permute-start | bytes 1327112 | tf_op jit(solution)/shard_map/ppermute | solution.py:777
  188.6 69.0 %collective-permute-start.21 = (bf16[2,2,2,96,1536]{4,3,2,1,0:T(8,128)(2,1)}, bf16[2,2,2,96,1536]{4,3,2,1,0:T(8,128)(2,1)}, u32[]{:S(2)}, u32[]{:S(2)}) collective-permute-start(bf16[2,2,2,96,1536]{4,3,2,1,0:T(8,128)(2,1)} %fusion.31), channel_id=1, source_target_pairs={{0,2},{2,0},{4,6},{6,4},{8,10},{10,8},{12,14},{14,12},{16,18},{18,... | collective-permute-start | bytes 7077896 | tf_op jit(solution)/shard_map/ppermute | solution.py:870
  193.2 68.1 %collective-permute-start.22 = (bf16[2,2,2,192,768]{4,3,0,1,2:T(8,128)(2,1)}, bf16[2,2,2,192,768]{4,3,0,1,2:T(8,128)(2,1)}, u32[]{:S(2)}, u32[]{:S(2)}) collective-permute-start(bf16[2,2,2,192,768]{4,3,0,1,2:T(8,128)(2,1)} %fusion.32), channel_id=1, source_target_pairs={{0,4},{2,6},{4,0},{6,2},{8,12},{10,14},{12,8},{14,10},{16,20},{18,... | collective-permute-start | bytes 7077896 | tf_op jit(solution)/shard_map/ppermute | solution.py:870
  194.7 21.5 %collective-permute-start.16 = (bf16[2,144,768]{2,1,0:T(8,128)(2,1)S(1)}, bf16[2,144,768]{2,1,0:T(8,128)(2,1)}, u32[]{:S(2)}, u32[]{:S(2)}) collective-permute-start(bf16[2,144,768]{2,1,0:T(8,128)(2,1)S(1)} %copy-done.14), channel_id=1, source_target_pairs={{8,0},{10,2},{12,4},{14,6},{16,8},{18,10},{20,12},{22,14},{24,16},... | collective-permute-start | bytes 1327112 | tf_op jit(solution)/shard_map/ppermute | solution.py:803
  218.1 30.8 %collective-permute-start.17 = (bf16[2,144,768]{2,1,0:T(8,128)(2,1)}, bf16[2,144,768]{2,1,0:T(8,128)(2,1)}, u32[]{:S(2)}, u32[]{:S(2)}) collective-permute-start(bf16[2,144,768]{2,1,0:T(8,128)(2,1)} %link.3), channel_id=1, source_target_pairs={{16,0},{18,2},{20,4},{22,6},{24,8},{26,10},{28,12},{30,14},{17,1},... | collective-permute-start | bytes 1327112 | tf_op jit(solution)/shard_map/ppermute | solution.py:803
  219.8 29.1 %copy-start.17 = (bf16[2,144,768]{2,1,0:T(8,128)(2,1)S(1)}, bf16[2,144,768]{2,1,0:T(8,128)(2,1)}, u32[]{:S(2)}) copy-start(bf16[2,144,768]{2,1,0:T(8,128)(2,1)} %copy-done.15) | copy-start | bytes 1327108
  254.0 20.7 %collective-permute-start.18 = (bf16[2,144,768]{2,1,0:T(8,128)(2,1)S(1)}, bf16[2,144,768]{2,1,0:T(8,128)(2,1)S(1)}, u32[]{:S(2)}, u32[]{:S(2)}) collective-permute-start(bf16[2,144,768]{2,1,0:T(8,128)(2,1)S(1)} %get-tuple-element.163), channel_id=1, source_target_pairs={{0,2},{2,0},{4,6},{6,4},{8,10},{10,8},{12,14},{14,12},{16,18},{18,... | collective-permute-start | bytes 1327112 | tf_op jit(solution)/shard_map/ppermute | solution.py:777
  255.5 19.5 %collective-permute-start.19 = (bf16[2,144,768]{2,1,0:T(8,128)(2,1)S(1)}, bf16[2,144,768]{2,1,0:T(8,128)(2,1)S(1)}, u32[]{:S(2)}, u32[]{:S(2)}) collective-permute-start(bf16[2,144,768]{2,1,0:T(8,128)(2,1)S(1)} %get-tuple-element.164), channel_id=1, source_target_pairs={{0,4},{2,6},{4,0},{6,2},{8,12},{10,14},{12,8},{14,10},{16,20},{18,... | collective-permute-start | bytes 1327112 | tf_op jit(solution)/shard_map/ppermute | solution.py:777
  256.8 17.9 %collective-permute-start.20 = (bf16[2,144,768]{2,1,0:T(8,128)(2,1)S(1)}, bf16[2,144,768]{2,1,0:T(8,128)(2,1)S(1)}, u32[]{:S(2)}, u32[]{:S(2)}) collective-permute-start(bf16[2,144,768]{2,1,0:T(8,128)(2,1)S(1)} %get-tuple-element.165), channel_id=1, source_target_pairs={{0,6},{2,4},{4,2},{6,0},{8,14},{10,12},{12,10},{14,8},{16,22},{18,... | collective-permute-start | bytes 1327112 | tf_op jit(solution)/shard_map/ppermute | solution.py:777
  261.3 16.2 %copy-start.48 = (f32[2,2,2,96,1536]{4,3,2,1,0:T(8,128)}, f32[2,2,2,96,1536]{4,3,2,1,0:T(8,128)S(1)}, u32[]{:S(2)}) copy-start(f32[2,2,2,96,1536]{4,3,2,1,0:T(8,128)S(1)} %bitcast_add_fusion.1) | copy-start | bytes 14155780
  279.9 26.5 %collective-permute-start.23 = (bf16[2,2,96,1536]{3,2,1,0:T(8,128)(2,1)}, bf16[2,2,96,1536]{3,2,1,0:T(8,128)(2,1)}, u32[]{:S(2)}, u32[]{:S(2)}) collective-permute-start(bf16[2,2,96,1536]{3,2,1,0:T(8,128)(2,1)} %fusion.44), channel_id=1, source_target_pairs={{0,4},{2,6},{4,0},{6,2},{8,12},{10,14},{12,8},{14,10},{16,20},{18,... | collective-permute-start | bytes 3538952 | tf_op jit(solution)/shard_map/ppermute | solution.py:870
  281.3 25.1 %collective-permute-start.24 = (bf16[2,2,192,768]{3,2,0,1:T(8,128)(2,1)}, bf16[2,2,192,768]{3,2,0,1:T(8,128)(2,1)}, u32[]{:S(2)}, u32[]{:S(2)}) collective-permute-start(bf16[2,2,192,768]{3,2,0,1:T(8,128)(2,1)} %fusion.45), channel_id=1, source_target_pairs={{0,2},{2,0},{4,6},{6,4},{8,10},{10,8},{12,14},{14,12},{16,18},{18,... | collective-permute-start | bytes 3538952 | tf_op jit(solution)/shard_map/ppermute | solution.py:870
  306.4 8.0 %collective-permute-start.25 = (bf16[2,16,3328]{2,1,0:T(8,128)(2,1)S(1)}, bf16[2,16,3328]{2,1,0:T(8,128)(2,1)S(1)}, u32[]{:S(2)}, u32[]{:S(2)}) collective-permute-start(bf16[2,16,3328]{2,1,0:T(8,128)(2,1)S(1)} %pad_maximum_fusion.12), channel_id=1, source_target_pairs={{2,0},{4,2},{6,4},{8,6},{10,8},{12,10},{14,12},{16,14},{18,16},{20... | collective-permute-start | bytes 638984 | tf_op jit(solution)/shard_map/ppermute | solution.py:1414
  318.7 10.8 %collective-permute-start.33 = (bf16[3072,768]{1,0:T(8,128)(2,1)S(1)}, bf16[3072,768]{1,0:T(8,128)(2,1)S(1)}, u32[]{:S(2)}, u32[]{:S(2)}) collective-permute-start(bf16[3072,768]{1,0:T(8,128)(2,1)S(1)} %convolution_convert_fusion.1), channel_id=1, source_target_pairs={{0,1},{1,0},{2,3},{3,2},{4,5},{5,4},{6,7},{7,6},{8,9},{9,8},{10,11... | collective-permute-start | bytes 14155784 | tf_op jit(solution)/shard_map/ppermute | solution.py:1189
  319.4 8.4 %collective-permute-start.34 = (bf16[512,768]{1,0:T(8,128)(2,1)S(1)}, bf16[512,768]{1,0:T(8,128)(2,1)S(1)}, u32[]{:S(2)}, u32[]{:S(2)}) collective-permute-start(bf16[512,768]{1,0:T(8,128)(2,1)S(1)} %convolution_convert_fusion.3), channel_id=1, source_target_pairs={{0,1},{1,0},{2,3},{3,2},{4,5},{5,4},{6,7},{7,6},{8,9},{9,8},{10,11... | collective-permute-start | bytes 2359304 | tf_op jit(solution)/shard_map/ppermute | solution.py:1189
  319.9 29.7 %collective-permute-start.31 = (bf16[2,384,768]{2,1,0:T(8,128)(2,1)}, bf16[2,384,768]{2,1,0:T(8,128)(2,1)}, u32[]{:S(2)}, u32[]{:S(2)}) collective-permute-start(bf16[2,384,768]{2,1,0:T(8,128)(2,1)} %pad_maximum_fusion.4), channel_id=1, source_target_pairs={{0,8},{2,10},{4,12},{6,14},{8,0},{10,2},{12,4},{14,6},{16,24},{18,... | collective-permute-start | bytes 3538952 | tf_op jit(solution)/shard_map/ppermute | solution.py:870
  338.7 33.9 %collective-permute-start.37 = (bf16[2,2,2,224,384]{4,3,0,1,2:T(8,128)(2,1)}, bf16[2,2,2,224,384]{4,3,0,1,2:T(8,128)(2,1)}, u32[]{:S(2)}, u32[]{:S(2)}) collective-permute-start(bf16[2,2,2,224,384]{4,3,0,1,2:T(8,128)(2,1)} %pad_maximum_fusion.3), channel_id=1, source_target_pairs={{0,4},{2,6},{4,0},{6,2},{8,12},{10,14},{12,8},{14,10},{16,20},{18,... | collective-permute-start | bytes 4128776 | tf_op jit(solution)/shard_map/ppermute | solution.py:870
  345.1 29.2 %slice-start.7 = ((s8[4718592]{0:T(1024)(128)(4,1)}), s8[4194304]{0:T(1024)(128)(4,1)S(1)}, s32[]{:S(2)}) async-start(s8[4718592]{0:T(1024)(128)(4,1)} %bitcast.243), calls=%async_computation.9 | async-start | bytes 8388608
  345.3 27.3 %copy-start.72 = (f32[512,384]{1,0:T(8,128)S(1)}, f32[512,384]{1,0:T(8,128)}, u32[]{:S(2)}) copy-start(f32[512,384]{1,0:T(8,128)} %copy-done.71) | copy-start | bytes 2359300
  345.3 29.0 %slice-start.8 = ((s8[4718592]{0:T(1024)(128)(4,1)}), s8[524288]{0:T(1024)(128)(4,1)S(1)}, s32[]{:S(2)}) async-start(s8[4718592]{0:T(1024)(128)(4,1)} %bitcast.243), calls=%async_computation.10 | async-start | bytes 1048576
  345.3 32.9 %collective-permute-start.35 = (bf16[2,2,2,224,384]{4,3,0,1,2:T(8,128)(2,1)S(1)}, bf16[2,2,2,224,384]{4,3,0,1,2:T(8,128)(2,1)S(1)}, u32[]{:S(2)}, u32[]{:S(2)}) collective-permute-start(bf16[2,2,2,224,384]{4,3,0,1,2:T(8,128)(2,1)S(1)} %pad_maximum_fusion.2), channel_id=1, source_target_pairs={{0,2},{2,0},{4,6},{6,4},{8,10},{10,8},{12,14},{14,12},{16,18},{18,... | collective-permute-start | bytes 4128776 | tf_op jit(solution)/shard_map/ppermute | solution.py:870
  351.2 24.8 %copy-start.66 = (f32[2,192,768]{2,1,0:T(8,128)}, f32[2,192,768]{2,1,0:T(8,128)S(1)}, u32[]{:S(2)}) copy-start(f32[2,192,768]{2,1,0:T(8,128)S(1)} %get-tuple-element.211) | copy-start | bytes 3538948
  351.2 24.8 %copy-start.67 = (f32[2,192,768]{2,1,0:T(8,128)}, f32[2,192,768]{2,1,0:T(8,128)S(1)}, u32[]{:S(2)}) copy-start(f32[2,192,768]{2,1,0:T(8,128)S(1)} %get-tuple-element.212) | copy-start | bytes 3538948
  352.3 30.2 %collective-permute-start.32 = (bf16[384,768]{1,0:T(8,128)(2,1)}, bf16[384,768]{1,0:T(8,128)(2,1)}, u32[]{:S(2)}, u32[]{:S(2)}) collective-permute-start(bf16[384,768]{1,0:T(8,128)(2,1)} %pad_maximum_fusion.9), channel_id=1, source_target_pairs={{0,16},{2,18},{4,20},{6,22},{8,24},{10,26},{12,28},{14,30},{16,0},... | collective-permute-start | bytes 1769480 | tf_op jit(solution)/shard_map/ppermute | solution.py:870
  377.2 17.3 %collective-permute-start.38 = (bf16[2,2,224,384]{3,2,0,1:T(8,128)(2,1)}, bf16[2,2,224,384]{3,2,0,1:T(8,128)(2,1)}, u32[]{:S(2)}, u32[]{:S(2)}) collective-permute-start(bf16[2,2,224,384]{3,2,0,1:T(8,128)(2,1)} %pad_maximum_fusion.7), channel_id=1, source_target_pairs={{0,2},{2,0},{4,6},{6,4},{8,10},{10,8},{12,14},{14,12},{16,18},{18,... | collective-permute-start | bytes 2064392 | tf_op jit(solution)/shard_map/ppermute | solution.py:870
  380.8 17.2 %collective-permute-start.36 = (bf16[2,2,224,384]{3,2,0,1:T(8,128)(2,1)}, bf16[2,2,224,384]{3,2,0,1:T(8,128)(2,1)}, u32[]{:S(2)}, u32[]{:S(2)}) collective-permute-start(bf16[2,2,224,384]{3,2,0,1:T(8,128)(2,1)} %pad_maximum_fusion.6), channel_id=1, source_target_pairs={{0,4},{2,6},{4,0},{6,2},{8,12},{10,14},{12,8},{14,10},{16,20},{18,... | collective-permute-start | bytes 2064392 | tf_op jit(solution)/shard_map/ppermute | solution.py:870
  382.5 15.5 %copy-start.62 = (f32[2,2,2,192,384]{4,3,0,1,2:T(8,128)S(1)}, f32[2,2,2,192,384]{4,3,0,1,2:T(8,128)}, u32[]{:S(2)}) copy-start(f32[2,2,2,192,384]{4,3,0,1,2:T(8,128)} %copy-done.61) | copy-start | bytes 7077892
  401.5 16.0 %collective-permute-start.39 = (bf16[2,224,768]{2,1,0:T(8,128)(2,1)S(1)}, bf16[2,224,768]{2,1,0:T(8,128)(2,1)S(1)}, u32[]{:S(2)}, u32[]{:S(2)}) collective-permute-start(bf16[2,224,768]{2,1,0:T(8,128)(2,1)S(1)} %pad_maximum_fusion.8), channel_id=1, source_target_pairs={{0,8},{2,10},{4,12},{6,14},{8,0},{10,2},{12,4},{14,6},{16,24},{18,... | collective-permute-start | bytes 2064392 | tf_op jit(solution)/shard_map/ppermute | solution.py:870
  417.7 19.0 %copy-start.87 = (f32[8,256]{1,0:T(8,128)S(1)}, f32[8,256]{1,0:T(8,128)}, u32[]{:S(2)}) copy-start(f32[8,256]{1,0:T(8,128)} %get-tuple-element.193) | copy-start | bytes 24580
  417.8 16.0 %collective-permute-start.40 = (bf16[224,768]{1,0:T(8,128)(2,1)S(1)}, bf16[224,768]{1,0:T(8,128)(2,1)S(1)}, u32[]{:S(2)}, u32[]{:S(2)}) collective-permute-start(bf16[224,768]{1,0:T(8,128)(2,1)S(1)} %pad_maximum_fusion.11), channel_id=1, source_target_pairs={{0,16},{2,18},{4,20},{6,22},{8,24},{10,26},{12,28},{14,30},{16,0},... | collective-permute-start | bytes 1032200 | tf_op jit(solution)/shard_map/ppermute | solution.py:870
  461.4 23.5 %slice-start.9 = ((s8[9437184]{0:T(1024)(128)(4,1)}), s8[4194304]{0:T(1024)(128)(4,1)S(1)}, s32[]{:S(2)}) async-start(s8[9437184]{0:T(1024)(128)(4,1)} %bitcast.270), calls=%async_computation.11 | async-start | bytes 8388608
  461.4 23.5 %slice-start.10 = ((s8[9437184]{0:T(1024)(128)(4,1)}), s8[4194304]{0:T(1024)(128)(4,1)S(1)}, s32[]{:S(2)}) async-start(s8[9437184]{0:T(1024)(128)(4,1)} %bitcast.270), calls=%async_computation.12 | async-start | bytes 8388608
  466.5 18.4 %slice-start.11 = ((s8[9437184]{0:T(1024)(128)(4,1)}), s8[1048576]{0:T(1024)(128)(4,1)S(1)}, s32[]{:S(2)}) async-start(s8[9437184]{0:T(1024)(128)(4,1)} %bitcast.270), calls=%async_computation.13 | async-start | bytes 2097152
  475.5 1.4 collective-permute-start.26
  476.8 7.2 %collective-permute-start.27 = (f32[169,128]{1,0:T(8,128)S(1)}, f32[169,128]{1,0:T(8,128)S(1)}, u32[]{:S(2)}, u32[]{:S(2)}) collective-permute-start(f32[169,128]{1,0:T(8,128)S(1)} %bitcast_add_fusion.19), channel_id=1, source_target_pairs={{0,2},{2,0},{4,6},{6,4},{8,10},{10,8},{12,14},{14,12},{16,18},{18,... | collective-permute-start | bytes 259592 | tf_op jit(solution)/shard_map/ppermute | solution.py:886
  484.0 17.3 %copy-start.75 = (bf16[1,512,1536]{2,1,0:T(8,128)(2,1)S(1)}, bf16[1,512,1536]{2,1,0:T(8,128)(2,1)}, u32[]{:S(2)}) copy-start(bf16[1,512,1536]{2,1,0:T(8,128)(2,1)} %param.21) | copy-start | bytes 4718596
  484.1 7.0 %collective-permute-start.28 = (f32[169,128]{1,0:T(8,128)S(1)}, f32[169,128]{1,0:T(8,128)S(1)}, u32[]{:S(2)}, u32[]{:S(2)}) collective-permute-start(f32[169,128]{1,0:T(8,128)S(1)} %fusion.115), channel_id=1, source_target_pairs={{0,4},{2,6},{4,0},{6,2},{8,12},{10,14},{12,8},{14,10},{16,20},{18,... | collective-permute-start | bytes 259592 | tf_op jit(solution)/shard_map/ppermute | solution.py:886
  491.0 9.5 %collective-permute-start.29 = (f32[169,128]{1,0:T(8,128)S(1)}, f32[169,128]{1,0:T(8,128)S(1)}, u32[]{:S(2)}, u32[]{:S(2)}) collective-permute-start(f32[169,128]{1,0:T(8,128)S(1)} %add.253), channel_id=1, source_target_pairs={{0,8},{2,10},{4,12},{6,14},{8,0},{10,2},{12,4},{14,6},{16,24},{18,... | collective-permute-start | bytes 259592 | tf_op jit(solution)/shard_map/ppermute | solution.py:886
  500.5 9.5 %collective-permute-start.30 = (f32[169,128]{1,0:T(8,128)S(1)}, f32[169,128]{1,0:T(8,128)S(1)}, u32[]{:S(2)}, u32[]{:S(2)}) collective-permute-start(f32[169,128]{1,0:T(8,128)S(1)} %add.254), channel_id=1, source_target_pairs={{0,16},{2,18},{4,20},{6,22},{8,24},{10,26},{12,28},{14,30},{16,0},... | collective-permute-start | bytes 259592 | tf_op jit(solution)/shard_map/ppermute | solution.py:886
  (82 other events, 476.3 us)
Sparse Core Ops, SparseCore 0:
  54.0 24.0 all-gather.2
  435.0 177.4 all-gather.4

commit v6 on v5

--- a/solution.py
+++ b/solution.py
@@ -964,7 +964,6 @@
 
     own_ext, other_ext = mine(normed_ext, 1)
     normed = normed_ext.reshape(2, half + EDGE, width)[:, EDGE:].reshape(tokens, width)
-    own_normed, other_normed = mine(normed, 1)
 
     small = jnp.pad(jnp.stack([step_bias, decay_log, skip_gain]), ((0, 5), (0, TILE - HEADS)))
     bias_row = conv_bias[None]
@@ -1056,7 +1055,7 @@
             out_specs=[own_lanes((2, half))] + [whole_block(MESSAGE)] * QUARTERS,
         ),
         out_shape=[shape((2, half, INNER))] + [shape(MESSAGE, BF16)] * QUARTERS,
-        compiler_params=params(16),
+        compiler_params=params(60),
         cost_estimate=cost(8),
         name="states",
     )(member, conv_input, conv_weight, bias_row, step_q, sum_q, bt, column_direction)
@@ -1076,7 +1075,8 @@
 
     def while_states_cross(sent):
         kept["rows"] = lax.ppermute(tie(rows_of, sent), "fsdp", other)[:INNER]
-        kept["gate"] = dot_last(tie(own_normed, sent), gate_rows)
+        kept["normed"] = mine(tie(normed, sent), 1)
+        kept["gate"] = dot_last(kept["normed"][0], gate_rows)
         return inside(0)(sent) + (kept["gate"],)
 
     def while_first_states(sent):
@@ -1112,7 +1112,7 @@
 
     def while_states_return(sent):
         kept["z"] = (
-            kept["gate"] + dot_last(tie(other_normed, sent), kept["rows"])
+            kept["gate"] + dot_last(tie(kept["normed"][1], sent), kept["rows"])
         ).reshape(2, half, INNER)
         return (kept["z"],)
 
@@ -1124,6 +1124,7 @@
         [while_states_cross, while_first_states, inside(half_grid), while_states_return],
     )
     gate_rows_other = kept["rows"]
+    own_normed, other_normed = kept["normed"]
     y_inside, z, grad_normed_out = kept["inside"], kept["z"], kept["grad"]
 
     token_rows = row_block(INNER)

time: 643 us -> 651 us (1.012)
    unnamed x212 -> x214, local copies, waits for them, and re-layouts: 18.6 us -> 23.3 us
  transfers between devices with their start and end apart: 43 -> 43, of which waited for: 22 -> 23; matrix products, arithmetic and copies ran while one was open for 23% -> 23% of each run, Pallas kernels for 15% -> 14%
where the time goes in v6:
time: 651 us; the launch traced here: 645 us
  waiting for transfers between devices  227 us (35%)
  Pallas kernels  144 us (22%)
  matrix products  99.5 us (15%)
  starting transfers between devices  59.3 us (9%)
  local copies, waits for them, and re-layouts  55 us (8%)
  other arithmetic  43 us (7%)
  between operations  16.2 us (2%)
    all_gather x1, waiting for transfers between devices, local(): gathered = lax.all_gather(shard, 'seq', axis=0)  100 us
    ppermute x12, waiting for transfers between devices, send(): lax.ppermute(away, self.axis, [(i, i ^ 1 << bit) for i in range(self.coun...  61.3 us
    dot_general x5, matrix products, dot_last(): lax.dot_general(left, right, (((1,), (1,)), ((), ())), preferred_element_...  41.9 us
    pallas_call x2, Pallas kernels, work(): pl.pallas_call(intra_back_kernel, grid=(half_grid,), in_specs=shifted(spe...  37.4 us
    dot_general x7, matrix products, dot(): return jnp.dot(left, right, preferred_element_type=F32)  29.7 us
    dot_general x8, matrix products, dot_first(): lax.dot_general(left, right, (((0,), (0,)), ((), ())), preferred_element_...  27.8 us
    add x16, other arithmetic, add(): self.values[i] = value + self.sent[..., begin:end, :].astype(F32)  23.4 us
    ppermute x12, waiting for transfers between devices, swap(): return lax.ppermute(value, axis, [(i, i ^ by) for i in range(count)])  23.3 us
  transfers between devices with their start and end apart: 43, of which 23 were waited for; matrix products, arithmetic and copies ran while one was open for 23% of the time, Pallas kernels for 14%

profile of v6, /device:TPU:0, one launch (start us, length us, event | category | flops | bytes accessed | tf_op | source)
XLA Modules:
  0.0 644.7 jit_solution(2681567932844063614)
XLA Ops:
  7.3 5.2 slice.238
  12.9 4.4 collective-permute-start
  22.8 7.9 %fusion.86 = f32[544,3376]{1,0:T(8,128)} fusion(bf16[544,768]{1,0:T(8,128)(2,1)S(1)} %broadcast_select_fusion, bf16[3376,768]{1,0:T(8,128)(2,1)} %slice.238), kind=kOutput, calls=%fused_computation.197 | convolution fusion | flops 2820931584 | bytes 13367296 | tf_op jit(solution)/shard_map/dot_general | solution.py:76
  30.8 7.2 %convolution_add_fusion = f32[544,3376]{1,0:T(8,128)S(1)} fusion(f32[544,3376]{1,0:T(8,128)} %fusion.86, bf16[3376,768]{1,0:T(8,128)(2,1)} %collective-permute-done.1, pred[]{:T(512)S(6)} %eq.4, bf16[544,1536]{1,0:T(8,128)(2,1)S(1)} %fusion.16), kind=kOutput, calls=%fused_computation.4 | convolution fusion | flops 2823185920 | bytes 21549056 | tf_op jit(solution)/shard_map/dot_general | solution.py:76
  48.4 12.6 %states.1 = (f32[2,256,3072]{2,1,0:T(8,128)}, bf16[2,144,768]{2,1,0:T(8,128)(2,1)}, bf16[2,144,768]{2,1,0:T(8,128)(2,1)}, bf16[2,144,768]{2,1,0:T(8,128)(2,1)}, bf16[2,144,768]{2,1,0:T(8,128)(2,1)}) custom-call(s32[1]{0:T(128)} %bitcast.1.member, f32[2,272,3376]{2,1,0:T(8,128)} %bitcast.205, f32[4,3328]{1,0:T(4,128)} %weight.11, f32[1,3328]{1,0:T(1,128)} %copy-done.27, ...), custom_call_target="tpu_custom_call" | custom-call | bytes 27200000 | tf_op jit(solution)/shard_map/states/pallas_call | solution.py:1041
  61.3 3.4 fusion.25
  64.7 2.5 collective-permute-start.2
  69.5 10.1 %inside.2.refs_0_ = f32[2,256,3072]{2,1,0:T(8,128)} custom-call(f32[2,256,3072]{2,1,0:T(8,128)} %get-tuple-element.125.x_ref, f32[4,2,256,16]{3,2,1,0:T(8,128)} %copy-done.1, f32[4,2,256,16]{3,2,1,0:T(8,128)} %copy-done.2, f32[4,2,16,256]{3,2,1,0:T(8,128)} %copy-done.9, f32[2,256,256]{2,1,0:T(8,128)} %copy-done.10, f32[1,3072]{1,0:T(1,128)} %broadcast_in_dim_reshape.3.skip), custom_call_target="tpu_custom_call" | custom-call | bytes 27200000 | tf_op jit(solution)/shard_map/inside/pallas_call | solution.py:1097
  79.6 2.4 broadcast_select_fusion.1
  82.0 7.2 %fusion.9 = f32[512,3072]{1,0:T(8,128)} fusion(bf16[512,768]{1,0:T(8,128)(2,1)S(1)} %get-tuple-element.210, bf16[6448,768]{1,0:T(8,128)(2,1)} %bitcast.212), kind=kOutput, calls=%fused_computation.21 | convolution fusion | flops 2415919104 | bytes 11796480 | tf_op jit(solution)/shard_map/dot_general | solution.py:76
  90.2 4.5 collective-permute-start.5
  94.7 9.8 %fusion.87 = f32[512,3072]{1,0:T(8,128)} fusion(bf16[512,1536]{1,0:T(8,128)(2,1)} %bitcast.259, bf16[3072,1536]{1,0:T(8,128)(2,1)} %all-gather.3.cloned.1.call-done), kind=kOutput, calls=%fused_computation.198 | convolution fusion | flops 4831838208 | bytes 17301504 | tf_op jit(solution)/shard_map/dot_general | solution.py:76
  104.7 4.7 collective-permute-start.6
  109.5 9.2 %inside.3.y_ref = f32[2,256,3072]{2,1,0:T(8,128)} custom-call(f32[2,256,3072]{2,1,0:T(8,128)} %get-tuple-element.125.x_ref, f32[4,2,256,16]{3,2,1,0:T(8,128)} %copy-done.1, f32[4,2,256,16]{3,2,1,0:T(8,128)} %copy-done.2, f32[4,2,16,256]{3,2,1,0:T(8,128)} %copy-done.9, f32[2,256,256]{2,1,0:T(8,128)} %copy-done.10, ...), custom_call_target="tpu_custom_call", output_to_operand_aliasing={{}: (6, {})} | custom-call | bytes 27200000 | tf_op jit(solution)/shard_map/inside/pallas_call | solution.py:1097
  124.8 9.8 %convolution_add_fusion.1 = f32[512,3072]{1,0:T(8,128)} fusion(f32[512,3072]{1,0:T(8,128)} %fusion.9, bf16[512,768]{1,0:T(8,128)(2,1)} %get-tuple-element.128, bf16[6448,768]{1,0:T(8,128)(2,1)} %collective-permute-done.7), kind=kOutput, calls=%fused_computation.15 | convolution fusion | flops 2417491968 | bytes 18087936 | tf_op jit(solution)/shard_map/dot_general | solution.py:76
  135.3 6.4 collective-permute-done.8.refs_1_
  143.2 17.8 %gates.1 = (bf16[2,256,3072]{2,1,0:T(8,128)(2,1)S(1)}, bf16[2,256,3072]{2,1,0:T(8,128)(2,1)S(1)}, f32[2,256,3072]{2,1,0:T(8,128)}, bf16[2,144,768]{2,1,0:T(8,128...) custom-call(s32[1]{0:T(128)} %bitcast.1.member, ...), custom_call_target="tpu_custom_call" | custom-call | bytes 47600000 | tf_op jit(solution)/shard_map/gates/pallas_call | solution.py:1132
  161.1 4.6 convolution_convert_fusion.2
  165.8 4.4 convolution_convert_fusion
  174.2 7.0 %convert_add_fusion.1 = f32[3072,768]{1,0:T(8,128)} fusion(bf16[3072,768]{1,0:T(8,128)(2,1)} %collective-permute-done.15, bf16[512,3072]{1,0:T(8,128)(2,1)S(1)} %bitcast.218, bf16[512,768]{1,0:T(8,128)(2,1)} %copy-done.51), kind=kOutput, calls=%fused_computation.1 | convolution fusion | flops 2420637696 | bytes 18087936 | tf_op jit(solution)/shard_map/dot_general | solution.py:86
  181.2 4.7 convert_add_fusion.2
  185.9 6.8 %collective-permute-done.13.refs_3_ = bf16[2,144,768]{2,1,0:T(8,128)(2,1)S(1)} collective-permute-done((bf16[2,144,768]{2,1,0:T(8,128)(2,1)}, bf16[2,144,768]{2,1,0:T(8,128)(2,1)S(1)}, u32[]{:S(2)}, u32[]{:S(2)}) %collective-permute-start.13) | collective-permute-done | bytes 442400 | tf_op jit(solution)/shard_map/ppermute | solution.py:777
  197.0 4.1 fusion.32
  203.4 18.7 %inside_back.2 = (f32[2,256,3072]{2,1,0:T(8,128)}, bf16[2,256,3072]{2,1,0:T(8,128)(2,1)}, f32[2,256,256]{2,1,0:T(8,128)}, f32[4,2,256,128]{3,2,1,0:T(8,128)}, f32[2,256,128]{2,1,0:T(8,128)}) custom-call(f32[2,256,3072]{2,1,0:T(8,128)} %get-tuple-element.125.x_ref, f32[2,256,3072]{2,1,0:T(8,128)} %get-tuple-element.155.grad_ref, ...), custom_call_target="tpu_custom_call" | custom-call | bytes 57800000 | tf_op jit(solution)/shard_map/inside_back/pallas_call | solution.py:1246
  222.1 2.3 collective-permute-done.16.refs_1_.refs_4_
  228.0 18.8 %inside_back.3 = (f32[2,256,3072]{2,1,0:T(8,128)}, bf16[2,256,3072]{2,1,0:T(8,128)(2,1)}, f32[2,256,256]{2,1,0:T(8,128)}, f32[4,2,256,128]{3,2,1,0:T(8,128)}, f32[2,256,128]{2,1,0:T(8,128)}) custom-call(f32[2,256,3072]{2,1,0:T(8,128)} %get-tuple-element.125.x_ref, ...), custom_call_target="tpu_custom_call", output_to_operand_aliasing={{0}: (15, {}), {1}: (16, {}), {3}: (17, {})} | custom-call | bytes 57800000 | tf_op jit(solution)/shard_map/inside_back/pallas_call | solution.py:1246
  246.8 10.4 %collective-permute-done.17.refs_5_ = bf16[2,144,768]{2,1,0:T(8,128)(2,1)} collective-permute-done((bf16[2,144,768]{2,1,0:T(8,128)(2,1)}, bf16[2,144,768]{2,1,0:T(8,128)(2,1)}, u32[]{:S(2)}, u32[]{:S(2)}) %collective-permute-start.17) | collective-permute-done | bytes 442400 | tf_op jit(solution)/shard_map/ppermute | solution.py:803
  260.2 2.0 spread.3
  265.8 3.7 bitcast_add_fusion.1
  269.6 5.3 bitcast_add_fusion
  274.9 7.8 %collective-permute-done.20.refs_3_ = bf16[2,144,768]{2,1,0:T(8,128)(2,1)S(1)} collective-permute-done((bf16[2,144,768]{2,1,0:T(8,128)(2,1)S(1)}, bf16[2,144,768]{2,1,0:T(8,128)(2,1)S(1)}, u32[]{:S(2)}, u32[]{:S(2)}) %collective-permute-start.20) | collective-permute-done | bytes 442400 | tf_op jit(solution)/shard_map/ppermute | solution.py:777
  289.8 13.9 %channels.1 = (bf16[2,256,3072]{2,1,0:T(8,128)(2,1)}, f32[2,16,3072]{2,1,0:T(8,128)}, bf16[2,16,3072]{2,1,0:T(8,128)(2,1)}, bf16[2,256,3072]{2,1,0:T(8,128)(2,1)...) custom-call(f32[2,256,3072]{2,1,0:T(8,128)} %get-tuple-element.156.known_ref, ...), custom_call_target="tpu_custom_call" | custom-call | bytes 40800000 | tf_op jit(solution)/shard_map/channels/pallas_call | solution.py:1303
  303.7 6.4 last.1
  311.9 2.2 slice.191
  317.6 2.4 bitcast_add_fusion.5
  323.4 3.1 convolution_convert_fusion.1
  327.7 3.2 collective-permute-start.31
  330.9 4.7 collective-permute-done.34
  337.3 2.8 convert_add_fusion
  340.1 2.8 fusion.83
  342.9 2.2 copy-done.50
  346.5 2.5 collective-permute-start.37
  350.1 2.2 fusion.46
  353.9 3.5 collective-permute-done.31
  360.1 2.0 collective-permute-start.32
  362.1 17.6 %collective-permute-done.37 = bf16[2,2,2,224,384]{4,3,0,1,2:T(8,128)(2,1)} collective-permute-done((bf16[2,2,2,224,384]{4,3,0,1,2:T(8,128)(2,1)}, bf16[2,2,2,224,384]{4,3,0,1,2:T(8,128)(2,1)}, u32[]{:S(2)}, u32[]{:S(2)}) %collective-permute-start.37) | collective-permute-done | bytes 1376288 | tf_op jit(solution)/shard_map/ppermute | solution.py:870
  391.9 9.8 %collective-permute-done.38 = bf16[2,2,224,384]{3,2,0,1:T(8,128)(2,1)} collective-permute-done((bf16[2,2,224,384]{3,2,0,1:T(8,128)(2,1)}, bf16[2,2,224,384]{3,2,0,1:T(8,128)(2,1)}, u32[]{:S(2)}, u32[]{:S(2)}) %collective-permute-start.38) | collective-permute-done | bytes 688160 | tf_op jit(solution)/shard_map/ppermute | solution.py:870
  402.9 2.4 collective-permute-done.36
  408.7 2.1 collective-permute-start.39
  410.9 14.0 %collective-permute-done.39 = bf16[2,224,768]{2,1,0:T(8,128)(2,1)S(1)} collective-permute-done((bf16[2,224,768]{2,1,0:T(8,128)(2,1)S(1)}, bf16[2,224,768]{2,1,0:T(8,128)(2,1)S(1)}, u32[]{:S(2)}, u32[]{:S(2)}) %collective-permute-start.39) | collective-permute-done | bytes 688160 | tf_op jit(solution)/shard_map/ppermute | solution.py:870
  425.1 2.1 collective-permute-start.40
  427.2 14.0 %collective-permute-done.40 = bf16[224,768]{1,0:T(8,128)(2,1)S(1)} collective-permute-done((bf16[224,768]{1,0:T(8,128)(2,1)S(1)}, bf16[224,768]{1,0:T(8,128)(2,1)S(1)}, u32[]{:S(2)}, u32[]{:S(2)}) %collective-permute-start.40) | collective-permute-done | bytes 344096 | tf_op jit(solution)/shard_map/ppermute | solution.py:870
  444.1 10.6 %sums.1 = f32[8,3072]{1,0:T(8,128)} custom-call(f32[2,272,3376]{2,1,0:T(8,128)} %bitcast.209, bf16[2,256,3072]{2,1,0:T(8,128)(2,1)} %get-tuple-element.192.grad_mix_ref, f32[2,256,3072]{2,1,0:T(8,128)} %get-tuple-element.155.grad_ref, f32[2,256,3072]{2,1,0:T(8,128)} %get-tuple-element.125.x_ref), custom_call_target="tpu_custom_call" | custom-call | bytes 34000000 | tf_op jit(solution)/shard_map/sums/pallas_call | solution.py:1499
  456.8 5.1 fusion.7
  461.9 5.0 fusion.2
  468.6 5.1 fusion.4
  473.7 5.1 fusion
  484.8 6.2 collective-permute-done.27
  492.5 6.2 fusion.30
  498.8 9.3 %collective-permute-done.29 = f32[169,128]{1,0:T(8,128)S(1)} collective-permute-done((f32[169,128]{1,0:T(8,128)S(1)}, f32[169,128]{1,0:T(8,128)S(1)}, u32[]{:S(2)}, u32[]{:S(2)}) %collective-permute-start.29) | collective-permute-done | bytes 86560 | tf_op jit(solution)/shard_map/ppermute | solution.py:886
  509.0 2.1 fusion.23
  511.2 6.3 collective-permute-done.30
  521.0 100.0 %all-gather.5.cloned.1.call-done.gate_rows.last_rows.out_rows = bf16[16,608,768]{2,1,0:T(8,128)(2,1)} async-done(((bf16[1,608,768]{2,1,0:T(8,128)(2,1)}), bf16[16,608,768]{2,1,0:T(8,128)(2,1)}) %all-gather.5.cloned.1.call-update) | async-done | bytes 14942224 | tf_op jit(solution)/shard_map/all_gather | solution.py:1474
  621.0 16.4 %finish.1 = (f32[6448,768]{1,0:T(8,128)}, f32[1536,1536]{1,0:T(8,128)}) custom-call(bf16[16,608,768]{2,1,0:T(8,128)(2,1)} %all-gather.5.cloned.1.call-done.gate_rows.last_rows.out_rows, bf16[16,608,768]{2,1,0:T(8,128)(2,1)} %all-gather.5.cloned.1.call-done.gate_rows.last_rows.out_rows, ...), custom_call_target="tpu_custom_call" | custom-call | bytes 47600000 | tf_op jit(solution)/shard_map/finish/pallas_call | solution.py:1536
  (386 shorter events, 109.9 us)
Async XLA Ops:
  7.2 87.5 %all-gather.3.cloned.1.call-start = ((), (), s32[]{:S(2)}) async-start(), calls=%async_computation | async-start | bytes 14155776 | tf_op jit(solution)/shard_map/all_gather | solution.py:1064
  12.5 18.3 %collective-permute-start.1 = (bf16[3376,768]{1,0:T(8,128)(2,1)}, bf16[3376,768]{1,0:T(8,128)(2,1)}, u32[]{:S(2)}, u32[]{:S(2)}) collective-permute-start(bf16[3376,768]{1,0:T(8,128)(2,1)} %slice.238), channel_id=1, source_target_pairs={{0,1},{1,0},{2,3},{3,2},{4,5},{5,4},{6,7},{7,6},{8,9},{9,8},{10,11... | collective-permute-start | bytes 15556616 | tf_op jit(solution)/shard_map/ppermute | solution.py:937
  12.9 7.1 %collective-permute-start = (bf16[2,16,1536]{2,1,0:T(8,128)(2,1)S(1)}, bf16[2,16,1536]{2,1,0:T(8,128)(2,1)S(1)}, u32[]{:S(2)}, u32[]{:S(2)}) collective-permute-start(bf16[2,16,1536]{2,1,0:T(8,128)(2,1)S(1)} %slice.237), channel_id=1, source_target_pairs={{0,2},{2,4},{4,6},{6,8},{8,10},{10,12},{12,14},{14,16},{16,18},{18... | collective-permute-start | bytes 294920 | tf_op jit(solution)/shard_map/ppermute | solution.py:940
  17.4 20.6 %copy-start.27 = (f32[1,3328]{1,0:T(1,128)}, f32[1,3328]{1,0:T(1,128)S(1)}, u32[]{:S(2)}) copy-start(f32[1,3328]{1,0:T(1,128)S(1)} %broadcast_in_dim.8.bias) | copy-start | bytes 39940
  18.2 19.8 %copy-start.33 = (f32[8,128]{1,0:T(8,128)}, f32[8,128]{1,0:T(8,128)S(1)}, u32[]{:S(2)}) copy-start(f32[8,128]{1,0:T(8,128)S(1)} %select_maximum_fusion.small) | copy-start | bytes 12292
  22.8 15.2 %slice-start = ((s8[9904128]{0:T(1024)(128)(4,1)}), s8[4194304]{0:T(1024)(128)(4,1)S(1)}, s32[]{:S(2)}) async-start(s8[9904128]{0:T(1024)(128)(4,1)} %bitcast.214), calls=%async_computation.2 | async-start | bytes 8388608
  48.4 94.7 %copy-start.4 = (f32[2,256,256]{2,1,0:T(8,128)}, f32[2,256,256]{2,1,0:T(8,128)S(1)}, u32[]{:S(2)}) copy-start(f32[2,256,256]{2,1,0:T(8,128)S(1)} %get-tuple-element.130.bc_ref) | copy-start | bytes 1572868
  61.1 559.9 %all-gather.5.cloned.1.call-start = ((), (), s32[]{:S(2)}) async-start(), calls=%async_computation.1 | async-start | bytes 15876096 | tf_op jit(solution)/shard_map/all_gather | solution.py:1474
  61.1 63.6 %collective-permute-start.7 = (bf16[6448,768]{1,0:T(8,128)(2,1)}, bf16[6448,768]{1,0:T(8,128)(2,1)}, u32[]{:S(2)}, u32[]{:S(2)}) collective-permute-start(bf16[6448,768]{1,0:T(8,128)(2,1)} %bitcast.211), channel_id=1, source_target_pairs={{0,1},{1,0},{2,3},{3,2},{4,5},{5,4},{6,7},{7,6},{8,9},{9,8},{10,11... | collective-permute-start | bytes 29712392 | tf_op jit(solution)/shard_map/ppermute | solution.py:1077
  64.7 25.1 %collective-permute-start.2 = (bf16[2,144,768]{2,1,0:T(8,128)(2,1)}, bf16[2,144,768]{2,1,0:T(8,128)(2,1)S(1)}, u32[]{:S(2)}, u32[]{:S(2)}) collective-permute-start(bf16[2,144,768]{2,1,0:T(8,128)(2,1)} %get-tuple-element.114), channel_id=1, source_target_pairs={{0,2},{2,0},{4,6},{6,4},{8,10},{10,8},{12,14},{14,12},{16,18},{18,... | collective-permute-start | bytes 1327112 | tf_op jit(solution)/shard_map/ppermute | solution.py:777
  67.1 22.6 %collective-permute-start.3 = (bf16[2,144,768]{2,1,0:T(8,128)(2,1)S(1)}, bf16[2,144,768]{2,1,0:T(8,128)(2,1)S(1)}, u32[]{:S(2)}, u32[]{:S(2)}) collective-permute-start(bf16[2,144,768]{2,1,0:T(8,128)(2,1)S(1)} %copy-done.91), channel_id=1, source_target_pairs={{0,4},{2,6},{4,0},{6,2},{8,12},{10,14},{12,8},{14,10},{16,20},{18,... | collective-permute-start | bytes 1327112 | tf_op jit(solution)/shard_map/ppermute | solution.py:777
  68.7 21.1 %collective-permute-start.4 = (bf16[2,144,768]{2,1,0:T(8,128)(2,1)}, bf16[2,144,768]{2,1,0:T(8,128)(2,1)S(1)}, u32[]{:S(2)}, u32[]{:S(2)}) collective-permute-start(bf16[2,144,768]{2,1,0:T(8,128)(2,1)} %get-tuple-element.116), channel_id=1, source_target_pairs={{0,6},{2,4},{4,2},{6,0},{8,14},{10,12},{12,10},{14,8},{16,22},{18,... | collective-permute-start | bytes 1327112 | tf_op jit(solution)/shard_map/ppermute | solution.py:777
  90.2 14.3 %collective-permute-start.5 = (bf16[2,144,768]{2,1,0:T(8,128)(2,1)S(1)}, bf16[2,144,768]{2,1,0:T(8,128)(2,1)S(1)}, u32[]{:S(2)}, u32[]{:S(2)}) collective-permute-start(bf16[2,144,768]{2,1,0:T(8,128)(2,1)S(1)} %plane.2.refs_0_), channel_id=1, source_target_pairs={{0,8},{2,10},{4,12},{6,14},{8,16},{10,18},{12,20},{14,22},{16,24},... | collective-permute-start | bytes 1327112 | tf_op jit(solution)/shard_map/ppermute | solution.py:803
  104.7 14.0 %collective-permute-start.6 = (bf16[2,144,768]{2,1,0:T(8,128)(2,1)S(1)}, bf16[2,144,768]{2,1,0:T(8,128)(2,1)S(1)}, u32[]{:S(2)}, u32[]{:S(2)}) collective-permute-start(bf16[2,144,768]{2,1,0:T(8,128)(2,1)S(1)} %link.2), channel_id=1, source_target_pairs={{0,16},{2,18},{4,20},{6,22},{8,24},{10,26},{12,28},{14,30},{1,17},... | collective-permute-start | bytes 1327112 | tf_op jit(solution)/shard_map/ppermute | solution.py:803
  121.2 14.1 %collective-permute-start.10 = (bf16[2,144,768]{2,1,0:T(8,128)(2,1)S(1)}, bf16[2,144,768]{2,1,0:T(8,128)(2,1)S(1)}, u32[]{:S(2)}, u32[]{:S(2)}) collective-permute-start(bf16[2,144,768]{2,1,0:T(8,128)(2,1)S(1)} %get-tuple-element.127), channel_id=1, source_target_pairs={{0,6},{2,4},{4,2},{6,0},{8,14},{10,12},{12,10},{14,8},{16,22},{18,... | collective-permute-start | bytes 1327112 | tf_op jit(solution)/shard_map/ppermute | solution.py:777
  122.3 19.4 %collective-permute-start.8 = (bf16[2,144,768]{2,1,0:T(8,128)(2,1)S(1)}, bf16[2,144,768]{2,1,0:T(8,128)(2,1)S(1)}, u32[]{:S(2)}, u32[]{:S(2)}) collective-permute-start(bf16[2,144,768]{2,1,0:T(8,128)(2,1)S(1)} %get-tuple-element.133), channel_id=1, source_target_pairs={{0,2},{2,0},{4,6},{6,4},{8,10},{10,8},{12,14},{14,12},{16,18},{18,... | collective-permute-start | bytes 1327112 | tf_op jit(solution)/shard_map/ppermute | solution.py:777
  123.4 19.7 %copy-start.26 = (f32[2,256,128]{2,1,0:T(8,128)S(1)}, f32[2,256,128]{2,1,0:T(8,128)}, u32[]{:S(2)}) copy-start(f32[2,256,128]{2,1,0:T(8,128)} %copy-done.25) | copy-start | bytes 786436
  123.4 19.7 %copy-start.34 = (f32[3072]{0:T(1024)S(1)}, f32[3072]{0:T(1024)}, u32[]{:S(2)}) copy-start(f32[3072]{0:T(1024)} %param.19) | copy-start | bytes 36868
  123.4 19.1 %collective-permute-start.9 = (bf16[2,144,768]{2,1,0:T(8,128)(2,1)S(1)}, bf16[2,144,768]{2,1,0:T(8,128)(2,1)S(1)}, u32[]{:S(2)}, u32[]{:S(2)}) collective-permute-start(bf16[2,144,768]{2,1,0:T(8,128)(2,1)S(1)} %get-tuple-element.134), channel_id=1, source_target_pairs={{0,4},{2,6},{4,0},{6,2},{8,12},{10,14},{12,8},{14,10},{16,20},{18,... | collective-permute-start | bytes 1327112 | tf_op jit(solution)/shard_map/ppermute | solution.py:777
  143.1 17.9 %copy-start.3 = (bf16[2,128,3072]{2,1,0:T(8,128)(2,1)}, bf16[2,128,3072]{2,1,0:T(8,128)(2,1)S(1)}, u32[]{:S(2)}) copy-start(bf16[2,128,3072]{2,1,0:T(8,128)(2,1)S(1)} %get-tuple-element.136.entering) | copy-start | bytes 4718596
  143.1 17.9 %copy-start.7 = (f32[2,8,3072]{2,1,0:T(8,128)}, f32[2,8,3072]{2,1,0:T(8,128)S(1)}, u32[]{:S(2)}) copy-start(f32[2,8,3072]{2,1,0:T(8,128)S(1)} %get-tuple-element.137.along) | copy-start | bytes 589828
  143.2 17.9 %copy-start.68 = (bf16[512,768]{1,0:T(8,128)(2,1)S(1)}, bf16[512,768]{1,0:T(8,128)(2,1)}, u32[]{:S(2)}) copy-start(bf16[512,768]{1,0:T(8,128)(2,1)} %get-tuple-element.128) | copy-start | bytes 2359300
  165.7 8.5 %collective-permute-start.15 = (bf16[3072,768]{1,0:T(8,128)(2,1)}, bf16[3072,768]{1,0:T(8,128)(2,1)}, u32[]{:S(2)}, u32[]{:S(2)}) collective-permute-start(bf16[3072,768]{1,0:T(8,128)(2,1)} %convolution_convert_fusion.2), channel_id=1, source_target_pairs={{0,1},{1,0},{2,3},{3,2},{4,5},{5,4},{6,7},{7,6},{8,9},{9,8},{10,11... | collective-permute-start | bytes 14155784 | tf_op jit(solution)/shard_map/ppermute | solution.py:1190
  170.1 11.1 %collective-permute-start.14 = (bf16[1536,1536]{1,0:T(8,128)(2,1)}, bf16[1536,1536]{1,0:T(8,128)(2,1)}, u32[]{:S(2)}, u32[]{:S(2)}) collective-permute-start(bf16[1536,1536]{1,0:T(8,128)(2,1)} %convolution_convert_fusion), channel_id=1, source_target_pairs={{0,1},{1,0},{2,3},{3,2},{4,5},{5,4},{6,7},{7,6},{8,9},{9,8},{10,11... | collective-permute-start | bytes 14155784 | tf_op jit(solution)/shard_map/ppermute | solution.py:1190
  170.7 23.7 %collective-permute-start.11 = (bf16[2,144,768]{2,1,0:T(8,128)(2,1)}, bf16[2,144,768]{2,1,0:T(8,128)(2,1)S(1)}, u32[]{:S(2)}, u32[]{:S(2)}) collective-permute-start(bf16[2,144,768]{2,1,0:T(8,128)(2,1)} %copy-done.40), channel_id=1, source_target_pairs={{0,2},{2,0},{4,6},{6,4},{8,10},{10,8},{12,14},{14,12},{16,18},{18,... | collective-permute-start | bytes 1327112 | tf_op jit(solution)/shard_map/ppermute | solution.py:777
  171.2 23.1 %collective-permute-start.12 = (bf16[2,144,768]{2,1,0:T(8,128)(2,1)}, bf16[2,144,768]{2,1,0:T(8,128)(2,1)S(1)}, u32[]{:S(2)}, u32[]{:S(2)}) collective-permute-start(bf16[2,144,768]{2,1,0:T(8,128)(2,1)} %copy-done.39), channel_id=1, source_target_pairs={{0,4},{2,6},{4,0},{6,2},{8,12},{10,14},{12,8},{14,10},{16,20},{18,... | collective-permute-start | bytes 1327112 | tf_op jit(solution)/shard_map/ppermute | solution.py:777
  172.2 20.4 %collective-permute-start.13 = (bf16[2,144,768]{2,1,0:T(8,128)(2,1)}, bf16[2,144,768]{2,1,0:T(8,128)(2,1)S(1)}, u32[]{:S(2)}, u32[]{:S(2)}) collective-permute-start(bf16[2,144,768]{2,1,0:T(8,128)(2,1)} %copy-done.41), channel_id=1, source_target_pairs={{0,6},{2,4},{4,2},{6,0},{8,14},{10,12},{12,10},{14,8},{16,22},{18,... | collective-permute-start | bytes 1327112 | tf_op jit(solution)/shard_map/ppermute | solution.py:777
  196.0 69.8 %collective-permute-start.21 = (bf16[2,2,2,96,1536]{4,3,2,1,0:T(8,128)(2,1)}, bf16[2,2,2,96,1536]{4,3,2,1,0:T(8,128)(2,1)}, u32[]{:S(2)}, u32[]{:S(2)}) collective-permute-start(bf16[2,2,2,96,1536]{4,3,2,1,0:T(8,128)(2,1)} %fusion.31), channel_id=1, source_target_pairs={{0,2},{2,0},{4,6},{6,4},{8,10},{10,8},{12,14},{14,12},{16,18},{18,... | collective-permute-start | bytes 7077896 | tf_op jit(solution)/shard_map/ppermute | solution.py:870
  201.1 68.5 %collective-permute-start.22 = (bf16[2,2,2,192,768]{4,3,0,1,2:T(8,128)(2,1)}, bf16[2,2,2,192,768]{4,3,0,1,2:T(8,128)(2,1)}, u32[]{:S(2)}, u32[]{:S(2)}) collective-permute-start(bf16[2,2,2,192,768]{4,3,0,1,2:T(8,128)(2,1)} %fusion.32), channel_id=1, source_target_pairs={{0,4},{2,6},{4,0},{6,2},{8,12},{10,14},{12,8},{14,10},{16,20},{18,... | collective-permute-start | bytes 7077896 | tf_op jit(solution)/shard_map/ppermute | solution.py:870
  202.1 22.2 %collective-permute-start.16 = (bf16[2,144,768]{2,1,0:T(8,128)(2,1)S(1)}, bf16[2,144,768]{2,1,0:T(8,128)(2,1)}, u32[]{:S(2)}, u32[]{:S(2)}) collective-permute-start(bf16[2,144,768]{2,1,0:T(8,128)(2,1)S(1)} %copy-done.13), channel_id=1, source_target_pairs={{8,0},{10,2},{12,4},{14,6},{16,8},{18,10},{20,12},{22,14},{24,16},... | collective-permute-start | bytes 1327112 | tf_op jit(solution)/shard_map/ppermute | solution.py:803
  226.3 30.8 %collective-permute-start.17 = (bf16[2,144,768]{2,1,0:T(8,128)(2,1)}, bf16[2,144,768]{2,1,0:T(8,128)(2,1)}, u32[]{:S(2)}, u32[]{:S(2)}) collective-permute-start(bf16[2,144,768]{2,1,0:T(8,128)(2,1)} %link.3), channel_id=1, source_target_pairs={{16,0},{18,2},{20,4},{22,6},{24,8},{26,10},{28,12},{30,14},{17,1},... | collective-permute-start | bytes 1327112 | tf_op jit(solution)/shard_map/ppermute | solution.py:803
  228.0 29.1 %copy-start.16 = (bf16[2,144,768]{2,1,0:T(8,128)(2,1)S(1)}, bf16[2,144,768]{2,1,0:T(8,128)(2,1)}, u32[]{:S(2)}) copy-start(bf16[2,144,768]{2,1,0:T(8,128)(2,1)} %copy-done.14) | copy-start | bytes 1327108
  262.2 20.4 %collective-permute-start.18 = (bf16[2,144,768]{2,1,0:T(8,128)(2,1)S(1)}, bf16[2,144,768]{2,1,0:T(8,128)(2,1)S(1)}, u32[]{:S(2)}, u32[]{:S(2)}) collective-permute-start(bf16[2,144,768]{2,1,0:T(8,128)(2,1)S(1)} %get-tuple-element.163), channel_id=1, source_target_pairs={{0,2},{2,0},{4,6},{6,4},{8,10},{10,8},{12,14},{14,12},{16,18},{18,... | collective-permute-start | bytes 1327112 | tf_op jit(solution)/shard_map/ppermute | solution.py:777
  263.4 19.4 %collective-permute-start.19 = (bf16[2,144,768]{2,1,0:T(8,128)(2,1)S(1)}, bf16[2,144,768]{2,1,0:T(8,128)(2,1)S(1)}, u32[]{:S(2)}, u32[]{:S(2)}) collective-permute-start(bf16[2,144,768]{2,1,0:T(8,128)(2,1)S(1)} %get-tuple-element.164), channel_id=1, source_target_pairs={{0,4},{2,6},{4,0},{6,2},{8,12},{10,14},{12,8},{14,10},{16,20},{18,... | collective-permute-start | bytes 1327112 | tf_op jit(solution)/shard_map/ppermute | solution.py:777
  264.1 18.5 %collective-permute-start.20 = (bf16[2,144,768]{2,1,0:T(8,128)(2,1)S(1)}, bf16[2,144,768]{2,1,0:T(8,128)(2,1)S(1)}, u32[]{:S(2)}, u32[]{:S(2)}) collective-permute-start(bf16[2,144,768]{2,1,0:T(8,128)(2,1)S(1)} %get-tuple-element.165), channel_id=1, source_target_pairs={{0,6},{2,4},{4,2},{6,0},{8,14},{10,12},{12,10},{14,8},{16,22},{18,... | collective-permute-start | bytes 1327112 | tf_op jit(solution)/shard_map/ppermute | solution.py:777
  269.5 15.9 %copy-start.47 = (f32[2,2,2,96,1536]{4,3,2,1,0:T(8,128)}, f32[2,2,2,96,1536]{4,3,2,1,0:T(8,128)S(1)}, u32[]{:S(2)}) copy-start(f32[2,2,2,96,1536]{4,3,2,1,0:T(8,128)S(1)} %bitcast_add_fusion.1) | copy-start | bytes 14155780
  287.8 26.3 %collective-permute-start.23 = (bf16[2,2,96,1536]{3,2,1,0:T(8,128)(2,1)}, bf16[2,2,96,1536]{3,2,1,0:T(8,128)(2,1)}, u32[]{:S(2)}, u32[]{:S(2)}) collective-permute-start(bf16[2,2,96,1536]{3,2,1,0:T(8,128)(2,1)} %fusion.44), channel_id=1, source_target_pairs={{0,4},{2,6},{4,0},{6,2},{8,12},{10,14},{12,8},{14,10},{16,20},{18,... | collective-permute-start | bytes 3538952 | tf_op jit(solution)/shard_map/ppermute | solution.py:870
  288.6 25.6 %collective-permute-start.24 = (bf16[2,2,192,768]{3,2,0,1:T(8,128)(2,1)}, bf16[2,2,192,768]{3,2,0,1:T(8,128)(2,1)}, u32[]{:S(2)}, u32[]{:S(2)}) collective-permute-start(bf16[2,2,192,768]{3,2,0,1:T(8,128)(2,1)} %fusion.45), channel_id=1, source_target_pairs={{0,2},{2,0},{4,6},{6,4},{8,10},{10,8},{12,14},{14,12},{16,18},{18,... | collective-permute-start | bytes 3538952 | tf_op jit(solution)/shard_map/ppermute | solution.py:870
  314.1 8.0 %collective-permute-start.25 = (bf16[2,16,3328]{2,1,0:T(8,128)(2,1)S(1)}, bf16[2,16,3328]{2,1,0:T(8,128)(2,1)S(1)}, u32[]{:S(2)}, u32[]{:S(2)}) collective-permute-start(bf16[2,16,3328]{2,1,0:T(8,128)(2,1)S(1)} %pad_maximum_fusion.12), channel_id=1, source_target_pairs={{2,0},{4,2},{6,4},{8,6},{10,8},{12,10},{14,12},{16,14},{18,16},{20... | collective-permute-start | bytes 638984 | tf_op jit(solution)/shard_map/ppermute | solution.py:1415
  326.5 10.8 %collective-permute-start.33 = (bf16[3072,768]{1,0:T(8,128)(2,1)S(1)}, bf16[3072,768]{1,0:T(8,128)(2,1)S(1)}, u32[]{:S(2)}, u32[]{:S(2)}) collective-permute-start(bf16[3072,768]{1,0:T(8,128)(2,1)S(1)} %convolution_convert_fusion.1), channel_id=1, source_target_pairs={{0,1},{1,0},{2,3},{3,2},{4,5},{5,4},{6,7},{7,6},{8,9},{9,8},{10,11... | collective-permute-start | bytes 14155784 | tf_op jit(solution)/shard_map/ppermute | solution.py:1190
  327.2 8.4 %collective-permute-start.34 = (bf16[512,768]{1,0:T(8,128)(2,1)S(1)}, bf16[512,768]{1,0:T(8,128)(2,1)S(1)}, u32[]{:S(2)}, u32[]{:S(2)}) collective-permute-start(bf16[512,768]{1,0:T(8,128)(2,1)S(1)} %convolution_convert_fusion.3), channel_id=1, source_target_pairs={{0,1},{1,0},{2,3},{3,2},{4,5},{5,4},{6,7},{7,6},{8,9},{9,8},{10,11... | collective-permute-start | bytes 2359304 | tf_op jit(solution)/shard_map/ppermute | solution.py:1190
  327.7 29.7 %collective-permute-start.31 = (bf16[2,384,768]{2,1,0:T(8,128)(2,1)}, bf16[2,384,768]{2,1,0:T(8,128)(2,1)}, u32[]{:S(2)}, u32[]{:S(2)}) collective-permute-start(bf16[2,384,768]{2,1,0:T(8,128)(2,1)} %pad_maximum_fusion.4), channel_id=1, source_target_pairs={{0,8},{2,10},{4,12},{6,14},{8,0},{10,2},{12,4},{14,6},{16,24},{18,... | collective-permute-start | bytes 3538952 | tf_op jit(solution)/shard_map/ppermute | solution.py:870
  346.5 33.3 %collective-permute-start.37 = (bf16[2,2,2,224,384]{4,3,0,1,2:T(8,128)(2,1)}, bf16[2,2,2,224,384]{4,3,0,1,2:T(8,128)(2,1)}, u32[]{:S(2)}, u32[]{:S(2)}) collective-permute-start(bf16[2,2,2,224,384]{4,3,0,1,2:T(8,128)(2,1)} %pad_maximum_fusion.3), channel_id=1, source_target_pairs={{0,4},{2,6},{4,0},{6,2},{8,12},{10,14},{12,8},{14,10},{16,20},{18,... | collective-permute-start | bytes 4128776 | tf_op jit(solution)/shard_map/ppermute | solution.py:870
  352.3 29.2 %slice-start.7 = ((s8[4718592]{0:T(1024)(128)(4,1)}), s8[4194304]{0:T(1024)(128)(4,1)S(1)}, s32[]{:S(2)}) async-start(s8[4718592]{0:T(1024)(128)(4,1)} %bitcast.243), calls=%async_computation.9 | async-start | bytes 8388608
  352.5 27.3 %copy-start.72 = (f32[512,384]{1,0:T(8,128)S(1)}, f32[512,384]{1,0:T(8,128)}, u32[]{:S(2)}) copy-start(f32[512,384]{1,0:T(8,128)} %copy-done.71) | copy-start | bytes 2359300
  352.5 29.0 %slice-start.8 = ((s8[4718592]{0:T(1024)(128)(4,1)}), s8[524288]{0:T(1024)(128)(4,1)S(1)}, s32[]{:S(2)}) async-start(s8[4718592]{0:T(1024)(128)(4,1)} %bitcast.243), calls=%async_computation.10 | async-start | bytes 1048576
  352.5 33.4 %collective-permute-start.35 = (bf16[2,2,2,224,384]{4,3,0,1,2:T(8,128)(2,1)S(1)}, bf16[2,2,2,224,384]{4,3,0,1,2:T(8,128)(2,1)S(1)}, u32[]{:S(2)}, u32[]{:S(2)}) collective-permute-start(bf16[2,2,2,224,384]{4,3,0,1,2:T(8,128)(2,1)S(1)} %pad_maximum_fusion.2), channel_id=1, source_target_pairs={{0,2},{2,0},{4,6},{6,4},{8,10},{10,8},{12,14},{14,12},{16,18},{18,... | collective-permute-start | bytes 4128776 | tf_op jit(solution)/shard_map/ppermute | solution.py:870
  359.0 24.2 %copy-start.66 = (f32[2,192,768]{2,1,0:T(8,128)}, f32[2,192,768]{2,1,0:T(8,128)S(1)}, u32[]{:S(2)}) copy-start(f32[2,192,768]{2,1,0:T(8,128)S(1)} %get-tuple-element.211) | copy-start | bytes 3538948
  359.0 24.2 %copy-start.67 = (f32[2,192,768]{2,1,0:T(8,128)}, f32[2,192,768]{2,1,0:T(8,128)S(1)}, u32[]{:S(2)}) copy-start(f32[2,192,768]{2,1,0:T(8,128)S(1)} %get-tuple-element.212) | copy-start | bytes 3538948
  360.1 30.1 %collective-permute-start.32 = (bf16[384,768]{1,0:T(8,128)(2,1)}, bf16[384,768]{1,0:T(8,128)(2,1)}, u32[]{:S(2)}, u32[]{:S(2)}) collective-permute-start(bf16[384,768]{1,0:T(8,128)(2,1)} %pad_maximum_fusion.9), channel_id=1, source_target_pairs={{0,16},{2,18},{4,20},{6,22},{8,24},{10,26},{12,28},{14,30},{16,0},... | collective-permute-start | bytes 1769480 | tf_op jit(solution)/shard_map/ppermute | solution.py:870
  384.4 17.3 %collective-permute-start.38 = (bf16[2,2,224,384]{3,2,0,1:T(8,128)(2,1)}, bf16[2,2,224,384]{3,2,0,1:T(8,128)(2,1)}, u32[]{:S(2)}, u32[]{:S(2)}) collective-permute-start(bf16[2,2,224,384]{3,2,0,1:T(8,128)(2,1)} %pad_maximum_fusion.7), channel_id=1, source_target_pairs={{0,2},{2,0},{4,6},{6,4},{8,10},{10,8},{12,14},{14,12},{16,18},{18,... | collective-permute-start | bytes 2064392 | tf_op jit(solution)/shard_map/ppermute | solution.py:870
  388.6 16.7 %collective-permute-start.36 = (bf16[2,2,224,384]{3,2,0,1:T(8,128)(2,1)}, bf16[2,2,224,384]{3,2,0,1:T(8,128)(2,1)}, u32[]{:S(2)}, u32[]{:S(2)}) collective-permute-start(bf16[2,2,224,384]{3,2,0,1:T(8,128)(2,1)} %pad_maximum_fusion.6), channel_id=1, source_target_pairs={{0,4},{2,6},{4,0},{6,2},{8,12},{10,14},{12,8},{14,10},{16,20},{18,... | collective-permute-start | bytes 2064392 | tf_op jit(solution)/shard_map/ppermute | solution.py:870
  408.7 16.1 %collective-permute-start.39 = (bf16[2,224,768]{2,1,0:T(8,128)(2,1)S(1)}, bf16[2,224,768]{2,1,0:T(8,128)(2,1)S(1)}, u32[]{:S(2)}, u32[]{:S(2)}) collective-permute-start(bf16[2,224,768]{2,1,0:T(8,128)(2,1)S(1)} %pad_maximum_fusion.8), channel_id=1, source_target_pairs={{0,8},{2,10},{4,12},{6,14},{8,0},{10,2},{12,4},{14,6},{16,24},{18,... | collective-permute-start | bytes 2064392 | tf_op jit(solution)/shard_map/ppermute | solution.py:870
  425.1 19.0 %copy-start.87 = (f32[8,256]{1,0:T(8,128)S(1)}, f32[8,256]{1,0:T(8,128)}, u32[]{:S(2)}) copy-start(f32[8,256]{1,0:T(8,128)} %get-tuple-element.193) | copy-start | bytes 24580
  425.1 16.0 %collective-permute-start.40 = (bf16[224,768]{1,0:T(8,128)(2,1)S(1)}, bf16[224,768]{1,0:T(8,128)(2,1)S(1)}, u32[]{:S(2)}, u32[]{:S(2)}) collective-permute-start(bf16[224,768]{1,0:T(8,128)(2,1)S(1)} %pad_maximum_fusion.11), channel_id=1, source_target_pairs={{0,16},{2,18},{4,20},{6,22},{8,24},{10,26},{12,28},{14,30},{16,0},... | collective-permute-start | bytes 1032200 | tf_op jit(solution)/shard_map/ppermute | solution.py:870
  468.5 23.9 %slice-start.9 = ((s8[9437184]{0:T(1024)(128)(4,1)}), s8[4194304]{0:T(1024)(128)(4,1)S(1)}, s32[]{:S(2)}) async-start(s8[9437184]{0:T(1024)(128)(4,1)} %bitcast.270), calls=%async_computation.11 | async-start | bytes 8388608
  468.6 23.9 %slice-start.10 = ((s8[9437184]{0:T(1024)(128)(4,1)}), s8[4194304]{0:T(1024)(128)(4,1)S(1)}, s32[]{:S(2)}) async-start(s8[9437184]{0:T(1024)(128)(4,1)} %bitcast.270), calls=%async_computation.12 | async-start | bytes 8388608
  473.7 18.8 %slice-start.11 = ((s8[9437184]{0:T(1024)(128)(4,1)}), s8[1048576]{0:T(1024)(128)(4,1)S(1)}, s32[]{:S(2)}) async-start(s8[9437184]{0:T(1024)(128)(4,1)} %bitcast.270), calls=%async_computation.13 | async-start | bytes 2097152
  482.5 1.4 collective-permute-start.26
  483.9 7.2 %collective-permute-start.27 = (f32[169,128]{1,0:T(8,128)S(1)}, f32[169,128]{1,0:T(8,128)S(1)}, u32[]{:S(2)}, u32[]{:S(2)}) collective-permute-start(f32[169,128]{1,0:T(8,128)S(1)} %bitcast_add_fusion.19), channel_id=1, source_target_pairs={{0,2},{2,0},{4,6},{6,4},{8,10},{10,8},{12,14},{14,12},{16,18},{18,... | collective-permute-start | bytes 259592 | tf_op jit(solution)/shard_map/ppermute | solution.py:886
  491.1 18.0 %copy-start.75 = (bf16[1,512,1536]{2,1,0:T(8,128)(2,1)S(1)}, bf16[1,512,1536]{2,1,0:T(8,128)(2,1)}, u32[]{:S(2)}) copy-start(bf16[1,512,1536]{2,1,0:T(8,128)(2,1)} %param.21) | copy-start | bytes 4718596
  491.1 7.6 %collective-permute-start.28 = (f32[169,128]{1,0:T(8,128)S(1)}, f32[169,128]{1,0:T(8,128)S(1)}, u32[]{:S(2)}, u32[]{:S(2)}) collective-permute-start(f32[169,128]{1,0:T(8,128)S(1)} %fusion.115), channel_id=1, source_target_pairs={{0,4},{2,6},{4,0},{6,2},{8,12},{10,14},{12,8},{14,10},{16,20},{18,... | collective-permute-start | bytes 259592 | tf_op jit(solution)/shard_map/ppermute | solution.py:886
  498.6 9.4 %collective-permute-start.29 = (f32[169,128]{1,0:T(8,128)S(1)}, f32[169,128]{1,0:T(8,128)S(1)}, u32[]{:S(2)}, u32[]{:S(2)}) collective-permute-start(f32[169,128]{1,0:T(8,128)S(1)} %add.253), channel_id=1, source_target_pairs={{0,8},{2,10},{4,12},{6,14},{8,0},{10,2},{12,4},{14,6},{16,24},{18,... | collective-permute-start | bytes 259592 | tf_op jit(solution)/shard_map/ppermute | solution.py:886
  508.1 9.3 %collective-permute-start.30 = (f32[169,128]{1,0:T(8,128)S(1)}, f32[169,128]{1,0:T(8,128)S(1)}, u32[]{:S(2)}, u32[]{:S(2)}) collective-permute-start(f32[169,128]{1,0:T(8,128)S(1)} %add.254), channel_id=1, source_target_pairs={{0,16},{2,18},{4,20},{6,22},{8,24},{10,26},{12,28},{14,30},{16,0},... | collective-permute-start | bytes 259592 | tf_op jit(solution)/shard_map/ppermute | solution.py:886
  (83 other events, 396.7 us)
Sparse Core Ops, SparseCore 0:
  61.2 24.0 all-gather.2
  442.4 178.6 all-gather.4
